TPU v7x, 256 devices: a whole 4x4x8 slice. The times are simulated.
256 devices in a mesh: dp: 32 (over z, y), height: 8 (over x, core).
Axes of the slice: x: 4, y: 4, z: 8, core: 2. Of those that a mesh axis runs over, the one named last changes fastest.
Arguments:
- inputs: bfloat16 [64, 48, 72, 1024], P('dp', 'height'), may hold values from -6 to 6
- conv_out: bfloat16 [64, 48, 72, 256], P('dp', 'height'), may hold values from -70 to 70
- grad_out: bfloat16 [64, 48, 72, 256], P('dp', 'height'), may hold values from -12 to 12
- relu_mask: int32 [64, 48, 72, 256], P('dp', 'height'), may hold values 0 or 1
- norm_gain: float32 [256], replicated, may hold values from 0.5 to 2
- weight: bfloat16 [1024, 9, 256], replicated, may hold values from -0.0625 to 0.0625
Outputs:
- input_grad: bfloat16 [64, 48, 72, 1024], P('dp', 'height')
- weight_grad: float32 [1024, 9, 256], P(('dp', 'height'))
All inputs are finite; a program needn't handle non-finite values. No bound on the sum of `relu_mask` on one device may be relied on, other than what follows from the above.
Results may differ from a plain program's by a relative error of at most 0.0049.
Values may be sent and summed in bfloat16 or wider, within the bound.
No kernel may reach another device: no remote copies, remote signals or barrier semaphores. Data moves between devices by JAX's collectives and lax.ppermute only.
A program may use at most 128 MiB of HBM per device.

v0:
```python
import jax
import jax.numpy as jnp
from jax import lax
from jax.sharding import PartitionSpec as P

RATE = 18


EPSILON = 1e-05


def shifted(value, axis, steps):
    count = lax.axis_size(axis)
    first, last = (max(0, -steps), min(count, count - steps))
    return lax.ppermute(value, axis, [(source, source + steps) for source in range(first, last)])


def per_device(inputs, conv_out, grad_out, relu_mask, norm_gain, weight):
    image_count, row_count, col_count, channels_in = inputs.shape
    channels_out = conv_out.shape[3]
    height_size = lax.axis_size("height")
    cell_count = row_count * col_count * height_size
    values = conv_out.astype(jnp.float32)
    passed_grad = grad_out.astype(jnp.float32) * relu_mask.astype(jnp.float32)
    scaled = norm_gain * passed_grad
    first_sum, second_sum = lax.psum(
        (jnp.sum(values, axis=(1, 2)), jnp.sum(values * values, axis=(1, 2))), "height"
    )
    chan_mean = first_sum / cell_count
    inv_std = 1.0 / jnp.sqrt(second_sum / cell_count - chan_mean * chan_mean + EPSILON)
    normed = (values - chan_mean[:, None, None, :]) * inv_std[:, None, None, :]
    grad_sum, cross_sum = lax.psum(
        (jnp.sum(scaled, axis=(1, 2)), jnp.sum(scaled * normed, axis=(1, 2))), "height"
    )
    grad_mean = grad_sum / cell_count
    cross_mean = cross_sum / cell_count
    pre_grad = (
        inv_std[:, None, None, :]
        * (scaled - grad_mean[:, None, None, :] - normed * cross_mean[:, None, None, :])
    ).astype(jnp.bfloat16)
    stored = {0: pre_grad}

    def moved(distance):
        if distance not in stored:
            stored[distance] = shifted(pre_grad, "height", distance)
        return stored[distance]

    pieces = []
    for row_step in (-1, 0, 1):
        whole_part = RATE * row_step // row_count
        row_block = moved(whole_part)
        for col_step in (-1, 0, 1):
            offset = RATE * col_step
            padded = jnp.pad(row_block, ((0, 0), (0, 0), (RATE, RATE), (0, 0)))
            pieces.append(padded[:, :, RATE - offset : RATE - offset + col_count, :])
    stacked = jnp.concatenate(pieces, axis=3).reshape(
        image_count * row_count * col_count, 9 * channels_out
    )
    weight_flat = weight.reshape(channels_in, 9 * channels_out)
    input_grad = lax.dot_general(
        stacked, weight_flat, (((1,), (1,)), ((), ())), preferred_element_type=jnp.float32
    ).astype(jnp.bfloat16)
    input_grad = input_grad.reshape(image_count, row_count, col_count, channels_in)
    input_flat = inputs.reshape(image_count * row_count * col_count, channels_in)
    inv_images = 1.0 / (image_count * lax.axis_size("dp"))
    weight_grad = lax.psum_scatter(
        lax.dot_general(
            input_flat, stacked, (((0,), (0,)), ((), ())), preferred_element_type=jnp.float32
        )
        * inv_images,
        ("dp", "height"),
        scatter_dimension=0,
        tiled=True,
    )
    return (input_grad, weight_grad.reshape(-1, 9, channels_out))


def solution(mesh):
    return jax.shard_map(
        per_device,
        mesh=mesh,
        in_specs=(
            P("dp", "height", None, None),
            P("dp", "height", None, None),
            P("dp", "height", None, None),
            P("dp", "height", None, None),
            P(),
            P(),
        ),
        out_specs=(P("dp", "height", None, None), P(("dp", "height"), None, None)),
        check_vma=False,
    )
```

profile of v0, /device:TPU:1, one launch (start us, length us, event | category | flops | bytes accessed | tf_op | source)
XLA Modules:
  0.0 357.1 jit_solution(15893109396034244252)
XLA Ops:
  7.2 0.0 copy-start
  7.2 0.0 all-reduce.8.cloned.1.call-start
  7.2 1.3 fusion.1
  8.5 15.0 %all-reduce.5 = (f32[2,256]{1,0:T(2,128)S(1)}, f32[2,256]{1,0:T(2,128)S(1)}) all-reduce(f32[2,256]{1,0:T(2,128)S(1)} %get-tuple-element.10, f32[2,256]{1,0:T(2,128)S(1)} %get-tuple-element.11), channel_id=1, replica_groups=mesh['dp'=32,'height'=8] {'height'}, use_global_device_ids=true, to_apply=%region_1.0 | all-reduce | flops 1024 | bytes 8192 | tf_op jit(solution)/shard_map/psum | solution.py:26
  23.5 1.7 fusion.15
  25.3 12.9 %all-reduce.4 = (f32[2,256]{1,0:T(2,128)S(1)}, f32[2,256]{1,0:T(2,128)S(1)}) all-reduce(f32[2,256]{1,0:T(2,128)S(1)} %get-tuple-element.9, f32[2,256]{1,0:T(2,128)S(1)} %get-tuple-element.8), channel_id=1, replica_groups=mesh['dp'=32,'height'=8] {'height'}, use_global_device_ids=true, to_apply=%region_7.0 | all-reduce | flops 1024 | bytes 8192 | tf_op jit(solution)/shard_map/psum | solution.py:32
  38.1 1.8 fusion.8
  39.9 1.3 collective-permute-start
  41.2 5.8 %collective-permute-start.1 = (bf16[2,6,72,256]{3,2,1,0:T(8,128)(2,1)S(1)}, bf16[2,6,72,256]{3,2,1,0:T(8,128)(2,1)S(1)}, u32[]{:S(2)}, u32[]{:S(2)}) collective-permute-start(bf16[2,6,72,256]{3,2,1,0:T(8,128)(2,1)S(1)} %fusion.8), channel_id=1, source_target_pairs={{0,3},{1,4},{2,5},{3,6},{4,7},{8,11},{9,12},{10,13},{11,14},{12,15... | collective-permute-start | bytes 1327112 | tf_op jit(solution)/shard_map/ppermute | solution.py:15
  47.0 4.0 %collective-permute-done = bf16[2,6,72,256]{3,2,1,0:T(8,128)(2,1)S(1)} collective-permute-done((bf16[2,6,72,256]{3,2,1,0:T(8,128)(2,1)S(1)}, bf16[2,6,72,256]{3,2,1,0:T(8,128)(2,1)S(1)}, u32[]{:S(2)}, u32[]{:S(2)}) %collective-permute-start) | collective-permute-done | bytes 442400 | tf_op jit(solution)/shard_map/ppermute | solution.py:15
  51.0 0.1 fusion.9
  51.1 0.1 fusion.10
  51.2 0.1 fusion.11
  51.4 0.1 fusion.12
  51.5 4.8 %collective-permute-done.1 = bf16[2,6,72,256]{3,2,1,0:T(8,128)(2,1)S(1)} collective-permute-done((bf16[2,6,72,256]{3,2,1,0:T(8,128)(2,1)S(1)}, bf16[2,6,72,256]{3,2,1,0:T(8,128)(2,1)S(1)}, u32[]{:S(2)}, u32[]{:S(2)}) %collective-permute-start.1) | collective-permute-done | bytes 442400 | tf_op jit(solution)/shard_map/ppermute | solution.py:15
  56.3 0.1 fusion.13
  56.4 0.1 fusion.14
  56.5 0.0 copy-start.1
  56.5 2.0 copy-done.1
  58.5 0.0 copy-done
  58.5 7.5 %fusion = f32[1024,2304]{0,1:T(8,128)} fusion(bf16[2,6,72,2304]{3,2,1,0:T(8,128)(2,1)S(1)} %fusion.14, bf16[2,6,72,1024]{3,2,1,0:T(8,128)(2,1)S(1)} %copy-done), kind=kOutput, calls=%fused_computation.1 | convolution fusion | flops 4079222784 | bytes 15187968 | tf_op jit(solution)/shard_map/dot_general | solution.py:67
  66.0 0.0 all-reduce.8.cloned.1.call-update
  66.0 6.7 %copy.11 = bf16[1024,9,256]{0,2,1:T(8,128)(2,1)} copy(bf16[1024,9,256]{2,0,1:T(8,128)(2,1)} %param.11) | data formatting | bytes 9437184 | tf_op args[5]
  72.7 9.0 %convolution_convert_fusion = bf16[864,1024]{1,0:T(8,128)(2,1)} fusion(bf16[864,2304]{1,0:T(8,128)(2,1)} %bitcast.20, bf16[1024,2304]{0,1:T(8,128)(2,1)} %bitcast.19), kind=kOutput, calls=%fused_computation.2 | convolution fusion | flops 4077748224 | bytes 10469376 | tf_op jit(solution)/shard_map/dot_general | solution.py:60
  81.7 266.0 %all-reduce.8.cloned.1.call-done = f32[1024,2304]{0,1:T(8,128)} async-done(((f32[1024,2304]{0,1:T(8,128)}), f32[1024,2304]{0,1:T(8,128)}) %all-reduce.8.cloned.1.call-update) | async-done | bytes 9437200
  347.6 1.6 constant_dynamic-slice_fusion
  349.3 1.0 copy.12
  (5 shorter events, 0.1 us)
Async XLA Ops:
  7.2 51.3 %copy-start = (bf16[2,6,72,1024]{3,2,1,0:T(8,128)(2,1)S(1)}, bf16[2,6,72,1024]{3,2,1,0:T(8,128)(2,1)}, u32[]{:S(2)}) copy-start(bf16[2,6,72,1024]{3,2,1,0:T(8,128)(2,1)} %param.6) | copy-start | bytes 5308420
  7.2 340.5 %all-reduce.8.cloned.1.call-start = ((), (), s32[]{:S(2)}) async-start(), calls=%async_computation | async-start | bytes 18874368
  39.9 11.1 %collective-permute-start = (bf16[2,6,72,256]{3,2,1,0:T(8,128)(2,1)S(1)}, bf16[2,6,72,256]{3,2,1,0:T(8,128)(2,1)S(1)}, u32[]{:S(2)}, u32[]{:S(2)}) collective-permute-start(bf16[2,6,72,256]{3,2,1,0:T(8,128)(2,1)S(1)} %fusion.8), channel_id=1, source_target_pairs={{3,0},{4,1},{5,2},{6,3},{7,4},{11,8},{12,9},{13,10},{14,11},{15,12... | collective-permute-start | bytes 1327112 | tf_op jit(solution)/shard_map/ppermute | solution.py:15
  41.2 15.1 %collective-permute-start.1 = (bf16[2,6,72,256]{3,2,1,0:T(8,128)(2,1)S(1)}, bf16[2,6,72,256]{3,2,1,0:T(8,128)(2,1)S(1)}, u32[]{:S(2)}, u32[]{:S(2)}) collective-permute-start(bf16[2,6,72,256]{3,2,1,0:T(8,128)(2,1)S(1)} %fusion.8), channel_id=1, source_target_pairs={{0,3},{1,4},{2,5},{3,6},{4,7},{8,11},{9,12},{10,13},{11,14},{12,15... | collective-permute-start | bytes 1327112 | tf_op jit(solution)/shard_map/ppermute | solution.py:15
  56.5 2.0 copy-start.1
Sparse Core Ops, SparseCore 0:
  66.1 281.4 all-reduce.7
where the time goes:
time: 358 us; the launch traced here: 357 us
  waiting for transfers between devices  275 us (77%)
  blocking collectives  27.9 us (8%)
  matrix products  16.5 us (5%)
  between operations  14.1 us (4%)
  local copies, waits for them, and re-layouts  11.9 us (3%)
  starting transfers between devices  7.13 us (2%)
  other arithmetic  4.77 us (1%)
    unnamed x2, waiting for transfers between devices  266 us
    psum x1, blocking collectives, per_device(): lax.psum((jnp.sum(values, axis=(1, 2)), jnp.sum(values * values, axis=(1,...  15 us
    psum x1, blocking collectives, per_device(): lax.psum((jnp.sum(scaled, axis=(1, 2)), jnp.sum(scaled * normed, axis=(1,...  12.9 us
    unnamed x15, local copies, waits for them, and re-layouts  11.8 us
    dot_general x1, matrix products, per_device(): lax.dot_general(stacked, weight_flat, (((1,), (1,)), ((), ())), preferred...  9.02 us
    ppermute x2, waiting for transfers between devices, shifted(): lax.ppermute(value, axis, [(source, source + steps) for source in range(f...  8.8 us
    dot_general x1, matrix products, per_device(): lax.dot_general(input_flat, stacked, (((0,), (0,)), ((), ())), preferred_...  7.47 us
  transfers between devices with their start and end apart: 3, of which 3 were waited for; matrix products, arithmetic and copies ran while one was open for 5% of the time, Pallas kernels for 0%

commit v1 on v0

v1 whole, which is shorter than its diff:
```python
import jax
import jax.numpy as jnp
from jax import lax
from jax.sharding import Mesh, PartitionSpec as P

RATE = 18
EPSILON = 1e-05
F32 = jnp.float32
BF16 = jnp.bfloat16


def ring(axis, steps):
    count = lax.axis_size(axis)
    return [(source, (source + steps) % count) for source in range(count)]


def rotated(value, axis, steps):
    return lax.ppermute(value, axis, ring(axis, steps))


def shifted(value, axis, steps):
    count = lax.axis_size(axis)
    first, last = (max(0, -steps), min(count, count - steps))
    return lax.ppermute(value, axis, [(source, source + steps) for source in range(first, last)])


def others(axis):
    count = lax.axis_size(axis)
    return sorted(range(1, count), key=lambda step: min(step, count - step))


def summed(value, axis):
    total = value
    for step in others(axis):
        total = total + rotated(value, axis, step)
    return total


def scattered(value, axis, dim):
    count = lax.axis_size(axis)
    index = lax.axis_index(axis)
    total = lax.dynamic_index_in_dim(value, index, dim, keepdims=False)
    terms = []
    for step in others(axis):
        block = lax.dynamic_index_in_dim(value, lax.rem(index + step, count), dim, keepdims=False)
        terms.append(rotated(block.astype(BF16), axis, step))
    for term in terms:
        total = total + term.astype(F32)
    return total


def column_taps(block):
    image_count, row_count, col_count, channels = block.shape
    padded = jnp.pad(block, ((0, 0), (0, 0), (RATE, RATE), (0, 0)))
    pieces = [
        padded[:, :, RATE - RATE * step : RATE - RATE * step + col_count, :] for step in (-1, 0, 1)
    ]
    return jnp.concatenate(pieces, axis=3).reshape(
        image_count * row_count * col_count, 3 * channels
    )


def per_device(inputs, conv_out, grad_out, relu_mask, norm_gain, weight):
    image_count, row_count, col_count, channels_in = inputs.shape
    channels_out = conv_out.shape[3]
    z_size, y_size, x_size = (lax.axis_size(axis) for axis in ("z", "y", "x"))
    height = ("x", "core")
    cell_count = row_count * col_count * lax.axis_size(height)
    core = lax.axis_index("core")
    values = conv_out.astype(F32)
    passed = grad_out.astype(F32) * relu_mask.astype(F32)
    sums = jnp.stack(
        [
            jnp.sum(values, axis=(1, 2)),
            jnp.sum(values * values, axis=(1, 2)),
            jnp.sum(passed, axis=(1, 2)),
            jnp.sum(passed * values, axis=(1, 2)),
        ]
    )
    sums = sums + rotated(sums, "core", 1)
    means = summed(sums, "x") / cell_count
    chan_mean, second, passed_mean, product_mean = (means[n] for n in range(4))
    inv_std = 1.0 / jnp.sqrt(second - chan_mean * chan_mean + EPSILON)
    grad_mean = norm_gain * passed_mean
    cross_mean = norm_gain * (product_mean - chan_mean * passed_mean) * inv_std

    def spread(value):
        return value[:, None, None, :]

    normed = (values - spread(chan_mean)) * spread(inv_std)
    pre_grad = (
        spread(inv_std) * (norm_gain * passed - spread(grad_mean) - normed * spread(cross_mean))
    ).astype(BF16)
    distance = RATE // row_count
    below = shifted(pre_grad, height, -distance)
    above = shifted(pre_grad, height, distance)
    taps = [column_taps(block) for block in (below, pre_grad, above)]

    input_flat = inputs.reshape(image_count * row_count * col_count, channels_in)
    half = 3 * channels_out // 2

    def kernel_grad(stacked):
        def product(which):
            columns = lax.dynamic_slice_in_dim(stacked, which * half, half, axis=1)
            return lax.dot_general(
                input_flat, columns, (((0,), (0,)), ((), ())), preferred_element_type=F32
            )

        sent = product(1 - core).astype(BF16)
        total = product(core) + rotated(sent, "core", 1).astype(F32)
        return total.reshape(z_size, y_size, x_size, -1, half)

    middle = scattered(scattered(kernel_grad(taps[1]), "y", 1), "x", 1)
    first = scattered(scattered(kernel_grad(taps[0]), "x", 2), "y", 1)
    last = scattered(scattered(kernel_grad(taps[2]), "y", 1), "x", 1)
    merged = jnp.concatenate([first, middle, last], axis=2)
    rows = merged.shape[1] // 2
    merged = merged.reshape(z_size, 2, rows, 3 * half).astype(BF16).reshape(z_size * 2, rows, 3 * half)
    merged = lax.all_to_all(merged, ("z", "core"), 0, 0)
    merged = jnp.sum(merged.reshape(z_size, 2, rows, 3, half).astype(F32), axis=0)
    inv_images = 1.0 / (image_count * lax.axis_size(("z", "y")))
    weight_grad = jnp.moveaxis(merged, 0, 2).reshape(rows, 9, channels_out) * inv_images

    weight_flat = weight.reshape(channels_in, 9 * channels_out)
    input_grad = lax.dot_general(
        jnp.concatenate(taps, axis=1), weight_flat, (((1,), (1,)), ((), ())), preferred_element_type=F32
    ).astype(BF16)
    return (input_grad.reshape(inputs.shape), weight_grad)


def solution(mesh):
    cores = 2
    x_size = mesh.shape["height"] // cores
    y_size = 4
    z_size = mesh.shape["dp"] // y_size
    parted = Mesh(
        mesh.devices.reshape(z_size, y_size, x_size, cores), ("z", "y", "x", "core")
    )
    cells = P(("z", "y"), ("x", "core"), None, None)
    return jax.shard_map(
        per_device,
        mesh=parted,
        in_specs=(cells, cells, cells, cells, P(), P()),
        out_specs=(cells, P(("z", "y", "x", "core"), None, None)),
        check_vma=False,
    )
```

time: 358 us -> 113 us (0.32)
  waiting for transfers between devices: 275 us -> 12.2 us
  starting transfers between devices: 7.13 us -> 50.2 us
  blocking collectives: 27.9 us -> 0 us
  between operations: 14.1 us -> 1.05 us
  local copies, waits for them, and re-layouts: 11.9 us -> 21.3 us
  other arithmetic: 4.77 us -> 8.43 us
    unnamed x2 -> x0, waiting for transfers between devices: 266 us -> none
    ppermute x0 -> x25, starting transfers between devices: none -> 29.5 us  [rotated(): return lax.ppermute(value, axis, ring(axis, steps))]
    psum x2 -> x0, blocking collectives: 27.9 us -> none  [the longest x1 15 us: per_device(): lax.psum((jnp.sum(values, axis=(1, 2)), jnp.sum(values * values, axis=(1,...]
    all_to_all x0 -> x1, starting transfers between devices: none -> 14.4 us  [per_device(): merged = lax.all_to_all(merged, ('z', 'core'), 0, 0)]
    ppermute x0 -> x25, waiting for transfers between devices: none -> 5.26 us  [rotated(): return lax.ppermute(value, axis, ring(axis, steps))]
    add x0 -> x3, local copies, waits for them, and re-layouts: none -> 4.91 us  [kernel_grad(): total = product(core) + rotated(sent, 'core', 1).astype(F32)]
    add x0 -> x4, other arithmetic: none -> 3.67 us  [the longest x3 3.66 us: scattered(): total = total + term.astype(F32)]
    dot_general x2 -> x7, matrix products: 16.5 us -> 19 us  [the longest x6 10.4 us: product(): lax.dot_general(input_flat, columns, (((0,), (0,)), ((), ())), preferred_...]
  transfers between devices with their start and end apart: 3 -> 28, of which waited for: 3 -> 7; matrix products, arithmetic and copies ran while one was open for 5% -> 38% of each run, Pallas kernels for 0% -> 0%
where the time goes in v1:
time: 113 us; the launch traced here: 112 us
  starting transfers between devices  50.2 us (44%)
  local copies, waits for them, and re-layouts  21.3 us (19%)
  matrix products  19 us (17%)
  waiting for transfers between devices  12.2 us (11%)
  other arithmetic  8.43 us (7%)
    ppermute x25, starting transfers between devices, rotated(): return lax.ppermute(value, axis, ring(axis, steps))  29.5 us
    all_to_all x1, starting transfers between devices, per_device(): merged = lax.all_to_all(merged, ('z', 'core'), 0, 0)  14.4 us
    unnamed x26, local copies, waits for them, and re-layouts  11.7 us
    dot_general x6, matrix products, product(): lax.dot_general(input_flat, columns, (((0,), (0,)), ((), ())), preferred_...  10.4 us
    dot_general x1, matrix products, per_device(): lax.dot_general(jnp.concatenate(taps, axis=1), weight_flat, (((1,), (1,))...  8.63 us
    ppermute x2, starting transfers between devices, shifted(): lax.ppermute(value, axis, [(source, source + steps) for source in range(f...  6.34 us
    ppermute x2, waiting for transfers between devices, shifted(): lax.ppermute(value, axis, [(source, source + steps) for source in range(f...  6.29 us
    ppermute x25, waiting for transfers between devices, rotated(): return lax.ppermute(value, axis, ring(axis, steps))  5.26 us
  transfers between devices with their start and end apart: 28, of which 7 were waited for; matrix products, arithmetic and copies ran while one was open for 38% of the time, Pallas kernels for 0%

profile of v1, /device:TPU:1, one launch (start us, length us, event | category | flops | bytes accessed | tf_op | source)
XLA Modules:
  0.0 112.3 jit_solution(15656397784357705400)
XLA Ops:
  0.6 1.9 %fusion.31 = (f32[2,256]{1,0:T(2,128)S(1)}, f32[2,256]{1,0:T(2,128)S(1)}, f32[2,256]{1,0:T(2,128)S(1)}, f32[2,256]{1,0:T(2,128)S(1)}) fusion(s32[2,6,72,256]{3,2,1,0:T(8,128)} %param.9, bf16[2,6,72,256]{3,2,1,0:T(8,128)(2,1)} %param.8, bf16[2,6,72,256]{3,2,1,0:T(8,128)(2,1)} %param.7), kind=kLoop, calls=%fused_computation.61 | loop fusion | flops 2209792 | bytes 1777664 | tf_op jit(solution)/shard_map/reduce_sum | solution.py:76
  2.5 3.3 %collective-permute-start = (f32[4,2,256]{2,1,0:T(2,128)S(1)}, f32[4,2,256]{2,1,0:T(2,128)S(1)}, u32[]{:S(2)}, u32[]{:S(2)}) collective-permute-start(f32[4,2,256]{2,1,0:T(2,128)S(1)} %pad_maximum_fusion.4), channel_id=1, source_target_pairs={{0,1},{1,0},{2,3},{3,2},{4,5},{5,4},{6,7},{7,6},{8,9},{9,8},{10,11... | collective-permute-start | bytes 24584 | tf_op jit(solution)/shard_map/ppermute | solution.py:18
  5.8 0.8 collective-permute-done
  6.7 1.0 collective-permute-start.3
  7.7 0.9 collective-permute-start.2
  9.2 6.8 %copy.85 = bf16[1024,9,256]{0,2,1:T(8,128)(2,1)} copy(bf16[1024,9,256]{2,0,1:T(8,128)(2,1)} %param.11) | data formatting | bytes 9437184 | tf_op args[5]
  15.9 0.7 add_multiply_fusion
  17.4 1.0 fusion.18
  18.4 5.0 %collective-permute-start.5 = (bf16[2,6,72,256]{3,2,1,0:T(8,128)(2,1)S(1)}, bf16[2,6,72,256]{3,2,1,0:T(8,128)(2,1)S(1)}, u32[]{:S(2)}, u32[]{:S(2)}) collective-permute-start(bf16[2,6,72,256]{3,2,1,0:T(8,128)(2,1)S(1)} %fusion.18), channel_id=1, source_target_pairs={{0,3},{1,4},{2,5},{3,6},{4,7},{8,11},{9,12},{10,13},{11,14},{12,15... | collective-permute-start | bytes 1327112 | tf_op jit(solution)/shard_map/ppermute | solution.py:24
  23.7 1.3 %collective-permute-start.4 = (bf16[2,6,72,256]{3,2,1,0:T(8,128)(2,1)S(1)}, bf16[2,6,72,256]{3,2,1,0:T(8,128)(2,1)S(1)}, u32[]{:S(2)}, u32[]{:S(2)}) collective-permute-start(bf16[2,6,72,256]{3,2,1,0:T(8,128)(2,1)S(1)} %fusion.18), channel_id=1, source_target_pairs={{3,0},{4,1},{5,2},{6,3},{7,4},{11,8},{12,9},{13,10},{14,11},{15,12... | collective-permute-start | bytes 1327112 | tf_op jit(solution)/shard_map/ppermute | solution.py:24
  25.2 1.0 fusion.10
  26.3 5.0 %collective-permute-done.5 = bf16[2,6,72,256]{3,2,1,0:T(8,128)(2,1)S(1)} collective-permute-done((bf16[2,6,72,256]{3,2,1,0:T(8,128)(2,1)S(1)}, bf16[2,6,72,256]{3,2,1,0:T(8,128)(2,1)S(1)}, u32[]{:S(2)}, u32[]{:S(2)}) %collective-permute-start.5) | collective-permute-done | bytes 442400 | tf_op jit(solution)/shard_map/ppermute | solution.py:24
  31.6 1.9 %fusion.11 = bf16[1024,384]{0,1:T(8,128)(2,1)} fusion(bf16[864,1024]{1,0:T(8,128)(2,1)S(1)} %bitcast.163, bf16[864,768]{1,0:T(8,128)(2,1)S(1)} %bitcast.167, s32[]{:T(128)S(6)} %select_n.54), kind=kOutput, calls=%fused_computation.22 | convolution fusion | flops 679870464 | bytes 3219460 | tf_op jit(solution)/shard_map/dot_general | solution.py:105
  33.5 1.3 %collective-permute-done.4 = bf16[2,6,72,256]{3,2,1,0:T(8,128)(2,1)S(1)} collective-permute-done((bf16[2,6,72,256]{3,2,1,0:T(8,128)(2,1)S(1)}, bf16[2,6,72,256]{3,2,1,0:T(8,128)(2,1)S(1)}, u32[]{:S(2)}, u32[]{:S(2)}) %collective-permute-start.4) | collective-permute-done | bytes 442400 | tf_op jit(solution)/shard_map/ppermute | solution.py:24
  35.2 1.9 %fusion.9 = bf16[1024,384]{0,1:T(8,128)(2,1)} fusion(bf16[864,1024]{1,0:T(8,128)(2,1)S(1)} %bitcast.159, bf16[864,768]{1,0:T(8,128)(2,1)S(1)} %bitcast.170, s32[]{:T(128)S(6)} %select_n.54), kind=kOutput, calls=%fused_computation.20 | convolution fusion | flops 679870464 | bytes 3219460 | tf_op jit(solution)/shard_map/dot_general | solution.py:105
  37.5 1.0 bitcast_add_fusion.1
  38.6 1.7 %copy.89 = f32[1024,384]{1,0:T(8,128)} copy(f32[1024,384]{0,1:T(8,128)S(1)} %bitcast_add_fusion.1) | data formatting | bytes 3145728 | tf_op jit(solution)/shard_map/add | solution.py:110
  40.3 2.3 %bitcast_add_fusion = f32[1024,384]{0,1:T(8,128)S(1)} fusion(bf16[1024,384]{0,1:T(8,128)(2,1)} %collective-permute-done.20, bf16[864,1024]{1,0:T(8,128)(2,1)S(1)} %bitcast.162, bf16[864,768]{1,0:T(8,128)(2,1)} %bitcast.168, s32[]{:T(128)S(6)} %select_n.53), kind=kOutput, calls=%fused_computation.7 | convolution fusion | flops 680263680 | bytes 4792324 | tf_op jit(solution)/shard_map/dot_general | solution.py:105
  42.6 1.6 %copy.94 = f32[1024,384]{1,0:T(8,128)} copy(f32[1024,384]{0,1:T(8,128)S(1)} %bitcast_add_fusion) | data formatting | bytes 3145728 | tf_op jit(solution)/shard_map/add | solution.py:110
  44.2 1.7 %constant_dynamic-slice_fusion.2 = (bf16[8,1,4,8,384]{4,3,2,1,0:T(8,128)(2,1)S(1)}, bf16[8,1,4,8,384]{4,3,2,1,0:T(8,128)(2,1)S(1)}, bf16[8,1,4,8,384]{4,3,2,1,0:...) fusion(f32[8,4,4,8,384]{4,3,2,1,0:T(8,128)} %bitcast.178, ...), kind=kLoop, calls=%fused_computation.108 | loop fusion | bytes 2359308 | tf_op jit(solution)/shard_map/jit(dynamic_index_in_dim)/dynamic_slice | solution.py:45
  46.0 0.7 copy.136
  46.7 2.9 %collective-permute-start.23 = (bf16[8,4,8,384]{3,2,0,1:T(8,128)(2,1)}, bf16[8,4,8,384]{3,2,0,1:T(8,128)(2,1)}, u32[]{:S(2)}, u32[]{:S(2)}) collective-permute-start(bf16[8,4,8,384]{3,2,0,1:T(8,128)(2,1)} %bitcast.157), channel_id=1, source_target_pairs={{0,16},{8,24},{16,0},{24,8},{1,17},{9,25},{17,1},{25,9},{2,18},{10... | collective-permute-start | bytes 589832 | tf_op jit(solution)/shard_map/ppermute | solution.py:18
  49.6 0.7 copy.135
  50.3 0.8 collective-permute-start.22
  51.8 0.7 collective-permute-start.21
  52.5 0.7 copy.133
  53.2 0.7 collective-permute-start.16
  53.9 0.7 copy.132
  54.6 2.1 %collective-permute-start.15 = (bf16[8,4,8,384]{3,2,0,1:T(8,128)(2,1)}, bf16[8,4,8,384]{3,2,0,1:T(8,128)(2,1)}, u32[]{:S(2)}, u32[]{:S(2)}) collective-permute-start(bf16[8,4,8,384]{3,2,0,1:T(8,128)(2,1)} %bitcast.153), channel_id=1, source_target_pairs={{0,24},{8,0},{16,8},{24,16},{1,25},{9,1},{17,9},{25,17},{2,26},{10... | collective-permute-start | bytes 589832 | tf_op jit(solution)/shard_map/ppermute | solution.py:18
  56.7 2.1 %bitcast_add_fusion.2 = f32[1024,384]{0,1:T(8,128)S(1)} fusion(bf16[1024,384]{0,1:T(8,128)(2,1)} %collective-permute-done.6, bf16[864,1024]{1,0:T(8,128)(2,1)S(1)} %bitcast.158, bf16[864,768]{1,0:T(8,128)(2,1)S(1)} %bitcast.172, s32[]{:T(128)S(6)} %select_n.53), kind=kOutput, calls=%fused_computation.9 | convolution fusion | flops 680263680 | bytes 4792324 | tf_op jit(solution)/shard_map/dot_general | solution.py:105
  58.8 0.7 copy.131
  59.5 1.6 %copy.86 = f32[1024,384]{1,0:T(8,128)} copy(f32[1024,384]{0,1:T(8,128)S(1)} %bitcast_add_fusion.2) | data formatting | bytes 3145728 | tf_op jit(solution)/shard_map/add | solution.py:110
  61.1 1.3 %fusion.40 = (bf16[8,4,8,384]{3,2,1,0:T(8,128)(2,1)S(1)}, bf16[8,4,8,384]{3,2,1,0:T(8,128)(2,1)S(1)}, bf16[8,4,8,384]{3,2,1,0:T(8,128)(2,1)S(1)}) fusion(f32[8,4,4,8,384]{4,3,2,1,0:T(8,128)} %bitcast.174, s32[]{:T(128)S(6)} %select_n.56, s32[]{:T(128)S(6)} %select_n.58, s32[]{:T(128)S(6)} %select_n.57), kind=kLoop, calls=%fused_computation.70 | loop fusion | bytes 1179660 | tf_op jit(solution)/shard_map/convert_element_type | solution.py:46
  62.6 2.4 %collective-permute-start.9 = (bf16[8,4,8,384]{3,2,1,0:T(8,128)(2,1)S(1)}, bf16[8,4,8,384]{3,2,1,0:T(8,128)(2,1)S(1)}, u32[]{:S(2)}, u32[]{:S(2)}) collective-permute-start(bf16[8,4,8,384]{3,2,1,0:T(8,128)(2,1)S(1)} %get-tuple-element.19), channel_id=1, source_target_pairs={{0,4},{2,6},{4,0},{6,2},{1,5},{3,7},{5,1},{7,3},{8,12},{10,14},{12... | collective-permute-start | bytes 589832 | tf_op jit(solution)/shard_map/ppermute | solution.py:18
  65.0 2.1 %collective-permute-start.8 = (bf16[8,4,8,384]{3,2,1,0:T(8,128)(2,1)S(1)}, bf16[8,4,8,384]{3,2,1,0:T(8,128)(2,1)S(1)}, u32[]{:S(2)}, u32[]{:S(2)}) collective-permute-start(bf16[8,4,8,384]{3,2,1,0:T(8,128)(2,1)S(1)} %get-tuple-element.20), channel_id=1, source_target_pairs={{0,6},{2,0},{4,2},{6,4},{1,7},{3,1},{5,3},{7,5},{8,14},{10,8},{12,... | collective-permute-start | bytes 589832 | tf_op jit(solution)/shard_map/ppermute | solution.py:18
  67.1 1.4 %fusion.26 = f32[8,4,8,384]{3,2,0,1:T(8,128)S(1)} fusion(bf16[8,4,8,384]{3,2,0,1:T(8,128)(2,1)} %collective-permute-done.23, bf16[8,4,8,384]{3,2,0,1:T(8,128)(2,1)} %collective-permute-done.22, bf16[8,4,8,384]{3,2,0,1:T(8,128)(2,1)} %collective-permute-done.21, f32[8,4,4,8,384]{4,3,2,1,0:T(8,128)} %bitcast.179, s32[]{:T(128)S(6)} %select_n.59), kind=kLoop, calls=%fused_computation.52 | loop fusion | flops 589824 | bytes 1376260 | tf_op jit(solution)/shard_map/add | solution.py:48
  68.7 1.3 %collective-permute-start.26 = (bf16[8,8,384]{2,1,0:T(8,128)(2,1)S(1)}, bf16[8,8,384]{2,1,0:T(8,128)(2,1)S(1)}, u32[]{:S(2)}, u32[]{:S(2)}) collective-permute-start(bf16[8,8,384]{2,1,0:T(8,128)(2,1)S(1)} %get-tuple-element.40), channel_id=1, source_target_pairs={{0,4},{2,6},{4,0},{6,2},{1,5},{3,7},{5,1},{7,3},{8,12},{10,14},{12... | collective-permute-start | bytes 147464 | tf_op jit(solution)/shard_map/ppermute | solution.py:18
  69.9 2.1 %collective-permute-start.25 = (bf16[8,8,384]{2,1,0:T(8,128)(2,1)S(1)}, bf16[8,8,384]{2,1,0:T(8,128)(2,1)S(1)}, u32[]{:S(2)}, u32[]{:S(2)}) collective-permute-start(bf16[8,8,384]{2,1,0:T(8,128)(2,1)S(1)} %get-tuple-element.41), channel_id=1, source_target_pairs={{0,6},{2,0},{4,2},{6,4},{1,7},{3,1},{5,3},{7,5},{8,14},{10,8},{12,... | collective-permute-start | bytes 147464 | tf_op jit(solution)/shard_map/ppermute | solution.py:18
  72.1 1.2 %fusion.28 = f32[8,4,8,384]{3,2,0,1:T(8,128)S(1)} fusion(bf16[8,4,8,384]{3,2,0,1:T(8,128)(2,1)S(1)} %collective-permute-done.16, bf16[8,4,8,384]{3,2,0,1:T(8,128)(2,1)} %collective-permute-done.15, bf16[8,4,8,384]{3,2,0,1:T(8,128)(2,1)S(1)} %collective-permute-done.14, f32[8,4,4,8,384]{4,3,2,1,0:T(8,128)} %bitcast.177, s32[]{:T(128)S(6)} %select_n.59), kind=kLoop, calls=%fused_computation.55 | loop fusion | flops 589824 | bytes 1376260 | tf_op jit(solution)/shard_map/add | solution.py:48
  73.4 2.3 %collective-permute-start.19 = (bf16[8,8,384]{2,1,0:T(8,128)(2,1)S(1)}, bf16[8,8,384]{2,1,0:T(8,128)(2,1)S(1)}, u32[]{:S(2)}, u32[]{:S(2)}) collective-permute-start(bf16[8,8,384]{2,1,0:T(8,128)(2,1)S(1)} %get-tuple-element.37), channel_id=1, source_target_pairs={{0,4},{2,6},{4,0},{6,2},{1,5},{3,7},{5,1},{7,3},{8,12},{10,14},{12... | collective-permute-start | bytes 147464 | tf_op jit(solution)/shard_map/ppermute | solution.py:18
  75.7 1.4 %collective-permute-start.18 = (bf16[8,8,384]{2,1,0:T(8,128)(2,1)S(1)}, bf16[8,8,384]{2,1,0:T(8,128)(2,1)S(1)}, u32[]{:S(2)}, u32[]{:S(2)}) collective-permute-start(bf16[8,8,384]{2,1,0:T(8,128)(2,1)S(1)} %get-tuple-element.38), channel_id=1, source_target_pairs={{0,6},{2,0},{4,2},{6,4},{1,7},{3,1},{5,3},{7,5},{8,14},{10,8},{12,... | collective-permute-start | bytes 147464 | tf_op jit(solution)/shard_map/ppermute | solution.py:18
  77.1 1.1 fusion.30
  78.4 1.6 %collective-permute-start.12 = (bf16[8,8,384]{2,1,0:T(8,128)(2,1)S(1)}, bf16[8,8,384]{2,1,0:T(8,128)(2,1)S(1)}, u32[]{:S(2)}, u32[]{:S(2)}) collective-permute-start(bf16[8,8,384]{2,1,0:T(8,128)(2,1)S(1)} %get-tuple-element.34), channel_id=1, source_target_pairs={{0,16},{8,24},{16,0},{24,8},{1,17},{9,25},{17,1},{25,9},{2,18},{10... | collective-permute-start | bytes 147464 | tf_op jit(solution)/shard_map/ppermute | solution.py:18
  80.0 2.1 %collective-permute-start.11 = (bf16[8,8,384]{2,1,0:T(8,128)(2,1)S(1)}, bf16[8,8,384]{2,1,0:T(8,128)(2,1)S(1)}, u32[]{:S(2)}, u32[]{:S(2)}) collective-permute-start(bf16[8,8,384]{2,1,0:T(8,128)(2,1)S(1)} %get-tuple-element.35), channel_id=1, source_target_pairs={{0,24},{8,0},{16,8},{24,16},{1,25},{9,1},{17,9},{25,17},{2,26},{10... | collective-permute-start | bytes 147464 | tf_op jit(solution)/shard_map/ppermute | solution.py:18
  82.9 0.8 collective-permute-done.11
  83.7 3.2 %collective-permute-done.10 = bf16[8,8,384]{2,1,0:T(8,128)(2,1)S(1)} collective-permute-done((bf16[8,8,384]{2,1,0:T(8,128)(2,1)S(1)}, bf16[8,8,384]{2,1,0:T(8,128)(2,1)S(1)}, u32[]{:S(2)}, u32[]{:S(2)}) %collective-permute-start.10) | collective-permute-done | bytes 49184 | tf_op jit(solution)/shard_map/ppermute | solution.py:18
  87.6 14.4 %all-to-all-start = ((bf16[16,4,1152]{2,1,0:T(4,128)(2,1)}), bf16[16,4,1152]{2,1,0:T(4,128)(2,1)S(1)}, u32[]{:S(2)}, u32[]{:S(2)}) async-start(bf16[16,4,1152]{2,1,0:T(4,128)(2,1)} %convert_element_type.287), calls=%async_computation | async-start | bytes 294912 | tf_op jit(solution)/shard_map/all_to_all | solution.py:119
  102.0 8.6 %fusion.6 = bf16[864,1024]{1,0:T(8,128)(2,1)} fusion(bf16[1024,2304]{0,1:T(8,128)(2,1)} %bitcast.173, bf16[864,768]{1,0:T(8,128)(2,1)} %bitcast.169, bf16[864,768]{1,0:T(8,128)(2,1)S(1)} %bitcast.166, bf16[864,768]{1,0:T(8,128)(2,1)} %bitcast.171), kind=kOutput, calls=%fused_computation.6 | convolution fusion | flops 4089692160 | bytes 10469376 | tf_op jit(solution)/shard_map/dot_general | solution.py:125
  (76 shorter events, 7.1 us)
Async XLA Ops:
  0.6 24.5 %copy-start = (bf16[2,6,72,1024]{3,2,1,0:T(8,128)(2,1)S(1)}, bf16[2,6,72,1024]{3,2,1,0:T(8,128)(2,1)}, u32[]{:S(2)}) copy-start(bf16[2,6,72,1024]{3,2,1,0:T(8,128)(2,1)} %param.6) | copy-start | bytes 5308420
  2.5 4.2 %collective-permute-start = (f32[4,2,256]{2,1,0:T(2,128)S(1)}, f32[4,2,256]{2,1,0:T(2,128)S(1)}, u32[]{:S(2)}, u32[]{:S(2)}) collective-permute-start(f32[4,2,256]{2,1,0:T(2,128)S(1)} %pad_maximum_fusion.4), channel_id=1, source_target_pairs={{0,1},{1,0},{2,3},{3,2},{4,5},{5,4},{6,7},{7,6},{8,9},{9,8},{10,11... | collective-permute-start | bytes 24584 | tf_op jit(solution)/shard_map/ppermute | solution.py:18
  6.7 9.3 %collective-permute-start.3 = (f32[4,2,256]{2,1,0:T(2,128)S(1)}, f32[4,2,256]{2,1,0:T(2,128)S(1)}, u32[]{:S(2)}, u32[]{:S(2)}) collective-permute-start(f32[4,2,256]{2,1,0:T(2,128)S(1)} %fusion.81), channel_id=1, source_target_pairs={{0,4},{2,6},{4,0},{6,2},{1,5},{3,7},{5,1},{7,3},{8,12},{10,14},{12... | collective-permute-start | bytes 24584 | tf_op jit(solution)/shard_map/ppermute | solution.py:18
  7.7 8.3 %collective-permute-start.2 = (f32[4,2,256]{2,1,0:T(2,128)S(1)}, f32[4,2,256]{2,1,0:T(2,128)}, u32[]{:S(2)}, u32[]{:S(2)}) collective-permute-start(f32[4,2,256]{2,1,0:T(2,128)S(1)} %fusion.81), channel_id=1, source_target_pairs={{0,6},{2,0},{4,2},{6,4},{1,7},{3,1},{5,3},{7,5},{8,14},{10,8},{12,... | collective-permute-start | bytes 24584 | tf_op jit(solution)/shard_map/ppermute | solution.py:18
  8.5 7.4 %collective-permute-start.1 = (f32[4,2,256]{2,1,0:T(2,128)S(1)}, f32[4,2,256]{2,1,0:T(2,128)}, u32[]{:S(2)}, u32[]{:S(2)}) collective-permute-start(f32[4,2,256]{2,1,0:T(2,128)S(1)} %fusion.81), channel_id=1, source_target_pairs={{0,2},{2,4},{4,6},{6,0},{1,3},{3,5},{5,7},{7,1},{8,10},{10,12},{12... | collective-permute-start | bytes 24584 | tf_op jit(solution)/shard_map/ppermute | solution.py:18
  9.2 8.2 %copy-start.6 = (s32[2,6,72,256]{3,2,1,0:T(8,128)S(1)}, s32[2,6,72,256]{3,2,1,0:T(8,128)}, u32[]{:S(2)}) copy-start(s32[2,6,72,256]{3,2,1,0:T(8,128)} %param.9) | copy-start | bytes 2654212
  9.2 8.2 %copy-start.7 = (bf16[2,6,72,256]{3,2,1,0:T(8,128)(2,1)S(1)}, bf16[2,6,72,256]{3,2,1,0:T(8,128)(2,1)}, u32[]{:S(2)}) copy-start(bf16[2,6,72,256]{3,2,1,0:T(8,128)(2,1)} %param.7) | copy-start | bytes 1327108
  9.2 8.2 %copy-start.8 = (bf16[2,6,72,256]{3,2,1,0:T(8,128)(2,1)S(1)}, bf16[2,6,72,256]{3,2,1,0:T(8,128)(2,1)}, u32[]{:S(2)}) copy-start(bf16[2,6,72,256]{3,2,1,0:T(8,128)(2,1)} %param.8) | copy-start | bytes 1327108
  18.4 12.8 %collective-permute-start.5 = (bf16[2,6,72,256]{3,2,1,0:T(8,128)(2,1)S(1)}, bf16[2,6,72,256]{3,2,1,0:T(8,128)(2,1)S(1)}, u32[]{:S(2)}, u32[]{:S(2)}) collective-permute-start(bf16[2,6,72,256]{3,2,1,0:T(8,128)(2,1)S(1)} %fusion.18), channel_id=1, source_target_pairs={{0,3},{1,4},{2,5},{3,6},{4,7},{8,11},{9,12},{10,13},{11,14},{12,15... | collective-permute-start | bytes 1327112 | tf_op jit(solution)/shard_map/ppermute | solution.py:24
  23.7 11.1 %collective-permute-start.4 = (bf16[2,6,72,256]{3,2,1,0:T(8,128)(2,1)S(1)}, bf16[2,6,72,256]{3,2,1,0:T(8,128)(2,1)S(1)}, u32[]{:S(2)}, u32[]{:S(2)}) collective-permute-start(bf16[2,6,72,256]{3,2,1,0:T(8,128)(2,1)S(1)} %fusion.18), channel_id=1, source_target_pairs={{3,0},{4,1},{5,2},{6,3},{7,4},{11,8},{12,9},{13,10},{14,11},{15,12... | collective-permute-start | bytes 1327112 | tf_op jit(solution)/shard_map/ppermute | solution.py:24
  25.1 12.4 %copy-start.1 = (bf16[2,6,72,768]{3,2,1,0:T(8,128)(2,1)}, bf16[2,6,72,768]{3,2,1,0:T(8,128)(2,1)S(1)}, u32[]{:S(2)}) copy-start(bf16[2,6,72,768]{3,2,1,0:T(8,128)(2,1)S(1)} %pad_maximum_fusion.1) | copy-start | bytes 3981316
  26.2 11.4 %collective-permute-start.13 = (bf16[1024,384]{0,1:T(8,128)(2,1)S(1)}, bf16[1024,384]{0,1:T(8,128)(2,1)S(1)}, u32[]{:S(2)}, u32[]{:S(2)}) collective-permute-start(bf16[1024,384]{0,1:T(8,128)(2,1)S(1)} %fusion.10), channel_id=1, source_target_pairs={{0,1},{1,0},{2,3},{3,2},{4,5},{5,4},{6,7},{7,6},{8,9},{9,8},{10,11... | collective-permute-start | bytes 2359304 | tf_op jit(solution)/shard_map/ppermute | solution.py:18
  31.6 1.9 %copy-start.3 = (bf16[2,6,72,768]{3,2,1,0:T(8,128)(2,1)}, bf16[2,6,72,768]{3,2,1,0:T(8,128)(2,1)S(1)}, u32[]{:S(2)}) copy-start(bf16[2,6,72,768]{3,2,1,0:T(8,128)(2,1)S(1)} %pad_maximum_fusion.2) | copy-start | bytes 3981316
  33.5 6.7 %collective-permute-start.20 = (bf16[1024,384]{0,1:T(8,128)(2,1)}, bf16[1024,384]{0,1:T(8,128)(2,1)}, u32[]{:S(2)}, u32[]{:S(2)}) collective-permute-start(bf16[1024,384]{0,1:T(8,128)(2,1)} %fusion.11), channel_id=1, source_target_pairs={{0,1},{1,0},{2,3},{3,2},{4,5},{5,4},{6,7},{7,6},{8,9},{9,8},{10,11... | collective-permute-start | bytes 2359304 | tf_op jit(solution)/shard_map/ppermute | solution.py:18
  35.2 1.9 %copy-start.4 = (bf16[2,6,72,768]{3,2,1,0:T(8,128)(2,1)}, bf16[2,6,72,768]{3,2,1,0:T(8,128)(2,1)S(1)}, u32[]{:S(2)}) copy-start(bf16[2,6,72,768]{3,2,1,0:T(8,128)(2,1)S(1)} %pad_maximum_fusion) | copy-start | bytes 3981316
  37.2 17.4 %collective-permute-start.6 = (bf16[1024,384]{0,1:T(8,128)(2,1)}, bf16[1024,384]{0,1:T(8,128)(2,1)}, u32[]{:S(2)}, u32[]{:S(2)}) collective-permute-start(bf16[1024,384]{0,1:T(8,128)(2,1)} %fusion.9), channel_id=1, source_target_pairs={{0,1},{1,0},{2,3},{3,2},{4,5},{5,4},{6,7},{7,6},{8,9},{9,8},{10,11... | collective-permute-start | bytes 2359304 | tf_op jit(solution)/shard_map/ppermute | solution.py:18
  46.0 10.7 %copy-start.5 = (bf16[2,6,72,768]{3,2,1,0:T(8,128)(2,1)S(1)}, bf16[2,6,72,768]{3,2,1,0:T(8,128)(2,1)}, u32[]{:S(2)}) copy-start(bf16[2,6,72,768]{3,2,1,0:T(8,128)(2,1)} %copy-done.4) | copy-start | bytes 3981316
  46.7 15.7 %collective-permute-start.23 = (bf16[8,4,8,384]{3,2,0,1:T(8,128)(2,1)}, bf16[8,4,8,384]{3,2,0,1:T(8,128)(2,1)}, u32[]{:S(2)}, u32[]{:S(2)}) collective-permute-start(bf16[8,4,8,384]{3,2,0,1:T(8,128)(2,1)} %bitcast.157), channel_id=1, source_target_pairs={{0,16},{8,24},{16,0},{24,8},{1,17},{9,25},{17,1},{25,9},{2,18},{10... | collective-permute-start | bytes 589832 | tf_op jit(solution)/shard_map/ppermute | solution.py:18
  50.3 12.2 %collective-permute-start.22 = (bf16[8,4,8,384]{3,2,0,1:T(8,128)(2,1)}, bf16[8,4,8,384]{3,2,0,1:T(8,128)(2,1)}, u32[]{:S(2)}, u32[]{:S(2)}) collective-permute-start(bf16[8,4,8,384]{3,2,0,1:T(8,128)(2,1)} %bitcast.156), channel_id=1, source_target_pairs={{0,24},{8,0},{16,8},{24,16},{1,25},{9,1},{17,9},{25,17},{2,26},{10... | collective-permute-start | bytes 589832 | tf_op jit(solution)/shard_map/ppermute | solution.py:18
  51.8 13.2 %collective-permute-start.21 = (bf16[8,4,8,384]{3,2,0,1:T(8,128)(2,1)}, bf16[8,4,8,384]{3,2,0,1:T(8,128)(2,1)}, u32[]{:S(2)}, u32[]{:S(2)}) collective-permute-start(bf16[8,4,8,384]{3,2,0,1:T(8,128)(2,1)} %bitcast.155), channel_id=1, source_target_pairs={{0,8},{8,16},{16,24},{24,0},{1,9},{9,17},{17,25},{25,1},{2,10},{10... | collective-permute-start | bytes 589832 | tf_op jit(solution)/shard_map/ppermute | solution.py:18
  53.2 15.4 %collective-permute-start.16 = (bf16[8,4,8,384]{3,2,0,1:T(8,128)(2,1)}, bf16[8,4,8,384]{3,2,0,1:T(8,128)(2,1)S(1)}, u32[]{:S(2)}, u32[]{:S(2)}) collective-permute-start(bf16[8,4,8,384]{3,2,0,1:T(8,128)(2,1)} %bitcast.154), channel_id=1, source_target_pairs={{0,16},{8,24},{16,0},{24,8},{1,17},{9,25},{17,1},{25,9},{2,18},{10... | collective-permute-start | bytes 589832 | tf_op jit(solution)/shard_map/ppermute | solution.py:18
  54.6 14.1 %collective-permute-start.15 = (bf16[8,4,8,384]{3,2,0,1:T(8,128)(2,1)}, bf16[8,4,8,384]{3,2,0,1:T(8,128)(2,1)}, u32[]{:S(2)}, u32[]{:S(2)}) collective-permute-start(bf16[8,4,8,384]{3,2,0,1:T(8,128)(2,1)} %bitcast.153), channel_id=1, source_target_pairs={{0,24},{8,0},{16,8},{24,16},{1,25},{9,1},{17,9},{25,17},{2,26},{10... | collective-permute-start | bytes 589832 | tf_op jit(solution)/shard_map/ppermute | solution.py:18
  62.5 7.5 %collective-permute-start.14 = (bf16[8,4,8,384]{3,2,0,1:T(8,128)(2,1)}, bf16[8,4,8,384]{3,2,0,1:T(8,128)(2,1)S(1)}, u32[]{:S(2)}, u32[]{:S(2)}) collective-permute-start(bf16[8,4,8,384]{3,2,0,1:T(8,128)(2,1)} %bitcast.180), channel_id=1, source_target_pairs={{0,8},{8,16},{16,24},{24,0},{1,9},{9,17},{17,25},{25,1},{2,10},{10... | collective-permute-start | bytes 589832 | tf_op jit(solution)/shard_map/ppermute | solution.py:18
  62.6 10.8 %collective-permute-start.9 = (bf16[8,4,8,384]{3,2,1,0:T(8,128)(2,1)S(1)}, bf16[8,4,8,384]{3,2,1,0:T(8,128)(2,1)S(1)}, u32[]{:S(2)}, u32[]{:S(2)}) collective-permute-start(bf16[8,4,8,384]{3,2,1,0:T(8,128)(2,1)S(1)} %get-tuple-element.19), channel_id=1, source_target_pairs={{0,4},{2,6},{4,0},{6,2},{1,5},{3,7},{5,1},{7,3},{8,12},{10,14},{12... | collective-permute-start | bytes 589832 | tf_op jit(solution)/shard_map/ppermute | solution.py:18
  65.0 8.4 %collective-permute-start.8 = (bf16[8,4,8,384]{3,2,1,0:T(8,128)(2,1)S(1)}, bf16[8,4,8,384]{3,2,1,0:T(8,128)(2,1)S(1)}, u32[]{:S(2)}, u32[]{:S(2)}) collective-permute-start(bf16[8,4,8,384]{3,2,1,0:T(8,128)(2,1)S(1)} %get-tuple-element.20), channel_id=1, source_target_pairs={{0,6},{2,0},{4,2},{6,4},{1,7},{3,1},{5,3},{7,5},{8,14},{10,8},{12,... | collective-permute-start | bytes 589832 | tf_op jit(solution)/shard_map/ppermute | solution.py:18
  68.6 7.1 %collective-permute-start.7 = (bf16[8,4,8,384]{3,2,1,0:T(8,128)(2,1)S(1)}, bf16[8,4,8,384]{3,2,1,0:T(8,128)(2,1)S(1)}, u32[]{:S(2)}, u32[]{:S(2)}) collective-permute-start(bf16[8,4,8,384]{3,2,1,0:T(8,128)(2,1)S(1)} %get-tuple-element.18), channel_id=1, source_target_pairs={{0,2},{2,4},{4,6},{6,0},{1,3},{3,5},{5,7},{7,1},{8,10},{10,12},{12... | collective-permute-start | bytes 589832 | tf_op jit(solution)/shard_map/ppermute | solution.py:18
  68.7 9.6 %collective-permute-start.26 = (bf16[8,8,384]{2,1,0:T(8,128)(2,1)S(1)}, bf16[8,8,384]{2,1,0:T(8,128)(2,1)S(1)}, u32[]{:S(2)}, u32[]{:S(2)}) collective-permute-start(bf16[8,8,384]{2,1,0:T(8,128)(2,1)S(1)} %get-tuple-element.40), channel_id=1, source_target_pairs={{0,4},{2,6},{4,0},{6,2},{1,5},{3,7},{5,1},{7,3},{8,12},{10,14},{12... | collective-permute-start | bytes 147464 | tf_op jit(solution)/shard_map/ppermute | solution.py:18
  69.9 8.5 %collective-permute-start.25 = (bf16[8,8,384]{2,1,0:T(8,128)(2,1)S(1)}, bf16[8,8,384]{2,1,0:T(8,128)(2,1)S(1)}, u32[]{:S(2)}, u32[]{:S(2)}) collective-permute-start(bf16[8,8,384]{2,1,0:T(8,128)(2,1)S(1)} %get-tuple-element.41), channel_id=1, source_target_pairs={{0,6},{2,0},{4,2},{6,4},{1,7},{3,1},{5,3},{7,5},{8,14},{10,8},{12,... | collective-permute-start | bytes 147464 | tf_op jit(solution)/shard_map/ppermute | solution.py:18
  73.3 6.7 %collective-permute-start.24 = (bf16[8,8,384]{2,1,0:T(8,128)(2,1)S(1)}, bf16[8,8,384]{2,1,0:T(8,128)(2,1)S(1)}, u32[]{:S(2)}, u32[]{:S(2)}) collective-permute-start(bf16[8,8,384]{2,1,0:T(8,128)(2,1)S(1)} %get-tuple-element.39), channel_id=1, source_target_pairs={{0,2},{2,4},{4,6},{6,0},{1,3},{3,5},{5,7},{7,1},{8,10},{10,12},{12... | collective-permute-start | bytes 147464 | tf_op jit(solution)/shard_map/ppermute | solution.py:18
  73.4 8.7 %collective-permute-start.19 = (bf16[8,8,384]{2,1,0:T(8,128)(2,1)S(1)}, bf16[8,8,384]{2,1,0:T(8,128)(2,1)S(1)}, u32[]{:S(2)}, u32[]{:S(2)}) collective-permute-start(bf16[8,8,384]{2,1,0:T(8,128)(2,1)S(1)} %get-tuple-element.37), channel_id=1, source_target_pairs={{0,4},{2,6},{4,0},{6,2},{1,5},{3,7},{5,1},{7,3},{8,12},{10,14},{12... | collective-permute-start | bytes 147464 | tf_op jit(solution)/shard_map/ppermute | solution.py:18
  75.7 26.3 %copy-start.2 = (bf16[2,6,72,768]{3,2,1,0:T(8,128)(2,1)S(1)}, bf16[2,6,72,768]{3,2,1,0:T(8,128)(2,1)}, u32[]{:S(2)}) copy-start(bf16[2,6,72,768]{3,2,1,0:T(8,128)(2,1)} %copy-done.1) | copy-start | bytes 3981316
  75.7 6.8 %collective-permute-start.18 = (bf16[8,8,384]{2,1,0:T(8,128)(2,1)S(1)}, bf16[8,8,384]{2,1,0:T(8,128)(2,1)S(1)}, u32[]{:S(2)}, u32[]{:S(2)}) collective-permute-start(bf16[8,8,384]{2,1,0:T(8,128)(2,1)S(1)} %get-tuple-element.38), channel_id=1, source_target_pairs={{0,6},{2,0},{4,2},{6,4},{1,7},{3,1},{5,3},{7,5},{8,14},{10,8},{12,... | collective-permute-start | bytes 147464 | tf_op jit(solution)/shard_map/ppermute | solution.py:18
  78.2 4.2 %collective-permute-start.17 = (bf16[8,8,384]{2,1,0:T(8,128)(2,1)S(1)}, bf16[8,8,384]{2,1,0:T(8,128)(2,1)S(1)}, u32[]{:S(2)}, u32[]{:S(2)}) collective-permute-start(bf16[8,8,384]{2,1,0:T(8,128)(2,1)S(1)} %get-tuple-element.36), channel_id=1, source_target_pairs={{0,2},{2,4},{4,6},{6,0},{1,3},{3,5},{5,7},{7,1},{8,10},{10,12},{12... | collective-permute-start | bytes 147464 | tf_op jit(solution)/shard_map/ppermute | solution.py:18
  78.4 4.5 %collective-permute-start.12 = (bf16[8,8,384]{2,1,0:T(8,128)(2,1)S(1)}, bf16[8,8,384]{2,1,0:T(8,128)(2,1)S(1)}, u32[]{:S(2)}, u32[]{:S(2)}) collective-permute-start(bf16[8,8,384]{2,1,0:T(8,128)(2,1)S(1)} %get-tuple-element.34), channel_id=1, source_target_pairs={{0,16},{8,24},{16,0},{24,8},{1,17},{9,25},{17,1},{25,9},{2,18},{10... | collective-permute-start | bytes 147464 | tf_op jit(solution)/shard_map/ppermute | solution.py:18
  80.0 3.7 %collective-permute-start.11 = (bf16[8,8,384]{2,1,0:T(8,128)(2,1)S(1)}, bf16[8,8,384]{2,1,0:T(8,128)(2,1)S(1)}, u32[]{:S(2)}, u32[]{:S(2)}) collective-permute-start(bf16[8,8,384]{2,1,0:T(8,128)(2,1)S(1)} %get-tuple-element.35), channel_id=1, source_target_pairs={{0,24},{8,0},{16,8},{24,16},{1,25},{9,1},{17,9},{25,17},{2,26},{10... | collective-permute-start | bytes 147464 | tf_op jit(solution)/shard_map/ppermute | solution.py:18
  82.2 4.7 %collective-permute-start.10 = (bf16[8,8,384]{2,1,0:T(8,128)(2,1)S(1)}, bf16[8,8,384]{2,1,0:T(8,128)(2,1)S(1)}, u32[]{:S(2)}, u32[]{:S(2)}) collective-permute-start(bf16[8,8,384]{2,1,0:T(8,128)(2,1)S(1)} %get-tuple-element.33), channel_id=1, source_target_pairs={{0,8},{8,16},{16,24},{24,0},{1,9},{9,17},{17,25},{25,1},{2,10},{10... | collective-permute-start | bytes 147464 | tf_op jit(solution)/shard_map/ppermute | solution.py:18
  87.6 23.7 %all-to-all-start = ((bf16[16,4,1152]{2,1,0:T(4,128)(2,1)}), bf16[16,4,1152]{2,1,0:T(4,128)(2,1)S(1)}, u32[]{:S(2)}, u32[]{:S(2)}) async-start(bf16[16,4,1152]{2,1,0:T(4,128)(2,1)} %convert_element_type.287), calls=%async_computation | async-start | bytes 294912 | tf_op jit(solution)/shard_map/all_to_all | solution.py:119

commit v2 on v0

v2 whole, which is shorter than its diff:
```python
import jax
import jax.numpy as jnp
from jax import lax
from jax.experimental import pallas as pl
from jax.experimental.pallas import tpu as pltpu
from jax.sharding import Mesh, PartitionSpec as P

RATE = 18
EPSILON = 1e-05
F32 = jnp.float32
BF16 = jnp.bfloat16
VMEM_LIMIT = 48 * 1024 * 1024


def swapped(value):
    return lax.ppermute(value, "core", [(0, 1), (1, 0)])


def around(value, steps):
    return lax.ppermute(value, "x", [(source, (source + steps) % 4) for source in range(4)])


def along(value, steps):
    pairs = [(source, source + steps) for source in range(4) if 0 <= source + steps < 4]
    return lax.ppermute(value, "x", pairs)


def column_taps(block, col_count):
    cells, channels = block.shape
    wide = block.astype(F32)
    column = lax.broadcasted_iota(jnp.int32, (cells // col_count, col_count, channels), 1)
    column = column.reshape(cells, channels)
    before = jnp.where(column < col_count - RATE, pltpu.roll(wide, cells - RATE, 0), 0.0)
    after = jnp.where(column >= RATE, pltpu.roll(wide, RATE, 0), 0.0)
    return [before.astype(BF16), block, after.astype(BF16)]


def transposed(value):
    rows, columns = value.shape
    width = 256

    def body(in_ref, out_ref):
        out_ref[...] = in_ref[...].T

    return pl.pallas_call(
        body,
        grid=(columns // width,),
        in_specs=[pl.BlockSpec((rows, width), lambda i: (0, i))],
        out_specs=pl.BlockSpec((width, rows), lambda i: (i, 0)),
        out_shape=jax.ShapeDtypeStruct((columns, rows), value.dtype),
        compiler_params=pltpu.CompilerParams(vmem_limit_bytes=VMEM_LIMIT),
        cost_estimate=pl.CostEstimate(flops=0, bytes_accessed=4 * rows * columns, transcendentals=0),
    )(value)


def product_call(body, whole, fixed, lhs, blocks, columns, extra):
    channels_in, cells = lhs[0].shape
    steps = 4
    tall = channels_in // steps
    deep = channels_in // blocks // steps
    resident = lambda value: pl.BlockSpec(value.shape, lambda i: (0,) * value.ndim)
    return pl.pallas_call(
        body,
        grid=(steps,),
        in_specs=[pl.BlockSpec(memory_space=pltpu.SMEM)] * len(whole)
        + [resident(value) for value in fixed]
        + [pl.BlockSpec((tall, cells), lambda i: (i, 0)) for _ in lhs],
        out_specs=[pl.BlockSpec((blocks, deep, columns), lambda i: (0, i, 0))]
        + [resident(value) for value in extra],
        out_shape=[jax.ShapeDtypeStruct((blocks, deep * steps, columns), BF16)] + extra,
        scratch_shapes=[pltpu.VMEM((2, cells, columns), BF16)],
        compiler_params=pltpu.CompilerParams(vmem_limit_bytes=VMEM_LIMIT),
        cost_estimate=pl.CostEstimate(
            flops=4 * channels_in * cells * columns,
            bytes_accessed=4 * channels_in * cells + 2 * channels_in * columns,
            transcendentals=0,
        ),
    )(*whole, *fixed, *lhs)


def multiply(own_ref, other_ref, stacked, out_ref):
    total = jnp.dot(own_ref[...], stacked[0], preferred_element_type=F32)
    total = total + jnp.dot(other_ref[...], stacked[1], preferred_element_type=F32)
    blocks, deep, columns = out_ref.shape
    total = total.reshape(deep // 8, blocks, 8, columns)
    for group in range(deep // 16):
        pair = jnp.concatenate([total[2 * group], total[2 * group + 1]], axis=1)
        out_ref[:, group * 16 : group * 16 + 16, :] = pair.astype(BF16)


def middle_terms(pre_own, pre_other, own, other, col_count, blocks):
    width = pre_own.shape[1]

    def body(a_ref, b_ref, own_ref, other_ref, out_ref, stacked):
        @pl.when(pl.program_id(0) == 0)
        def _():
            for which, ref in enumerate((a_ref, b_ref)):
                for place, tap in enumerate(column_taps(ref[...], col_count)):
                    stacked[which, :, place * width : (place + 1) * width] = tap

        multiply(own_ref, other_ref, stacked, out_ref)

    return product_call(body, [], [pre_own, pre_other], [own, other], blocks, 3 * width, [])[0]


def side_terms(place, up, down, far, own, other, col_count, blocks):
    width = up.shape[1]

    def body(place_ref, up_ref, down_ref, far_ref, own_ref, other_ref, out_ref, mine_ref, theirs_ref, stacked):
        @pl.when(pl.program_id(0) == 0)
        def _():
            first = place_ref[1] == 0
            early = place_ref[0] < 2
            far_block = far_ref[...]
            zero = jnp.zeros_like(far_block)
            far_down = jnp.where(early, far_block, zero)
            far_up = jnp.where(early, zero, far_block)
            up_block, down_block = up_ref[...], down_ref[...]
            mine_ref[0] = jnp.where(first, down_block, far_down)
            theirs_ref[0] = jnp.where(first, far_down, down_block)
            mine_ref[1] = jnp.where(first, far_up, up_block)
            theirs_ref[1] = jnp.where(first, up_block, far_up)
            for which, ref in enumerate((mine_ref, theirs_ref)):
                for side in range(2):
                    for spot, tap in enumerate(column_taps(ref[side], col_count)):
                        at = (3 * side + spot) * width
                        stacked[which, :, at : at + width] = tap

        multiply(own_ref, other_ref, stacked, out_ref)

    pair = jax.ShapeDtypeStruct((2,) + up.shape, BF16)
    return product_call(body, [place], [up, down, far], [own, other], blocks, 6 * width, [pair, pair])


def per_device(inputs, conv_out, grad_out, relu_mask, norm_gain, weight):
    image_count, row_count, col_count, channels_in = inputs.shape
    channels_out = conv_out.shape[3]
    z_size, y_size, x_size = (lax.axis_size(axis) for axis in ("z", "y", "x"))
    cell_count = row_count * col_count * x_size * 2
    cells = image_count * row_count * col_count
    half = channels_out // 2
    core = lax.axis_index("core")
    x_place = lax.axis_index("x")

    input_flat = inputs.reshape(cells, channels_in)
    input_other = swapped(input_flat)
    passed = grad_out * relu_mask.astype(BF16)
    raw = jnp.stack([conv_out.reshape(cells, channels_out), passed.reshape(cells, channels_out)])
    mine = lax.dynamic_slice_in_dim(raw, core * half, half, axis=2)
    theirs = swapped(lax.dynamic_slice_in_dim(raw, (1 - core) * half, half, axis=2))
    both = jnp.stack([mine, theirs]).reshape(2, 2, image_count, row_count * col_count, half).astype(F32)
    values, passed = both[:, 0], both[:, 1]
    sums = jnp.stack(
        [jnp.sum(term, axis=(0, 2)) for term in (values, values * values, passed, passed * values)]
    )
    received = [around(sums, steps) for steps in (2, 1, 3)]
    means = (sums + received[0] + received[1] + received[2]) / cell_count
    chan_mean, second, passed_mean, product_mean = (means[n] for n in range(4))
    gain = lax.dynamic_slice_in_dim(norm_gain, core * half, half, axis=0)
    inv_std = 1.0 / jnp.sqrt(second - chan_mean * chan_mean + EPSILON)
    grad_mean = gain * passed_mean
    cross_mean = gain * (product_mean - chan_mean * passed_mean) * inv_std

    def spread(value):
        return value[None, :, None, :]

    normed = (values - spread(chan_mean)) * spread(inv_std)
    pre_grad = spread(inv_std) * (gain * passed - spread(grad_mean) - normed * spread(cross_mean))
    pre_grad = pre_grad.astype(BF16).reshape(2, cells, half)
    pre_own, pre_other = pre_grad[0], pre_grad[1]
    even = jnp.where(core == 0, pre_own, pre_other)
    odd = jnp.where(core == 0, pre_other, pre_own)
    far = around(jnp.where(x_place < 2, odd, even), 2)
    up = along(even, 1)
    down = along(odd, -1)

    own_t, other_t = transposed(input_flat), transposed(input_other)
    blocks = y_size * x_size
    middle = middle_terms(pre_own, pre_other, own_t, other_t, col_count, blocks)
    middle = lax.all_to_all(middle, ("y", "x"), 0, 0)
    place = jnp.stack([x_place, core]).astype(jnp.int32)
    sides, side_own, side_other = side_terms(
        place, up, down, far, own_t, other_t, col_count, blocks
    )
    sides = lax.all_to_all(sides, ("y", "x"), 0, 0)
    middle = jnp.sum(middle.astype(F32), axis=0)
    sides = jnp.sum(sides.astype(F32), axis=0)
    merged = jnp.concatenate([sides[:, : 3 * half], middle, sides[:, 3 * half :]], axis=1)
    rows = merged.shape[0] // z_size // 2
    merged = merged.astype(BF16).reshape(z_size * 2, rows, 9 * half)
    merged = lax.all_to_all(merged, ("z", "core"), 0, 0)
    merged = jnp.sum(merged.reshape(z_size, 2, rows, 9, half).astype(F32), axis=0)
    inv_images = 1.0 / (image_count * lax.axis_size(("z", "y")))
    weight_grad = jnp.moveaxis(merged, 0, 2).reshape(rows, 9, channels_out) * inv_images

    held = jnp.stack([side_own[0], pre_own, side_own[1]])
    got = swapped(jnp.stack([side_other[0], pre_other, side_other[1]]))
    lower = jnp.where(core == 0, held, got)
    upper = jnp.where(core == 0, got, held)
    full = jnp.concatenate([lower, upper], axis=2).reshape(
        3, image_count, row_count, col_count, channels_out
    )
    padded = jnp.pad(full, ((0, 0), (0, 0), (0, 0), (RATE, RATE), (0, 0)))
    pieces = [
        padded[n, :, :, RATE - RATE * step : RATE - RATE * step + col_count, :]
        for n in range(3)
        for step in (-1, 0, 1)
    ]
    stacked = jnp.concatenate(pieces, axis=3).reshape(cells, 9 * channels_out)
    weight, _ = lax.optimization_barrier((weight, pre_own))
    input_grad = lax.dot_general(
        stacked,
        weight.reshape(channels_in, 9 * channels_out),
        (((1,), (1,)), ((), ())),
        preferred_element_type=F32,
    ).astype(BF16)
    return (input_grad.reshape(inputs.shape), weight_grad)


def solution(mesh):
    parted = Mesh(mesh.devices.reshape(8, 4, 4, 2), ("z", "y", "x", "core"))
    cells = P(("z", "y"), ("x", "core"), None, None)
    return jax.shard_map(
        per_device,
        mesh=parted,
        in_specs=(cells, cells, cells, cells, P(), P()),
        out_specs=(cells, P(("z", "y", "x", "core"), None, None)),
        check_vma=False,
    )
```

time: 358 us -> 109 us (0.30)
  waiting for transfers between devices: 275 us -> 18.3 us
  starting transfers between devices: 7.13 us -> 36.6 us
  blocking collectives: 27.9 us -> 0 us
  Pallas kernels: 0 us -> 14.4 us
  between operations: 14.1 us -> 0.9 us
  matrix products: 16.5 us -> 9.02 us
  other arithmetic: 4.77 us -> 11.5 us
  local copies, waits for them, and re-layouts: 11.9 us -> 17.7 us
    unnamed x2 -> x0, waiting for transfers between devices: 266 us -> none
    psum x2 -> x0, blocking collectives: 27.9 us -> none  [the longest x1 15 us: per_device(): lax.psum((jnp.sum(values, axis=(1, 2)), jnp.sum(values * values, axis=(1,...]
    all_to_all x0 -> x3, starting transfers between devices: none -> 20.9 us  [the longest x1 9.76 us: per_device(): merged = lax.all_to_all(merged, ('z', 'core'), 0, 0)]
    all_to_all x0 -> x3, waiting for transfers between devices: none -> 15.6 us  [the longest x1 15.3 us: per_device(): sides = lax.all_to_all(sides, ('y', 'x'), 0, 0)]
    pallas_call x0 -> x4, Pallas kernels: none -> 14.4 us  [the longest x2 10.8 us: product_call(): pl.pallas_call(body, grid=(steps,), in_specs=[pl.BlockSpec(memory_space=p...]
    ppermute x2 -> x9, starting transfers between devices: 7.09 us -> 15.7 us  [the longest x3 6.05 us: swapped(): return lax.ppermute(value, 'core', [(0, 1), (1, 0)])]
    dot_general x2 -> x1, matrix products: 16.5 us -> 9.02 us  [per_device(): lax.dot_general(stacked, weight.reshape(channels_in, 9 * channels_out), (...]
    optimization_barrier x0 -> x1, local copies, waits for them, and re-layouts: none -> 6.64 us  [per_device(): weight, _ = lax.optimization_barrier((weight, pre_own))]
  transfers between devices with their start and end apart: 3 -> 12, of which waited for: 3 -> 4; matrix products, arithmetic and copies ran while one was open for 5% -> 28% of each run, Pallas kernels for 0% -> 13%
where the time goes in v2:
time: 109 us; the launch traced here: 108 us
  starting transfers between devices  36.6 us (34%)
  waiting for transfers between devices  18.3 us (17%)
  local copies, waits for them, and re-layouts  17.7 us (16%)
  Pallas kernels  14.4 us (13%)
  other arithmetic  11.5 us (11%)
  matrix products  9.02 us (8%)
    all_to_all x1, waiting for transfers between devices, per_device(): sides = lax.all_to_all(sides, ('y', 'x'), 0, 0)  15.3 us
    pallas_call x2, Pallas kernels, product_call(): pl.pallas_call(body, grid=(steps,), in_specs=[pl.BlockSpec(memory_space=p...  10.8 us
    all_to_all x1, starting transfers between devices, per_device(): merged = lax.all_to_all(merged, ('z', 'core'), 0, 0)  9.76 us
    dot_general x1, matrix products, per_device(): lax.dot_general(stacked, weight.reshape(channels_in, 9 * channels_out), (...  9.02 us
    unnamed x13, local copies, waits for them, and re-layouts  7.99 us
    all_to_all x1, starting transfers between devices, per_device(): sides = lax.all_to_all(sides, ('y', 'x'), 0, 0)  6.9 us
    optimization_barrier x1, local copies, waits for them, and re-layouts, per_device(): weight, _ = lax.optimization_barrier((weight, pre_own))  6.64 us
    ppermute x3, starting transfers between devices, swapped(): return lax.ppermute(value, 'core', [(0, 1), (1, 0)])  6.05 us
  transfers between devices with their start and end apart: 12, of which 4 were waited for; matrix products, arithmetic and copies ran while one was open for 28% of the time, Pallas kernels for 13%

profile of v2, /device:TPU:1, one launch (start us, length us, event | category | flops | bytes accessed | tf_op | source)
XLA Modules:
  0.0 108.5 jit_solution(14654400663556938369)
XLA Ops:
  0.6 1.4 %convert_multiply_fusion = bf16[2,6,72,256]{3,2,1,0:T(8,128)(2,1)S(1)} fusion(bf16[2,6,72,256]{3,2,1,0:T(8,128)(2,1)} %param.8, s32[2,6,72,256]{3,2,1,0:T(8,128)} %param.9), kind=kLoop, calls=%fused_computation.48 | loop fusion | flops 442368 | bytes 1769472 | tf_op jit(solution)/shard_map/mul | solution.py:147
  2.0 1.1 %fusion.9 = (bf16[2,864,128]{2,1,0:T(8,128)(2,1)S(1)}, bf16[2,864,128]{2,1,0:T(8,128)(2,1)S(1)}) fusion(s32[]{:T(128)S(6)} %select_n.39, bf16[1,864,256]{2,1,0:T(8,128)(2,1)} %bitcast.123, bf16[1,864,256]{2,1,0:T(8,128)(2,1)S(1)} %bitcast.115, s32[]{:T(128)S(6)} %select_n.40), kind=kLoop, calls=%fused_computation.38 | loop fusion | flops 1769472 | bytes 1769480 | tf_op jit(solution)/shard_map/stack | solution.py:148
  3.2 3.3 %collective-permute-start = (bf16[2,864,128]{2,1,0:T(8,128)(2,1)S(1)}, bf16[2,864,128]{2,1,0:T(8,128)(2,1)S(1)}, u32[]{:S(2)}, u32[]{:S(2)}) collective-permute-start(bf16[2,864,128]{2,1,0:T(8,128)(2,1)S(1)} %get-tuple-element.28), channel_id=1, source_target_pairs={{0,1},{1,0},{2,3},{3,2},{4,5},{5,4},{6,7},{7,6},{8,9},{9,8},{10,11... | collective-permute-start | bytes 1327112 | tf_op jit(solution)/shard_map/ppermute | solution.py:16
  6.5 0.1 collective-permute-start.7
  6.6 1.3 %collective-permute-done = bf16[2,864,128]{2,1,0:T(8,128)(2,1)S(1)} collective-permute-done((bf16[2,864,128]{2,1,0:T(8,128)(2,1)S(1)}, bf16[2,864,128]{2,1,0:T(8,128)(2,1)S(1)}, u32[]{:S(2)}, u32[]{:S(2)}) %collective-permute-start) | collective-permute-done | bytes 442400 | tf_op jit(solution)/shard_map/ppermute | solution.py:16
  7.9 0.1 maximum_convert_fusion
  8.1 0.1 fusion.5
  8.2 1.1 copy-done.2
  9.2 0.1 slice_reduce_fusion.1
  9.4 0.1 collective-permute-start.2
  9.5 2.7 %collective-permute-start.3 = (f32[4,2,128]{2,1,0:T(2,128)S(1)}, f32[4,2,128]{2,1,0:T(2,128)S(1)}, u32[]{:S(2)}, u32[]{:S(2)}) collective-permute-start(f32[4,2,128]{2,1,0:T(2,128)S(1)} %pad_maximum_fusion.4), channel_id=1, source_target_pairs={{0,6},{2,0},{4,2},{6,4},{1,7},{3,1},{5,3},{7,5},{8,14},{10,8},{12,... | collective-permute-start | bytes 12296 | tf_op jit(solution)/shard_map/ppermute | solution.py:20
  12.1 1.5 %copy-done.1 = bf16[2,6,72,1024]{3,2,1,0:T(8,128)(2,1)S(1)} copy-done((bf16[2,6,72,1024]{3,2,1,0:T(8,128)(2,1)S(1)}, bf16[2,6,72,1024]{3,2,1,0:T(8,128)(2,1)}, u32[]{:S(2)}) %copy-start.1) | copy-done | bytes 1769496
  13.6 1.0 shard_map.77.own_ref
  14.7 1.4 %collective-permute-done.1 = f32[4,2,128]{2,1,0:T(2,128)S(1)} collective-permute-done((f32[4,2,128]{2,1,0:T(2,128)S(1)}, f32[4,2,128]{2,1,0:T(2,128)S(1)}, u32[]{:S(2)}, u32[]{:S(2)}) %collective-permute-start.1) | collective-permute-done | bytes 4128 | tf_op jit(solution)/shard_map/ppermute | solution.py:20
  16.1 1.7 %fusion.4 = bf16[2,2,432,128]{3,2,1,0:T(8,128)(2,1)S(1)} fusion(f32[2,2,2,432,128]{4,3,2,0,1:T(8,128)} %copy-done.2, f32[2,128]{1,0:T(2,128)S(1)} %get-tuple-element.17, f32[2,128]{1,0:T(2,128)S(1)} %slice_bitcast_fusion.2, f32[2,128]{1,0:T(2,128)S(1)} %get-tuple-element.37, f32[128]{0:T(128)S(1)} %dynamic_slice.11, f32[2,128]{1,0:T(2,128)S(1)} %get-tuple-element.18), kind=kLoop, calls=%fused_computation.25 | loop fusion | flops 1769472 | bytes 2216448 | tf_op jit(solution)/shard_map/convert_element_type | solution.py:169
  17.9 0.8 broadcast_select_fusion.2
  18.6 1.6 %collective-permute-start.6 = (bf16[864,128]{1,0:T(8,128)(2,1)}, bf16[864,128]{1,0:T(8,128)(2,1)S(1)}, u32[]{:S(2)}, u32[]{:S(2)}) collective-permute-start(bf16[864,128]{1,0:T(8,128)(2,1)} %get-tuple-element.14), channel_id=1, source_target_pairs={{0,4},{2,6},{4,0},{6,2},{1,5},{3,7},{5,1},{7,3},{8,12},{10,14},{12... | collective-permute-start | bytes 663560 | tf_op jit(solution)/shard_map/ppermute | solution.py:20
  20.2 1.3 %collective-permute-start.5 = (bf16[864,128]{1,0:T(8,128)(2,1)S(1)}, bf16[864,128]{1,0:T(8,128)(2,1)S(1)}, u32[]{:S(2)}, u32[]{:S(2)}) collective-permute-start(bf16[864,128]{1,0:T(8,128)(2,1)S(1)} %get-tuple-element.15), channel_id=1, source_target_pairs={{2,0},{4,2},{6,4},{3,1},{5,3},{7,5},{10,8},{12,10},{14,12},{11,9},... | collective-permute-start | bytes 663560 | tf_op jit(solution)/shard_map/ppermute | solution.py:25
  21.5 4.0 %collective-permute-start.4 = (bf16[864,128]{1,0:T(8,128)(2,1)S(1)}, bf16[864,128]{1,0:T(8,128)(2,1)S(1)}, u32[]{:S(2)}, u32[]{:S(2)}) collective-permute-start(bf16[864,128]{1,0:T(8,128)(2,1)S(1)} %get-tuple-element.16), channel_id=1, source_target_pairs={{0,2},{2,4},{4,6},{1,3},{3,5},{5,7},{8,10},{10,12},{12,14},{9,11},... | collective-permute-start | bytes 663560 | tf_op jit(solution)/shard_map/ppermute | solution.py:25
  25.6 2.6 %shard_map.78.other_ref = bf16[1024,864]{1,0:T(8,128)(2,1)S(1)} custom-call(bf16[864,1024]{1,0:T(8,128)(2,1)} %collective-permute-done.7.in_ref), custom_call_target="tpu_custom_call" | custom-call | bytes 3538944 | tf_op jit(solution)/shard_map/pallas_call | solution.py:45
  28.2 3.8 %shard_map.80 = bf16[16,64,384]{2,1,0:T(8,128)(2,1)} custom-call(bf16[864,128]{1,0:T(8,128)(2,1)S(1)} %bitcast.107, bf16[864,128]{1,0:T(8,128)(2,1)S(1)} %bitcast.109, bf16[1024,864]{1,0:T(8,128)(2,1)S(1)} %shard_map.77.own_ref, bf16[1024,864]{1,0:T(8,128)(2,1)S(1)} %shard_map.78.other_ref), custom_call_target="tpu_custom_call" | custom-call | flops 1358954496 | bytes 4325376 | tf_op jit(solution)/shard_map/pallas_call | solution.py:62
  32.0 1.3 %copy-done = bf16[1024,864]{1,0:T(8,128)(2,1)} copy-done((bf16[1024,864]{1,0:T(8,128)(2,1)}, bf16[1024,864]{1,0:T(8,128)(2,1)S(1)}, u32[]{:S(2)}) %copy-start) | copy-done | bytes 1769496
  33.2 4.3 %all-to-all-start.1 = ((bf16[16,64,384]{2,1,0:T(8,128)(2,1)}), bf16[16,64,384]{2,1,0:T(8,128)(2,1)}, u32[]{:S(2)}, u32[]{:S(2)}) async-start(bf16[16,64,384]{2,1,0:T(8,128)(2,1)} %shard_map.80), calls=%async_computation.1 | async-start | bytes 1572864 | tf_op jit(solution)/shard_map/all_to_all | solution.py:180
  37.6 7.1 %shard_map.79 = (bf16[16,64,768]{2,1,0:T(8,128)(2,1)}, bf16[2,864,128]{2,1,0:T(8,128)(2,1)S(1)}, bf16[2,864,128]{2,1,0:T(8,128)(2,1)S(1)}) custom-call(s32[2]{0:T(128)S(1)} %pad_add_fusion.place_ref, bf16[864,128]{1,0:T(8,128)(2,1)S(1)} %collective-permute-done.4.up_ref, bf16[864,128]{1,0:T(8,128)(2,1)S(1)} %collective-permute-done.5.down_ref, ...), custom_call_target="tpu_custom_call" | custom-call | flops 2717908992 | bytes 5111808 | tf_op jit(solution)/shard_map/pallas_call | solution.py:62
  44.7 0.9 pad_maximum_fusion.2
  45.6 2.6 %collective-permute-start.8 = (bf16[3,864,128]{2,1,0:T(8,128)(2,1)}, bf16[3,864,128]{2,1,0:T(8,128)(2,1)S(1)}, u32[]{:S(2)}, u32[]{:S(2)}) collective-permute-start(bf16[3,864,128]{2,1,0:T(8,128)(2,1)} %pad_maximum_fusion.2), channel_id=1, source_target_pairs={{0,1},{1,0},{2,3},{3,2},{4,5},{5,4},{6,7},{7,6},{8,9},{9,8},{10,11... | collective-permute-start | bytes 1990664 | tf_op jit(solution)/shard_map/ppermute | solution.py:16
  48.2 6.6 %copy.21 = bf16[1024,9,256]{0,2,1:T(8,128)(2,1)} copy(bf16[1024,9,256]{2,0,1:T(8,128)(2,1)} %param.11) | data formatting | bytes 9437184 | tf_op jit(solution)/shard_map/optimization_barrier | solution.py:210
  54.9 6.9 %all-to-all-start = ((bf16[16,64,768]{2,1,0:T(8,128)(2,1)}), bf16[16,64,768]{2,1,0:T(8,128)(2,1)S(1)}, u32[]{:S(2)}, u32[]{:S(2)}) async-start(bf16[16,64,768]{2,1,0:T(8,128)(2,1)} %get-tuple-element.9), calls=%async_computation | async-start | bytes 3145728 | tf_op jit(solution)/shard_map/all_to_all | solution.py:185
  61.8 0.1 broadcast_select_fusion.1
  61.9 0.2 pad_maximum_fusion
  62.1 1.2 %pad_slice_fusion = (bf16[1,2,6,72,256]{4,3,2,1,0:T(8,128)(2,1)S(1)}, bf16[1,2,6,72,256]{4,3,2,1,0:T(8,128)(2,1)S(1)}, bf16[1,2,6,72,256]{4,3,2,1,0:T(8,128)(2,1...) fusion(bf16[3,2,6,72,256]{4,3,2,1,0:T(8,128)(2,1)S(1)} %bitcast.113), kind=kLoop, calls=%fused_computation | loop fusion | bytes 3981312 | tf_op jit(solution)/shard_map/slice | solution.py:205
  63.3 0.9 constant_dynamic-update-slice_fusion.5
  64.2 0.9 fusion.12
  65.0 0.8 constant_dynamic-update-slice_fusion.4
  65.9 0.8 constant_dynamic-update-slice_fusion.3
  66.7 0.9 fusion.15
  67.6 0.8 constant_dynamic-update-slice_fusion.2
  68.4 0.8 constant_dynamic-update-slice_fusion.1
  69.3 0.9 fusion.18
  70.2 0.8 constant_dynamic-update-slice_fusion
  71.0 1.2 %reduce.3 = bf16[64,384]{1,0:T(8,128)(2,1)S(1)} reduce(bf16[16,64,384]{2,1,0:T(8,128)(2,1)} %all-to-all-done.1, bf16[]{:T(256)} %constant.28.clone.1), dimensions={0}, to_apply=%region_5.6.clone | reduce | flops 368640 | bytes 835586 | tf_op jit(solution)/shard_map/reduce_sum | solution.py:186
  72.3 15.3 %all-to-all-done = bf16[16,64,768]{2,1,0:T(8,128)(2,1)S(1)} async-done(((bf16[16,64,768]{2,1,0:T(8,128)(2,1)}), bf16[16,64,768]{2,1,0:T(8,128)(2,1)S(1)}, u32[]{:S(2)}, u32[]{:S(2)}) %all-to-all-start) | async-done | bytes 1572896 | tf_op jit(solution)/shard_map/all_to_all | solution.py:185
  87.6 0.2 reduce.2
  87.9 0.7 pad_maximum_fusion.3
  88.6 9.8 %all-to-all-start.2 = ((bf16[16,4,1152]{2,1,0:T(4,128)(2,1)}), bf16[16,4,1152]{2,1,0:T(4,128)(2,1)S(1)}, u32[]{:S(2)}, u32[]{:S(2)}) async-start(bf16[16,4,1152]{2,1,0:T(4,128)(2,1)} %pad_maximum_fusion.3), calls=%async_computation.2 | async-start | bytes 294912 | tf_op jit(solution)/shard_map/all_to_all | solution.py:191
  98.3 9.0 %convolution_convert_fusion = bf16[864,1024]{1,0:T(8,128)(2,1)} fusion(bf16[864,2304]{1,0:T(8,128)(2,1)} %constant_dynamic-update-slice_fusion, bf16[1024,2304]{0,1:T(8,128)(2,1)} %bitcast.114), kind=kOutput, calls=%fused_computation.13 | convolution fusion | flops 4077748224 | bytes 10469376 | tf_op jit(solution)/shard_map/dot_general | solution.py:211
  107.4 0.3 all-to-all-done.2
  107.8 0.7 mul.125
  (32 shorter events, 0.5 us)
Async XLA Ops:
  3.2 4.7 %collective-permute-start = (bf16[2,864,128]{2,1,0:T(8,128)(2,1)S(1)}, bf16[2,864,128]{2,1,0:T(8,128)(2,1)S(1)}, u32[]{:S(2)}, u32[]{:S(2)}) collective-permute-start(bf16[2,864,128]{2,1,0:T(8,128)(2,1)S(1)} %get-tuple-element.28), channel_id=1, source_target_pairs={{0,1},{1,0},{2,3},{3,2},{4,5},{5,4},{6,7},{7,6},{8,9},{9,8},{10,11... | collective-permute-start | bytes 1327112 | tf_op jit(solution)/shard_map/ppermute | solution.py:16
  6.5 19.1 %collective-permute-start.7 = (bf16[864,1024]{1,0:T(8,128)(2,1)}, bf16[864,1024]{1,0:T(8,128)(2,1)}, u32[]{:S(2)}, u32[]{:S(2)}) collective-permute-start(bf16[864,1024]{1,0:T(8,128)(2,1)} %bitcast.111), channel_id=1, source_target_pairs={{0,1},{1,0},{2,3},{3,2},{4,5},{5,4},{6,7},{7,6},{8,9},{9,8},{10,11... | collective-permute-start | bytes 5308424 | tf_op jit(solution)/shard_map/ppermute | solution.py:16
  8.0 1.2 %copy-start.2 = (f32[2,2,2,432,128]{4,3,2,0,1:T(8,128)}, f32[2,2,2,432,128]{4,3,2,0,1:T(8,128)S(1)}, u32[]{:S(2)}) copy-start(f32[2,2,2,432,128]{4,3,2,0,1:T(8,128)S(1)} %maximum_convert_fusion) | copy-start | bytes 5308420
  8.0 6.6 %copy-start.3 = (f32[256]{0:T(256)S(1)}, f32[256]{0:T(256)}, u32[]{:S(2)}) copy-start(f32[256]{0:T(256)} %param.10) | copy-start | bytes 3076
  9.4 5.3 %collective-permute-start.2 = (f32[4,2,128]{2,1,0:T(2,128)S(1)}, f32[4,2,128]{2,1,0:T(2,128)S(1)}, u32[]{:S(2)}, u32[]{:S(2)}) collective-permute-start(f32[4,2,128]{2,1,0:T(2,128)S(1)} %pad_maximum_fusion.4), channel_id=1, source_target_pairs={{0,2},{2,4},{4,6},{6,0},{1,3},{3,5},{5,7},{7,1},{8,10},{10,12},{12... | collective-permute-start | bytes 12296 | tf_op jit(solution)/shard_map/ppermute | solution.py:20
  9.5 5.2 %collective-permute-start.3 = (f32[4,2,128]{2,1,0:T(2,128)S(1)}, f32[4,2,128]{2,1,0:T(2,128)S(1)}, u32[]{:S(2)}, u32[]{:S(2)}) collective-permute-start(f32[4,2,128]{2,1,0:T(2,128)S(1)} %pad_maximum_fusion.4), channel_id=1, source_target_pairs={{0,6},{2,0},{4,2},{6,4},{1,7},{3,1},{5,3},{7,5},{8,14},{10,8},{12,... | collective-permute-start | bytes 12296 | tf_op jit(solution)/shard_map/ppermute | solution.py:20
  12.1 4.0 %collective-permute-start.1 = (f32[4,2,128]{2,1,0:T(2,128)S(1)}, f32[4,2,128]{2,1,0:T(2,128)S(1)}, u32[]{:S(2)}, u32[]{:S(2)}) collective-permute-start(f32[4,2,128]{2,1,0:T(2,128)S(1)} %pad_maximum_fusion.4), channel_id=1, source_target_pairs={{0,4},{2,6},{4,0},{6,2},{1,5},{3,7},{5,1},{7,3},{8,12},{10,14},{12... | collective-permute-start | bytes 12296 | tf_op jit(solution)/shard_map/ppermute | solution.py:20
  12.1 1.5 %copy-start.1 = (bf16[2,6,72,1024]{3,2,1,0:T(8,128)(2,1)S(1)}, bf16[2,6,72,1024]{3,2,1,0:T(8,128)(2,1)}, u32[]{:S(2)}) copy-start(bf16[2,6,72,1024]{3,2,1,0:T(8,128)(2,1)} %param.6) | copy-start | bytes 5308420
  18.6 18.9 %collective-permute-start.6 = (bf16[864,128]{1,0:T(8,128)(2,1)}, bf16[864,128]{1,0:T(8,128)(2,1)S(1)}, u32[]{:S(2)}, u32[]{:S(2)}) collective-permute-start(bf16[864,128]{1,0:T(8,128)(2,1)} %get-tuple-element.14), channel_id=1, source_target_pairs={{0,4},{2,6},{4,0},{6,2},{1,5},{3,7},{5,1},{7,3},{8,12},{10,14},{12... | collective-permute-start | bytes 663560 | tf_op jit(solution)/shard_map/ppermute | solution.py:20
  20.2 17.3 %collective-permute-start.5 = (bf16[864,128]{1,0:T(8,128)(2,1)S(1)}, bf16[864,128]{1,0:T(8,128)(2,1)S(1)}, u32[]{:S(2)}, u32[]{:S(2)}) collective-permute-start(bf16[864,128]{1,0:T(8,128)(2,1)S(1)} %get-tuple-element.15), channel_id=1, source_target_pairs={{2,0},{4,2},{6,4},{3,1},{5,3},{7,5},{10,8},{12,10},{14,12},{11,9},... | collective-permute-start | bytes 663560 | tf_op jit(solution)/shard_map/ppermute | solution.py:25
  21.5 16.1 %collective-permute-start.4 = (bf16[864,128]{1,0:T(8,128)(2,1)S(1)}, bf16[864,128]{1,0:T(8,128)(2,1)S(1)}, u32[]{:S(2)}, u32[]{:S(2)}) collective-permute-start(bf16[864,128]{1,0:T(8,128)(2,1)S(1)} %get-tuple-element.16), channel_id=1, source_target_pairs={{0,2},{2,4},{4,6},{1,3},{3,5},{5,7},{8,10},{10,12},{12,14},{9,11},... | collective-permute-start | bytes 663560 | tf_op jit(solution)/shard_map/ppermute | solution.py:25
  32.0 1.3 %copy-start = (bf16[1024,864]{1,0:T(8,128)(2,1)}, bf16[1024,864]{1,0:T(8,128)(2,1)S(1)}, u32[]{:S(2)}) copy-start(bf16[1024,864]{1,0:T(8,128)(2,1)S(1)} %shard_map.78.other_ref) | copy-start | bytes 5308420
  33.2 21.6 %all-to-all-start.1 = ((bf16[16,64,384]{2,1,0:T(8,128)(2,1)}), bf16[16,64,384]{2,1,0:T(8,128)(2,1)}, u32[]{:S(2)}, u32[]{:S(2)}) async-start(bf16[16,64,384]{2,1,0:T(8,128)(2,1)} %shard_map.80), calls=%async_computation.1 | async-start | bytes 1572864 | tf_op jit(solution)/shard_map/all_to_all | solution.py:180
  45.6 16.2 %collective-permute-start.8 = (bf16[3,864,128]{2,1,0:T(8,128)(2,1)}, bf16[3,864,128]{2,1,0:T(8,128)(2,1)S(1)}, u32[]{:S(2)}, u32[]{:S(2)}) collective-permute-start(bf16[3,864,128]{2,1,0:T(8,128)(2,1)} %pad_maximum_fusion.2), channel_id=1, source_target_pairs={{0,1},{1,0},{2,3},{3,2},{4,5},{5,4},{6,7},{7,6},{8,9},{9,8},{10,11... | collective-permute-start | bytes 1990664 | tf_op jit(solution)/shard_map/ppermute | solution.py:16
  54.9 32.7 %all-to-all-start = ((bf16[16,64,768]{2,1,0:T(8,128)(2,1)}), bf16[16,64,768]{2,1,0:T(8,128)(2,1)S(1)}, u32[]{:S(2)}, u32[]{:S(2)}) async-start(bf16[16,64,768]{2,1,0:T(8,128)(2,1)} %get-tuple-element.9), calls=%async_computation | async-start | bytes 3145728 | tf_op jit(solution)/shard_map/all_to_all | solution.py:185
  88.6 19.1 %all-to-all-start.2 = ((bf16[16,4,1152]{2,1,0:T(4,128)(2,1)}), bf16[16,4,1152]{2,1,0:T(4,128)(2,1)S(1)}, u32[]{:S(2)}, u32[]{:S(2)}) async-start(bf16[16,4,1152]{2,1,0:T(4,128)(2,1)} %pad_maximum_fusion.3), calls=%async_computation.2 | async-start | bytes 294912 | tf_op jit(solution)/shard_map/all_to_all | solution.py:191

commit v3 on v0

v3 whole, which is shorter than its diff:
```python
import jax
import jax.numpy as jnp
from jax import lax
from jax.experimental import pallas as pl
from jax.experimental.pallas import tpu as pltpu
from jax.sharding import Mesh, PartitionSpec as P

RATE = 18
EPSILON = 1e-05
F32 = jnp.float32
BF16 = jnp.bfloat16
VMEM_LIMIT = 40 * 1024 * 1024
AXES = ("z", "y", "x", "core")
Z, Y, X, CORES = 8, 4, 4, 2
SMEM = pl.BlockSpec(memory_space=pltpu.SMEM)


def device(z, y, x, core):
    return ((z * Y + y) * X + x) * CORES + core


def swapped(value):
    return lax.ppermute(value, "core", [(0, 1), (1, 0)])


def around(value, steps):
    return lax.ppermute(value, "x", [(source, (source + steps) % X) for source in range(X)])


def along(value, steps):
    pairs = [(source, source + steps) for source in range(X) if 0 <= source + steps < X]
    return lax.ppermute(value, "x", pairs)


def crossed(value, steps):
    pairs = []
    for z in range(Z):
        for y in range(Y):
            for x in range(X):
                pairs.append((device(z, y, x, 0), device(z, (y + steps) % Y, x, 0)))
                pairs.append((device(z, y, x, 1), device(z, y, (x + steps) % X, 1)))
    return lax.ppermute(value, AXES, pairs)


def exchanged(value):
    groups = [[device(z, y, x, 0) for z in range(Z) for x in range(X)] for y in range(Y)]
    groups += [[device(z, y, x, 1) for z in range(Z) for y in range(Y)] for x in range(X)]
    return lax.all_to_all(value, AXES, 0, 0, axis_index_groups=groups)


def whole(shape):
    return pl.BlockSpec(shape, lambda *_: (0,) * len(shape))


def kernel_call(body, operands, in_specs, out_shape, out_specs, grid=(1,), scratch=(), flops=0):
    moved = sum(value.size * value.dtype.itemsize for value in operands)
    moved += sum(value.size * value.dtype.itemsize for value in out_shape)
    return pl.pallas_call(
        body,
        grid=grid,
        in_specs=in_specs,
        out_specs=out_specs,
        out_shape=out_shape,
        scratch_shapes=list(scratch),
        compiler_params=pltpu.CompilerParams(vmem_limit_bytes=VMEM_LIMIT),
        cost_estimate=pl.CostEstimate(flops=flops, bytes_accessed=moved, transcendentals=0),
    )(*operands)


def prepare(place, conv, grad, mask):
    cells, channels = conv.shape
    half = channels // 2
    steps = 2
    tall = cells // steps

    def body(place_ref, conv_ref, grad_ref, mask_ref, mine_ref, sent_ref):
        core = place_ref[2]
        passed = (grad_ref[...].astype(F32) * mask_ref[...].astype(F32)).astype(BF16)
        conv_block = conv_ref[...]
        first = core == 0
        for which, value in enumerate((conv_block, passed)):
            lower, upper = value[:, :half], value[:, half:]
            mine_ref[which] = jnp.where(first, lower, upper)
            sent_ref[which] = jnp.where(first, upper, lower)

    rows = pl.BlockSpec((tall, channels), lambda i: (i, 0))
    out = jax.ShapeDtypeStruct((2, cells, half), BF16)
    spec = pl.BlockSpec((2, tall, half), lambda i: (0, i, 0))
    return kernel_call(
        body, (place, conv, grad, mask), [SMEM, rows, rows, rows], [out, out], [spec, spec], (steps,)
    )


def statistics(mine, theirs, images):
    _, cells, half = mine.shape
    each = cells // images

    def body(mine_ref, theirs_ref, out_ref):
        for image in range(images):
            rows = pl.ds(image * each, each)
            total = [jnp.zeros((1, half), F32)] * 4
            for ref in (mine_ref, theirs_ref):
                values, passed = ref[0, rows, :].astype(F32), ref[1, rows, :].astype(F32)
                terms = (values, values * values, passed, passed * values)
                total = [old + jnp.sum(new, axis=0, keepdims=True) for old, new in zip(total, terms)]
            for kind in range(4):
                out_ref[pl.ds(kind * images + image, 1), :] = total[kind]

    out = jax.ShapeDtypeStruct((4 * images, half), F32)
    return kernel_call(
        body, (mine, theirs), [whole(mine.shape)] * 2, [out], [whole(out.shape)]
    )[0]


def pre_gradient(place, gain, sums, mine, theirs, images, cell_count):
    _, cells, half = mine.shape
    each = cells // images

    def body(place_ref, gain_ref, a_ref, b_ref, c_ref, d_ref, mine_ref, theirs_ref, even_ref, odd_ref, far_ref):
        first = place_ref[2] == 0
        early = place_ref[1] < X // 2
        means = (a_ref[...] + b_ref[...] + c_ref[...] + d_ref[...]) / cell_count
        gain_row = gain_ref[...]
        for image in range(images):
            rows = pl.ds(image * each, each)
            chan_mean, second, passed_mean, product_mean = (
                means[kind * images + image : kind * images + image + 1] for kind in range(4)
            )
            inv_std = 1.0 / jnp.sqrt(second - chan_mean * chan_mean + EPSILON)
            grad_mean = gain_row * passed_mean
            cross_mean = gain_row * (product_mean - chan_mean * passed_mean) * inv_std
            blocks = []
            for ref in (mine_ref, theirs_ref):
                values, passed = ref[0, rows, :].astype(F32), ref[1, rows, :].astype(F32)
                normed = (values - chan_mean) * inv_std
                blocks.append(inv_std * (gain_row * passed - grad_mean - normed * cross_mean))
            even = jnp.where(first, blocks[0], blocks[1])
            odd = jnp.where(first, blocks[1], blocks[0])
            even_ref[rows, :] = even.astype(BF16)
            odd_ref[rows, :] = odd.astype(BF16)
            far_ref[rows, :] = jnp.where(early, odd, even).astype(BF16)

    out = jax.ShapeDtypeStruct((cells, half), BF16)
    return kernel_call(
        body,
        (place, gain, *sums, mine, theirs),
        [SMEM, whole(gain.shape)] + [whole(sums[0].shape)] * 4 + [whole(mine.shape)] * 2,
        [out] * 3,
        [whole(out.shape)] * 3,
    )


def padded_count(cells):
    return -(-cells // 128) * 128


def transposed(own, other):
    cells, channels = own.shape
    deep = padded_count(cells)
    width = 256

    def body(own_ref, other_ref, out_ref):
        for which, ref in enumerate((own_ref, other_ref)):
            block = jnp.concatenate([ref[...], jnp.zeros((deep - cells, width), BF16)], axis=0)
            out_ref[:, which * deep : (which + 1) * deep] = block.T

    spec = pl.BlockSpec((cells, width), lambda i: (0, i))
    return kernel_call(
        body,
        (own, other),
        [spec, spec],
        [jax.ShapeDtypeStruct((channels, 2 * deep), BF16)],
        [pl.BlockSpec((width, 2 * deep), lambda i: (i, 0))],
        (channels // width,),
    )[0]


def column_taps(block, col_count):
    cells, channels = block.shape
    wide = block.astype(F32)
    column = lax.broadcasted_iota(jnp.int32, (cells // col_count, col_count, channels), 1)
    column = column.reshape(cells, channels)
    before = jnp.where(column < col_count - RATE, pltpu.roll(wide, cells - RATE, 0), 0.0)
    after = jnp.where(column >= RATE, pltpu.roll(wide, RATE, 0), 0.0)
    return before.astype(BF16), block, after.astype(BF16)


def fill(stacked, slot, place, block, col_count):
    cells, width = block.shape
    deep = padded_count(cells)
    for spot, tap in enumerate(column_taps(block, col_count)):
        columns = slice((place + spot) * width, (place + spot + 1) * width)
        stacked[slot * deep : slot * deep + cells, columns] = tap


def multiply(place_ref, lhs_ref, stacked, total, out_refs):
    columns = stacked.shape[1]
    product = jnp.dot(lhs_ref[...], stacked[...], preferred_element_type=F32)
    total[...] = product.reshape(total.shape)
    tall = total.shape[0] * 32

    @pl.when(place_ref[2] == 0)
    def _():
        for steps, ref in enumerate(out_refs):
            chunk = total[:, lax.rem(place_ref[0] + steps, Y), :, :, :]
            ref[...] = chunk.reshape(tall, columns).astype(BF16)

    @pl.when(place_ref[2] != 0)
    def _():
        for steps, ref in enumerate(out_refs):
            chunk = total[:, :, lax.rem(place_ref[1] + steps, X), :, :]
            ref[...] = chunk.reshape(tall, columns).astype(BF16)


def product_call(body, place, fixed, lhs, columns, extra):
    channels_in, deep = lhs.shape
    steps = 2
    tall = channels_in // steps
    chunk = jax.ShapeDtypeStruct((channels_in // 4, columns), BF16)
    return kernel_call(
        body,
        (place, *fixed, lhs),
        [SMEM] + [whole(value.shape) for value in fixed] + [pl.BlockSpec((tall, deep), lambda i: (i, 0))],
        [chunk] * 4 + extra,
        [pl.BlockSpec((tall // 4, columns), lambda i: (i, 0))] * 4 + [whole(value.shape) for value in extra],
        (steps,),
        [pltpu.VMEM((deep, columns), BF16), pltpu.VMEM((tall // 128, Y, X, 8, columns), F32)],
        2 * channels_in * deep * columns,
    )


def middle_terms(place, even, odd, lhs, col_count):
    cells, width = even.shape

    def body(place_ref, even_ref, odd_ref, lhs_ref, *rest):
        stacked, total = rest[4:]

        @pl.when(pl.program_id(0) == 0)
        def _():
            stacked[...] = jnp.zeros_like(stacked)
            first = place_ref[2] == 0
            even_block, odd_block = even_ref[...], odd_ref[...]
            fill(stacked, 0, 0, jnp.where(first, even_block, odd_block), col_count)
            fill(stacked, 1, 0, jnp.where(first, odd_block, even_block), col_count)

        multiply(place_ref, lhs_ref, stacked, total, rest[:4])

    return product_call(body, place, [even, odd], lhs, 3 * width, [])


def side_terms(place, even, odd, up, down, far, lhs, col_count):
    cells, width = up.shape

    def body(place_ref, even_ref, odd_ref, up_ref, down_ref, far_ref, lhs_ref, *rest):
        mine_ref, theirs_ref, stacked, total = rest[4:]

        @pl.when(pl.program_id(0) == 0)
        def _():
            stacked[...] = jnp.zeros_like(stacked)
            first = place_ref[2] == 0
            early = place_ref[1] < X // 2
            far_block = far_ref[...]
            zero = jnp.zeros_like(far_block)
            far_down = jnp.where(early, far_block, zero)
            far_up = jnp.where(early, zero, far_block)
            pairs = ((down_ref[...], far_down), (even_ref[...], odd_ref[...]), (far_up, up_ref[...]))
            for side, (lower, upper) in enumerate(pairs):
                mine = jnp.where(first, lower, upper)
                theirs = jnp.where(first, upper, lower)
                mine_ref[side] = mine
                theirs_ref[side] = theirs
                if side != 1:
                    fill(stacked, 0, 3 * (side // 2), mine, col_count)
                    fill(stacked, 1, 3 * (side // 2), theirs, col_count)

        multiply(place_ref, lhs_ref, stacked, total, rest[:4])

    triple = jax.ShapeDtypeStruct((3, cells, width), BF16)
    return product_call(body, place, [even, odd, up, down, far], lhs, 6 * width, [triple, triple])


def first_sum(middle, sides):
    rows, third = middle[0].shape

    def body(*refs):
        out_ref = refs[-1]
        middle_total = sum(ref[...].astype(F32) for ref in refs[:4])
        side_total = sum(ref[...].astype(F32) for ref in refs[4:8])
        out_ref[:, :third] = side_total[:, :third].astype(BF16)
        out_ref[:, third : 2 * third] = middle_total.astype(BF16)
        out_ref[:, 2 * third :] = side_total[:, third:].astype(BF16)

    steps = 2
    spec = lambda columns: pl.BlockSpec((rows // steps, columns), lambda i: (i, 0))
    return kernel_call(
        body,
        (*middle, *sides),
        [spec(third)] * 4 + [spec(2 * third)] * 4,
        [jax.ShapeDtypeStruct((rows, 3 * third), BF16)],
        [spec(3 * third)],
        (steps,),
    )[0]


def input_gradient(place, held, got, weight, col_count):
    _, cells, half = held.shape
    channels_in, deep = weight.shape
    width = 256

    def body(place_ref, held_ref, got_ref, weight_ref, out_ref, stacked):
        @pl.when(pl.program_id(0) == 0)
        def _():
            first = place_ref[2] == 0
            for side in range(3):
                mine, theirs = held_ref[side], got_ref[side]
                lower, upper = jnp.where(first, mine, theirs), jnp.where(first, theirs, mine)
                for part, block in enumerate((lower, upper)):
                    for spot, tap in enumerate(column_taps(block, col_count)):
                        start = (2 * (3 * side + spot) + part) * half
                        stacked[:, start : start + half] = tap

        out_ref[...] = lax.dot_general(
            stacked[...], weight_ref[...], (((1,), (1,)), ((), ())), preferred_element_type=F32
        ).astype(BF16)

    return kernel_call(
        body,
        (place, held, got, weight),
        [SMEM, whole(held.shape), whole(got.shape), pl.BlockSpec((width, deep), lambda i: (i, 0))],
        [jax.ShapeDtypeStruct((cells, channels_in), BF16)],
        [pl.BlockSpec((cells, width), lambda i: (0, i))],
        (channels_in // width,),
        [pltpu.VMEM((cells, deep), BF16)],
        2 * cells * deep * channels_in,
    )[0]


def per_device(inputs, conv_out, grad_out, relu_mask, norm_gain, weight):
    image_count, row_count, col_count, channels_in = inputs.shape
    channels_out = conv_out.shape[3]
    cell_count = row_count * col_count * X * CORES
    cells = image_count * row_count * col_count
    half = channels_out // 2
    core = lax.axis_index("core")
    place = jnp.stack([lax.axis_index("y"), lax.axis_index("x"), core]).astype(jnp.int32)

    input_flat = inputs.reshape(cells, channels_in)
    mine, sent = prepare(
        place,
        *(value.reshape(cells, channels_out) for value in (conv_out, grad_out, relu_mask)),
    )
    theirs = swapped(sent)
    input_other = swapped(input_flat)
    sums = statistics(mine, theirs, image_count)
    sums = [sums] + [around(sums, steps) for steps in (2, 1, 3)]
    gain = lax.dynamic_slice_in_dim(norm_gain, core * half, half, axis=0).reshape(1, half)
    even, odd, far = pre_gradient(place, gain, sums, mine, theirs, image_count, cell_count)
    far = around(far, 2)
    up = along(even, 1)
    down = along(odd, -1)

    lhs = transposed(input_flat, input_other)
    middle = middle_terms(place, even, odd, lhs, col_count)
    middle = [middle[0]] + [crossed(middle[steps], steps) for steps in (2, 1, 3)]
    *sides, held, sent = side_terms(place, even, odd, up, down, far, lhs, col_count)
    sides = [sides[0]] + [crossed(sides[steps], steps) for steps in (2, 1, 3)]
    merged = first_sum(middle, sides)
    merged = exchanged(merged.reshape(Z * 4, 8, 9 * half))
    inv_images = 1.0 / (image_count * Z * Y)
    merged = jnp.sum(merged.astype(F32), axis=0) * inv_images
    rows = merged.shape[0] // CORES
    kept = lax.dynamic_slice_in_dim(merged, core * rows, rows, axis=0)
    came = swapped(lax.dynamic_slice_in_dim(merged, (1 - core) * rows, rows, axis=0))
    kept, came = kept.reshape(rows, 9, half), came.reshape(rows, 9, half)
    weight_grad = jnp.concatenate(
        [jnp.where(core == 0, kept, came), jnp.where(core == 0, came, kept)], axis=2
    )

    weight, sent, _ = lax.optimization_barrier((weight, sent, sides[1]))
    got = swapped(sent)
    input_grad = input_gradient(
        place, held, got, weight.reshape(channels_in, 9 * channels_out), col_count
    )
    return (input_grad.reshape(inputs.shape), weight_grad)


def solution(mesh):
    parted = Mesh(mesh.devices.reshape(Z, Y, X, CORES), AXES)
    cells = P(("z", "y"), ("x", "core"), None, None)
    return jax.shard_map(
        per_device,
        mesh=parted,
        in_specs=(cells, cells, cells, cells, P(), P()),
        out_specs=(cells, P(AXES, None, None)),
        check_vma=False,
    )
```

time: 358 us -> 98.6 us (0.28)
  waiting for transfers between devices: 275 us -> 13.8 us
  starting transfers between devices: 7.13 us -> 38 us
  blocking collectives: 27.9 us -> 0 us
  Pallas kernels: 0 us -> 22.4 us
  matrix products: 16.5 us -> 0 us
  between operations: 14.1 us -> 0.78 us
  local copies, waits for them, and re-layouts: 11.9 us -> 21.9 us
  other arithmetic: 4.77 us -> 0.81 us
    unnamed x2 -> x0, waiting for transfers between devices: 266 us -> none
    psum x2 -> x0, blocking collectives: 27.9 us -> none  [the longest x1 15 us: per_device(): lax.psum((jnp.sum(values, axis=(1, 2)), jnp.sum(values * values, axis=(1,...]
    pallas_call x0 -> x8, Pallas kernels: none -> 22.4 us  [kernel_call(): pl.pallas_call(body, grid=grid, in_specs=in_specs, out_specs=out_specs, o...]
    ppermute x2 -> x16, starting transfers between devices: 7.09 us -> 27.1 us  [the longest x4 10.3 us: swapped(): return lax.ppermute(value, 'core', [(0, 1), (1, 0)])]
    dot_general x2 -> x0, matrix products: 16.5 us -> none  [the longest x1 9.02 us: per_device(): lax.dot_general(stacked, weight_flat, (((1,), (1,)), ((), ())), preferred...]
    all_to_all x0 -> x1, starting transfers between devices: none -> 10.9 us  [exchanged(): return lax.all_to_all(value, AXES, 0, 0, axis_index_groups=groups)]
    reshape x0 -> x2, local copies, waits for them, and re-layouts: none -> 6.88 us  [the longest x1 6.81 us: per_device(): weight.reshape(channels_in, 9 * channels_out)]
    optimization_barrier x0 -> x1, local copies, waits for them, and re-layouts: none -> 6.64 us  [per_device(): weight, sent, _ = lax.optimization_barrier((weight, sent, sides[1]))]
  transfers between devices with their start and end apart: 3 -> 17, of which waited for: 3 -> 4; matrix products, arithmetic and copies ran while one was open for 5% -> 14% of each run, Pallas kernels for 0% -> 22%
where the time goes in v3:
time: 98.6 us; the launch traced here: 97.8 us
  starting transfers between devices  38 us (39%)
  Pallas kernels  22.4 us (23%)
  local copies, waits for them, and re-layouts  21.9 us (22%)
  waiting for transfers between devices  13.8 us (14%)
    pallas_call x8, Pallas kernels, kernel_call(): pl.pallas_call(body, grid=grid, in_specs=in_specs, out_specs=out_specs, o...  22.4 us
    all_to_all x1, starting transfers between devices, exchanged(): return lax.all_to_all(value, AXES, 0, 0, axis_index_groups=groups)  10.9 us
    ppermute x4, starting transfers between devices, swapped(): return lax.ppermute(value, 'core', [(0, 1), (1, 0)])  10.3 us
    ppermute x6, waiting for transfers between devices, crossed(): return lax.ppermute(value, AXES, pairs)  8.94 us
    ppermute x6, starting transfers between devices, crossed(): return lax.ppermute(value, AXES, pairs)  8.5 us
    unnamed x18, local copies, waits for them, and re-layouts  8.34 us
    reshape x1, local copies, waits for them, and re-layouts, per_device(): weight.reshape(channels_in, 9 * channels_out)  6.81 us
    optimization_barrier x1, local copies, waits for them, and re-layouts, per_device(): weight, sent, _ = lax.optimization_barrier((weight, sent, sides[1]))  6.64 us
  transfers between devices with their start and end apart: 17, of which 4 were waited for; matrix products, arithmetic and copies ran while one was open for 14% of the time, Pallas kernels for 22%

profile of v3, /device:TPU:1, one launch (start us, length us, event | category | flops | bytes accessed | tf_op | source)
XLA Modules:
  0.0 97.8 jit_solution(1955290405849665963)
XLA Ops:
  0.6 0.0 copy-start
  0.7 3.3 %collective-permute-start.7 = (bf16[864,1024]{1,0:T(8,128)(2,1)}, bf16[864,1024]{1,0:T(8,128)(2,1)S(1)}, u32[]{:S(2)}, u32[]{:S(2)}) collective-permute-start(bf16[864,1024]{1,0:T(8,128)(2,1)} %bitcast.16), channel_id=1, source_target_pairs={{0,1},{1,0},{2,3},{3,2},{4,5},{5,4},{6,7},{7,6},{8,9},{9,8},{10,11... | collective-permute-start | bytes 5308424 | tf_op jit(solution)/shard_map/ppermute | solution.py:23
  4.0 0.1 pad_add_fusion.place_ref
  4.1 1.2 %copy-done.6 = s32[2,6,72,256]{3,2,1,0:T(8,128)S(1)} copy-done((s32[2,6,72,256]{3,2,1,0:T(8,128)S(1)}, s32[2,6,72,256]{3,2,1,0:T(8,128)}, u32[]{:S(2)}) %copy-start.6) | copy-done | bytes 884760
  5.2 1.0 %copy-done.7 = bf16[2,6,72,256]{3,2,1,0:T(8,128)(2,1)S(1)} copy-done((bf16[2,6,72,256]{3,2,1,0:T(8,128)(2,1)S(1)}, bf16[2,6,72,256]{3,2,1,0:T(8,128)(2,1)}, u32[]{:S(2)}) %copy-start.7) | copy-done | bytes 442392
  6.2 1.0 %copy-done.8 = bf16[2,6,72,256]{3,2,1,0:T(8,128)(2,1)S(1)} copy-done((bf16[2,6,72,256]{3,2,1,0:T(8,128)(2,1)S(1)}, bf16[2,6,72,256]{3,2,1,0:T(8,128)(2,1)}, u32[]{:S(2)}) %copy-start.8) | copy-done | bytes 442392
  7.3 1.5 %shard_map.77 = (bf16[2,864,128]{2,1,0:T(8,128)(2,1)S(1)}, bf16[2,864,128]{2,1,0:T(8,128)(2,1)}) custom-call(s32[3]{0:T(128)S(1)} %pad_add_fusion.place_ref, bf16[864,256]{1,0:T(8,128)(2,1)S(1)} %bitcast.19, bf16[864,256]{1,0:T(8,128)(2,1)S(1)} %bitcast.20, s32[864,256]{1,0:T(8,128)S(1)} %bitcast.18), custom_call_target="tpu_custom_call" | custom-call | bytes 2654220 | tf_op jit(solution)/shard_map/pallas_call | solution.py:58
  8.8 0.8 copy-done.3
  9.5 0.1 collective-permute-start
  9.7 2.0 %collective-permute-done.theirs_ref = bf16[2,864,128]{2,1,0:T(8,128)(2,1)} collective-permute-done((bf16[2,864,128]{2,1,0:T(8,128)(2,1)}, bf16[2,864,128]{2,1,0:T(8,128)(2,1)}, u32[]{:S(2)}, u32[]{:S(2)}) %collective-permute-start) | collective-permute-done | bytes 442400 | tf_op jit(solution)/shard_map/ppermute | solution.py:23
  11.7 1.0 %copy-done.4 = bf16[2,864,128]{2,1,0:T(8,128)(2,1)S(1)} copy-done((bf16[2,864,128]{2,1,0:T(8,128)(2,1)S(1)}, bf16[2,864,128]{2,1,0:T(8,128)(2,1)}, u32[]{:S(2)}) %copy-start.4) | copy-done | bytes 442392
  12.7 1.3 %shard_map.78.a_ref = f32[8,128]{1,0:T(8,128)S(1)} custom-call(bf16[2,864,128]{2,1,0:T(8,128)(2,1)S(1)} %copy-done.4, bf16[2,864,128]{2,1,0:T(8,128)(2,1)} %collective-permute-done.theirs_ref), custom_call_target="tpu_custom_call" | custom-call | bytes 888832 | tf_op jit(solution)/shard_map/pallas_call | solution.py:58
  14.0 0.8 collective-permute-start.3
  14.8 0.7 collective-permute-start.2
  15.5 1.0 %collective-permute-start.1 = (f32[8,128]{1,0:T(8,128)S(1)}, f32[8,128]{1,0:T(8,128)S(1)}, u32[]{:S(2)}, u32[]{:S(2)}) collective-permute-start(f32[8,128]{1,0:T(8,128)S(1)} %shard_map.78.a_ref), channel_id=1, source_target_pairs={{0,4},{2,6},{4,0},{6,2},{1,5},{3,7},{5,1},{7,3},{8,12},{10,14},{12... | collective-permute-start | bytes 12296 | tf_op jit(solution)/shard_map/ppermute | solution.py:27
  16.6 0.1 dynamic-slice_bitcast_fusion.gain_ref
  16.6 1.9 %collective-permute-done.2.c_ref = f32[8,128]{1,0:T(8,128)S(1)} collective-permute-done((f32[8,128]{1,0:T(8,128)S(1)}, f32[8,128]{1,0:T(8,128)S(1)}, u32[]{:S(2)}, u32[]{:S(2)}) %collective-permute-start.2) | collective-permute-done | bytes 4128 | tf_op jit(solution)/shard_map/ppermute | solution.py:27
  18.5 1.0 %collective-permute-done.1.b_ref = f32[8,128]{1,0:T(8,128)S(1)} collective-permute-done((f32[8,128]{1,0:T(8,128)S(1)}, f32[8,128]{1,0:T(8,128)S(1)}, u32[]{:S(2)}, u32[]{:S(2)}) %collective-permute-start.1) | collective-permute-done | bytes 4128 | tf_op jit(solution)/shard_map/ppermute | solution.py:27
  19.5 1.0 %copy-done.5 = bf16[2,864,128]{2,1,0:T(8,128)(2,1)S(1)} copy-done((bf16[2,864,128]{2,1,0:T(8,128)(2,1)S(1)}, bf16[2,864,128]{2,1,0:T(8,128)(2,1)}, u32[]{:S(2)}) %copy-start.5) | copy-done | bytes 442392
  20.5 1.4 %shard_map.79 = (bf16[864,128]{1,0:T(8,128)(2,1)S(1)}, bf16[864,128]{1,0:T(8,128)(2,1)S(1)}, bf16[864,128]{1,0:T(8,128)(2,1)S(1)}) custom-call(s32[3]{0:T(128)S(1)} %pad_add_fusion.place_ref, f32[1,128]{1,0:T(1,128)S(1)} %dynamic-slice_bitcast_fusion.gain_ref, f32[8,128]{1,0:T(8,128)S(1)} %shard_map.78.a_ref, f32[8,128]{1,0:T(8,128)S(1)} %collective-permute-done.1.b_ref, ...), custom_call_target="tpu_custom_call" | custom-call | bytes 1565196 | tf_op jit(solution)/shard_map/pallas_call | solution.py:58
  21.9 1.1 %collective-permute-start.6 = (bf16[864,128]{1,0:T(8,128)(2,1)S(1)}, bf16[864,128]{1,0:T(8,128)(2,1)S(1)}, u32[]{:S(2)}, u32[]{:S(2)}) collective-permute-start(bf16[864,128]{1,0:T(8,128)(2,1)S(1)} %get-tuple-element.23), channel_id=1, source_target_pairs={{0,4},{2,6},{4,0},{6,2},{1,5},{3,7},{5,1},{7,3},{8,12},{10,14},{12... | collective-permute-start | bytes 663560 | tf_op jit(solution)/shard_map/ppermute | solution.py:27
  23.0 3.4 %collective-permute-start.4 = (bf16[864,128]{1,0:T(8,128)(2,1)S(1)}, bf16[864,128]{1,0:T(8,128)(2,1)S(1)}, u32[]{:S(2)}, u32[]{:S(2)}) collective-permute-start(bf16[864,128]{1,0:T(8,128)(2,1)S(1)} %get-tuple-element.21.even_ref), channel_id=1, source_target_pairs={{0,2},{2,4},{4,6},{1,3},{3,5},{5,7},{8,10},{10,12},{12,14},{9,11},... | collective-permute-start | bytes 663560 | tf_op jit(solution)/shard_map/ppermute | solution.py:32
  26.4 1.3 %collective-permute-start.5 = (bf16[864,128]{1,0:T(8,128)(2,1)S(1)}, bf16[864,128]{1,0:T(8,128)(2,1)S(1)}, u32[]{:S(2)}, u32[]{:S(2)}) collective-permute-start(bf16[864,128]{1,0:T(8,128)(2,1)S(1)} %get-tuple-element.22.odd_ref), channel_id=1, source_target_pairs={{2,0},{4,2},{6,4},{3,1},{5,3},{7,5},{10,8},{12,10},{14,12},{11,9},... | collective-permute-start | bytes 663560 | tf_op jit(solution)/shard_map/ppermute | solution.py:32
  27.7 0.0 collective-permute-done.7.other_ref
  27.7 1.7 %shard_map.80.lhs_ref = bf16[1024,1792]{1,0:T(8,128)(2,1)S(1)} custom-call(bf16[864,1024]{1,0:T(8,128)(2,1)S(1)} %bitcast.17, bf16[864,1024]{1,0:T(8,128)(2,1)S(1)} %collective-permute-done.7.other_ref), custom_call_target="tpu_custom_call" | custom-call | bytes 7208960 | tf_op jit(solution)/shard_map/pallas_call | solution.py:58
  29.5 3.3 %shard_map.83 = (bf16[256,384]{1,0:T(8,128)(2,1)S(1)}, bf16[256,384]{1,0:T(8,128)(2,1)S(1)}, bf16[256,384]{1,0:T(8,128)(2,1)S(1)}, bf16[256,384]{1,0:T(8,128)(2,1)S(1)}) custom-call(s32[3]{0:T(128)S(1)} %pad_add_fusion.place_ref, bf16[864,128]{1,0:T(8,128)(2,1)S(1)} %get-tuple-element.21.even_ref, bf16[864,128]{1,0:T(8,128)(2,1)S(1)} %get-tuple-element.22.odd_ref, ...), custom_call_target="tpu_custom_call" | custom-call | flops 1409286144 | bytes 4898828 | tf_op jit(solution)/shard_map/pallas_call | solution.py:58
  32.8 2.6 %collective-permute-start.10 = (bf16[256,384]{1,0:T(8,128)(2,1)S(1)}, bf16[256,384]{1,0:T(8,128)(2,1)S(1)}, u32[]{:S(2)}, u32[]{:S(2)}) collective-permute-start(bf16[256,384]{1,0:T(8,128)(2,1)S(1)} %get-tuple-element.30), channel_id=1, source_target_pairs={{0,16},{1,5},{2,18},{3,7},{4,20},{5,1},{6,22},{7,3},{8,24},{9,13},... | collective-permute-start | bytes 589832 | tf_op jit(solution)/shard_map/ppermute | solution.py:42
  35.4 0.0 collective-permute-done.6.far_ref
  35.4 5.0 %shard_map.81 = (bf16[256,768]{1,0:T(8,128)(2,1)S(1)}, bf16[256,768]{1,0:T(8,128)(2,1)S(1)}, bf16[256,768]{1,0:T(8,128)(2,1)S(1)}, bf16[256,768]{1,0:T(8,128)(2,...) custom-call(s32[3]{0:T(128)S(1)} %pad_add_fusion.place_ref, ...), custom_call_target="tpu_custom_call" | custom-call | flops 2818572288 | bytes 7675916 | tf_op jit(solution)/shard_map/pallas_call | solution.py:58
  40.4 0.5 collective-permute-start.8
  40.9 2.1 %collective-permute-start.13 = (bf16[256,768]{1,0:T(8,128)(2,1)S(1)}, bf16[256,768]{1,0:T(8,128)(2,1)S(1)}, u32[]{:S(2)}, u32[]{:S(2)}) collective-permute-start(bf16[256,768]{1,0:T(8,128)(2,1)S(1)} %get-tuple-element.34), channel_id=1, source_target_pairs={{0,8},{1,3},{2,10},{3,5},{4,12},{5,7},{6,14},{7,1},{8,16},{9,11},{... | collective-permute-start | bytes 1179656 | tf_op jit(solution)/shard_map/ppermute | solution.py:42
  43.0 0.6 collective-permute-start.14
  43.6 0.9 collective-permute-start.11
  44.5 1.8 %collective-permute-start.12 = (bf16[256,384]{1,0:T(8,128)(2,1)S(1)}, bf16[256,384]{1,0:T(8,128)(2,1)S(1)}, u32[]{:S(2)}, u32[]{:S(2)}) collective-permute-start(bf16[256,384]{1,0:T(8,128)(2,1)S(1)} %get-tuple-element.32), channel_id=1, source_target_pairs={{0,24},{1,7},{2,26},{3,1},{4,28},{5,3},{6,30},{7,5},{8,0},{9,15},{... | collective-permute-start | bytes 589832 | tf_op jit(solution)/shard_map/ppermute | solution.py:42
  46.3 8.9 %collective-permute-done.11.refs_2_ = bf16[256,384]{1,0:T(8,128)(2,1)S(1)} collective-permute-done((bf16[256,384]{1,0:T(8,128)(2,1)S(1)}, bf16[256,384]{1,0:T(8,128)(2,1)S(1)}, u32[]{:S(2)}, u32[]{:S(2)}) %collective-permute-start.11) | collective-permute-done | bytes 196640 | tf_op jit(solution)/shard_map/ppermute | solution.py:42
  55.2 0.0 collective-permute-done.12.refs_3_
  55.2 0.0 collective-permute-done.8.refs_5_
  55.2 1.1 %shard_map.84 = bf16[256,1152]{1,0:T(8,128)(2,1)} custom-call(bf16[256,384]{1,0:T(8,128)(2,1)S(1)} %get-tuple-element.29.refs_0_, bf16[256,384]{1,0:T(8,128)(2,1)S(1)} %collective-permute-done.10.refs_1_, bf16[256,384]{1,0:T(8,128)(2,1)S(1)} %collective-permute-done.11.refs_2_, bf16[256,384]{1,0:T(8,128)(2,1)S(1)} %collective-permute-done.12.refs_3_, ...), custom_call_target="tpu_custom_call" | custom-call | bytes 2949120 | tf_op jit(solution)/shard_map/pallas_call | solution.py:58
  56.3 10.9 %all-to-all-start = ((bf16[32,8,1152]{2,1,0:T(8,128)(2,1)}), bf16[32,8,1152]{2,1,0:T(8,128)(2,1)S(1)}, u32[]{:S(2)}, u32[]{:S(2)}) async-start(bf16[32,8,1152]{2,1,0:T(8,128)(2,1)} %bitcast.10), calls=%async_computation | async-start | bytes 1179648 | tf_op jit(solution)/shard_map/all_to_all | solution.py:48
  67.2 4.1 %collective-permute-start.9 = (bf16[3,864,128]{2,1,0:T(8,128)(2,1)S(1)}, bf16[3,864,128]{2,1,0:T(8,128)(2,1)S(1)}, u32[]{:S(2)}, u32[]{:S(2)}) collective-permute-start(bf16[3,864,128]{2,1,0:T(8,128)(2,1)S(1)} %get-tuple-element.27), channel_id=1, source_target_pairs={{0,1},{1,0},{2,3},{3,2},{4,5},{5,4},{6,7},{7,6},{8,9},{9,8},{10,11... | collective-permute-start | bytes 1990664 | tf_op jit(solution)/shard_map/ppermute | solution.py:23
  71.4 6.6 %copy.9 = bf16[1024,9,256]{0,2,1:T(8,128)(2,1)} copy(bf16[1024,9,256]{2,0,1:T(8,128)(2,1)} %param.11) | data formatting | bytes 9437184 | tf_op jit(solution)/shard_map/optimization_barrier | solution.py:379
  78.0 6.8 %copy.10.weight_ref = bf16[1024,2304]{1,0:T(8,128)(2,1)} copy(bf16[1024,2304]{0,1:T(8,128)(2,1)} %bitcast.21) | data formatting | bytes 9437184 | tf_op jit(solution)/shard_map/reshape | solution.py:382
  84.8 0.0 all-to-all-done
  84.8 0.1 convert_reduce_fusion
  84.9 2.7 %collective-permute-start.15 = (f32[4,1152]{1,0:T(4,128)S(1)}, f32[4,1152]{1,0:T(4,128)S(1)}, u32[]{:S(2)}, u32[]{:S(2)}) collective-permute-start(f32[4,1152]{1,0:T(4,128)S(1)} %constant_dynamic-slice_fusion), channel_id=1, source_target_pairs={{0,1},{1,0},{2,3},{3,2},{4,5},{5,4},{6,7},{7,6},{8,9},{9,8},{10,11... | collective-permute-start | bytes 55304 | tf_op jit(solution)/shard_map/ppermute | solution.py:23
  87.6 2.3 %copy-done.1 = bf16[1024,2304]{1,0:T(8,128)(2,1)S(1)} copy-done((bf16[1024,2304]{1,0:T(8,128)(2,1)S(1)}, bf16[1024,2304]{1,0:T(8,128)(2,1)}, u32[]{:S(2)}) %copy-start.1) | copy-done | bytes 4718616
  90.0 7.2 %shard_map.82 = bf16[864,1024]{1,0:T(8,128)(2,1)} custom-call(s32[3]{0:T(128)S(1)} %pad_add_fusion.place_ref, bf16[3,864,128]{2,1,0:T(8,128)(2,1)S(1)} %get-tuple-element.24.held_ref, bf16[3,864,128]{2,1,0:T(8,128)(2,1)S(1)} %collective-permute-done.9.got_ref, bf16[1024,2304]{1,0:T(8,128)(2,1)S(1)} %copy-done.1), custom_call_target="tpu_custom_call" | custom-call | flops 4076863488 | bytes 7815180 | tf_op jit(solution)/shard_map/pallas_call | solution.py:58
  97.2 0.6 pad_maximum_fusion
  (21 shorter events, 0.1 us)
Async XLA Ops:
  0.6 15.9 %copy-start = (f32[256]{0:T(256)S(1)}, f32[256]{0:T(256)}, u32[]{:S(2)}) copy-start(f32[256]{0:T(256)} %param.10) | copy-start | bytes 3076
  0.6 27.1 %copy-start.2 = (bf16[2,6,72,1024]{3,2,1,0:T(8,128)(2,1)S(1)}, bf16[2,6,72,1024]{3,2,1,0:T(8,128)(2,1)}, u32[]{:S(2)}) copy-start(bf16[2,6,72,1024]{3,2,1,0:T(8,128)(2,1)} %param.6) | copy-start | bytes 5308420
  0.7 27.1 %collective-permute-start.7 = (bf16[864,1024]{1,0:T(8,128)(2,1)}, bf16[864,1024]{1,0:T(8,128)(2,1)S(1)}, u32[]{:S(2)}, u32[]{:S(2)}) collective-permute-start(bf16[864,1024]{1,0:T(8,128)(2,1)} %bitcast.16), channel_id=1, source_target_pairs={{0,1},{1,0},{2,3},{3,2},{4,5},{5,4},{6,7},{7,6},{8,9},{9,8},{10,11... | collective-permute-start | bytes 5308424 | tf_op jit(solution)/shard_map/ppermute | solution.py:23
  4.1 1.2 %copy-start.6 = (s32[2,6,72,256]{3,2,1,0:T(8,128)S(1)}, s32[2,6,72,256]{3,2,1,0:T(8,128)}, u32[]{:S(2)}) copy-start(s32[2,6,72,256]{3,2,1,0:T(8,128)} %param.9) | copy-start | bytes 2654212
  5.2 1.0 %copy-start.7 = (bf16[2,6,72,256]{3,2,1,0:T(8,128)(2,1)S(1)}, bf16[2,6,72,256]{3,2,1,0:T(8,128)(2,1)}, u32[]{:S(2)}) copy-start(bf16[2,6,72,256]{3,2,1,0:T(8,128)(2,1)} %param.7) | copy-start | bytes 1327108
  6.2 1.0 %copy-start.8 = (bf16[2,6,72,256]{3,2,1,0:T(8,128)(2,1)S(1)}, bf16[2,6,72,256]{3,2,1,0:T(8,128)(2,1)}, u32[]{:S(2)}) copy-start(bf16[2,6,72,256]{3,2,1,0:T(8,128)(2,1)} %param.8) | copy-start | bytes 1327108
  8.8 0.8 copy-start.3
  9.5 2.1 %collective-permute-start = (bf16[2,864,128]{2,1,0:T(8,128)(2,1)}, bf16[2,864,128]{2,1,0:T(8,128)(2,1)}, u32[]{:S(2)}, u32[]{:S(2)}) collective-permute-start(bf16[2,864,128]{2,1,0:T(8,128)(2,1)} %get-tuple-element.20), channel_id=1, source_target_pairs={{0,1},{1,0},{2,3},{3,2},{4,5},{5,4},{6,7},{7,6},{8,9},{9,8},{10,11... | collective-permute-start | bytes 1327112 | tf_op jit(solution)/shard_map/ppermute | solution.py:23
  11.7 1.0 %copy-start.4 = (bf16[2,864,128]{2,1,0:T(8,128)(2,1)S(1)}, bf16[2,864,128]{2,1,0:T(8,128)(2,1)}, u32[]{:S(2)}) copy-start(bf16[2,864,128]{2,1,0:T(8,128)(2,1)} %copy-done.3) | copy-start | bytes 1327108
  14.0 2.6 %collective-permute-start.3 = (f32[8,128]{1,0:T(8,128)S(1)}, f32[8,128]{1,0:T(8,128)S(1)}, u32[]{:S(2)}, u32[]{:S(2)}) collective-permute-start(f32[8,128]{1,0:T(8,128)S(1)} %shard_map.78.a_ref), channel_id=1, source_target_pairs={{0,6},{2,0},{4,2},{6,4},{1,7},{3,1},{5,3},{7,5},{8,14},{10,8},{12,... | collective-permute-start | bytes 12296 | tf_op jit(solution)/shard_map/ppermute | solution.py:27
  14.8 3.7 %collective-permute-start.2 = (f32[8,128]{1,0:T(8,128)S(1)}, f32[8,128]{1,0:T(8,128)S(1)}, u32[]{:S(2)}, u32[]{:S(2)}) collective-permute-start(f32[8,128]{1,0:T(8,128)S(1)} %shard_map.78.a_ref), channel_id=1, source_target_pairs={{0,2},{2,4},{4,6},{6,0},{1,3},{3,5},{5,7},{7,1},{8,10},{10,12},{12... | collective-permute-start | bytes 12296 | tf_op jit(solution)/shard_map/ppermute | solution.py:27
  15.5 4.0 %collective-permute-start.1 = (f32[8,128]{1,0:T(8,128)S(1)}, f32[8,128]{1,0:T(8,128)S(1)}, u32[]{:S(2)}, u32[]{:S(2)}) collective-permute-start(f32[8,128]{1,0:T(8,128)S(1)} %shard_map.78.a_ref), channel_id=1, source_target_pairs={{0,4},{2,6},{4,0},{6,2},{1,5},{3,7},{5,1},{7,3},{8,12},{10,14},{12... | collective-permute-start | bytes 12296 | tf_op jit(solution)/shard_map/ppermute | solution.py:27
  19.5 1.0 %copy-start.5 = (bf16[2,864,128]{2,1,0:T(8,128)(2,1)S(1)}, bf16[2,864,128]{2,1,0:T(8,128)(2,1)}, u32[]{:S(2)}) copy-start(bf16[2,864,128]{2,1,0:T(8,128)(2,1)} %copy-done.3) | copy-start | bytes 1327108
  21.9 13.5 %collective-permute-start.6 = (bf16[864,128]{1,0:T(8,128)(2,1)S(1)}, bf16[864,128]{1,0:T(8,128)(2,1)S(1)}, u32[]{:S(2)}, u32[]{:S(2)}) collective-permute-start(bf16[864,128]{1,0:T(8,128)(2,1)S(1)} %get-tuple-element.23), channel_id=1, source_target_pairs={{0,4},{2,6},{4,0},{6,2},{1,5},{3,7},{5,1},{7,3},{8,12},{10,14},{12... | collective-permute-start | bytes 663560 | tf_op jit(solution)/shard_map/ppermute | solution.py:27
  23.0 12.4 %collective-permute-start.4 = (bf16[864,128]{1,0:T(8,128)(2,1)S(1)}, bf16[864,128]{1,0:T(8,128)(2,1)S(1)}, u32[]{:S(2)}, u32[]{:S(2)}) collective-permute-start(bf16[864,128]{1,0:T(8,128)(2,1)S(1)} %get-tuple-element.21.even_ref), channel_id=1, source_target_pairs={{0,2},{2,4},{4,6},{1,3},{3,5},{5,7},{8,10},{10,12},{12,14},{9,11},... | collective-permute-start | bytes 663560 | tf_op jit(solution)/shard_map/ppermute | solution.py:32
  26.4 9.0 %collective-permute-start.5 = (bf16[864,128]{1,0:T(8,128)(2,1)S(1)}, bf16[864,128]{1,0:T(8,128)(2,1)S(1)}, u32[]{:S(2)}, u32[]{:S(2)}) collective-permute-start(bf16[864,128]{1,0:T(8,128)(2,1)S(1)} %get-tuple-element.22.odd_ref), channel_id=1, source_target_pairs={{2,0},{4,2},{6,4},{3,1},{5,3},{7,5},{10,8},{12,10},{14,12},{11,9},... | collective-permute-start | bytes 663560 | tf_op jit(solution)/shard_map/ppermute | solution.py:32
  32.8 11.7 %collective-permute-start.10 = (bf16[256,384]{1,0:T(8,128)(2,1)S(1)}, bf16[256,384]{1,0:T(8,128)(2,1)S(1)}, u32[]{:S(2)}, u32[]{:S(2)}) collective-permute-start(bf16[256,384]{1,0:T(8,128)(2,1)S(1)} %get-tuple-element.30), channel_id=1, source_target_pairs={{0,16},{1,5},{2,18},{3,7},{4,20},{5,1},{6,22},{7,3},{8,24},{9,13},... | collective-permute-start | bytes 589832 | tf_op jit(solution)/shard_map/ppermute | solution.py:42
  40.4 14.8 %collective-permute-start.8 = (bf16[256,768]{1,0:T(8,128)(2,1)S(1)}, bf16[256,768]{1,0:T(8,128)(2,1)S(1)}, u32[]{:S(2)}, u32[]{:S(2)}) collective-permute-start(bf16[256,768]{1,0:T(8,128)(2,1)S(1)} %get-tuple-element.26), channel_id=1, source_target_pairs={{0,16},{1,5},{2,18},{3,7},{4,20},{5,1},{6,22},{7,3},{8,24},{9,13},... | collective-permute-start | bytes 1179656 | tf_op jit(solution)/shard_map/ppermute | solution.py:42
  40.9 14.3 %collective-permute-start.13 = (bf16[256,768]{1,0:T(8,128)(2,1)S(1)}, bf16[256,768]{1,0:T(8,128)(2,1)S(1)}, u32[]{:S(2)}, u32[]{:S(2)}) collective-permute-start(bf16[256,768]{1,0:T(8,128)(2,1)S(1)} %get-tuple-element.34), channel_id=1, source_target_pairs={{0,8},{1,3},{2,10},{3,5},{4,12},{5,7},{6,14},{7,1},{8,16},{9,11},{... | collective-permute-start | bytes 1179656 | tf_op jit(solution)/shard_map/ppermute | solution.py:42
  43.0 12.2 %collective-permute-start.14 = (bf16[256,768]{1,0:T(8,128)(2,1)S(1)}, bf16[256,768]{1,0:T(8,128)(2,1)S(1)}, u32[]{:S(2)}, u32[]{:S(2)}) collective-permute-start(bf16[256,768]{1,0:T(8,128)(2,1)S(1)} %get-tuple-element.35), channel_id=1, source_target_pairs={{0,24},{1,7},{2,26},{3,1},{4,28},{5,3},{6,30},{7,5},{8,0},{9,15},{... | collective-permute-start | bytes 1179656 | tf_op jit(solution)/shard_map/ppermute | solution.py:42
  43.6 11.6 %collective-permute-start.11 = (bf16[256,384]{1,0:T(8,128)(2,1)S(1)}, bf16[256,384]{1,0:T(8,128)(2,1)S(1)}, u32[]{:S(2)}, u32[]{:S(2)}) collective-permute-start(bf16[256,384]{1,0:T(8,128)(2,1)S(1)} %get-tuple-element.31), channel_id=1, source_target_pairs={{0,8},{1,3},{2,10},{3,5},{4,12},{5,7},{6,14},{7,1},{8,16},{9,11},{... | collective-permute-start | bytes 589832 | tf_op jit(solution)/shard_map/ppermute | solution.py:42
  44.5 10.7 %collective-permute-start.12 = (bf16[256,384]{1,0:T(8,128)(2,1)S(1)}, bf16[256,384]{1,0:T(8,128)(2,1)S(1)}, u32[]{:S(2)}, u32[]{:S(2)}) collective-permute-start(bf16[256,384]{1,0:T(8,128)(2,1)S(1)} %get-tuple-element.32), channel_id=1, source_target_pairs={{0,24},{1,7},{2,26},{3,1},{4,28},{5,3},{6,30},{7,5},{8,0},{9,15},{... | collective-permute-start | bytes 589832 | tf_op jit(solution)/shard_map/ppermute | solution.py:42
  56.3 28.5 %all-to-all-start = ((bf16[32,8,1152]{2,1,0:T(8,128)(2,1)}), bf16[32,8,1152]{2,1,0:T(8,128)(2,1)S(1)}, u32[]{:S(2)}, u32[]{:S(2)}) async-start(bf16[32,8,1152]{2,1,0:T(8,128)(2,1)} %bitcast.10), calls=%async_computation | async-start | bytes 1179648 | tf_op jit(solution)/shard_map/all_to_all | solution.py:48
  67.2 20.4 %collective-permute-start.9 = (bf16[3,864,128]{2,1,0:T(8,128)(2,1)S(1)}, bf16[3,864,128]{2,1,0:T(8,128)(2,1)S(1)}, u32[]{:S(2)}, u32[]{:S(2)}) collective-permute-start(bf16[3,864,128]{2,1,0:T(8,128)(2,1)S(1)} %get-tuple-element.27), channel_id=1, source_target_pairs={{0,1},{1,0},{2,3},{3,2},{4,5},{5,4},{6,7},{7,6},{8,9},{9,8},{10,11... | collective-permute-start | bytes 1990664 | tf_op jit(solution)/shard_map/ppermute | solution.py:23
  84.9 12.2 %collective-permute-start.15 = (f32[4,1152]{1,0:T(4,128)S(1)}, f32[4,1152]{1,0:T(4,128)S(1)}, u32[]{:S(2)}, u32[]{:S(2)}) collective-permute-start(f32[4,1152]{1,0:T(4,128)S(1)} %constant_dynamic-slice_fusion), channel_id=1, source_target_pairs={{0,1},{1,0},{2,3},{3,2},{4,5},{5,4},{6,7},{7,6},{8,9},{9,8},{10,11... | collective-permute-start | bytes 55304 | tf_op jit(solution)/shard_map/ppermute | solution.py:23
  87.6 2.3 %copy-start.1 = (bf16[1024,2304]{1,0:T(8,128)(2,1)S(1)}, bf16[1024,2304]{1,0:T(8,128)(2,1)}, u32[]{:S(2)}) copy-start(bf16[1024,2304]{1,0:T(8,128)(2,1)} %copy.10.weight_ref) | copy-start | bytes 14155780

commit v4 on v3

--- a/solution.py
+++ b/solution.py
@@ -9,7 +9,7 @@
 EPSILON = 1e-05
 F32 = jnp.float32
 BF16 = jnp.bfloat16
-VMEM_LIMIT = 40 * 1024 * 1024
+MIB = 1024 * 1024
 AXES = ("z", "y", "x", "core")
 Z, Y, X, CORES = 8, 4, 4, 2
 SMEM = pl.BlockSpec(memory_space=pltpu.SMEM)
@@ -52,9 +52,11 @@
     return pl.BlockSpec(shape, lambda *_: (0,) * len(shape))
 
 
-def kernel_call(body, operands, in_specs, out_shape, out_specs, grid=(1,), scratch=(), flops=0):
+def kernel_call(body, operands, in_specs, out_shape, out_specs, grid=(1,), scratch=(), flops=0, vmem=8, light=False):
     moved = sum(value.size * value.dtype.itemsize for value in operands)
     moved += sum(value.size * value.dtype.itemsize for value in out_shape)
+    if light:
+        moved, flops = 0, 0
     return pl.pallas_call(
         body,
         grid=grid,
@@ -62,54 +64,62 @@
         out_specs=out_specs,
         out_shape=out_shape,
         scratch_shapes=list(scratch),
-        compiler_params=pltpu.CompilerParams(vmem_limit_bytes=VMEM_LIMIT),
+        compiler_params=pltpu.CompilerParams(vmem_limit_bytes=vmem * MIB),
         cost_estimate=pl.CostEstimate(flops=flops, bytes_accessed=moved, transcendentals=0),
     )(*operands)
 
 
-def prepare(place, conv, grad, mask):
-    cells, channels = conv.shape
+def prepare(place, conv, grad, mask, images):
+    channels = conv.shape[3]
     half = channels // 2
-    steps = 2
-    tall = cells // steps
-
-    def body(place_ref, conv_ref, grad_ref, mask_ref, mine_ref, sent_ref):
-        core = place_ref[2]
-        passed = (grad_ref[...].astype(F32) * mask_ref[...].astype(F32)).astype(BF16)
-        conv_block = conv_ref[...]
-        first = core == 0
-        for which, value in enumerate((conv_block, passed)):
-            lower, upper = value[:, :half], value[:, half:]
-            mine_ref[which] = jnp.where(first, lower, upper)
-            sent_ref[which] = jnp.where(first, upper, lower)
-
-    rows = pl.BlockSpec((tall, channels), lambda i: (i, 0))
+    each = conv.shape[1] * conv.shape[2]
+    cells = images * each
+
+    def body(place_ref, *refs):
+        sources, (mine_ref, sent_ref, mine_sum_ref, sent_sum_ref) = refs[:3], refs[3:7]
+        buffers, sems = refs[7:10], refs[10]
+        first = place_ref[2] == 0
+        copies = [
+            [
+                pltpu.make_async_copy(source.at[image], buffer.at[image], sems.at[image, n])
+                for n, (source, buffer) in enumerate(zip(sources, buffers))
+            ]
+            for image in range(images)
+        ]
+        for group in copies:
+            for copy in group:
+                copy.start()
+        for image in range(images):
+            for copy in copies[image]:
+                copy.wait()
+            rows = slice(image * each, (image + 1) * each)
+            conv_block, grad_block, mask_block = (buffer[image].reshape(each, channels) for buffer in buffers)
+            passed = grad_block.astype(F32) * mask_block.astype(F32)
+            values = conv_block.astype(F32)
+            for which, value in enumerate((conv_block, passed.astype(BF16))):
+                lower, upper = value[:, :half], value[:, half:]
+                mine_ref[which, rows, :] = jnp.where(first, lower, upper)
+                sent_ref[which, rows, :] = jnp.where(first, upper, lower)
+            for kind, term in enumerate((values, values * values, passed, passed * values)):
+                total = jnp.sum(term, axis=0, keepdims=True)
+                lower, upper = total[:, :half], total[:, half:]
+                row = slice(kind * images + image, kind * images + image + 1)
+                mine_sum_ref[row, :] = jnp.where(first, lower, upper)
+                sent_sum_ref[row, :] = jnp.where(first, upper, lower)
+
     out = jax.ShapeDtypeStruct((2, cells, half), BF16)
-    spec = pl.BlockSpec((2, tall, half), lambda i: (0, i, 0))
-    return kernel_call(
-        body, (place, conv, grad, mask), [SMEM, rows, rows, rows], [out, out], [spec, spec], (steps,)
-    )
-
-
-def statistics(mine, theirs, images):
-    _, cells, half = mine.shape
-    each = cells // images
-
-    def body(mine_ref, theirs_ref, out_ref):
-        for image in range(images):
-            rows = pl.ds(image * each, each)
-            total = [jnp.zeros((1, half), F32)] * 4
-            for ref in (mine_ref, theirs_ref):
-                values, passed = ref[0, rows, :].astype(F32), ref[1, rows, :].astype(F32)
-                terms = (values, values * values, passed, passed * values)
-                total = [old + jnp.sum(new, axis=0, keepdims=True) for old, new in zip(total, terms)]
-            for kind in range(4):
-                out_ref[pl.ds(kind * images + image, 1), :] = total[kind]
-
-    out = jax.ShapeDtypeStruct((4 * images, half), F32)
-    return kernel_call(
-        body, (mine, theirs), [whole(mine.shape)] * 2, [out], [whole(out.shape)]
-    )[0]
+    total = jax.ShapeDtypeStruct((4 * images, half), F32)
+    outs = [out, out, total, total]
+    return kernel_call(
+        body,
+        (place, conv, grad, mask),
+        [SMEM] + [pl.BlockSpec(memory_space=pltpu.HBM)] * 3,
+        outs,
+        [whole(value.shape) for value in outs],
+        scratch=[pltpu.VMEM(value.shape, value.dtype) for value in (conv, grad, mask)]
+        + [pltpu.SemaphoreType.DMA((images, 3))],
+        vmem=60,
+    )
 
 
 def pre_gradient(place, gain, sums, mine, theirs, images, cell_count):
@@ -172,6 +182,7 @@
         [jax.ShapeDtypeStruct((channels, 2 * deep), BF16)],
         [pl.BlockSpec((width, 2 * deep), lambda i: (i, 0))],
         (channels // width,),
+        light=True,
     )[0]
 
 
@@ -193,7 +204,14 @@
         stacked[slot * deep : slot * deep + cells, columns] = tap
 
 
-def multiply(place_ref, lhs_ref, stacked, total, out_refs):
+def clear_padding(stacked, cells):
+    deep, columns = stacked.shape
+    block = deep // 2
+    for slot in range(2):
+        stacked[slot * block + cells : (slot + 1) * block, :] = jnp.zeros((block - cells, columns), BF16)
+
+
+def multiply(place_ref, lhs_ref, stacked, total, store):
     columns = stacked.shape[1]
     product = jnp.dot(lhs_ref[...], stacked[...], preferred_element_type=F32)
     total[...] = product.reshape(total.shape)
@@ -201,31 +219,34 @@
 
     @pl.when(place_ref[2] == 0)
     def _():
-        for steps, ref in enumerate(out_refs):
+        for steps in range(Y):
             chunk = total[:, lax.rem(place_ref[0] + steps, Y), :, :, :]
-            ref[...] = chunk.reshape(tall, columns).astype(BF16)
+            store(steps, chunk.reshape(tall, columns).astype(BF16))
 
     @pl.when(place_ref[2] != 0)
     def _():
-        for steps, ref in enumerate(out_refs):
+        for steps in range(X):
             chunk = total[:, :, lax.rem(place_ref[1] + steps, X), :, :]
-            ref[...] = chunk.reshape(tall, columns).astype(BF16)
-
-
-def product_call(body, place, fixed, lhs, columns, extra):
+            store(steps, chunk.reshape(tall, columns).astype(BF16))
+
+
+def product_call(body, place, fixed, lhs, terms, columns, wide, extra, light=False):
     channels_in, deep = lhs.shape
     steps = 2
     tall = channels_in // steps
-    chunk = jax.ShapeDtypeStruct((channels_in // 4, columns), BF16)
-    return kernel_call(
-        body,
-        (place, *fixed, lhs),
-        [SMEM] + [whole(value.shape) for value in fixed] + [pl.BlockSpec((tall, deep), lambda i: (i, 0))],
-        [chunk] * 4 + extra,
-        [pl.BlockSpec((tall // 4, columns), lambda i: (i, 0))] * 4 + [whole(value.shape) for value in extra],
+    chunk = lambda width: pl.BlockSpec((tall // 4, width), lambda i: (i, 0))
+    return kernel_call(
+        body,
+        (place, *fixed, lhs, *terms),
+        [SMEM] + [whole(value.shape) for value in fixed] + [pl.BlockSpec((tall, deep), lambda i: (i, 0))]
+        + [chunk(value.shape[1]) for value in terms],
+        [jax.ShapeDtypeStruct((channels_in // 4, wide), BF16)] * 4 + extra,
+        [chunk(wide)] * 4 + [whole(value.shape) for value in extra],
         (steps,),
         [pltpu.VMEM((deep, columns), BF16), pltpu.VMEM((tall // 128, Y, X, 8, columns), F32)],
         2 * channels_in * deep * columns,
+        24,
+        light,
     )
 
 
@@ -237,26 +258,31 @@
 
         @pl.when(pl.program_id(0) == 0)
         def _():
-            stacked[...] = jnp.zeros_like(stacked)
+            clear_padding(stacked, cells)
             first = place_ref[2] == 0
             even_block, odd_block = even_ref[...], odd_ref[...]
             fill(stacked, 0, 0, jnp.where(first, even_block, odd_block), col_count)
             fill(stacked, 1, 0, jnp.where(first, odd_block, even_block), col_count)
 
-        multiply(place_ref, lhs_ref, stacked, total, rest[:4])
-
-    return product_call(body, place, [even, odd], lhs, 3 * width, [])
-
-
-def side_terms(place, even, odd, up, down, far, lhs, col_count):
+        def store(steps, chunk):
+            rest[steps][...] = chunk
+
+        multiply(place_ref, lhs_ref, stacked, total, store)
+
+    return product_call(body, place, [even, odd], lhs, [], 3 * width, 3 * width, [], True)
+
+
+def all_terms(place, even, odd, up, down, far, lhs, middle, col_count):
     cells, width = up.shape
+    third = 3 * width
 
     def body(place_ref, even_ref, odd_ref, up_ref, down_ref, far_ref, lhs_ref, *rest):
-        mine_ref, theirs_ref, stacked, total = rest[4:]
+        middle_refs, out_refs = rest[:4], rest[4:8]
+        mine_ref, theirs_ref, stacked, total = rest[8:]
 
         @pl.when(pl.program_id(0) == 0)
         def _():
-            stacked[...] = jnp.zeros_like(stacked)
+            clear_padding(stacked, cells)
             first = place_ref[2] == 0
             early = place_ref[1] < X // 2
             far_block = far_ref[...]
@@ -273,38 +299,35 @@
                     fill(stacked, 0, 3 * (side // 2), mine, col_count)
                     fill(stacked, 1, 3 * (side // 2), theirs, col_count)
 
-        multiply(place_ref, lhs_ref, stacked, total, rest[:4])
+        def store(steps, chunk):
+            out_refs[steps][:, :third] = chunk[:, :third]
+            out_refs[steps][:, third : 2 * third] = middle_refs[steps][...]
+            out_refs[steps][:, 2 * third :] = chunk[:, third:]
+
+        multiply(place_ref, lhs_ref, stacked, total, store)
 
     triple = jax.ShapeDtypeStruct((3, cells, width), BF16)
-    return product_call(body, place, [even, odd, up, down, far], lhs, 6 * width, [triple, triple])
-
-
-def first_sum(middle, sides):
-    rows, third = middle[0].shape
+    return product_call(
+        body, place, [even, odd, up, down, far], lhs, middle, 2 * third, 3 * third, [triple, triple]
+    )
+
+
+def first_sum(terms):
+    rows, columns = terms[0].shape
 
     def body(*refs):
-        out_ref = refs[-1]
-        middle_total = sum(ref[...].astype(F32) for ref in refs[:4])
-        side_total = sum(ref[...].astype(F32) for ref in refs[4:8])
-        out_ref[:, :third] = side_total[:, :third].astype(BF16)
-        out_ref[:, third : 2 * third] = middle_total.astype(BF16)
-        out_ref[:, 2 * third :] = side_total[:, third:].astype(BF16)
+        refs[-1][...] = sum(ref[...].astype(F32) for ref in refs[:-1]).astype(BF16)
 
     steps = 2
-    spec = lambda columns: pl.BlockSpec((rows // steps, columns), lambda i: (i, 0))
-    return kernel_call(
-        body,
-        (*middle, *sides),
-        [spec(third)] * 4 + [spec(2 * third)] * 4,
-        [jax.ShapeDtypeStruct((rows, 3 * third), BF16)],
-        [spec(3 * third)],
-        (steps,),
+    spec = pl.BlockSpec((rows // steps, columns), lambda i: (i, 0))
+    return kernel_call(
+        body, terms, [spec] * 4, [jax.ShapeDtypeStruct((rows, columns), BF16)], [spec], (steps,)
     )[0]
 
 
 def input_gradient(place, held, got, weight, col_count):
     _, cells, half = held.shape
-    channels_in, deep = weight.shape
+    deep, channels_in = weight.shape
     width = 256
 
     def body(place_ref, held_ref, got_ref, weight_ref, out_ref, stacked):
@@ -319,19 +342,20 @@
                         start = (2 * (3 * side + spot) + part) * half
                         stacked[:, start : start + half] = tap
 
-        out_ref[...] = lax.dot_general(
-            stacked[...], weight_ref[...], (((1,), (1,)), ((), ())), preferred_element_type=F32
+        out_ref[...] = jnp.dot(
+            stacked[...], weight_ref[...], preferred_element_type=F32
         ).astype(BF16)
 
     return kernel_call(
         body,
         (place, held, got, weight),
-        [SMEM, whole(held.shape), whole(got.shape), pl.BlockSpec((width, deep), lambda i: (i, 0))],
+        [SMEM, whole(held.shape), whole(got.shape), pl.BlockSpec((deep, width), lambda i: (0, i))],
         [jax.ShapeDtypeStruct((cells, channels_in), BF16)],
         [pl.BlockSpec((cells, width), lambda i: (0, i))],
         (channels_in // width,),
         [pltpu.VMEM((cells, deep), BF16)],
         2 * cells * deep * channels_in,
+        24,
     )[0]
 
 
@@ -345,26 +369,24 @@
     place = jnp.stack([lax.axis_index("y"), lax.axis_index("x"), core]).astype(jnp.int32)
 
     input_flat = inputs.reshape(cells, channels_in)
-    mine, sent = prepare(
-        place,
-        *(value.reshape(cells, channels_out) for value in (conv_out, grad_out, relu_mask)),
-    )
+    mine, sent, sums, sent_sums = prepare(place, conv_out, grad_out, relu_mask, image_count)
+    got_sums = swapped(sent_sums)
+    input_flat, sent, got_sums = lax.optimization_barrier((input_flat, sent, got_sums))
     theirs = swapped(sent)
     input_other = swapped(input_flat)
-    sums = statistics(mine, theirs, image_count)
+    sums = sums + got_sums
     sums = [sums] + [around(sums, steps) for steps in (2, 1, 3)]
     gain = lax.dynamic_slice_in_dim(norm_gain, core * half, half, axis=0).reshape(1, half)
+    lhs = transposed(input_flat, input_other)
     even, odd, far = pre_gradient(place, gain, sums, mine, theirs, image_count, cell_count)
     far = around(far, 2)
     up = along(even, 1)
     down = along(odd, -1)
 
-    lhs = transposed(input_flat, input_other)
     middle = middle_terms(place, even, odd, lhs, col_count)
-    middle = [middle[0]] + [crossed(middle[steps], steps) for steps in (2, 1, 3)]
-    *sides, held, sent = side_terms(place, even, odd, up, down, far, lhs, col_count)
-    sides = [sides[0]] + [crossed(sides[steps], steps) for steps in (2, 1, 3)]
-    merged = first_sum(middle, sides)
+    *terms, held, sent = all_terms(place, even, odd, up, down, far, lhs, middle, col_count)
+    terms = [terms[0]] + [crossed(terms[steps], steps) for steps in (2, 1, 3)]
+    merged = first_sum(terms)
     merged = exchanged(merged.reshape(Z * 4, 8, 9 * half))
     inv_images = 1.0 / (image_count * Z * Y)
     merged = jnp.sum(merged.astype(F32), axis=0) * inv_images
@@ -376,11 +398,9 @@
         [jnp.where(core == 0, kept, came), jnp.where(core == 0, came, kept)], axis=2
     )
 
-    weight, sent, _ = lax.optimization_barrier((weight, sent, sides[1]))
-    got = swapped(sent)
-    input_grad = input_gradient(
-        place, held, got, weight.reshape(channels_in, 9 * channels_out), col_count
-    )
+    weight, held = lax.optimization_barrier((weight, held))
+    weight = jnp.transpose(weight, (1, 2, 0)).reshape(9 * channels_out, channels_in)
+    input_grad = input_gradient(place, held, swapped(sent), weight, col_count)
     return (input_grad.reshape(inputs.shape), weight_grad)
 
 

time: 98.6 us -> 96.7 us (0.981)
  local copies, waits for them, and re-layouts: 21.9 us -> 10.1 us
  waiting for transfers between devices: 13.8 us -> 18 us
  starting transfers between devices: 38 us -> 42 us
  other arithmetic: 0.81 us -> 2.1 us
    reshape x1 -> x0, local copies, waits for them, and re-layouts: 6.81 us -> none  [per_device(): weight.reshape(channels_in, 9 * channels_out)]
    transpose x0 -> x1, local copies, waits for them, and re-layouts: none -> 6.65 us  [per_device(): jnp.transpose(weight, (1, 2, 0)).reshape(9 * channels_out, channels_in)]
    optimization_barrier x1 -> x0, local copies, waits for them, and re-layouts: 6.64 us -> none  [per_device(): weight, sent, _ = lax.optimization_barrier((weight, sent, sides[1]))]
    ppermute x4 -> x5, starting transfers between devices: 10.3 us -> 15.8 us  [swapped(): return lax.ppermute(value, 'core', [(0, 1), (1, 0)])]
    unnamed x18 -> x10, local copies, waits for them, and re-layouts: 8.34 us -> 3.36 us
    ppermute x4, starting transfers between devices: 3.64 us -> 7.77 us  [around(): lax.ppermute(value, 'x', [(source, (source + steps) % X) for source in ra...]
    ppermute x6 -> x3, waiting for transfers between devices: 8.94 us -> 13 us  [crossed(): return lax.ppermute(value, AXES, pairs)]
    ppermute x6 -> x3, starting transfers between devices: 8.5 us -> 4.98 us  [crossed(): return lax.ppermute(value, AXES, pairs)]
  transfers between devices with their start and end apart: 17 -> 15, of which waited for: 4 -> 8; matrix products, arithmetic and copies ran while one was open for 14% -> 8% of each run, Pallas kernels for 22% -> 14%
where the time goes in v4:
time: 96.7 us; the launch traced here: 96.1 us
  starting transfers between devices  42 us (43%)
  Pallas kernels  23.1 us (24%)
  waiting for transfers between devices  18 us (19%)
  local copies, waits for them, and re-layouts  10.1 us (10%)
  other arithmetic  2.1 us (2%)
    pallas_call x7, Pallas kernels, kernel_call(): pl.pallas_call(body, grid=grid, in_specs=in_specs, out_specs=out_specs, o...  23.1 us
    ppermute x5, starting transfers between devices, swapped(): return lax.ppermute(value, 'core', [(0, 1), (1, 0)])  15.8 us
    ppermute x3, waiting for transfers between devices, crossed(): return lax.ppermute(value, AXES, pairs)  13 us
    all_to_all x1, starting transfers between devices, exchanged(): return lax.all_to_all(value, AXES, 0, 0, axis_index_groups=groups)  10 us
    ppermute x4, starting transfers between devices, around(): lax.ppermute(value, 'x', [(source, (source + steps) % X) for source in ra...  7.77 us
    transpose x1, local copies, waits for them, and re-layouts, per_device(): jnp.transpose(weight, (1, 2, 0)).reshape(9 * channels_out, channels_in)  6.65 us
    ppermute x3, starting transfers between devices, crossed(): return lax.ppermute(value, AXES, pairs)  4.98 us
    ppermute x2, starting transfers between devices, along(): return lax.ppermute(value, 'x', pairs)  3.39 us
  transfers between devices with their start and end apart: 15, of which 8 were waited for; matrix products, arithmetic and copies ran while one was open for 8% of the time, Pallas kernels for 14%

profile of v4, /device:TPU:1, one launch (start us, length us, event | category | flops | bytes accessed | tf_op | source)
XLA Modules:
  0.0 96.1 jit_solution(8775805045668956842)
XLA Ops:
  0.6 0.0 copy-start
  0.6 0.0 copy-start.2
  0.7 0.7 pad_add_fusion.place_ref
  1.3 3.4 %shard_map.77 = (bf16[2,864,128]{2,1,0:T(8,128)(2,1)}, bf16[2,864,128]{2,1,0:T(8,128)(2,1)}, f32[8,128]{1,0:T(8,128)}, f32[8,128]{1,0:T(8,128)}) custom-call(s32[3]{0:T(128)} %pad_add_fusion.place_ref, bf16[2,6,72,256]{3,2,1,0:T(8,128)(2,1)} %refs_0_.1, bf16[2,6,72,256]{3,2,1,0:T(8,128)(2,1)} %refs_1_.1, s32[2,6,72,256]{3,2,1,0:T(8,128)} %refs_2_.1), custom_call_target="tpu_custom_call" | custom-call | bytes 2662412 | tf_op jit(solution)/shard_map/pallas_call | solution.py:60
  4.7 3.3 %collective-permute-start = (f32[8,128]{1,0:T(8,128)}, f32[8,128]{1,0:T(8,128)S(1)}, u32[]{:S(2)}, u32[]{:S(2)}) collective-permute-start(f32[8,128]{1,0:T(8,128)} %get-tuple-element.26), channel_id=1, source_target_pairs={{0,1},{1,0},{2,3},{3,2},{4,5},{5,4},{6,7},{7,6},{8,9},{9,8},{10,11... | collective-permute-start | bytes 12296 | tf_op jit(solution)/shard_map/ppermute | solution.py:23
  8.0 1.0 %collective-permute-done = f32[8,128]{1,0:T(8,128)S(1)} collective-permute-done((f32[8,128]{1,0:T(8,128)}, f32[8,128]{1,0:T(8,128)S(1)}, u32[]{:S(2)}, u32[]{:S(2)}) %collective-permute-start) | collective-permute-done | bytes 4128 | tf_op jit(solution)/shard_map/ppermute | solution.py:23
  9.1 0.3 collective-permute-start.8
  9.4 0.2 collective-permute-start.4
  9.6 0.7 add.13.a_ref
  10.3 1.0 %collective-permute-start.1 = (f32[8,128]{1,0:T(8,128)S(1)}, f32[8,128]{1,0:T(8,128)S(1)}, u32[]{:S(2)}, u32[]{:S(2)}) collective-permute-start(f32[8,128]{1,0:T(8,128)S(1)} %add.13.a_ref), channel_id=1, source_target_pairs={{0,4},{2,6},{4,0},{6,2},{1,5},{3,7},{5,1},{7,3},{8,12},{10,14},{12... | collective-permute-start | bytes 12296 | tf_op jit(solution)/shard_map/ppermute | solution.py:27
  11.3 0.3 collective-permute-start.2
  11.6 2.4 %collective-permute-start.3 = (f32[8,128]{1,0:T(8,128)S(1)}, f32[8,128]{1,0:T(8,128)S(1)}, u32[]{:S(2)}, u32[]{:S(2)}) collective-permute-start(f32[8,128]{1,0:T(8,128)S(1)} %add.13.a_ref), channel_id=1, source_target_pairs={{0,6},{2,0},{4,2},{6,4},{1,7},{3,1},{5,3},{7,5},{8,14},{10,8},{12,... | collective-permute-start | bytes 12296 | tf_op jit(solution)/shard_map/ppermute | solution.py:27
  14.0 0.1 dynamic-slice_bitcast_fusion.gain_ref
  14.0 0.2 collective-permute-done.1.b_ref
  14.2 1.0 %collective-permute-done.2.c_ref = f32[8,128]{1,0:T(8,128)S(1)} collective-permute-done((f32[8,128]{1,0:T(8,128)S(1)}, f32[8,128]{1,0:T(8,128)S(1)}, u32[]{:S(2)}, u32[]{:S(2)}) %collective-permute-start.2) | collective-permute-done | bytes 4128 | tf_op jit(solution)/shard_map/ppermute | solution.py:27
  15.3 0.0 collective-permute-done.3.d_ref
  15.3 0.0 collective-permute-done.4.theirs_ref
  15.3 0.0 copy-start.3
  15.3 1.0 %copy-done.3 = bf16[2,864,128]{2,1,0:T(8,128)(2,1)S(1)} copy-done((bf16[2,864,128]{2,1,0:T(8,128)(2,1)S(1)}, bf16[2,864,128]{2,1,0:T(8,128)(2,1)}, u32[]{:S(2)}) %copy-start.3) | copy-done | bytes 442392
  16.3 1.4 %shard_map.78 = (bf16[864,128]{1,0:T(8,128)(2,1)S(1)}, bf16[864,128]{1,0:T(8,128)(2,1)S(1)}, bf16[864,128]{1,0:T(8,128)(2,1)S(1)}) custom-call(s32[3]{0:T(128)S(1)} %copy-done.4, f32[1,128]{1,0:T(1,128)S(1)} %dynamic-slice_bitcast_fusion.gain_ref, f32[8,128]{1,0:T(8,128)S(1)} %add.13.a_ref, f32[8,128]{1,0:T(8,128)S(1)} %collective-permute-done.1.b_ref, ...), custom_call_target="tpu_custom_call" | custom-call | bytes 1565196 | tf_op jit(solution)/shard_map/pallas_call | solution.py:60
  17.7 2.1 %collective-permute-start.5 = (bf16[864,128]{1,0:T(8,128)(2,1)S(1)}, bf16[864,128]{1,0:T(8,128)(2,1)S(1)}, u32[]{:S(2)}, u32[]{:S(2)}) collective-permute-start(bf16[864,128]{1,0:T(8,128)(2,1)S(1)} %get-tuple-element.30.even_ref), channel_id=1, source_target_pairs={{0,2},{2,4},{4,6},{1,3},{3,5},{5,7},{8,10},{10,12},{12,14},{9,11},... | collective-permute-start | bytes 663560 | tf_op jit(solution)/shard_map/ppermute | solution.py:32
  19.8 1.3 %collective-permute-start.6 = (bf16[864,128]{1,0:T(8,128)(2,1)S(1)}, bf16[864,128]{1,0:T(8,128)(2,1)S(1)}, u32[]{:S(2)}, u32[]{:S(2)}) collective-permute-start(bf16[864,128]{1,0:T(8,128)(2,1)S(1)} %get-tuple-element.31.odd_ref), channel_id=1, source_target_pairs={{2,0},{4,2},{6,4},{3,1},{5,3},{7,5},{10,8},{12,10},{14,12},{11,9},... | collective-permute-start | bytes 663560 | tf_op jit(solution)/shard_map/ppermute | solution.py:32
  21.1 4.1 %collective-permute-start.7 = (bf16[864,128]{1,0:T(8,128)(2,1)S(1)}, bf16[864,128]{1,0:T(8,128)(2,1)S(1)}, u32[]{:S(2)}, u32[]{:S(2)}) collective-permute-start(bf16[864,128]{1,0:T(8,128)(2,1)S(1)} %get-tuple-element.32), channel_id=1, source_target_pairs={{0,4},{2,6},{4,0},{6,2},{1,5},{3,7},{5,1},{7,3},{8,12},{10,14},{12... | collective-permute-start | bytes 663560 | tf_op jit(solution)/shard_map/ppermute | solution.py:27
  25.1 0.0 collective-permute-done.8.other_ref
  25.1 1.7 %shard_map.79.lhs_ref = bf16[1024,1792]{1,0:T(8,128)(2,1)S(1)} custom-call(bf16[864,1024]{1,0:T(8,128)(2,1)S(1)} %bitcast.16, bf16[864,1024]{1,0:T(8,128)(2,1)S(1)} %collective-permute-done.8.other_ref), custom_call_target="tpu_custom_call" | custom-call | tf_op jit(solution)/shard_map/pallas_call | solution.py:60
  26.8 3.2 %shard_map.80 = (bf16[256,384]{1,0:T(8,128)(2,1)S(1)}, bf16[256,384]{1,0:T(8,128)(2,1)S(1)}, bf16[256,384]{1,0:T(8,128)(2,1)S(1)}, bf16[256,384]{1,0:T(8,128)(2,1)S(1)}) custom-call(s32[3]{0:T(128)S(1)} %copy-done.4, bf16[864,128]{1,0:T(8,128)(2,1)S(1)} %get-tuple-element.30.even_ref, bf16[864,128]{1,0:T(8,128)(2,1)S(1)} %get-tuple-element.31.odd_ref, ...), custom_call_target="tpu_custom_call" | custom-call | tf_op jit(solution)/shard_map/pallas_call | solution.py:60
  30.1 0.0 collective-permute-done.5.up_ref
  30.1 0.0 collective-permute-done.6.down_ref
  30.1 0.9 collective-permute-done.7.far_ref
  31.0 4.9 %shard_map.81 = (bf16[256,1152]{1,0:T(8,128)(2,1)S(1)}, bf16[256,1152]{1,0:T(8,128)(2,1)S(1)}, bf16[256,1152]{1,0:T(8,128)(2,1)S(1)}, bf16[256,1152]{1,0:T(8,128...) custom-call(s32[3]{0:T(128)S(1)} %copy-done.4, ...), custom_call_target="tpu_custom_call" | custom-call | flops 2818572288 | bytes 9248780 | tf_op jit(solution)/shard_map/pallas_call | solution.py:60
  35.9 0.6 collective-permute-start.10
  36.5 3.5 %collective-permute-start.11 = (bf16[256,1152]{1,0:T(8,128)(2,1)S(1)}, bf16[256,1152]{1,0:T(8,128)(2,1)S(1)}, u32[]{:S(2)}, u32[]{:S(2)}) collective-permute-start(bf16[256,1152]{1,0:T(8,128)(2,1)S(1)} %get-tuple-element.44), channel_id=1, source_target_pairs={{0,8},{1,3},{2,10},{3,5},{4,12},{5,7},{6,14},{7,1},{8,16},{9,11},{... | collective-permute-start | bytes 1769480 | tf_op jit(solution)/shard_map/ppermute | solution.py:42
  40.0 0.9 collective-permute-start.12
  40.9 5.7 %collective-permute-done.10.refs_1_ = bf16[256,1152]{1,0:T(8,128)(2,1)S(1)} collective-permute-done((bf16[256,1152]{1,0:T(8,128)(2,1)S(1)}, bf16[256,1152]{1,0:T(8,128)(2,1)S(1)}, u32[]{:S(2)}, u32[]{:S(2)}) %collective-permute-start.10) | collective-permute-done | bytes 589856 | tf_op jit(solution)/shard_map/ppermute | solution.py:42
  46.6 6.3 %collective-permute-done.11.refs_2_ = bf16[256,1152]{1,0:T(8,128)(2,1)S(1)} collective-permute-done((bf16[256,1152]{1,0:T(8,128)(2,1)S(1)}, bf16[256,1152]{1,0:T(8,128)(2,1)S(1)}, u32[]{:S(2)}, u32[]{:S(2)}) %collective-permute-start.11) | collective-permute-done | bytes 589856 | tf_op jit(solution)/shard_map/ppermute | solution.py:42
  52.8 1.1 %collective-permute-done.12.refs_3_ = bf16[256,1152]{1,0:T(8,128)(2,1)S(1)} collective-permute-done((bf16[256,1152]{1,0:T(8,128)(2,1)S(1)}, bf16[256,1152]{1,0:T(8,128)(2,1)S(1)}, u32[]{:S(2)}, u32[]{:S(2)}) %collective-permute-start.12) | collective-permute-done | bytes 589856 | tf_op jit(solution)/shard_map/ppermute | solution.py:42
  53.9 1.0 %shard_map.83 = bf16[256,1152]{1,0:T(8,128)(2,1)} custom-call(bf16[256,1152]{1,0:T(8,128)(2,1)S(1)} %get-tuple-element.42.refs_0_, bf16[256,1152]{1,0:T(8,128)(2,1)S(1)} %collective-permute-done.10.refs_1_, bf16[256,1152]{1,0:T(8,128)(2,1)S(1)} %collective-permute-done.11.refs_2_, bf16[256,1152]{1,0:T(8,128)(2,1)S(1)} %collective-permute-done.12.refs_3_), custom_call_target="tpu_custom_call" | custom-call | bytes 2949120 | tf_op jit(solution)/shard_map/pallas_call | solution.py:60
  54.9 10.0 %all-to-all-start = ((bf16[32,8,1152]{2,1,0:T(8,128)(2,1)}), bf16[32,8,1152]{2,1,0:T(8,128)(2,1)S(1)}, u32[]{:S(2)}, u32[]{:S(2)}) async-start(bf16[32,8,1152]{2,1,0:T(8,128)(2,1)} %bitcast.8), calls=%async_computation | async-start | bytes 1179648 | tf_op jit(solution)/shard_map/all_to_all | solution.py:48
  65.0 6.6 %copy.8 = bf16[9,256,1024]{2,1,0:T(8,128)(2,1)} copy(bf16[9,256,1024]{1,2,0:T(8,128)(2,1)} %bitcast.17) | data formatting | bytes 9437184 | tf_op jit(solution)/shard_map/transpose | solution.py:402
  71.6 4.7 %collective-permute-start.9 = (bf16[3,864,128]{2,1,0:T(8,128)(2,1)S(1)}, bf16[3,864,128]{2,1,0:T(8,128)(2,1)S(1)}, u32[]{:S(2)}, u32[]{:S(2)}) collective-permute-start(bf16[3,864,128]{2,1,0:T(8,128)(2,1)S(1)} %get-tuple-element.40), channel_id=1, source_target_pairs={{0,1},{1,0},{2,3},{3,2},{4,5},{5,4},{6,7},{7,6},{8,9},{9,8},{10,11... | collective-permute-start | bytes 1990664 | tf_op jit(solution)/shard_map/ppermute | solution.py:23
  76.4 1.8 %all-to-all-done = bf16[32,8,1152]{2,1,0:T(8,128)(2,1)S(1)} async-done(((bf16[32,8,1152]{2,1,0:T(8,128)(2,1)}), bf16[32,8,1152]{2,1,0:T(8,128)(2,1)S(1)}, u32[]{:S(2)}, u32[]{:S(2)}) %all-to-all-start) | async-done | bytes 589856 | tf_op jit(solution)/shard_map/all_to_all | solution.py:48
  78.2 0.1 convert_reduce_fusion
  78.3 7.3 %collective-permute-start.13 = (f32[4,1152]{1,0:T(4,128)S(1)}, f32[4,1152]{1,0:T(4,128)S(1)}, u32[]{:S(2)}, u32[]{:S(2)}) collective-permute-start(f32[4,1152]{1,0:T(4,128)S(1)} %constant_dynamic-slice_fusion), channel_id=1, source_target_pairs={{0,1},{1,0},{2,3},{3,2},{4,5},{5,4},{6,7},{7,6},{8,9},{9,8},{10,11... | collective-permute-start | bytes 55304 | tf_op jit(solution)/shard_map/ppermute | solution.py:23
  85.6 0.0 collective-permute-done.9.got_ref
  85.6 2.3 %copy-done.1 = bf16[9,256,1024]{2,1,0:T(8,128)(2,1)S(1)} copy-done((bf16[9,256,1024]{2,1,0:T(8,128)(2,1)S(1)}, bf16[9,256,1024]{2,1,0:T(8,128)(2,1)}, u32[]{:S(2)}) %copy-start.1) | copy-done | bytes 4718616
  88.0 7.5 %shard_map.82 = bf16[864,1024]{1,0:T(8,128)(2,1)} custom-call(s32[3]{0:T(128)S(1)} %copy-done.4, bf16[3,864,128]{2,1,0:T(8,128)(2,1)S(1)} %get-tuple-element.39.held_ref, bf16[3,864,128]{2,1,0:T(8,128)(2,1)S(1)} %collective-permute-done.9.got_ref, bf16[2304,1024]{1,0:T(8,128)(2,1)S(1)} %bitcast.14), custom_call_target="tpu_custom_call" | custom-call | flops 4076863488 | bytes 7815180 | tf_op jit(solution)/shard_map/pallas_call | solution.py:60
  95.5 0.0 collective-permute-done.13
  95.5 0.6 pad_maximum_fusion
  (8 shorter events, 0.0 us)
Async XLA Ops:
  0.6 13.3 %copy-start = (f32[256]{0:T(256)S(1)}, f32[256]{0:T(256)}, u32[]{:S(2)}) copy-start(f32[256]{0:T(256)} %param.10) | copy-start | bytes 3076
  0.6 8.4 %copy-start.2 = (bf16[2,6,72,1024]{3,2,1,0:T(8,128)(2,1)S(1)}, bf16[2,6,72,1024]{3,2,1,0:T(8,128)(2,1)}, u32[]{:S(2)}) copy-start(bf16[2,6,72,1024]{3,2,1,0:T(8,128)(2,1)} %param.6) | copy-start | bytes 5308420
  1.3 13.9 %copy-start.4 = (s32[3]{0:T(128)S(1)}, s32[3]{0:T(128)}, u32[]{:S(2)}) copy-start(s32[3]{0:T(128)} %pad_add_fusion.place_ref) | copy-start | bytes 40
  4.7 4.4 %collective-permute-start = (f32[8,128]{1,0:T(8,128)}, f32[8,128]{1,0:T(8,128)S(1)}, u32[]{:S(2)}, u32[]{:S(2)}) collective-permute-start(f32[8,128]{1,0:T(8,128)} %get-tuple-element.26), channel_id=1, source_target_pairs={{0,1},{1,0},{2,3},{3,2},{4,5},{5,4},{6,7},{7,6},{8,9},{9,8},{10,11... | collective-permute-start | bytes 12296 | tf_op jit(solution)/shard_map/ppermute | solution.py:23
  9.1 16.1 %collective-permute-start.8 = (bf16[864,1024]{1,0:T(8,128)(2,1)S(1)}, bf16[864,1024]{1,0:T(8,128)(2,1)S(1)}, u32[]{:S(2)}, u32[]{:S(2)}) collective-permute-start(bf16[864,1024]{1,0:T(8,128)(2,1)S(1)} %bitcast.15), channel_id=1, source_target_pairs={{0,1},{1,0},{2,3},{3,2},{4,5},{5,4},{6,7},{7,6},{8,9},{9,8},{10,11... | collective-permute-start | bytes 5308424 | tf_op jit(solution)/shard_map/ppermute | solution.py:23
  9.4 5.8 %collective-permute-start.4 = (bf16[2,864,128]{2,1,0:T(8,128)(2,1)}, bf16[2,864,128]{2,1,0:T(8,128)(2,1)}, u32[]{:S(2)}, u32[]{:S(2)}) collective-permute-start(bf16[2,864,128]{2,1,0:T(8,128)(2,1)} %get-tuple-element.29), channel_id=1, source_target_pairs={{0,1},{1,0},{2,3},{3,2},{4,5},{5,4},{6,7},{7,6},{8,9},{9,8},{10,11... | collective-permute-start | bytes 1327112 | tf_op jit(solution)/shard_map/ppermute | solution.py:23
  10.3 4.0 %collective-permute-start.1 = (f32[8,128]{1,0:T(8,128)S(1)}, f32[8,128]{1,0:T(8,128)S(1)}, u32[]{:S(2)}, u32[]{:S(2)}) collective-permute-start(f32[8,128]{1,0:T(8,128)S(1)} %add.13.a_ref), channel_id=1, source_target_pairs={{0,4},{2,6},{4,0},{6,2},{1,5},{3,7},{5,1},{7,3},{8,12},{10,14},{12... | collective-permute-start | bytes 12296 | tf_op jit(solution)/shard_map/ppermute | solution.py:27
  11.3 4.0 %collective-permute-start.2 = (f32[8,128]{1,0:T(8,128)S(1)}, f32[8,128]{1,0:T(8,128)S(1)}, u32[]{:S(2)}, u32[]{:S(2)}) collective-permute-start(f32[8,128]{1,0:T(8,128)S(1)} %add.13.a_ref), channel_id=1, source_target_pairs={{0,2},{2,4},{4,6},{6,0},{1,3},{3,5},{5,7},{7,1},{8,10},{10,12},{12... | collective-permute-start | bytes 12296 | tf_op jit(solution)/shard_map/ppermute | solution.py:27
  11.6 3.7 %collective-permute-start.3 = (f32[8,128]{1,0:T(8,128)S(1)}, f32[8,128]{1,0:T(8,128)S(1)}, u32[]{:S(2)}, u32[]{:S(2)}) collective-permute-start(f32[8,128]{1,0:T(8,128)S(1)} %add.13.a_ref), channel_id=1, source_target_pairs={{0,6},{2,0},{4,2},{6,4},{1,7},{3,1},{5,3},{7,5},{8,14},{10,8},{12,... | collective-permute-start | bytes 12296 | tf_op jit(solution)/shard_map/ppermute | solution.py:27
  15.3 1.0 %copy-start.3 = (bf16[2,864,128]{2,1,0:T(8,128)(2,1)S(1)}, bf16[2,864,128]{2,1,0:T(8,128)(2,1)}, u32[]{:S(2)}) copy-start(bf16[2,864,128]{2,1,0:T(8,128)(2,1)} %get-tuple-element.28.mine_ref) | copy-start | bytes 1327108
  17.7 12.4 %collective-permute-start.5 = (bf16[864,128]{1,0:T(8,128)(2,1)S(1)}, bf16[864,128]{1,0:T(8,128)(2,1)S(1)}, u32[]{:S(2)}, u32[]{:S(2)}) collective-permute-start(bf16[864,128]{1,0:T(8,128)(2,1)S(1)} %get-tuple-element.30.even_ref), channel_id=1, source_target_pairs={{0,2},{2,4},{4,6},{1,3},{3,5},{5,7},{8,10},{10,12},{12,14},{9,11},... | collective-permute-start | bytes 663560 | tf_op jit(solution)/shard_map/ppermute | solution.py:32
  19.8 10.3 %collective-permute-start.6 = (bf16[864,128]{1,0:T(8,128)(2,1)S(1)}, bf16[864,128]{1,0:T(8,128)(2,1)S(1)}, u32[]{:S(2)}, u32[]{:S(2)}) collective-permute-start(bf16[864,128]{1,0:T(8,128)(2,1)S(1)} %get-tuple-element.31.odd_ref), channel_id=1, source_target_pairs={{2,0},{4,2},{6,4},{3,1},{5,3},{7,5},{10,8},{12,10},{14,12},{11,9},... | collective-permute-start | bytes 663560 | tf_op jit(solution)/shard_map/ppermute | solution.py:32
  21.1 9.9 %collective-permute-start.7 = (bf16[864,128]{1,0:T(8,128)(2,1)S(1)}, bf16[864,128]{1,0:T(8,128)(2,1)S(1)}, u32[]{:S(2)}, u32[]{:S(2)}) collective-permute-start(bf16[864,128]{1,0:T(8,128)(2,1)S(1)} %get-tuple-element.32), channel_id=1, source_target_pairs={{0,4},{2,6},{4,0},{6,2},{1,5},{3,7},{5,1},{7,3},{8,12},{10,14},{12... | collective-permute-start | bytes 663560 | tf_op jit(solution)/shard_map/ppermute | solution.py:27
  35.9 10.7 %collective-permute-start.10 = (bf16[256,1152]{1,0:T(8,128)(2,1)S(1)}, bf16[256,1152]{1,0:T(8,128)(2,1)S(1)}, u32[]{:S(2)}, u32[]{:S(2)}) collective-permute-start(bf16[256,1152]{1,0:T(8,128)(2,1)S(1)} %get-tuple-element.43), channel_id=1, source_target_pairs={{0,16},{1,5},{2,18},{3,7},{4,20},{5,1},{6,22},{7,3},{8,24},{9,13},... | collective-permute-start | bytes 1769480 | tf_op jit(solution)/shard_map/ppermute | solution.py:42
  36.5 16.4 %collective-permute-start.11 = (bf16[256,1152]{1,0:T(8,128)(2,1)S(1)}, bf16[256,1152]{1,0:T(8,128)(2,1)S(1)}, u32[]{:S(2)}, u32[]{:S(2)}) collective-permute-start(bf16[256,1152]{1,0:T(8,128)(2,1)S(1)} %get-tuple-element.44), channel_id=1, source_target_pairs={{0,8},{1,3},{2,10},{3,5},{4,12},{5,7},{6,14},{7,1},{8,16},{9,11},{... | collective-permute-start | bytes 1769480 | tf_op jit(solution)/shard_map/ppermute | solution.py:42
  40.0 13.9 %collective-permute-start.12 = (bf16[256,1152]{1,0:T(8,128)(2,1)S(1)}, bf16[256,1152]{1,0:T(8,128)(2,1)S(1)}, u32[]{:S(2)}, u32[]{:S(2)}) collective-permute-start(bf16[256,1152]{1,0:T(8,128)(2,1)S(1)} %get-tuple-element.45), channel_id=1, source_target_pairs={{0,24},{1,7},{2,26},{3,1},{4,28},{5,3},{6,30},{7,5},{8,0},{9,15},{... | collective-permute-start | bytes 1769480 | tf_op jit(solution)/shard_map/ppermute | solution.py:42
  54.9 23.3 %all-to-all-start = ((bf16[32,8,1152]{2,1,0:T(8,128)(2,1)}), bf16[32,8,1152]{2,1,0:T(8,128)(2,1)S(1)}, u32[]{:S(2)}, u32[]{:S(2)}) async-start(bf16[32,8,1152]{2,1,0:T(8,128)(2,1)} %bitcast.8), calls=%async_computation | async-start | bytes 1179648 | tf_op jit(solution)/shard_map/all_to_all | solution.py:48
  71.6 14.0 %collective-permute-start.9 = (bf16[3,864,128]{2,1,0:T(8,128)(2,1)S(1)}, bf16[3,864,128]{2,1,0:T(8,128)(2,1)S(1)}, u32[]{:S(2)}, u32[]{:S(2)}) collective-permute-start(bf16[3,864,128]{2,1,0:T(8,128)(2,1)S(1)} %get-tuple-element.40), channel_id=1, source_target_pairs={{0,1},{1,0},{2,3},{3,2},{4,5},{5,4},{6,7},{7,6},{8,9},{9,8},{10,11... | collective-permute-start | bytes 1990664 | tf_op jit(solution)/shard_map/ppermute | solution.py:23
  78.3 17.1 %collective-permute-start.13 = (f32[4,1152]{1,0:T(4,128)S(1)}, f32[4,1152]{1,0:T(4,128)S(1)}, u32[]{:S(2)}, u32[]{:S(2)}) collective-permute-start(f32[4,1152]{1,0:T(4,128)S(1)} %constant_dynamic-slice_fusion), channel_id=1, source_target_pairs={{0,1},{1,0},{2,3},{3,2},{4,5},{5,4},{6,7},{7,6},{8,9},{9,8},{10,11... | collective-permute-start | bytes 55304 | tf_op jit(solution)/shard_map/ppermute | solution.py:23
  85.6 2.3 %copy-start.1 = (bf16[9,256,1024]{2,1,0:T(8,128)(2,1)S(1)}, bf16[9,256,1024]{2,1,0:T(8,128)(2,1)}, u32[]{:S(2)}) copy-start(bf16[9,256,1024]{2,1,0:T(8,128)(2,1)} %copy.8) | copy-start | bytes 14155780

commit v5 on v4

--- a/solution.py
+++ b/solution.py
@@ -27,11 +27,6 @@
     return lax.ppermute(value, "x", [(source, (source + steps) % X) for source in range(X)])
 
 
-def along(value, steps):
-    pairs = [(source, source + steps) for source in range(X) if 0 <= source + steps < X]
-    return lax.ppermute(value, "x", pairs)
-
-
 def crossed(value, steps):
     pairs = []
     for z in range(Z):
@@ -69,55 +64,37 @@
     )(*operands)
 
 
-def prepare(place, conv, grad, mask, images):
-    channels = conv.shape[3]
+def channel_sums(conv, grad, mask):
+    values = conv.astype(F32)
+    passed = grad.astype(F32) * mask.astype(F32)
+    terms = (values, values * values, passed, passed * values)
+    return jnp.stack([jnp.sum(term, axis=(1, 2)) for term in terms]).reshape(-1, conv.shape[3])
+
+
+def prepare(place, conv, grad, mask):
+    cells, channels = conv.shape
     half = channels // 2
-    each = conv.shape[1] * conv.shape[2]
-    cells = images * each
-
-    def body(place_ref, *refs):
-        sources, (mine_ref, sent_ref, mine_sum_ref, sent_sum_ref) = refs[:3], refs[3:7]
-        buffers, sems = refs[7:10], refs[10]
+    steps = 2
+    tall = cells // steps
+
+    def body(place_ref, conv_ref, grad_ref, mask_ref, mine_ref, sent_ref):
         first = place_ref[2] == 0
-        copies = [
-            [
-                pltpu.make_async_copy(source.at[image], buffer.at[image], sems.at[image, n])
-                for n, (source, buffer) in enumerate(zip(sources, buffers))
-            ]
-            for image in range(images)
-        ]
-        for group in copies:
-            for copy in group:
-                copy.start()
-        for image in range(images):
-            for copy in copies[image]:
-                copy.wait()
-            rows = slice(image * each, (image + 1) * each)
-            conv_block, grad_block, mask_block = (buffer[image].reshape(each, channels) for buffer in buffers)
-            passed = grad_block.astype(F32) * mask_block.astype(F32)
-            values = conv_block.astype(F32)
-            for which, value in enumerate((conv_block, passed.astype(BF16))):
-                lower, upper = value[:, :half], value[:, half:]
-                mine_ref[which, rows, :] = jnp.where(first, lower, upper)
-                sent_ref[which, rows, :] = jnp.where(first, upper, lower)
-            for kind, term in enumerate((values, values * values, passed, passed * values)):
-                total = jnp.sum(term, axis=0, keepdims=True)
-                lower, upper = total[:, :half], total[:, half:]
-                row = slice(kind * images + image, kind * images + image + 1)
-                mine_sum_ref[row, :] = jnp.where(first, lower, upper)
-                sent_sum_ref[row, :] = jnp.where(first, upper, lower)
-
+        passed = (grad_ref[...].astype(F32) * mask_ref[...].astype(F32)).astype(BF16)
+        for which, value in enumerate((conv_ref[...], passed)):
+            lower, upper = value[:, :half], value[:, half:]
+            mine_ref[which] = jnp.where(first, lower, upper)
+            sent_ref[which] = jnp.where(first, upper, lower)
+
+    rows = pl.BlockSpec((tall, channels), lambda i: (i, 0))
     out = jax.ShapeDtypeStruct((2, cells, half), BF16)
-    total = jax.ShapeDtypeStruct((4 * images, half), F32)
-    outs = [out, out, total, total]
+    spec = pl.BlockSpec((2, tall, half), lambda i: (0, i, 0))
     return kernel_call(
         body,
         (place, conv, grad, mask),
-        [SMEM] + [pl.BlockSpec(memory_space=pltpu.HBM)] * 3,
-        outs,
-        [whole(value.shape) for value in outs],
-        scratch=[pltpu.VMEM(value.shape, value.dtype) for value in (conv, grad, mask)]
-        + [pltpu.SemaphoreType.DMA((images, 3))],
+        [SMEM, rows, rows, rows],
+        [out, out],
+        [spec, spec],
+        (steps,),
         vmem=60,
     )
 
@@ -130,7 +107,8 @@
         first = place_ref[2] == 0
         early = place_ref[1] < X // 2
         means = (a_ref[...] + b_ref[...] + c_ref[...] + d_ref[...]) / cell_count
-        gain_row = gain_ref[...]
+        means = jnp.where(first, means[:, :half], means[:, half:])
+        gain_row = jnp.where(first, gain_ref[:, :half], gain_ref[:, half:])
         for image in range(images):
             rows = pl.ds(image * each, each)
             chan_mean, second, passed_mean, product_mean = (
@@ -289,7 +267,9 @@
             zero = jnp.zeros_like(far_block)
             far_down = jnp.where(early, far_block, zero)
             far_up = jnp.where(early, zero, far_block)
-            pairs = ((down_ref[...], far_down), (even_ref[...], odd_ref[...]), (far_up, up_ref[...]))
+            down_block = jnp.where(place_ref[1] < X - 1, down_ref[...], zero)
+            up_block = jnp.where(place_ref[1] > 0, up_ref[...], zero)
+            pairs = ((down_block, far_down), (even_ref[...], odd_ref[...]), (far_up, up_block))
             for side, (lower, upper) in enumerate(pairs):
                 mine = jnp.where(first, lower, upper)
                 theirs = jnp.where(first, upper, lower)
@@ -369,25 +349,36 @@
     place = jnp.stack([lax.axis_index("y"), lax.axis_index("x"), core]).astype(jnp.int32)
 
     input_flat = inputs.reshape(cells, channels_in)
-    mine, sent, sums, sent_sums = prepare(place, conv_out, grad_out, relu_mask, image_count)
-    got_sums = swapped(sent_sums)
+    sums = channel_sums(conv_out, grad_out, relu_mask)
+    got_sums = swapped(sums)
+    mine, sent = prepare(
+        place,
+        *(value.reshape(cells, channels_out) for value in (conv_out, grad_out, relu_mask)),
+    )
     input_flat, sent, got_sums = lax.optimization_barrier((input_flat, sent, got_sums))
     theirs = swapped(sent)
     input_other = swapped(input_flat)
     sums = sums + got_sums
     sums = [sums] + [around(sums, steps) for steps in (2, 1, 3)]
-    gain = lax.dynamic_slice_in_dim(norm_gain, core * half, half, axis=0).reshape(1, half)
     lhs = transposed(input_flat, input_other)
+    gain = norm_gain.reshape(1, channels_out)
     even, odd, far = pre_gradient(place, gain, sums, mine, theirs, image_count, cell_count)
     far = around(far, 2)
-    up = along(even, 1)
-    down = along(odd, -1)
+    up = around(even, 1)
+    down = around(odd, X - 1)
 
     middle = middle_terms(place, even, odd, lhs, col_count)
     *terms, held, sent = all_terms(place, even, odd, up, down, far, lhs, middle, col_count)
     terms = [terms[0]] + [crossed(terms[steps], steps) for steps in (2, 1, 3)]
+    weight, held = lax.optimization_barrier((weight, held))
+    weight = jnp.transpose(weight, (1, 2, 0)).reshape(9 * channels_out, channels_in)
+    got = swapped(sent)
+    terms, weight, got = lax.optimization_barrier((terms, weight, got))
     merged = first_sum(terms)
+    held, merged = lax.optimization_barrier((held, merged))
+    input_grad = input_gradient(place, held, got, weight, col_count)
     merged = exchanged(merged.reshape(Z * 4, 8, 9 * half))
+    merged, input_grad = lax.optimization_barrier((merged, input_grad))
     inv_images = 1.0 / (image_count * Z * Y)
     merged = jnp.sum(merged.astype(F32), axis=0) * inv_images
     rows = merged.shape[0] // CORES
@@ -398,9 +389,6 @@
         [jnp.where(core == 0, kept, came), jnp.where(core == 0, came, kept)], axis=2
     )
 
-    weight, held = lax.optimization_barrier((weight, held))
-    weight = jnp.transpose(weight, (1, 2, 0)).reshape(9 * channels_out, channels_in)
-    input_grad = input_gradient(place, held, swapped(sent), weight, col_count)
     return (input_grad.reshape(inputs.shape), weight_grad)
 
 

time: 96.7 us -> 89.8 us (0.929)
  starting transfers between devices: 42 us -> 31.1 us
  local copies, waits for them, and re-layouts: 10.1 us -> 11.9 us
  waiting for transfers between devices: 18 us -> 19.4 us
  other arithmetic: 2.1 us -> 3.21 us
    ppermute x5, starting transfers between devices: 15.8 us -> 9.78 us  [swapped(): return lax.ppermute(value, 'core', [(0, 1), (1, 0)])]
    ppermute x3, waiting for transfers between devices: 13 us -> 7.44 us  [crossed(): return lax.ppermute(value, AXES, pairs)]
    all_to_all x1, waiting for transfers between devices: 1.84 us -> 6.47 us  [exchanged(): return lax.all_to_all(value, AXES, 0, 0, axis_index_groups=groups)]
    ppermute x2 -> x0, starting transfers between devices: 3.39 us -> none  [along(): return lax.ppermute(value, 'x', pairs)]
    ppermute x4 -> x6, waiting for transfers between devices: 2.08 us -> 4.62 us  [around(): lax.ppermute(value, 'x', [(source, (source + steps) % X) for source in ra...]
    ppermute x3, starting transfers between devices: 4.98 us -> 2.82 us  [crossed(): return lax.ppermute(value, AXES, pairs)]
    unnamed x10 -> x14, local copies, waits for them, and re-layouts: 3.36 us -> 5.28 us
    reduce_sum x0 -> x1, other arithmetic: none -> 1.85 us  [channel_sums(): jnp.sum(term, axis=(1, 2))]
  transfers between devices with their start and end apart: 15 -> 15, of which waited for: 8 -> 8; matrix products, arithmetic and copies ran while one was open for 8% -> 8% of each run, Pallas kernels for 14% -> 18%
where the time goes in v5:
time: 89.8 us; the launch traced here: 89.3 us
  starting transfers between devices  31.1 us (35%)
  Pallas kernels  22.9 us (26%)
  waiting for transfers between devices  19.4 us (22%)
  local copies, waits for them, and re-layouts  11.9 us (13%)
  other arithmetic  3.21 us (4%)
    pallas_call x7, Pallas kernels, kernel_call(): pl.pallas_call(body, grid=grid, in_specs=in_specs, out_specs=out_specs, o...  22.9 us
    all_to_all x1, starting transfers between devices, exchanged(): return lax.all_to_all(value, AXES, 0, 0, axis_index_groups=groups)  11 us
    ppermute x5, starting transfers between devices, swapped(): return lax.ppermute(value, 'core', [(0, 1), (1, 0)])  9.78 us
    ppermute x6, starting transfers between devices, around(): lax.ppermute(value, 'x', [(source, (source + steps) % X) for source in ra...  7.51 us
    ppermute x3, waiting for transfers between devices, crossed(): return lax.ppermute(value, AXES, pairs)  7.44 us
    transpose x1, local copies, waits for them, and re-layouts, per_device(): jnp.transpose(weight, (1, 2, 0)).reshape(9 * channels_out, channels_in)  6.64 us
    all_to_all x1, waiting for transfers between devices, exchanged(): return lax.all_to_all(value, AXES, 0, 0, axis_index_groups=groups)  6.47 us
    unnamed x14, local copies, waits for them, and re-layouts  5.28 us
  transfers between devices with their start and end apart: 15, of which 8 were waited for; matrix products, arithmetic and copies ran while one was open for 8% of the time, Pallas kernels for 18%

profile of v5, /device:TPU:1, one launch (start us, length us, event | category | flops | bytes accessed | tf_op | source)
XLA Modules:
  0.0 89.3 jit_solution(15590232059404924407)
XLA Ops:
  0.6 0.0 copy-start.1
  0.6 1.9 %fusion.2 = (f32[2,256]{1,0:T(2,128)S(1)}, f32[2,256]{1,0:T(2,128)S(1)}, f32[2,256]{1,0:T(2,128)S(1)}, f32[2,256]{1,0:T(2,128)S(1)}) fusion(s32[2,6,72,256]{3,2,1,0:T(8,128)} %param.9, bf16[2,6,72,256]{3,2,1,0:T(8,128)(2,1)} %param.8, bf16[2,6,72,256]{3,2,1,0:T(8,128)(2,1)} %param.7), kind=kLoop, calls=%fused_computation.7 | loop fusion | flops 2209792 | bytes 1777664 | tf_op jit(solution)/shard_map/reduce_sum | solution.py:71
  2.5 3.3 %collective-permute-start = (f32[8,256]{1,0:T(8,128)S(1)}, f32[8,256]{1,0:T(8,128)S(1)}, u32[]{:S(2)}, u32[]{:S(2)}) collective-permute-start(f32[8,256]{1,0:T(8,128)S(1)} %reshape.38), channel_id=1, source_target_pairs={{0,1},{1,0},{2,3},{3,2},{4,5},{5,4},{6,7},{7,6},{8,9},{9,8},{10,11... | collective-permute-start | bytes 24584 | tf_op jit(solution)/shard_map/ppermute | solution.py:23
  5.9 0.6 pad_add_fusion.place_ref
  6.5 2.4 %shard_map.77 = (bf16[2,864,128]{2,1,0:T(8,128)(2,1)}, bf16[2,864,128]{2,1,0:T(8,128)(2,1)}) custom-call(s32[3]{0:T(128)} %pad_add_fusion.place_ref, bf16[864,256]{1,0:T(8,128)(2,1)} %bitcast.27, bf16[864,256]{1,0:T(8,128)(2,1)} %bitcast.26, s32[864,256]{1,0:T(8,128)} %bitcast.25), custom_call_target="tpu_custom_call" | custom-call | bytes 2654220 | tf_op jit(solution)/shard_map/pallas_call | solution.py:55
  8.9 0.0 collective-permute-done
  8.9 0.1 collective-permute-start.8
  9.0 0.5 collective-permute-start.4
  9.5 1.0 %collective-permute-start.1 = (f32[8,256]{1,0:T(8,128)S(1)}, f32[8,256]{1,0:T(8,128)S(1)}, u32[]{:S(2)}, u32[]{:S(2)}) collective-permute-start(f32[8,256]{1,0:T(8,128)S(1)} %add.9.a_ref), channel_id=1, source_target_pairs={{0,4},{2,6},{4,0},{6,2},{1,5},{3,7},{5,1},{7,3},{8,12},{10,14},{12... | collective-permute-start | bytes 24584 | tf_op jit(solution)/shard_map/ppermute | solution.py:27
  10.5 0.3 collective-permute-start.2
  10.8 2.4 %collective-permute-start.3 = (f32[8,256]{1,0:T(8,128)S(1)}, f32[8,256]{1,0:T(8,128)S(1)}, u32[]{:S(2)}, u32[]{:S(2)}) collective-permute-start(f32[8,256]{1,0:T(8,128)S(1)} %add.9.a_ref), channel_id=1, source_target_pairs={{0,6},{2,0},{4,2},{6,4},{1,7},{3,1},{5,3},{7,5},{8,14},{10,8},{12,... | collective-permute-start | bytes 24584 | tf_op jit(solution)/shard_map/ppermute | solution.py:27
  13.2 0.3 collective-permute-done.1.b_ref
  13.5 0.8 collective-permute-done.2.c_ref
  14.3 0.0 collective-permute-done.3.d_ref
  14.3 0.0 collective-permute-done.4.theirs_ref
  14.4 0.0 copy-start.2
  14.4 1.0 %copy-done.2 = bf16[2,864,128]{2,1,0:T(8,128)(2,1)S(1)} copy-done((bf16[2,864,128]{2,1,0:T(8,128)(2,1)S(1)}, bf16[2,864,128]{2,1,0:T(8,128)(2,1)}, u32[]{:S(2)}) %copy-start.2) | copy-done | bytes 442392
  15.4 0.9 shard_map.78
  16.3 0.4 collective-permute-start.5
  16.6 2.4 %collective-permute-start.6 = (bf16[864,128]{1,0:T(8,128)(2,1)S(1)}, bf16[864,128]{1,0:T(8,128)(2,1)S(1)}, u32[]{:S(2)}, u32[]{:S(2)}) collective-permute-start(bf16[864,128]{1,0:T(8,128)(2,1)S(1)} %get-tuple-element.37.odd_ref), channel_id=1, source_target_pairs={{0,6},{2,0},{4,2},{6,4},{1,7},{3,1},{5,3},{7,5},{8,14},{10,8},{12,... | collective-permute-start | bytes 663560 | tf_op jit(solution)/shard_map/ppermute | solution.py:27
  19.0 1.1 %collective-permute-start.7 = (bf16[864,128]{1,0:T(8,128)(2,1)S(1)}, bf16[864,128]{1,0:T(8,128)(2,1)S(1)}, u32[]{:S(2)}, u32[]{:S(2)}) collective-permute-start(bf16[864,128]{1,0:T(8,128)(2,1)S(1)} %get-tuple-element.38), channel_id=1, source_target_pairs={{0,4},{2,6},{4,0},{6,2},{1,5},{3,7},{5,1},{7,3},{8,12},{10,14},{12... | collective-permute-start | bytes 663560 | tf_op jit(solution)/shard_map/ppermute | solution.py:27
  20.1 0.0 collective-permute-done.8.other_ref
  20.1 1.7 %shard_map.79.lhs_ref = bf16[1024,1792]{1,0:T(8,128)(2,1)S(1)} custom-call(bf16[864,1024]{1,0:T(8,128)(2,1)S(1)} %bitcast.22, bf16[864,1024]{1,0:T(8,128)(2,1)S(1)} %collective-permute-done.8.other_ref), custom_call_target="tpu_custom_call" | custom-call | tf_op jit(solution)/shard_map/pallas_call | solution.py:55
  21.8 3.2 %shard_map.80 = (bf16[256,384]{1,0:T(8,128)(2,1)S(1)}, bf16[256,384]{1,0:T(8,128)(2,1)S(1)}, bf16[256,384]{1,0:T(8,128)(2,1)S(1)}, bf16[256,384]{1,0:T(8,128)(2,1)S(1)}) custom-call(s32[3]{0:T(128)S(1)} %copy-done.3, bf16[864,128]{1,0:T(8,128)(2,1)S(1)} %get-tuple-element.36.even_ref, bf16[864,128]{1,0:T(8,128)(2,1)S(1)} %get-tuple-element.37.odd_ref, ...), custom_call_target="tpu_custom_call" | custom-call | tf_op jit(solution)/shard_map/pallas_call | solution.py:55
  25.0 0.0 collective-permute-done.5.up_ref
  25.0 0.0 collective-permute-done.6.down_ref
  25.0 3.5 %collective-permute-done.7.far_ref = bf16[864,128]{1,0:T(8,128)(2,1)S(1)} collective-permute-done((bf16[864,128]{1,0:T(8,128)(2,1)S(1)}, bf16[864,128]{1,0:T(8,128)(2,1)S(1)}, u32[]{:S(2)}, u32[]{:S(2)}) %collective-permute-start.7) | collective-permute-done | bytes 221216 | tf_op jit(solution)/shard_map/ppermute | solution.py:27
  28.5 6.1 %shard_map.81 = (bf16[256,1152]{1,0:T(8,128)(2,1)S(1)}, bf16[256,1152]{1,0:T(8,128)(2,1)}, bf16[256,1152]{1,0:T(8,128)(2,1)}, bf16[256,1152]{1,0:T(8,128)(2,1)},...) custom-call(s32[3]{0:T(128)S(1)} %copy-done.3, bf16[864,128]{1,0:T(8,128)(2,1)S(1)} %get-tuple-element.36.even_ref, ...), custom_call_target="tpu_custom_call" | custom-call | flops 2818572288 | bytes 9248780 | tf_op jit(solution)/shard_map/pallas_call | solution.py:55
  34.6 0.8 copy-done.5
  35.5 2.7 %collective-permute-start.12 = (bf16[3,864,128]{2,1,0:T(8,128)(2,1)}, bf16[3,864,128]{2,1,0:T(8,128)(2,1)S(1)}, u32[]{:S(2)}, u32[]{:S(2)}) collective-permute-start(bf16[3,864,128]{2,1,0:T(8,128)(2,1)} %get-tuple-element.51), channel_id=1, source_target_pairs={{0,1},{1,0},{2,3},{3,2},{4,5},{5,4},{6,7},{7,6},{8,9},{9,8},{10,11... | collective-permute-start | bytes 1990664 | tf_op jit(solution)/shard_map/ppermute | solution.py:23
  38.2 0.9 collective-permute-start.10
  39.0 1.8 %collective-permute-start.11 = (bf16[256,1152]{1,0:T(8,128)(2,1)}, bf16[256,1152]{1,0:T(8,128)(2,1)S(1)}, u32[]{:S(2)}, u32[]{:S(2)}) collective-permute-start(bf16[256,1152]{1,0:T(8,128)(2,1)} %get-tuple-element.49), channel_id=1, source_target_pairs={{0,24},{1,7},{2,26},{3,1},{4,28},{5,3},{6,30},{7,5},{8,0},{9,15},{... | collective-permute-start | bytes 1769480 | tf_op jit(solution)/shard_map/ppermute | solution.py:37
  40.8 0.1 collective-permute-start.9
  41.0 6.6 %copy.8 = bf16[9,256,1024]{2,1,0:T(8,128)(2,1)} copy(bf16[9,256,1024]{1,2,0:T(8,128)(2,1)} %bitcast.24) | data formatting | bytes 9437184 | tf_op jit(solution)/shard_map/transpose | solution.py:374
  47.6 1.0 %collective-permute-done.10.refs_2_ = bf16[256,1152]{1,0:T(8,128)(2,1)S(1)} collective-permute-done((bf16[256,1152]{1,0:T(8,128)(2,1)}, bf16[256,1152]{1,0:T(8,128)(2,1)S(1)}, u32[]{:S(2)}, u32[]{:S(2)}) %collective-permute-start.10) | collective-permute-done | bytes 589856 | tf_op jit(solution)/shard_map/ppermute | solution.py:37
  48.6 5.7 %collective-permute-done.11.refs_3_ = bf16[256,1152]{1,0:T(8,128)(2,1)S(1)} collective-permute-done((bf16[256,1152]{1,0:T(8,128)(2,1)}, bf16[256,1152]{1,0:T(8,128)(2,1)S(1)}, u32[]{:S(2)}, u32[]{:S(2)}) %collective-permute-start.11) | collective-permute-done | bytes 589856 | tf_op jit(solution)/shard_map/ppermute | solution.py:37
  54.3 0.7 collective-permute-done.9.refs_1_
  55.1 0.0 collective-permute-done.12.got_ref
  55.1 1.0 %shard_map.82 = bf16[256,1152]{1,0:T(8,128)(2,1)} custom-call(bf16[256,1152]{1,0:T(8,128)(2,1)S(1)} %get-tuple-element.52.refs_0_, bf16[256,1152]{1,0:T(8,128)(2,1)S(1)} %collective-permute-done.9.refs_1_, bf16[256,1152]{1,0:T(8,128)(2,1)S(1)} %collective-permute-done.10.refs_2_, bf16[256,1152]{1,0:T(8,128)(2,1)S(1)} %collective-permute-done.11.refs_3_), custom_call_target="tpu_custom_call" | custom-call | bytes 2949120 | tf_op jit(solution)/shard_map/pallas_call | solution.py:55
  56.1 11.0 %all-to-all-start = ((bf16[32,8,1152]{2,1,0:T(8,128)(2,1)}), bf16[32,8,1152]{2,1,0:T(8,128)(2,1)S(1)}, u32[]{:S(2)}, u32[]{:S(2)}) async-start(bf16[32,8,1152]{2,1,0:T(8,128)(2,1)} %bitcast.14), calls=%async_computation | async-start | bytes 1179648 | tf_op jit(solution)/shard_map/all_to_all | solution.py:43
  67.1 2.3 %copy-done = bf16[9,256,1024]{2,1,0:T(8,128)(2,1)S(1)} copy-done((bf16[9,256,1024]{2,1,0:T(8,128)(2,1)S(1)}, bf16[9,256,1024]{2,1,0:T(8,128)(2,1)}, u32[]{:S(2)}) %copy-start) | copy-done | bytes 4718616
  69.5 1.1 %copy-done.6 = bf16[3,864,128]{2,1,0:T(8,128)(2,1)S(1)} copy-done((bf16[3,864,128]{2,1,0:T(8,128)(2,1)S(1)}, bf16[3,864,128]{2,1,0:T(8,128)(2,1)}, u32[]{:S(2)}) %copy-start.6) | copy-done | bytes 663576
  70.5 7.5 %shard_map.83 = bf16[864,1024]{1,0:T(8,128)(2,1)} custom-call(s32[3]{0:T(128)S(1)} %copy-done.3, bf16[3,864,128]{2,1,0:T(8,128)(2,1)S(1)} %copy-done.6, bf16[3,864,128]{2,1,0:T(8,128)(2,1)S(1)} %collective-permute-done.12.got_ref, bf16[2304,1024]{1,0:T(8,128)(2,1)S(1)} %bitcast.20), custom_call_target="tpu_custom_call" | custom-call | flops 4076863488 | bytes 7815180 | tf_op jit(solution)/shard_map/pallas_call | solution.py:55
  78.1 6.5 %all-to-all-done = bf16[32,8,1152]{2,1,0:T(8,128)(2,1)S(1)} async-done(((bf16[32,8,1152]{2,1,0:T(8,128)(2,1)}), bf16[32,8,1152]{2,1,0:T(8,128)(2,1)S(1)}, u32[]{:S(2)}, u32[]{:S(2)}) %all-to-all-start) | async-done | bytes 589856 | tf_op jit(solution)/shard_map/all_to_all | solution.py:43
  84.5 0.1 convert_reduce_fusion.1
  84.7 3.2 %collective-permute-start.13 = (f32[4,1152]{1,0:T(4,128)S(1)}, f32[4,1152]{1,0:T(4,128)S(1)}, u32[]{:S(2)}, u32[]{:S(2)}) collective-permute-start(f32[4,1152]{1,0:T(4,128)S(1)} %constant_dynamic-slice_fusion), channel_id=1, source_target_pairs={{0,1},{1,0},{2,3},{3,2},{4,5},{5,4},{6,7},{7,6},{8,9},{9,8},{10,11... | collective-permute-start | bytes 55304 | tf_op jit(solution)/shard_map/ppermute | solution.py:23
  87.8 0.8 collective-permute-done.13
  88.7 0.6 pad_maximum_fusion
  (14 shorter events, 0.1 us)
Async XLA Ops:
  0.6 8.2 %copy-start.1 = (bf16[2,6,72,1024]{3,2,1,0:T(8,128)(2,1)S(1)}, bf16[2,6,72,1024]{3,2,1,0:T(8,128)(2,1)}, u32[]{:S(2)}) copy-start(bf16[2,6,72,1024]{3,2,1,0:T(8,128)(2,1)} %param.6) | copy-start | bytes 5308420
  0.6 13.7 %copy-start.4 = (f32[256]{0:T(256)S(1)}, f32[256]{0:T(256)}, u32[]{:S(2)}) copy-start(f32[256]{0:T(256)} %param.10) | copy-start | bytes 3076
  2.5 6.3 %collective-permute-start = (f32[8,256]{1,0:T(8,128)S(1)}, f32[8,256]{1,0:T(8,128)S(1)}, u32[]{:S(2)}, u32[]{:S(2)}) collective-permute-start(f32[8,256]{1,0:T(8,128)S(1)} %reshape.38), channel_id=1, source_target_pairs={{0,1},{1,0},{2,3},{3,2},{4,5},{5,4},{6,7},{7,6},{8,9},{9,8},{10,11... | collective-permute-start | bytes 24584 | tf_op jit(solution)/shard_map/ppermute | solution.py:23
  6.5 7.9 %copy-start.3 = (s32[3]{0:T(128)S(1)}, s32[3]{0:T(128)}, u32[]{:S(2)}) copy-start(s32[3]{0:T(128)} %pad_add_fusion.place_ref) | copy-start | bytes 40
  8.9 11.2 %collective-permute-start.8 = (bf16[864,1024]{1,0:T(8,128)(2,1)S(1)}, bf16[864,1024]{1,0:T(8,128)(2,1)S(1)}, u32[]{:S(2)}, u32[]{:S(2)}) collective-permute-start(bf16[864,1024]{1,0:T(8,128)(2,1)S(1)} %bitcast.21), channel_id=1, source_target_pairs={{0,1},{1,0},{2,3},{3,2},{4,5},{5,4},{6,7},{7,6},{8,9},{9,8},{10,11... | collective-permute-start | bytes 5308424 | tf_op jit(solution)/shard_map/ppermute | solution.py:23
  9.0 5.4 %collective-permute-start.4 = (bf16[2,864,128]{2,1,0:T(8,128)(2,1)}, bf16[2,864,128]{2,1,0:T(8,128)(2,1)S(1)}, u32[]{:S(2)}, u32[]{:S(2)}) collective-permute-start(bf16[2,864,128]{2,1,0:T(8,128)(2,1)} %get-tuple-element.35), channel_id=1, source_target_pairs={{0,1},{1,0},{2,3},{3,2},{4,5},{5,4},{6,7},{7,6},{8,9},{9,8},{10,11... | collective-permute-start | bytes 1327112 | tf_op jit(solution)/shard_map/ppermute | solution.py:23
  9.5 4.0 %collective-permute-start.1 = (f32[8,256]{1,0:T(8,128)S(1)}, f32[8,256]{1,0:T(8,128)S(1)}, u32[]{:S(2)}, u32[]{:S(2)}) collective-permute-start(f32[8,256]{1,0:T(8,128)S(1)} %add.9.a_ref), channel_id=1, source_target_pairs={{0,4},{2,6},{4,0},{6,2},{1,5},{3,7},{5,1},{7,3},{8,12},{10,14},{12... | collective-permute-start | bytes 24584 | tf_op jit(solution)/shard_map/ppermute | solution.py:27
  10.5 3.8 %collective-permute-start.2 = (f32[8,256]{1,0:T(8,128)S(1)}, f32[8,256]{1,0:T(8,128)S(1)}, u32[]{:S(2)}, u32[]{:S(2)}) collective-permute-start(f32[8,256]{1,0:T(8,128)S(1)} %add.9.a_ref), channel_id=1, source_target_pairs={{0,2},{2,4},{4,6},{6,0},{1,3},{3,5},{5,7},{7,1},{8,10},{10,12},{12... | collective-permute-start | bytes 24584 | tf_op jit(solution)/shard_map/ppermute | solution.py:27
  10.8 3.5 %collective-permute-start.3 = (f32[8,256]{1,0:T(8,128)S(1)}, f32[8,256]{1,0:T(8,128)S(1)}, u32[]{:S(2)}, u32[]{:S(2)}) collective-permute-start(f32[8,256]{1,0:T(8,128)S(1)} %add.9.a_ref), channel_id=1, source_target_pairs={{0,6},{2,0},{4,2},{6,4},{1,7},{3,1},{5,3},{7,5},{8,14},{10,8},{12,... | collective-permute-start | bytes 24584 | tf_op jit(solution)/shard_map/ppermute | solution.py:27
  14.4 1.0 %copy-start.2 = (bf16[2,864,128]{2,1,0:T(8,128)(2,1)S(1)}, bf16[2,864,128]{2,1,0:T(8,128)(2,1)}, u32[]{:S(2)}) copy-start(bf16[2,864,128]{2,1,0:T(8,128)(2,1)} %get-tuple-element.34.mine_ref) | copy-start | bytes 1327108
  16.3 8.7 %collective-permute-start.5 = (bf16[864,128]{1,0:T(8,128)(2,1)S(1)}, bf16[864,128]{1,0:T(8,128)(2,1)S(1)}, u32[]{:S(2)}, u32[]{:S(2)}) collective-permute-start(bf16[864,128]{1,0:T(8,128)(2,1)S(1)} %get-tuple-element.36.even_ref), channel_id=1, source_target_pairs={{0,2},{2,4},{4,6},{6,0},{1,3},{3,5},{5,7},{7,1},{8,10},{10,12},{12... | collective-permute-start | bytes 663560 | tf_op jit(solution)/shard_map/ppermute | solution.py:27
  16.6 8.4 %collective-permute-start.6 = (bf16[864,128]{1,0:T(8,128)(2,1)S(1)}, bf16[864,128]{1,0:T(8,128)(2,1)S(1)}, u32[]{:S(2)}, u32[]{:S(2)}) collective-permute-start(bf16[864,128]{1,0:T(8,128)(2,1)S(1)} %get-tuple-element.37.odd_ref), channel_id=1, source_target_pairs={{0,6},{2,0},{4,2},{6,4},{1,7},{3,1},{5,3},{7,5},{8,14},{10,8},{12,... | collective-permute-start | bytes 663560 | tf_op jit(solution)/shard_map/ppermute | solution.py:27
  19.0 9.5 %collective-permute-start.7 = (bf16[864,128]{1,0:T(8,128)(2,1)S(1)}, bf16[864,128]{1,0:T(8,128)(2,1)S(1)}, u32[]{:S(2)}, u32[]{:S(2)}) collective-permute-start(bf16[864,128]{1,0:T(8,128)(2,1)S(1)} %get-tuple-element.38), channel_id=1, source_target_pairs={{0,4},{2,6},{4,0},{6,2},{1,5},{3,7},{5,1},{7,3},{8,12},{10,14},{12... | collective-permute-start | bytes 663560 | tf_op jit(solution)/shard_map/ppermute | solution.py:27
  34.6 0.8 copy-start.5
  35.5 19.6 %collective-permute-start.12 = (bf16[3,864,128]{2,1,0:T(8,128)(2,1)}, bf16[3,864,128]{2,1,0:T(8,128)(2,1)S(1)}, u32[]{:S(2)}, u32[]{:S(2)}) collective-permute-start(bf16[3,864,128]{2,1,0:T(8,128)(2,1)} %get-tuple-element.51), channel_id=1, source_target_pairs={{0,1},{1,0},{2,3},{3,2},{4,5},{5,4},{6,7},{7,6},{8,9},{9,8},{10,11... | collective-permute-start | bytes 1990664 | tf_op jit(solution)/shard_map/ppermute | solution.py:23
  38.2 10.4 %collective-permute-start.10 = (bf16[256,1152]{1,0:T(8,128)(2,1)}, bf16[256,1152]{1,0:T(8,128)(2,1)S(1)}, u32[]{:S(2)}, u32[]{:S(2)}) collective-permute-start(bf16[256,1152]{1,0:T(8,128)(2,1)} %get-tuple-element.48), channel_id=1, source_target_pairs={{0,8},{1,3},{2,10},{3,5},{4,12},{5,7},{6,14},{7,1},{8,16},{9,11},{... | collective-permute-start | bytes 1769480 | tf_op jit(solution)/shard_map/ppermute | solution.py:37
  39.0 15.3 %collective-permute-start.11 = (bf16[256,1152]{1,0:T(8,128)(2,1)}, bf16[256,1152]{1,0:T(8,128)(2,1)S(1)}, u32[]{:S(2)}, u32[]{:S(2)}) collective-permute-start(bf16[256,1152]{1,0:T(8,128)(2,1)} %get-tuple-element.49), channel_id=1, source_target_pairs={{0,24},{1,7},{2,26},{3,1},{4,28},{5,3},{6,30},{7,5},{8,0},{9,15},{... | collective-permute-start | bytes 1769480 | tf_op jit(solution)/shard_map/ppermute | solution.py:37
  40.8 14.2 %collective-permute-start.9 = (bf16[256,1152]{1,0:T(8,128)(2,1)}, bf16[256,1152]{1,0:T(8,128)(2,1)S(1)}, u32[]{:S(2)}, u32[]{:S(2)}) collective-permute-start(bf16[256,1152]{1,0:T(8,128)(2,1)} %get-tuple-element.47), channel_id=1, source_target_pairs={{0,16},{1,5},{2,18},{3,7},{4,20},{5,1},{6,22},{7,3},{8,24},{9,13},... | collective-permute-start | bytes 1769480 | tf_op jit(solution)/shard_map/ppermute | solution.py:37
  56.1 28.4 %all-to-all-start = ((bf16[32,8,1152]{2,1,0:T(8,128)(2,1)}), bf16[32,8,1152]{2,1,0:T(8,128)(2,1)S(1)}, u32[]{:S(2)}, u32[]{:S(2)}) async-start(bf16[32,8,1152]{2,1,0:T(8,128)(2,1)} %bitcast.14), calls=%async_computation | async-start | bytes 1179648 | tf_op jit(solution)/shard_map/all_to_all | solution.py:43
  67.1 2.3 %copy-start = (bf16[9,256,1024]{2,1,0:T(8,128)(2,1)S(1)}, bf16[9,256,1024]{2,1,0:T(8,128)(2,1)}, u32[]{:S(2)}) copy-start(bf16[9,256,1024]{2,1,0:T(8,128)(2,1)} %copy.8) | copy-start | bytes 14155780
  69.4 1.1 %copy-start.6 = (bf16[3,864,128]{2,1,0:T(8,128)(2,1)S(1)}, bf16[3,864,128]{2,1,0:T(8,128)(2,1)}, u32[]{:S(2)}) copy-start(bf16[3,864,128]{2,1,0:T(8,128)(2,1)} %copy-done.5) | copy-start | bytes 1990660
  84.7 4.0 %collective-permute-start.13 = (f32[4,1152]{1,0:T(4,128)S(1)}, f32[4,1152]{1,0:T(4,128)S(1)}, u32[]{:S(2)}, u32[]{:S(2)}) collective-permute-start(f32[4,1152]{1,0:T(4,128)S(1)} %constant_dynamic-slice_fusion), channel_id=1, source_target_pairs={{0,1},{1,0},{2,3},{3,2},{4,5},{5,4},{6,7},{7,6},{8,9},{9,8},{10,11... | collective-permute-start | bytes 55304 | tf_op jit(solution)/shard_map/ppermute | solution.py:23

commit v6 on v5

--- a/solution.py
+++ b/solution.py
@@ -19,6 +19,18 @@
     return ((z * Y + y) * X + x) * CORES + core
 
 
+def core_of(place_ref):
+    return lax.rem(place_ref[0], CORES)
+
+
+def x_of(place_ref):
+    return lax.rem(lax.div(place_ref[0], CORES), X)
+
+
+def y_of(place_ref):
+    return lax.rem(lax.div(place_ref[0], CORES * X), Y)
+
+
 def swapped(value):
     return lax.ppermute(value, "core", [(0, 1), (1, 0)])
 
@@ -47,11 +59,9 @@
     return pl.BlockSpec(shape, lambda *_: (0,) * len(shape))
 
 
-def kernel_call(body, operands, in_specs, out_shape, out_specs, grid=(1,), scratch=(), flops=0, vmem=8, light=False):
+def kernel_call(body, operands, in_specs, out_shape, out_specs, grid=(1,), scratch=(), flops=0, vmem=8):
     moved = sum(value.size * value.dtype.itemsize for value in operands)
     moved += sum(value.size * value.dtype.itemsize for value in out_shape)
-    if light:
-        moved, flops = 0, 0
     return pl.pallas_call(
         body,
         grid=grid,
@@ -78,7 +88,7 @@
     tall = cells // steps
 
     def body(place_ref, conv_ref, grad_ref, mask_ref, mine_ref, sent_ref):
-        first = place_ref[2] == 0
+        first = core_of(place_ref) == 0
         passed = (grad_ref[...].astype(F32) * mask_ref[...].astype(F32)).astype(BF16)
         for which, value in enumerate((conv_ref[...], passed)):
             lower, upper = value[:, :half], value[:, half:]
@@ -104,8 +114,8 @@
     each = cells // images
 
     def body(place_ref, gain_ref, a_ref, b_ref, c_ref, d_ref, mine_ref, theirs_ref, even_ref, odd_ref, far_ref):
-        first = place_ref[2] == 0
-        early = place_ref[1] < X // 2
+        first = core_of(place_ref) == 0
+        early = x_of(place_ref) < X // 2
         means = (a_ref[...] + b_ref[...] + c_ref[...] + d_ref[...]) / cell_count
         means = jnp.where(first, means[:, :half], means[:, half:])
         gain_row = jnp.where(first, gain_ref[:, :half], gain_ref[:, half:])
@@ -160,7 +170,6 @@
         [jax.ShapeDtypeStruct((channels, 2 * deep), BF16)],
         [pl.BlockSpec((width, 2 * deep), lambda i: (i, 0))],
         (channels // width,),
-        light=True,
     )[0]
 
 
@@ -189,42 +198,39 @@
         stacked[slot * block + cells : (slot + 1) * block, :] = jnp.zeros((block - cells, columns), BF16)
 
 
-def multiply(place_ref, lhs_ref, stacked, total, store):
+def multiply(place_ref, lhs_ref, stacked, total, out_refs):
     columns = stacked.shape[1]
     product = jnp.dot(lhs_ref[...], stacked[...], preferred_element_type=F32)
     total[...] = product.reshape(total.shape)
     tall = total.shape[0] * 32
 
-    @pl.when(place_ref[2] == 0)
+    @pl.when(core_of(place_ref) == 0)
     def _():
         for steps in range(Y):
-            chunk = total[:, lax.rem(place_ref[0] + steps, Y), :, :, :]
-            store(steps, chunk.reshape(tall, columns).astype(BF16))
-
-    @pl.when(place_ref[2] != 0)
+            chunk = total[:, lax.rem(y_of(place_ref) + steps, Y), :, :, :]
+            out_refs[steps][...] = chunk.reshape(tall, columns).astype(BF16)
+
+    @pl.when(core_of(place_ref) != 0)
     def _():
         for steps in range(X):
-            chunk = total[:, :, lax.rem(place_ref[1] + steps, X), :, :]
-            store(steps, chunk.reshape(tall, columns).astype(BF16))
-
-
-def product_call(body, place, fixed, lhs, terms, columns, wide, extra, light=False):
+            chunk = total[:, :, lax.rem(x_of(place_ref) + steps, X), :, :]
+            out_refs[steps][...] = chunk.reshape(tall, columns).astype(BF16)
+
+
+def product_call(body, place, fixed, lhs, columns, extra):
     channels_in, deep = lhs.shape
     steps = 2
     tall = channels_in // steps
-    chunk = lambda width: pl.BlockSpec((tall // 4, width), lambda i: (i, 0))
-    return kernel_call(
-        body,
-        (place, *fixed, lhs, *terms),
-        [SMEM] + [whole(value.shape) for value in fixed] + [pl.BlockSpec((tall, deep), lambda i: (i, 0))]
-        + [chunk(value.shape[1]) for value in terms],
-        [jax.ShapeDtypeStruct((channels_in // 4, wide), BF16)] * 4 + extra,
-        [chunk(wide)] * 4 + [whole(value.shape) for value in extra],
+    return kernel_call(
+        body,
+        (place, *fixed, lhs),
+        [SMEM] + [whole(value.shape) for value in fixed] + [pl.BlockSpec((tall, deep), lambda i: (i, 0))],
+        [jax.ShapeDtypeStruct((channels_in // 4, columns), BF16)] * 4 + extra,
+        [pl.BlockSpec((tall // 4, columns), lambda i: (i, 0))] * 4 + [whole(value.shape) for value in extra],
         (steps,),
         [pltpu.VMEM((deep, columns), BF16), pltpu.VMEM((tall // 128, Y, X, 8, columns), F32)],
-        2 * channels_in * deep * columns,
-        24,
-        light,
+        flops=2 * channels_in * deep * columns,
+        vmem=24,
     )
 
 
@@ -237,38 +243,33 @@
         @pl.when(pl.program_id(0) == 0)
         def _():
             clear_padding(stacked, cells)
-            first = place_ref[2] == 0
+            first = core_of(place_ref) == 0
             even_block, odd_block = even_ref[...], odd_ref[...]
             fill(stacked, 0, 0, jnp.where(first, even_block, odd_block), col_count)
             fill(stacked, 1, 0, jnp.where(first, odd_block, even_block), col_count)
 
-        def store(steps, chunk):
-            rest[steps][...] = chunk
-
-        multiply(place_ref, lhs_ref, stacked, total, store)
-
-    return product_call(body, place, [even, odd], lhs, [], 3 * width, 3 * width, [], True)
-
-
-def all_terms(place, even, odd, up, down, far, lhs, middle, col_count):
+        multiply(place_ref, lhs_ref, stacked, total, rest[:4])
+
+    return product_call(body, place, [even, odd], lhs, 3 * width, [])
+
+
+def side_terms(place, even, odd, up, down, far, lhs, col_count):
     cells, width = up.shape
-    third = 3 * width
 
     def body(place_ref, even_ref, odd_ref, up_ref, down_ref, far_ref, lhs_ref, *rest):
-        middle_refs, out_refs = rest[:4], rest[4:8]
-        mine_ref, theirs_ref, stacked, total = rest[8:]
+        mine_ref, theirs_ref, stacked, total = rest[4:]
 
         @pl.when(pl.program_id(0) == 0)
         def _():
             clear_padding(stacked, cells)
-            first = place_ref[2] == 0
-            early = place_ref[1] < X // 2
+            first = core_of(place_ref) == 0
+            early = x_of(place_ref) < X // 2
             far_block = far_ref[...]
             zero = jnp.zeros_like(far_block)
             far_down = jnp.where(early, far_block, zero)
             far_up = jnp.where(early, zero, far_block)
-            down_block = jnp.where(place_ref[1] < X - 1, down_ref[...], zero)
-            up_block = jnp.where(place_ref[1] > 0, up_ref[...], zero)
+            down_block = jnp.where(x_of(place_ref) < X - 1, down_ref[...], zero)
+            up_block = jnp.where(x_of(place_ref) > 0, up_ref[...], zero)
             pairs = ((down_block, far_down), (even_ref[...], odd_ref[...]), (far_up, up_block))
             for side, (lower, upper) in enumerate(pairs):
                 mine = jnp.where(first, lower, upper)
@@ -279,29 +280,32 @@
                     fill(stacked, 0, 3 * (side // 2), mine, col_count)
                     fill(stacked, 1, 3 * (side // 2), theirs, col_count)
 
-        def store(steps, chunk):
-            out_refs[steps][:, :third] = chunk[:, :third]
-            out_refs[steps][:, third : 2 * third] = middle_refs[steps][...]
-            out_refs[steps][:, 2 * third :] = chunk[:, third:]
-
-        multiply(place_ref, lhs_ref, stacked, total, store)
+        multiply(place_ref, lhs_ref, stacked, total, rest[:4])
 
     triple = jax.ShapeDtypeStruct((3, cells, width), BF16)
-    return product_call(
-        body, place, [even, odd, up, down, far], lhs, middle, 2 * third, 3 * third, [triple, triple]
-    )
-
-
-def first_sum(terms):
-    rows, columns = terms[0].shape
+    return product_call(body, place, [even, odd, up, down, far], lhs, 6 * width, [triple, triple])
+
+
+def first_sum(middle, sides):
+    rows, third = middle[0].shape
 
     def body(*refs):
-        refs[-1][...] = sum(ref[...].astype(F32) for ref in refs[:-1]).astype(BF16)
+        out_ref = refs[-1]
+        middle_total = sum(ref[...].astype(F32) for ref in refs[:4])
+        side_total = sum(ref[...].astype(F32) for ref in refs[4:8])
+        out_ref[:, :third] = side_total[:, :third].astype(BF16)
+        out_ref[:, third : 2 * third] = middle_total.astype(BF16)
+        out_ref[:, 2 * third :] = side_total[:, third:].astype(BF16)
 
     steps = 2
-    spec = pl.BlockSpec((rows // steps, columns), lambda i: (i, 0))
-    return kernel_call(
-        body, terms, [spec] * 4, [jax.ShapeDtypeStruct((rows, columns), BF16)], [spec], (steps,)
+    spec = lambda columns: pl.BlockSpec((rows // steps, columns), lambda i: (i, 0))
+    return kernel_call(
+        body,
+        (*middle, *sides),
+        [spec(third)] * 4 + [spec(2 * third)] * 4,
+        [jax.ShapeDtypeStruct((rows, 3 * third), BF16)],
+        [spec(3 * third)],
+        (steps,),
     )[0]
 
 
@@ -313,7 +317,7 @@
     def body(place_ref, held_ref, got_ref, weight_ref, out_ref, stacked):
         @pl.when(pl.program_id(0) == 0)
         def _():
-            first = place_ref[2] == 0
+            first = core_of(place_ref) == 0
             for side in range(3):
                 mine, theirs = held_ref[side], got_ref[side]
                 lower, upper = jnp.where(first, mine, theirs), jnp.where(first, theirs, mine)
@@ -346,7 +350,7 @@
     cells = image_count * row_count * col_count
     half = channels_out // 2
     core = lax.axis_index("core")
-    place = jnp.stack([lax.axis_index("y"), lax.axis_index("x"), core]).astype(jnp.int32)
+    place = jnp.reshape(lax.axis_index(AXES), (1,)).astype(jnp.int32)
 
     input_flat = inputs.reshape(cells, channels_in)
     sums = channel_sums(conv_out, grad_out, relu_mask)
@@ -368,13 +372,16 @@
     down = around(odd, X - 1)
 
     middle = middle_terms(place, even, odd, lhs, col_count)
-    *terms, held, sent = all_terms(place, even, odd, up, down, far, lhs, middle, col_count)
-    terms = [terms[0]] + [crossed(terms[steps], steps) for steps in (2, 1, 3)]
+    middle = [middle[0]] + [crossed(middle[steps], steps) for steps in (2, 1, 3)]
+    lhs, middle[1], middle[2] = lax.optimization_barrier((lhs, middle[1], middle[2]))
+    *sides, held, sent = side_terms(place, even, odd, up, down, far, lhs, col_count)
+    sides = [sides[0]] + [crossed(sides[steps], steps) for steps in (2, 1, 3)]
+
     weight, held = lax.optimization_barrier((weight, held))
     weight = jnp.transpose(weight, (1, 2, 0)).reshape(9 * channels_out, channels_in)
+    sides, weight = lax.optimization_barrier((sides, weight))
+    merged = first_sum(middle, sides)
     got = swapped(sent)
-    terms, weight, got = lax.optimization_barrier((terms, weight, got))
-    merged = first_sum(terms)
     held, merged = lax.optimization_barrier((held, merged))
     input_grad = input_gradient(place, held, got, weight, col_count)
     merged = exchanged(merged.reshape(Z * 4, 8, 9 * half))

time: 89.8 us -> 86.9 us (0.968)
  waiting for transfers between devices: 19.4 us -> 15.3 us
  starting transfers between devices: 31.1 us -> 34.9 us
  Pallas kernels: 22.9 us -> 21.1 us
    all_to_all x1, waiting for transfers between devices: 6.47 us -> 0.81 us  [exchanged(): return lax.all_to_all(value, AXES, 0, 0, axis_index_groups=groups)]
    ppermute x6, waiting for transfers between devices: 4.62 us -> 1.17 us  [around(): lax.ppermute(value, 'x', [(source, (source + steps) % X) for source in ra...]
    ppermute x3 -> x6, waiting for transfers between devices: 7.44 us -> 10.7 us  [crossed(): return lax.ppermute(value, AXES, pairs)]
    ppermute x3 -> x6, starting transfers between devices: 2.82 us -> 5.17 us  [crossed(): return lax.ppermute(value, AXES, pairs)]
    pallas_call x7, Pallas kernels: 22.9 us -> 21.1 us  [kernel_call(): pl.pallas_call(body, grid=grid, in_specs=in_specs, out_specs=out_specs, o...]
    ppermute x5, waiting for transfers between devices: 0.85 us -> 2.59 us  [swapped(): return lax.ppermute(value, 'core', [(0, 1), (1, 0)])]
    unnamed x14 -> x12, local copies, waits for them, and re-layouts: 5.28 us -> 5.28 us
  transfers between devices with their start and end apart: 15 -> 18, of which waited for: 8 -> 9; matrix products, arithmetic and copies ran while one was open for 8% -> 8% of each run, Pallas kernels for 18% -> 17%
where the time goes in v6:
time: 86.9 us; the launch traced here: 86.5 us
  starting transfers between devices  34.9 us (40%)
  Pallas kernels  21.1 us (24%)
  waiting for transfers between devices  15.3 us (18%)
  local copies, waits for them, and re-layouts  11.9 us (14%)
  other arithmetic  2.6 us (3%)
    pallas_call x7, Pallas kernels, kernel_call(): pl.pallas_call(body, grid=grid, in_specs=in_specs, out_specs=out_specs, o...  21.1 us
    all_to_all x1, starting transfers between devices, exchanged(): return lax.all_to_all(value, AXES, 0, 0, axis_index_groups=groups)  11.5 us
    ppermute x6, waiting for transfers between devices, crossed(): return lax.ppermute(value, AXES, pairs)  10.7 us
    ppermute x5, starting transfers between devices, swapped(): return lax.ppermute(value, 'core', [(0, 1), (1, 0)])  10.7 us
    ppermute x6, starting transfers between devices, around(): lax.ppermute(value, 'x', [(source, (source + steps) % X) for source in ra...  7.51 us
    transpose x1, local copies, waits for them, and re-layouts, per_device(): jnp.transpose(weight, (1, 2, 0)).reshape(9 * channels_out, channels_in)  6.63 us
    unnamed x12, local copies, waits for them, and re-layouts  5.28 us
    ppermute x6, starting transfers between devices, crossed(): return lax.ppermute(value, AXES, pairs)  5.17 us
  transfers between devices with their start and end apart: 18, of which 9 were waited for; matrix products, arithmetic and copies ran while one was open for 8% of the time, Pallas kernels for 17%

profile of v6, /device:TPU:1, one launch (start us, length us, event | category | flops | bytes accessed | tf_op | source)
XLA Modules:
  0.0 86.5 jit_solution(15469920153115764317)
XLA Ops:
  0.6 1.9 %fusion.2 = (f32[2,256]{1,0:T(2,128)S(1)}, f32[2,256]{1,0:T(2,128)S(1)}, f32[2,256]{1,0:T(2,128)S(1)}, f32[2,256]{1,0:T(2,128)S(1)}) fusion(s32[2,6,72,256]{3,2,1,0:T(8,128)} %param.9, bf16[2,6,72,256]{3,2,1,0:T(8,128)(2,1)} %param.8, bf16[2,6,72,256]{3,2,1,0:T(8,128)(2,1)} %param.7), kind=kLoop, calls=%fused_computation.7 | loop fusion | flops 2209792 | bytes 1777664 | tf_op jit(solution)/shard_map/reduce_sum | solution.py:81
  2.5 3.3 %collective-permute-start = (f32[8,256]{1,0:T(8,128)S(1)}, f32[8,256]{1,0:T(8,128)S(1)}, u32[]{:S(2)}, u32[]{:S(2)}) collective-permute-start(f32[8,256]{1,0:T(8,128)S(1)} %reshape.42), channel_id=1, source_target_pairs={{0,1},{1,0},{2,3},{3,2},{4,5},{5,4},{6,7},{7,6},{8,9},{9,8},{10,11... | collective-permute-start | bytes 24584 | tf_op jit(solution)/shard_map/ppermute | solution.py:35
  5.9 2.4 %shard_map.77 = (bf16[2,864,128]{2,1,0:T(8,128)(2,1)}, bf16[2,864,128]{2,1,0:T(8,128)(2,1)}) custom-call(s32[1]{0:T(128)} %bitcast.place_ref, bf16[864,256]{1,0:T(8,128)(2,1)} %bitcast.25, bf16[864,256]{1,0:T(8,128)(2,1)} %bitcast.24, s32[864,256]{1,0:T(8,128)} %bitcast.23), custom_call_target="tpu_custom_call" | custom-call | bytes 2654212 | tf_op jit(solution)/shard_map/pallas_call | solution.py:65
  8.2 0.0 collective-permute-done
  8.2 0.1 collective-permute-start.8
  8.4 0.5 collective-permute-start.4
  8.8 1.0 %collective-permute-start.1 = (f32[8,256]{1,0:T(8,128)S(1)}, f32[8,256]{1,0:T(8,128)S(1)}, u32[]{:S(2)}, u32[]{:S(2)}) collective-permute-start(f32[8,256]{1,0:T(8,128)S(1)} %add.21.a_ref), channel_id=1, source_target_pairs={{0,4},{2,6},{4,0},{6,2},{1,5},{3,7},{5,1},{7,3},{8,12},{10,14},{12... | collective-permute-start | bytes 24584 | tf_op jit(solution)/shard_map/ppermute | solution.py:39
  9.9 0.3 collective-permute-start.2
  10.2 2.4 %collective-permute-start.3 = (f32[8,256]{1,0:T(8,128)S(1)}, f32[8,256]{1,0:T(8,128)S(1)}, u32[]{:S(2)}, u32[]{:S(2)}) collective-permute-start(f32[8,256]{1,0:T(8,128)S(1)} %add.21.a_ref), channel_id=1, source_target_pairs={{0,6},{2,0},{4,2},{6,4},{1,7},{3,1},{5,3},{7,5},{8,14},{10,8},{12,... | collective-permute-start | bytes 24584 | tf_op jit(solution)/shard_map/ppermute | solution.py:39
  12.5 0.3 collective-permute-done.1.b_ref
  12.9 0.8 collective-permute-done.2.c_ref
  13.7 0.0 collective-permute-done.3.d_ref
  13.7 0.0 collective-permute-done.4.theirs_ref
  13.7 0.0 copy-start.2
  13.7 1.0 %copy-done.2 = bf16[2,864,128]{2,1,0:T(8,128)(2,1)S(1)} copy-done((bf16[2,864,128]{2,1,0:T(8,128)(2,1)S(1)}, bf16[2,864,128]{2,1,0:T(8,128)(2,1)}, u32[]{:S(2)}) %copy-start.2) | copy-done | bytes 442392
  14.7 0.3 shard_map.78
  15.1 0.4 collective-permute-start.5
  15.5 2.4 %collective-permute-start.6 = (bf16[864,128]{1,0:T(8,128)(2,1)S(1)}, bf16[864,128]{1,0:T(8,128)(2,1)S(1)}, u32[]{:S(2)}, u32[]{:S(2)}) collective-permute-start(bf16[864,128]{1,0:T(8,128)(2,1)S(1)} %get-tuple-element.39.odd_ref), channel_id=1, source_target_pairs={{0,6},{2,0},{4,2},{6,4},{1,7},{3,1},{5,3},{7,5},{8,14},{10,8},{12,... | collective-permute-start | bytes 663560 | tf_op jit(solution)/shard_map/ppermute | solution.py:39
  17.8 1.1 %collective-permute-start.7 = (bf16[864,128]{1,0:T(8,128)(2,1)S(1)}, bf16[864,128]{1,0:T(8,128)(2,1)S(1)}, u32[]{:S(2)}, u32[]{:S(2)}) collective-permute-start(bf16[864,128]{1,0:T(8,128)(2,1)S(1)} %get-tuple-element.40), channel_id=1, source_target_pairs={{0,4},{2,6},{4,0},{6,2},{1,5},{3,7},{5,1},{7,3},{8,12},{10,14},{12... | collective-permute-start | bytes 663560 | tf_op jit(solution)/shard_map/ppermute | solution.py:39
  18.9 0.0 collective-permute-done.8.other_ref
  18.9 1.7 %shard_map.79.lhs_ref = bf16[1024,1792]{1,0:T(8,128)(2,1)S(1)} custom-call(bf16[864,1024]{1,0:T(8,128)(2,1)S(1)} %bitcast.20, bf16[864,1024]{1,0:T(8,128)(2,1)S(1)} %collective-permute-done.8.other_ref), custom_call_target="tpu_custom_call" | custom-call | bytes 7208960 | tf_op jit(solution)/shard_map/pallas_call | solution.py:65
  20.6 3.4 %shard_map.80 = (bf16[256,384]{1,0:T(8,128)(2,1)S(1)}, bf16[256,384]{1,0:T(8,128)(2,1)S(1)}, bf16[256,384]{1,0:T(8,128)(2,1)S(1)}, bf16[256,384]{1,0:T(8,128)(2,1)}) custom-call(s32[1]{0:T(128)} %bitcast.place_ref, bf16[864,128]{1,0:T(8,128)(2,1)S(1)} %get-tuple-element.38.even_ref, bf16[864,128]{1,0:T(8,128)(2,1)S(1)} %get-tuple-element.39.odd_ref, ...), custom_call_target="tpu_custom_call" | custom-call | flops 1409286144 | bytes 4898820 | tf_op jit(solution)/shard_map/pallas_call | solution.py:65
  24.0 1.9 %collective-permute-start.9 = (bf16[256,384]{1,0:T(8,128)(2,1)S(1)}, bf16[256,384]{1,0:T(8,128)(2,1)S(1)}, u32[]{:S(2)}, u32[]{:S(2)}) collective-permute-start(bf16[256,384]{1,0:T(8,128)(2,1)S(1)} %get-tuple-element.42), channel_id=1, source_target_pairs={{0,16},{1,5},{2,18},{3,7},{4,20},{5,1},{6,22},{7,3},{8,24},{9,13},... | collective-permute-start | bytes 589832 | tf_op jit(solution)/shard_map/ppermute | solution.py:49
  25.9 5.9 %collective-permute-done.9.refs_1_ = bf16[256,384]{1,0:T(8,128)(2,1)S(1)} collective-permute-done((bf16[256,384]{1,0:T(8,128)(2,1)S(1)}, bf16[256,384]{1,0:T(8,128)(2,1)S(1)}, u32[]{:S(2)}, u32[]{:S(2)}) %collective-permute-start.9) | collective-permute-done | bytes 196640 | tf_op jit(solution)/shard_map/ppermute | solution.py:49
  31.8 1.8 %collective-permute-done.10.refs_2_ = bf16[256,384]{1,0:T(8,128)(2,1)S(1)} collective-permute-done((bf16[256,384]{1,0:T(8,128)(2,1)S(1)}, bf16[256,384]{1,0:T(8,128)(2,1)S(1)}, u32[]{:S(2)}, u32[]{:S(2)}) %collective-permute-start.10) | collective-permute-done | bytes 196640 | tf_op jit(solution)/shard_map/ppermute | solution.py:49
  33.5 0.0 collective-permute-done.7.far_ref
  33.5 5.2 %shard_map.81 = (bf16[256,768]{1,0:T(8,128)(2,1)S(1)}, bf16[256,768]{1,0:T(8,128)(2,1)}, bf16[256,768]{1,0:T(8,128)(2,1)}, bf16[256,768]{1,0:T(8,128)(2,1)S(1)},...) custom-call(s32[1]{0:T(128)} %bitcast.place_ref, bf16[864,128]{1,0:T(8,128)(2,1)S(1)} %get-tuple-element.38.even_ref, ...), custom_call_target="tpu_custom_call" | custom-call | flops 2818572288 | bytes 7675908 | tf_op jit(solution)/shard_map/pallas_call | solution.py:65
  38.7 0.8 copy-done.4
  39.6 0.3 collective-permute-start.12
  39.9 0.6 collective-permute-start.13
  40.5 2.1 %collective-permute-start.14 = (bf16[256,768]{1,0:T(8,128)(2,1)S(1)}, bf16[256,768]{1,0:T(8,128)(2,1)S(1)}, u32[]{:S(2)}, u32[]{:S(2)}) collective-permute-start(bf16[256,768]{1,0:T(8,128)(2,1)S(1)} %get-tuple-element.54), channel_id=1, source_target_pairs={{0,24},{1,7},{2,26},{3,1},{4,28},{5,3},{6,30},{7,5},{8,0},{9,15},{... | collective-permute-start | bytes 1179656 | tf_op jit(solution)/shard_map/ppermute | solution.py:49
  42.6 0.3 collective-permute-start.11
  42.8 6.6 %copy.8 = bf16[9,256,1024]{2,1,0:T(8,128)(2,1)} copy(bf16[9,256,1024]{1,2,0:T(8,128)(2,1)} %bitcast.22) | data formatting | bytes 9437184 | tf_op jit(solution)/shard_map/transpose | solution.py:381
  49.5 3.0 %collective-permute-done.13.refs_6_ = bf16[256,768]{1,0:T(8,128)(2,1)S(1)} collective-permute-done((bf16[256,768]{1,0:T(8,128)(2,1)}, bf16[256,768]{1,0:T(8,128)(2,1)S(1)}, u32[]{:S(2)}, u32[]{:S(2)}) %collective-permute-start.13) | collective-permute-done | bytes 393248 | tf_op jit(solution)/shard_map/ppermute | solution.py:49
  52.4 0.0 collective-permute-done.14.refs_7_
  52.4 0.1 collective-permute-done.11.refs_3_
  52.5 1.0 %shard_map.82 = bf16[256,1152]{1,0:T(8,128)(2,1)} custom-call(bf16[256,384]{1,0:T(8,128)(2,1)S(1)} %get-tuple-element.47.refs_0_, bf16[256,384]{1,0:T(8,128)(2,1)S(1)} %collective-permute-done.9.refs_1_, bf16[256,384]{1,0:T(8,128)(2,1)S(1)} %collective-permute-done.10.refs_2_, bf16[256,384]{1,0:T(8,128)(2,1)S(1)} %collective-permute-done.11.refs_3_, ...), custom_call_target="tpu_custom_call" | custom-call | bytes 2949120 | tf_op jit(solution)/shard_map/pallas_call | solution.py:65
  53.5 11.5 %all-to-all-start = ((bf16[32,8,1152]{2,1,0:T(8,128)(2,1)}), bf16[32,8,1152]{2,1,0:T(8,128)(2,1)S(1)}, u32[]{:S(2)}, u32[]{:S(2)}) async-start(bf16[32,8,1152]{2,1,0:T(8,128)(2,1)} %bitcast.12), calls=%async_computation | async-start | bytes 1179648 | tf_op jit(solution)/shard_map/all_to_all | solution.py:55
  65.0 2.7 %collective-permute-start.15 = (bf16[3,864,128]{2,1,0:T(8,128)(2,1)S(1)}, bf16[3,864,128]{2,1,0:T(8,128)(2,1)S(1)}, u32[]{:S(2)}, u32[]{:S(2)}) collective-permute-start(bf16[3,864,128]{2,1,0:T(8,128)(2,1)S(1)} %get-tuple-element.62), channel_id=1, source_target_pairs={{0,1},{1,0},{2,3},{3,2},{4,5},{5,4},{6,7},{7,6},{8,9},{9,8},{10,11... | collective-permute-start | bytes 1990664 | tf_op jit(solution)/shard_map/ppermute | solution.py:35
  67.7 1.7 %collective-permute-done.15.got_ref = bf16[3,864,128]{2,1,0:T(8,128)(2,1)S(1)} collective-permute-done((bf16[3,864,128]{2,1,0:T(8,128)(2,1)S(1)}, bf16[3,864,128]{2,1,0:T(8,128)(2,1)S(1)}, u32[]{:S(2)}, u32[]{:S(2)}) %collective-permute-start.15) | collective-permute-done | bytes 663584 | tf_op jit(solution)/shard_map/ppermute | solution.py:35
  69.5 2.3 %copy-done = bf16[9,256,1024]{2,1,0:T(8,128)(2,1)S(1)} copy-done((bf16[9,256,1024]{2,1,0:T(8,128)(2,1)S(1)}, bf16[9,256,1024]{2,1,0:T(8,128)(2,1)}, u32[]{:S(2)}) %copy-start) | copy-done | bytes 4718616
  71.8 1.1 %copy-done.5 = bf16[3,864,128]{2,1,0:T(8,128)(2,1)S(1)} copy-done((bf16[3,864,128]{2,1,0:T(8,128)(2,1)S(1)}, bf16[3,864,128]{2,1,0:T(8,128)(2,1)}, u32[]{:S(2)}) %copy-start.5) | copy-done | bytes 663576
  72.9 7.1 %shard_map.83 = bf16[864,1024]{1,0:T(8,128)(2,1)} custom-call(s32[1]{0:T(128)} %bitcast.place_ref, bf16[3,864,128]{2,1,0:T(8,128)(2,1)S(1)} %copy-done.5, bf16[3,864,128]{2,1,0:T(8,128)(2,1)S(1)} %collective-permute-done.15.got_ref, bf16[2304,1024]{1,0:T(8,128)(2,1)S(1)} %bitcast.18), custom_call_target="tpu_custom_call" | custom-call | flops 4076863488 | bytes 7815172 | tf_op jit(solution)/shard_map/pallas_call | solution.py:65
  80.0 0.8 all-to-all-done
  80.8 0.1 convert_reduce_fusion.1
  80.9 4.1 %collective-permute-start.16 = (f32[4,1152]{1,0:T(4,128)S(1)}, f32[4,1152]{1,0:T(4,128)S(1)}, u32[]{:S(2)}, u32[]{:S(2)}) collective-permute-start(f32[4,1152]{1,0:T(4,128)S(1)} %constant_dynamic-slice_fusion), channel_id=1, source_target_pairs={{0,1},{1,0},{2,3},{3,2},{4,5},{5,4},{6,7},{7,6},{8,9},{9,8},{10,11... | collective-permute-start | bytes 55304 | tf_op jit(solution)/shard_map/ppermute | solution.py:35
  85.0 0.8 collective-permute-done.16
  85.8 0.6 pad_maximum_fusion
  (17 shorter events, 0.1 us)
Async XLA Ops:
  0.6 7.6 %copy-start.1 = (bf16[2,6,72,1024]{3,2,1,0:T(8,128)(2,1)S(1)}, bf16[2,6,72,1024]{3,2,1,0:T(8,128)(2,1)}, u32[]{:S(2)}) copy-start(bf16[2,6,72,1024]{3,2,1,0:T(8,128)(2,1)} %param.6) | copy-start | bytes 5308420
  0.6 13.1 %copy-start.3 = (f32[256]{0:T(256)S(1)}, f32[256]{0:T(256)}, u32[]{:S(2)}) copy-start(f32[256]{0:T(256)} %param.10) | copy-start | bytes 3076
  2.5 5.7 %collective-permute-start = (f32[8,256]{1,0:T(8,128)S(1)}, f32[8,256]{1,0:T(8,128)S(1)}, u32[]{:S(2)}, u32[]{:S(2)}) collective-permute-start(f32[8,256]{1,0:T(8,128)S(1)} %reshape.42), channel_id=1, source_target_pairs={{0,1},{1,0},{2,3},{3,2},{4,5},{5,4},{6,7},{7,6},{8,9},{9,8},{10,11... | collective-permute-start | bytes 24584 | tf_op jit(solution)/shard_map/ppermute | solution.py:35
  8.2 10.7 %collective-permute-start.8 = (bf16[864,1024]{1,0:T(8,128)(2,1)S(1)}, bf16[864,1024]{1,0:T(8,128)(2,1)S(1)}, u32[]{:S(2)}, u32[]{:S(2)}) collective-permute-start(bf16[864,1024]{1,0:T(8,128)(2,1)S(1)} %bitcast.19), channel_id=1, source_target_pairs={{0,1},{1,0},{2,3},{3,2},{4,5},{5,4},{6,7},{7,6},{8,9},{9,8},{10,11... | collective-permute-start | bytes 5308424 | tf_op jit(solution)/shard_map/ppermute | solution.py:35
  8.4 5.3 %collective-permute-start.4 = (bf16[2,864,128]{2,1,0:T(8,128)(2,1)}, bf16[2,864,128]{2,1,0:T(8,128)(2,1)S(1)}, u32[]{:S(2)}, u32[]{:S(2)}) collective-permute-start(bf16[2,864,128]{2,1,0:T(8,128)(2,1)} %get-tuple-element.37), channel_id=1, source_target_pairs={{0,1},{1,0},{2,3},{3,2},{4,5},{5,4},{6,7},{7,6},{8,9},{9,8},{10,11... | collective-permute-start | bytes 1327112 | tf_op jit(solution)/shard_map/ppermute | solution.py:35
  8.8 4.0 %collective-permute-start.1 = (f32[8,256]{1,0:T(8,128)S(1)}, f32[8,256]{1,0:T(8,128)S(1)}, u32[]{:S(2)}, u32[]{:S(2)}) collective-permute-start(f32[8,256]{1,0:T(8,128)S(1)} %add.21.a_ref), channel_id=1, source_target_pairs={{0,4},{2,6},{4,0},{6,2},{1,5},{3,7},{5,1},{7,3},{8,12},{10,14},{12... | collective-permute-start | bytes 24584 | tf_op jit(solution)/shard_map/ppermute | solution.py:39
  9.9 3.8 %collective-permute-start.2 = (f32[8,256]{1,0:T(8,128)S(1)}, f32[8,256]{1,0:T(8,128)S(1)}, u32[]{:S(2)}, u32[]{:S(2)}) collective-permute-start(f32[8,256]{1,0:T(8,128)S(1)} %add.21.a_ref), channel_id=1, source_target_pairs={{0,2},{2,4},{4,6},{6,0},{1,3},{3,5},{5,7},{7,1},{8,10},{10,12},{12... | collective-permute-start | bytes 24584 | tf_op jit(solution)/shard_map/ppermute | solution.py:39
  10.2 3.5 %collective-permute-start.3 = (f32[8,256]{1,0:T(8,128)S(1)}, f32[8,256]{1,0:T(8,128)S(1)}, u32[]{:S(2)}, u32[]{:S(2)}) collective-permute-start(f32[8,256]{1,0:T(8,128)S(1)} %add.21.a_ref), channel_id=1, source_target_pairs={{0,6},{2,0},{4,2},{6,4},{1,7},{3,1},{5,3},{7,5},{8,14},{10,8},{12,... | collective-permute-start | bytes 24584 | tf_op jit(solution)/shard_map/ppermute | solution.py:39
  13.7 1.0 %copy-start.2 = (bf16[2,864,128]{2,1,0:T(8,128)(2,1)S(1)}, bf16[2,864,128]{2,1,0:T(8,128)(2,1)}, u32[]{:S(2)}) copy-start(bf16[2,864,128]{2,1,0:T(8,128)(2,1)} %get-tuple-element.36.mine_ref) | copy-start | bytes 1327108
  15.1 18.5 %collective-permute-start.5 = (bf16[864,128]{1,0:T(8,128)(2,1)S(1)}, bf16[864,128]{1,0:T(8,128)(2,1)S(1)}, u32[]{:S(2)}, u32[]{:S(2)}) collective-permute-start(bf16[864,128]{1,0:T(8,128)(2,1)S(1)} %get-tuple-element.38.even_ref), channel_id=1, source_target_pairs={{0,2},{2,4},{4,6},{6,0},{1,3},{3,5},{5,7},{7,1},{8,10},{10,12},{12... | collective-permute-start | bytes 663560 | tf_op jit(solution)/shard_map/ppermute | solution.py:39
  15.5 18.1 %collective-permute-start.6 = (bf16[864,128]{1,0:T(8,128)(2,1)S(1)}, bf16[864,128]{1,0:T(8,128)(2,1)S(1)}, u32[]{:S(2)}, u32[]{:S(2)}) collective-permute-start(bf16[864,128]{1,0:T(8,128)(2,1)S(1)} %get-tuple-element.39.odd_ref), channel_id=1, source_target_pairs={{0,6},{2,0},{4,2},{6,4},{1,7},{3,1},{5,3},{7,5},{8,14},{10,8},{12,... | collective-permute-start | bytes 663560 | tf_op jit(solution)/shard_map/ppermute | solution.py:39
  17.8 15.7 %collective-permute-start.7 = (bf16[864,128]{1,0:T(8,128)(2,1)S(1)}, bf16[864,128]{1,0:T(8,128)(2,1)S(1)}, u32[]{:S(2)}, u32[]{:S(2)}) collective-permute-start(bf16[864,128]{1,0:T(8,128)(2,1)S(1)} %get-tuple-element.40), channel_id=1, source_target_pairs={{0,4},{2,6},{4,0},{6,2},{1,5},{3,7},{5,1},{7,3},{8,12},{10,14},{12... | collective-permute-start | bytes 663560 | tf_op jit(solution)/shard_map/ppermute | solution.py:39
  24.0 7.8 %collective-permute-start.9 = (bf16[256,384]{1,0:T(8,128)(2,1)S(1)}, bf16[256,384]{1,0:T(8,128)(2,1)S(1)}, u32[]{:S(2)}, u32[]{:S(2)}) collective-permute-start(bf16[256,384]{1,0:T(8,128)(2,1)S(1)} %get-tuple-element.42), channel_id=1, source_target_pairs={{0,16},{1,5},{2,18},{3,7},{4,20},{5,1},{6,22},{7,3},{8,24},{9,13},... | collective-permute-start | bytes 589832 | tf_op jit(solution)/shard_map/ppermute | solution.py:49
  25.9 7.7 %collective-permute-start.10 = (bf16[256,384]{1,0:T(8,128)(2,1)S(1)}, bf16[256,384]{1,0:T(8,128)(2,1)S(1)}, u32[]{:S(2)}, u32[]{:S(2)}) collective-permute-start(bf16[256,384]{1,0:T(8,128)(2,1)S(1)} %get-tuple-element.43), channel_id=1, source_target_pairs={{0,8},{1,3},{2,10},{3,5},{4,12},{5,7},{6,14},{7,1},{8,16},{9,11},{... | collective-permute-start | bytes 589832 | tf_op jit(solution)/shard_map/ppermute | solution.py:49
  38.7 0.8 copy-start.4
  39.6 9.9 %collective-permute-start.12 = (bf16[256,768]{1,0:T(8,128)(2,1)}, bf16[256,768]{1,0:T(8,128)(2,1)S(1)}, u32[]{:S(2)}, u32[]{:S(2)}) collective-permute-start(bf16[256,768]{1,0:T(8,128)(2,1)} %get-tuple-element.52), channel_id=1, source_target_pairs={{0,16},{1,5},{2,18},{3,7},{4,20},{5,1},{6,22},{7,3},{8,24},{9,13},... | collective-permute-start | bytes 1179656 | tf_op jit(solution)/shard_map/ppermute | solution.py:49
  39.9 12.5 %collective-permute-start.13 = (bf16[256,768]{1,0:T(8,128)(2,1)}, bf16[256,768]{1,0:T(8,128)(2,1)S(1)}, u32[]{:S(2)}, u32[]{:S(2)}) collective-permute-start(bf16[256,768]{1,0:T(8,128)(2,1)} %get-tuple-element.53), channel_id=1, source_target_pairs={{0,8},{1,3},{2,10},{3,5},{4,12},{5,7},{6,14},{7,1},{8,16},{9,11},{... | collective-permute-start | bytes 1179656 | tf_op jit(solution)/shard_map/ppermute | solution.py:49
  40.5 11.9 %collective-permute-start.14 = (bf16[256,768]{1,0:T(8,128)(2,1)S(1)}, bf16[256,768]{1,0:T(8,128)(2,1)S(1)}, u32[]{:S(2)}, u32[]{:S(2)}) collective-permute-start(bf16[256,768]{1,0:T(8,128)(2,1)S(1)} %get-tuple-element.54), channel_id=1, source_target_pairs={{0,24},{1,7},{2,26},{3,1},{4,28},{5,3},{6,30},{7,5},{8,0},{9,15},{... | collective-permute-start | bytes 1179656 | tf_op jit(solution)/shard_map/ppermute | solution.py:49
  42.6 9.9 %collective-permute-start.11 = (bf16[256,384]{1,0:T(8,128)(2,1)}, bf16[256,384]{1,0:T(8,128)(2,1)S(1)}, u32[]{:S(2)}, u32[]{:S(2)}) collective-permute-start(bf16[256,384]{1,0:T(8,128)(2,1)} %get-tuple-element.50), channel_id=1, source_target_pairs={{0,24},{1,7},{2,26},{3,1},{4,28},{5,3},{6,30},{7,5},{8,0},{9,15},{... | collective-permute-start | bytes 589832 | tf_op jit(solution)/shard_map/ppermute | solution.py:49
  53.5 27.3 %all-to-all-start = ((bf16[32,8,1152]{2,1,0:T(8,128)(2,1)}), bf16[32,8,1152]{2,1,0:T(8,128)(2,1)S(1)}, u32[]{:S(2)}, u32[]{:S(2)}) async-start(bf16[32,8,1152]{2,1,0:T(8,128)(2,1)} %bitcast.12), calls=%async_computation | async-start | bytes 1179648 | tf_op jit(solution)/shard_map/all_to_all | solution.py:55
  65.0 4.4 %collective-permute-start.15 = (bf16[3,864,128]{2,1,0:T(8,128)(2,1)S(1)}, bf16[3,864,128]{2,1,0:T(8,128)(2,1)S(1)}, u32[]{:S(2)}, u32[]{:S(2)}) collective-permute-start(bf16[3,864,128]{2,1,0:T(8,128)(2,1)S(1)} %get-tuple-element.62), channel_id=1, source_target_pairs={{0,1},{1,0},{2,3},{3,2},{4,5},{5,4},{6,7},{7,6},{8,9},{9,8},{10,11... | collective-permute-start | bytes 1990664 | tf_op jit(solution)/shard_map/ppermute | solution.py:35
  69.5 2.3 %copy-start = (bf16[9,256,1024]{2,1,0:T(8,128)(2,1)S(1)}, bf16[9,256,1024]{2,1,0:T(8,128)(2,1)}, u32[]{:S(2)}) copy-start(bf16[9,256,1024]{2,1,0:T(8,128)(2,1)} %copy.8) | copy-start | bytes 14155780
  71.8 1.1 %copy-start.5 = (bf16[3,864,128]{2,1,0:T(8,128)(2,1)S(1)}, bf16[3,864,128]{2,1,0:T(8,128)(2,1)}, u32[]{:S(2)}) copy-start(bf16[3,864,128]{2,1,0:T(8,128)(2,1)} %copy-done.4) | copy-start | bytes 1990660
  80.9 4.9 %collective-permute-start.16 = (f32[4,1152]{1,0:T(4,128)S(1)}, f32[4,1152]{1,0:T(4,128)S(1)}, u32[]{:S(2)}, u32[]{:S(2)}) collective-permute-start(f32[4,1152]{1,0:T(4,128)S(1)} %constant_dynamic-slice_fusion), channel_id=1, source_target_pairs={{0,1},{1,0},{2,3},{3,2},{4,5},{5,4},{6,7},{7,6},{8,9},{9,8},{10,11... | collective-permute-start | bytes 55304 | tf_op jit(solution)/shard_map/ppermute | solution.py:35

commit v7 on v6

--- a/solution.py
+++ b/solution.py
@@ -339,7 +339,7 @@
         (channels_in // width,),
         [pltpu.VMEM((cells, deep), BF16)],
         2 * cells * deep * channels_in,
-        24,
+        60,
     )[0]
 
 
@@ -371,18 +371,16 @@
     up = around(even, 1)
     down = around(odd, X - 1)
 
-    middle = middle_terms(place, even, odd, lhs, col_count)
+    middle = list(middle_terms(place, even, odd, lhs, col_count))
+    weight, middle[0] = lax.optimization_barrier((weight, middle[0]))
+    weight = jnp.transpose(weight, (1, 2, 0)).reshape(9 * channels_out, channels_in)
     middle = [middle[0]] + [crossed(middle[steps], steps) for steps in (2, 1, 3)]
-    lhs, middle[1], middle[2] = lax.optimization_barrier((lhs, middle[1], middle[2]))
+    lhs, weight, middle[1], middle[2] = lax.optimization_barrier((lhs, weight, middle[1], middle[2]))
     *sides, held, sent = side_terms(place, even, odd, up, down, far, lhs, col_count)
     sides = [sides[0]] + [crossed(sides[steps], steps) for steps in (2, 1, 3)]
-
-    weight, held = lax.optimization_barrier((weight, held))
-    weight = jnp.transpose(weight, (1, 2, 0)).reshape(9 * channels_out, channels_in)
-    sides, weight = lax.optimization_barrier((sides, weight))
     merged = first_sum(middle, sides)
     got = swapped(sent)
-    held, merged = lax.optimization_barrier((held, merged))
+    place, merged = lax.optimization_barrier((place, merged))
     input_grad = input_gradient(place, held, got, weight, col_count)
     merged = exchanged(merged.reshape(Z * 4, 8, 9 * half))
     merged, input_grad = lax.optimization_barrier((merged, input_grad))

time: 86.9 us -> 88.5 us (1.018)
  starting transfers between devices: 34.9 us -> 37.6 us
  local copies, waits for them, and re-layouts: 11.9 us -> 10.6 us
    ppermute x5, starting transfers between devices: 10.7 us -> 13.3 us  [swapped(): return lax.ppermute(value, 'core', [(0, 1), (1, 0)])]
    unnamed x12 -> x14, local copies, waits for them, and re-layouts: 5.28 us -> 3.9 us
    ppermute x6, waiting for transfers between devices: 10.7 us -> 11.7 us  [crossed(): return lax.ppermute(value, AXES, pairs)]
  transfers between devices with their start and end apart: 18 -> 18, of which waited for: 9 -> 6; matrix products, arithmetic and copies ran while one was open for 8% -> 8% of each run, Pallas kernels for 17% -> 18%
where the time goes in v7:
time: 88.5 us; the launch traced here: 88 us
  starting transfers between devices  37.6 us (42%)
  Pallas kernels  21 us (24%)
  waiting for transfers between devices  15.5 us (18%)
  local copies, waits for them, and re-layouts  10.6 us (12%)
  other arithmetic  2.6 us (3%)
    pallas_call x7, Pallas kernels, kernel_call(): pl.pallas_call(body, grid=grid, in_specs=in_specs, out_specs=out_specs, o...  21 us
    ppermute x5, starting transfers between devices, swapped(): return lax.ppermute(value, 'core', [(0, 1), (1, 0)])  13.3 us
    ppermute x6, waiting for transfers between devices, crossed(): return lax.ppermute(value, AXES, pairs)  11.7 us
    all_to_all x1, starting transfers between devices, exchanged(): return lax.all_to_all(value, AXES, 0, 0, axis_index_groups=groups)  11.2 us
    ppermute x6, starting transfers between devices, around(): lax.ppermute(value, 'x', [(source, (source + steps) % X) for source in ra...  7.51 us
    transpose x1, local copies, waits for them, and re-layouts, per_device(): jnp.transpose(weight, (1, 2, 0)).reshape(9 * channels_out, channels_in)  6.66 us
    ppermute x6, starting transfers between devices, crossed(): return lax.ppermute(value, AXES, pairs)  5.66 us
    unnamed x14, local copies, waits for them, and re-layouts  3.9 us
  transfers between devices with their start and end apart: 18, of which 6 were waited for; matrix products, arithmetic and copies ran while one was open for 8% of the time, Pallas kernels for 18%

profile of v7, /device:TPU:1, one launch (start us, length us, event | category | flops | bytes accessed | tf_op | source)
XLA Modules:
  0.0 88.0 jit_solution(2505887908839345136)
XLA Ops:
  0.6 1.9 %fusion.2 = (f32[2,256]{1,0:T(2,128)S(1)}, f32[2,256]{1,0:T(2,128)S(1)}, f32[2,256]{1,0:T(2,128)S(1)}, f32[2,256]{1,0:T(2,128)S(1)}) fusion(s32[2,6,72,256]{3,2,1,0:T(8,128)} %param.9, bf16[2,6,72,256]{3,2,1,0:T(8,128)(2,1)} %param.8, bf16[2,6,72,256]{3,2,1,0:T(8,128)(2,1)} %param.7), kind=kLoop, calls=%fused_computation.7 | loop fusion | flops 2209792 | bytes 1777664 | tf_op jit(solution)/shard_map/reduce_sum | solution.py:81
  2.5 3.3 %collective-permute-start = (f32[8,256]{1,0:T(8,128)S(1)}, f32[8,256]{1,0:T(8,128)S(1)}, u32[]{:S(2)}, u32[]{:S(2)}) collective-permute-start(f32[8,256]{1,0:T(8,128)S(1)} %reshape.42), channel_id=1, source_target_pairs={{0,1},{1,0},{2,3},{3,2},{4,5},{5,4},{6,7},{7,6},{8,9},{9,8},{10,11... | collective-permute-start | bytes 24584 | tf_op jit(solution)/shard_map/ppermute | solution.py:35
  5.9 2.4 %shard_map.77 = (bf16[2,864,128]{2,1,0:T(8,128)(2,1)}, bf16[2,864,128]{2,1,0:T(8,128)(2,1)}) custom-call(s32[1]{0:T(128)} %bitcast.place_ref, bf16[864,256]{1,0:T(8,128)(2,1)} %bitcast.25, bf16[864,256]{1,0:T(8,128)(2,1)} %bitcast.24, s32[864,256]{1,0:T(8,128)} %bitcast.23), custom_call_target="tpu_custom_call" | custom-call | bytes 2654212 | tf_op jit(solution)/shard_map/pallas_call | solution.py:65
  8.2 0.0 collective-permute-done
  8.2 0.1 collective-permute-start.5
  8.4 0.5 collective-permute-start.4
  8.8 1.0 %collective-permute-start.1 = (f32[8,256]{1,0:T(8,128)S(1)}, f32[8,256]{1,0:T(8,128)S(1)}, u32[]{:S(2)}, u32[]{:S(2)}) collective-permute-start(f32[8,256]{1,0:T(8,128)S(1)} %add.21.a_ref), channel_id=1, source_target_pairs={{0,4},{2,6},{4,0},{6,2},{1,5},{3,7},{5,1},{7,3},{8,12},{10,14},{12... | collective-permute-start | bytes 24584 | tf_op jit(solution)/shard_map/ppermute | solution.py:39
  9.9 0.3 collective-permute-start.2
  10.2 2.4 %collective-permute-start.3 = (f32[8,256]{1,0:T(8,128)S(1)}, f32[8,256]{1,0:T(8,128)S(1)}, u32[]{:S(2)}, u32[]{:S(2)}) collective-permute-start(f32[8,256]{1,0:T(8,128)S(1)} %add.21.a_ref), channel_id=1, source_target_pairs={{0,6},{2,0},{4,2},{6,4},{1,7},{3,1},{5,3},{7,5},{8,14},{10,8},{12,... | collective-permute-start | bytes 24584 | tf_op jit(solution)/shard_map/ppermute | solution.py:39
  12.6 0.3 collective-permute-done.1.b_ref
  12.9 0.8 collective-permute-done.2.c_ref
  13.7 0.0 collective-permute-done.3.d_ref
  13.7 0.0 collective-permute-done.4.theirs_ref
  13.7 0.0 copy-start.3
  13.7 1.0 %copy-done.3 = bf16[2,864,128]{2,1,0:T(8,128)(2,1)S(1)} copy-done((bf16[2,864,128]{2,1,0:T(8,128)(2,1)S(1)}, bf16[2,864,128]{2,1,0:T(8,128)(2,1)}, u32[]{:S(2)}) %copy-start.3) | copy-done | bytes 442392
  14.7 0.3 shard_map.78
  15.1 0.4 collective-permute-start.9
  15.5 2.4 %collective-permute-start.10 = (bf16[864,128]{1,0:T(8,128)(2,1)S(1)}, bf16[864,128]{1,0:T(8,128)(2,1)S(1)}, u32[]{:S(2)}, u32[]{:S(2)}) collective-permute-start(bf16[864,128]{1,0:T(8,128)(2,1)S(1)} %get-tuple-element.35.odd_ref), channel_id=1, source_target_pairs={{0,6},{2,0},{4,2},{6,4},{1,7},{3,1},{5,3},{7,5},{8,14},{10,8},{12,... | collective-permute-start | bytes 663560 | tf_op jit(solution)/shard_map/ppermute | solution.py:39
  17.8 1.1 %collective-permute-start.11 = (bf16[864,128]{1,0:T(8,128)(2,1)S(1)}, bf16[864,128]{1,0:T(8,128)(2,1)S(1)}, u32[]{:S(2)}, u32[]{:S(2)}) collective-permute-start(bf16[864,128]{1,0:T(8,128)(2,1)S(1)} %get-tuple-element.45), channel_id=1, source_target_pairs={{0,4},{2,6},{4,0},{6,2},{1,5},{3,7},{5,1},{7,3},{8,12},{10,14},{12... | collective-permute-start | bytes 663560 | tf_op jit(solution)/shard_map/ppermute | solution.py:39
  18.9 0.0 collective-permute-done.5.other_ref
  18.9 1.7 %shard_map.79.lhs_ref = bf16[1024,1792]{1,0:T(8,128)(2,1)S(1)} custom-call(bf16[864,1024]{1,0:T(8,128)(2,1)S(1)} %bitcast.19, bf16[864,1024]{1,0:T(8,128)(2,1)S(1)} %collective-permute-done.5.other_ref), custom_call_target="tpu_custom_call" | custom-call | bytes 7208960 | tf_op jit(solution)/shard_map/pallas_call | solution.py:65
  20.6 2.7 %shard_map.80 = (bf16[256,384]{1,0:T(8,128)(2,1)S(1)}, bf16[256,384]{1,0:T(8,128)(2,1)S(1)}, bf16[256,384]{1,0:T(8,128)(2,1)S(1)}, bf16[256,384]{1,0:T(8,128)(2,1)S(1)}) custom-call(s32[1]{0:T(128)} %bitcast.place_ref, bf16[864,128]{1,0:T(8,128)(2,1)S(1)} %get-tuple-element.34.even_ref, bf16[864,128]{1,0:T(8,128)(2,1)S(1)} %get-tuple-element.35.odd_ref, ...), custom_call_target="tpu_custom_call" | custom-call | flops 1409286144 | bytes 4898820 | tf_op jit(solution)/shard_map/pallas_call | solution.py:65
  23.3 2.0 %collective-permute-start.6 = (bf16[256,384]{1,0:T(8,128)(2,1)S(1)}, bf16[256,384]{1,0:T(8,128)(2,1)S(1)}, u32[]{:S(2)}, u32[]{:S(2)}) collective-permute-start(bf16[256,384]{1,0:T(8,128)(2,1)S(1)} %get-tuple-element.40), channel_id=1, source_target_pairs={{0,16},{1,5},{2,18},{3,7},{4,20},{5,1},{6,22},{7,3},{8,24},{9,13},... | collective-permute-start | bytes 589832 | tf_op jit(solution)/shard_map/ppermute | solution.py:49
  25.3 0.0 collective-permute-start.7
  25.3 6.7 %copy.8 = bf16[9,256,1024]{2,1,0:T(8,128)(2,1)} copy(bf16[9,256,1024]{1,2,0:T(8,128)(2,1)} %bitcast.21) | data formatting | bytes 9437184 | tf_op jit(solution)/shard_map/transpose | solution.py:376
  32.0 0.0 collective-permute-done.6.refs_1_
  32.0 1.9 %collective-permute-done.7.refs_2_ = bf16[256,384]{1,0:T(8,128)(2,1)S(1)} collective-permute-done((bf16[256,384]{1,0:T(8,128)(2,1)S(1)}, bf16[256,384]{1,0:T(8,128)(2,1)S(1)}, u32[]{:S(2)}, u32[]{:S(2)}) %collective-permute-start.7) | collective-permute-done | bytes 196640 | tf_op jit(solution)/shard_map/ppermute | solution.py:49
  33.8 0.0 collective-permute-done.9.up_ref
  33.8 0.0 collective-permute-done.10.down_ref
  33.8 0.0 collective-permute-done.11.far_ref
  33.9 2.0 %copy-done.1 = bf16[1024,1792]{1,0:T(8,128)(2,1)S(1)} copy-done((bf16[1024,1792]{1,0:T(8,128)(2,1)S(1)}, bf16[1024,1792]{1,0:T(8,128)(2,1)}, u32[]{:S(2)}) %copy-start.1) | copy-done | bytes 3670040
  35.9 4.4 %shard_map.81 = (bf16[256,768]{1,0:T(8,128)(2,1)S(1)}, bf16[256,768]{1,0:T(8,128)(2,1)S(1)}, bf16[256,768]{1,0:T(8,128)(2,1)S(1)}, bf16[256,768]{1,0:T(8,128)(2,...) custom-call(s32[1]{0:T(128)} %bitcast.place_ref, ...), custom_call_target="tpu_custom_call" | custom-call | flops 2818572288 | bytes 7675908 | tf_op jit(solution)/shard_map/pallas_call | solution.py:65
  40.3 1.0 %collective-permute-start.12 = (bf16[256,768]{1,0:T(8,128)(2,1)S(1)}, bf16[256,768]{1,0:T(8,128)(2,1)S(1)}, u32[]{:S(2)}, u32[]{:S(2)}) collective-permute-start(bf16[256,768]{1,0:T(8,128)(2,1)S(1)} %get-tuple-element.48), channel_id=1, source_target_pairs={{0,16},{1,5},{2,18},{3,7},{4,20},{5,1},{6,22},{7,3},{8,24},{9,13},... | collective-permute-start | bytes 1179656 | tf_op jit(solution)/shard_map/ppermute | solution.py:49
  41.2 0.7 collective-permute-start.13
  42.0 1.9 %collective-permute-start.14 = (bf16[256,768]{1,0:T(8,128)(2,1)S(1)}, bf16[256,768]{1,0:T(8,128)(2,1)S(1)}, u32[]{:S(2)}, u32[]{:S(2)}) collective-permute-start(bf16[256,768]{1,0:T(8,128)(2,1)S(1)} %get-tuple-element.50), channel_id=1, source_target_pairs={{0,24},{1,7},{2,26},{3,1},{4,28},{5,3},{6,30},{7,5},{8,0},{9,15},{... | collective-permute-start | bytes 1179656 | tf_op jit(solution)/shard_map/ppermute | solution.py:49
  43.9 0.0 collective-permute-start.8
  43.9 9.8 %collective-permute-done.8.refs_3_ = bf16[256,384]{1,0:T(8,128)(2,1)S(1)} collective-permute-done((bf16[256,384]{1,0:T(8,128)(2,1)S(1)}, bf16[256,384]{1,0:T(8,128)(2,1)S(1)}, u32[]{:S(2)}, u32[]{:S(2)}) %collective-permute-start.8) | collective-permute-done | bytes 196640 | tf_op jit(solution)/shard_map/ppermute | solution.py:49
  53.8 1.1 %shard_map.82 = bf16[256,1152]{1,0:T(8,128)(2,1)} custom-call(bf16[256,384]{1,0:T(8,128)(2,1)S(1)} %get-tuple-element.38.refs_0_, bf16[256,384]{1,0:T(8,128)(2,1)S(1)} %collective-permute-done.6.refs_1_, bf16[256,384]{1,0:T(8,128)(2,1)S(1)} %collective-permute-done.7.refs_2_, bf16[256,384]{1,0:T(8,128)(2,1)S(1)} %collective-permute-done.8.refs_3_, ...), custom_call_target="tpu_custom_call" | custom-call | bytes 2949120 | tf_op jit(solution)/shard_map/pallas_call | solution.py:65
  54.9 11.2 %all-to-all-start = ((bf16[32,8,1152]{2,1,0:T(8,128)(2,1)}), bf16[32,8,1152]{2,1,0:T(8,128)(2,1)S(1)}, u32[]{:S(2)}, u32[]{:S(2)}) async-start(bf16[32,8,1152]{2,1,0:T(8,128)(2,1)} %bitcast.12), calls=%async_computation | async-start | bytes 1179648 | tf_op jit(solution)/shard_map/all_to_all | solution.py:55
  66.1 4.1 %collective-permute-start.15 = (bf16[3,864,128]{2,1,0:T(8,128)(2,1)S(1)}, bf16[3,864,128]{2,1,0:T(8,128)(2,1)S(1)}, u32[]{:S(2)}, u32[]{:S(2)}) collective-permute-start(bf16[3,864,128]{2,1,0:T(8,128)(2,1)S(1)} %get-tuple-element.54), channel_id=1, source_target_pairs={{0,1},{1,0},{2,3},{3,2},{4,5},{5,4},{6,7},{7,6},{8,9},{9,8},{10,11... | collective-permute-start | bytes 1990664 | tf_op jit(solution)/shard_map/ppermute | solution.py:35
  70.2 1.7 %collective-permute-done.15.got_ref = bf16[3,864,128]{2,1,0:T(8,128)(2,1)S(1)} collective-permute-done((bf16[3,864,128]{2,1,0:T(8,128)(2,1)S(1)}, bf16[3,864,128]{2,1,0:T(8,128)(2,1)S(1)}, u32[]{:S(2)}, u32[]{:S(2)}) %collective-permute-start.15) | collective-permute-done | bytes 663584 | tf_op jit(solution)/shard_map/ppermute | solution.py:35
  71.9 0.8 copy-done.6
  72.8 8.4 %shard_map.83 = bf16[864,1024]{1,0:T(8,128)(2,1)} custom-call(s32[1]{0:T(128)} %bitcast.place_ref, bf16[3,864,128]{2,1,0:T(8,128)(2,1)} %copy-done.5, bf16[3,864,128]{2,1,0:T(8,128)(2,1)} %copy-done.6, bf16[2304,1024]{1,0:T(8,128)(2,1)} %bitcast.22), custom_call_target="tpu_custom_call" | custom-call | flops 4076863488 | bytes 7815172 | tf_op jit(solution)/shard_map/pallas_call | solution.py:65
  81.2 0.0 all-to-all-done
  81.2 0.1 convert_reduce_fusion.1
  81.3 5.2 %collective-permute-start.16 = (f32[4,1152]{1,0:T(4,128)S(1)}, f32[4,1152]{1,0:T(4,128)S(1)}, u32[]{:S(2)}, u32[]{:S(2)}) collective-permute-start(f32[4,1152]{1,0:T(4,128)S(1)} %constant_dynamic-slice_fusion), channel_id=1, source_target_pairs={{0,1},{1,0},{2,3},{3,2},{4,5},{5,4},{6,7},{7,6},{8,9},{9,8},{10,11... | collective-permute-start | bytes 55304 | tf_op jit(solution)/shard_map/ppermute | solution.py:35
  86.5 0.8 collective-permute-done.16
  87.4 0.6 pad_maximum_fusion
  (19 shorter events, 0.1 us)
Async XLA Ops:
  0.6 7.6 %copy-start.2 = (bf16[2,6,72,1024]{3,2,1,0:T(8,128)(2,1)S(1)}, bf16[2,6,72,1024]{3,2,1,0:T(8,128)(2,1)}, u32[]{:S(2)}) copy-start(bf16[2,6,72,1024]{3,2,1,0:T(8,128)(2,1)} %param.6) | copy-start | bytes 5308420
  0.6 13.1 %copy-start.4 = (f32[256]{0:T(256)S(1)}, f32[256]{0:T(256)}, u32[]{:S(2)}) copy-start(f32[256]{0:T(256)} %param.10) | copy-start | bytes 3076
  2.5 5.7 %collective-permute-start = (f32[8,256]{1,0:T(8,128)S(1)}, f32[8,256]{1,0:T(8,128)S(1)}, u32[]{:S(2)}, u32[]{:S(2)}) collective-permute-start(f32[8,256]{1,0:T(8,128)S(1)} %reshape.42), channel_id=1, source_target_pairs={{0,1},{1,0},{2,3},{3,2},{4,5},{5,4},{6,7},{7,6},{8,9},{9,8},{10,11... | collective-permute-start | bytes 24584 | tf_op jit(solution)/shard_map/ppermute | solution.py:35
  8.2 10.7 %collective-permute-start.5 = (bf16[864,1024]{1,0:T(8,128)(2,1)S(1)}, bf16[864,1024]{1,0:T(8,128)(2,1)S(1)}, u32[]{:S(2)}, u32[]{:S(2)}) collective-permute-start(bf16[864,1024]{1,0:T(8,128)(2,1)S(1)} %bitcast.18), channel_id=1, source_target_pairs={{0,1},{1,0},{2,3},{3,2},{4,5},{5,4},{6,7},{7,6},{8,9},{9,8},{10,11... | collective-permute-start | bytes 5308424 | tf_op jit(solution)/shard_map/ppermute | solution.py:35
  8.4 5.3 %collective-permute-start.4 = (bf16[2,864,128]{2,1,0:T(8,128)(2,1)}, bf16[2,864,128]{2,1,0:T(8,128)(2,1)S(1)}, u32[]{:S(2)}, u32[]{:S(2)}) collective-permute-start(bf16[2,864,128]{2,1,0:T(8,128)(2,1)} %get-tuple-element.33), channel_id=1, source_target_pairs={{0,1},{1,0},{2,3},{3,2},{4,5},{5,4},{6,7},{7,6},{8,9},{9,8},{10,11... | collective-permute-start | bytes 1327112 | tf_op jit(solution)/shard_map/ppermute | solution.py:35
  8.8 4.0 %collective-permute-start.1 = (f32[8,256]{1,0:T(8,128)S(1)}, f32[8,256]{1,0:T(8,128)S(1)}, u32[]{:S(2)}, u32[]{:S(2)}) collective-permute-start(f32[8,256]{1,0:T(8,128)S(1)} %add.21.a_ref), channel_id=1, source_target_pairs={{0,4},{2,6},{4,0},{6,2},{1,5},{3,7},{5,1},{7,3},{8,12},{10,14},{12... | collective-permute-start | bytes 24584 | tf_op jit(solution)/shard_map/ppermute | solution.py:39
  9.9 3.8 %collective-permute-start.2 = (f32[8,256]{1,0:T(8,128)S(1)}, f32[8,256]{1,0:T(8,128)S(1)}, u32[]{:S(2)}, u32[]{:S(2)}) collective-permute-start(f32[8,256]{1,0:T(8,128)S(1)} %add.21.a_ref), channel_id=1, source_target_pairs={{0,2},{2,4},{4,6},{6,0},{1,3},{3,5},{5,7},{7,1},{8,10},{10,12},{12... | collective-permute-start | bytes 24584 | tf_op jit(solution)/shard_map/ppermute | solution.py:39
  10.2 3.5 %collective-permute-start.3 = (f32[8,256]{1,0:T(8,128)S(1)}, f32[8,256]{1,0:T(8,128)S(1)}, u32[]{:S(2)}, u32[]{:S(2)}) collective-permute-start(f32[8,256]{1,0:T(8,128)S(1)} %add.21.a_ref), channel_id=1, source_target_pairs={{0,6},{2,0},{4,2},{6,4},{1,7},{3,1},{5,3},{7,5},{8,14},{10,8},{12,... | collective-permute-start | bytes 24584 | tf_op jit(solution)/shard_map/ppermute | solution.py:39
  13.7 1.0 %copy-start.3 = (bf16[2,864,128]{2,1,0:T(8,128)(2,1)S(1)}, bf16[2,864,128]{2,1,0:T(8,128)(2,1)}, u32[]{:S(2)}) copy-start(bf16[2,864,128]{2,1,0:T(8,128)(2,1)} %get-tuple-element.32.mine_ref) | copy-start | bytes 1327108
  15.1 18.7 %collective-permute-start.9 = (bf16[864,128]{1,0:T(8,128)(2,1)S(1)}, bf16[864,128]{1,0:T(8,128)(2,1)S(1)}, u32[]{:S(2)}, u32[]{:S(2)}) collective-permute-start(bf16[864,128]{1,0:T(8,128)(2,1)S(1)} %get-tuple-element.34.even_ref), channel_id=1, source_target_pairs={{0,2},{2,4},{4,6},{6,0},{1,3},{3,5},{5,7},{7,1},{8,10},{10,12},{12... | collective-permute-start | bytes 663560 | tf_op jit(solution)/shard_map/ppermute | solution.py:39
  15.5 18.4 %collective-permute-start.10 = (bf16[864,128]{1,0:T(8,128)(2,1)S(1)}, bf16[864,128]{1,0:T(8,128)(2,1)S(1)}, u32[]{:S(2)}, u32[]{:S(2)}) collective-permute-start(bf16[864,128]{1,0:T(8,128)(2,1)S(1)} %get-tuple-element.35.odd_ref), channel_id=1, source_target_pairs={{0,6},{2,0},{4,2},{6,4},{1,7},{3,1},{5,3},{7,5},{8,14},{10,8},{12,... | collective-permute-start | bytes 663560 | tf_op jit(solution)/shard_map/ppermute | solution.py:39
  17.8 16.0 %collective-permute-start.11 = (bf16[864,128]{1,0:T(8,128)(2,1)S(1)}, bf16[864,128]{1,0:T(8,128)(2,1)S(1)}, u32[]{:S(2)}, u32[]{:S(2)}) collective-permute-start(bf16[864,128]{1,0:T(8,128)(2,1)S(1)} %get-tuple-element.45), channel_id=1, source_target_pairs={{0,4},{2,6},{4,0},{6,2},{1,5},{3,7},{5,1},{7,3},{8,12},{10,14},{12... | collective-permute-start | bytes 663560 | tf_op jit(solution)/shard_map/ppermute | solution.py:39
  20.6 2.7 %copy-start = (bf16[1024,1792]{1,0:T(8,128)(2,1)}, bf16[1024,1792]{1,0:T(8,128)(2,1)S(1)}, u32[]{:S(2)}) copy-start(bf16[1024,1792]{1,0:T(8,128)(2,1)S(1)} %shard_map.79.lhs_ref) | copy-start | bytes 11010052
  23.3 8.7 %collective-permute-start.6 = (bf16[256,384]{1,0:T(8,128)(2,1)S(1)}, bf16[256,384]{1,0:T(8,128)(2,1)S(1)}, u32[]{:S(2)}, u32[]{:S(2)}) collective-permute-start(bf16[256,384]{1,0:T(8,128)(2,1)S(1)} %get-tuple-element.40), channel_id=1, source_target_pairs={{0,16},{1,5},{2,18},{3,7},{4,20},{5,1},{6,22},{7,3},{8,24},{9,13},... | collective-permute-start | bytes 589832 | tf_op jit(solution)/shard_map/ppermute | solution.py:49
  25.3 8.5 %collective-permute-start.7 = (bf16[256,384]{1,0:T(8,128)(2,1)S(1)}, bf16[256,384]{1,0:T(8,128)(2,1)S(1)}, u32[]{:S(2)}, u32[]{:S(2)}) collective-permute-start(bf16[256,384]{1,0:T(8,128)(2,1)S(1)} %get-tuple-element.41), channel_id=1, source_target_pairs={{0,8},{1,3},{2,10},{3,5},{4,12},{5,7},{6,14},{7,1},{8,16},{9,11},{... | collective-permute-start | bytes 589832 | tf_op jit(solution)/shard_map/ppermute | solution.py:49
  33.9 2.0 %copy-start.1 = (bf16[1024,1792]{1,0:T(8,128)(2,1)S(1)}, bf16[1024,1792]{1,0:T(8,128)(2,1)}, u32[]{:S(2)}) copy-start(bf16[1024,1792]{1,0:T(8,128)(2,1)} %copy-done) | copy-start | bytes 11010052
  40.3 14.6 %copy-start.5 = (bf16[3,864,128]{2,1,0:T(8,128)(2,1)}, bf16[3,864,128]{2,1,0:T(8,128)(2,1)S(1)}, u32[]{:S(2)}) copy-start(bf16[3,864,128]{2,1,0:T(8,128)(2,1)S(1)} %get-tuple-element.53.held_ref) | copy-start | bytes 1990660
  40.3 13.5 %collective-permute-start.12 = (bf16[256,768]{1,0:T(8,128)(2,1)S(1)}, bf16[256,768]{1,0:T(8,128)(2,1)S(1)}, u32[]{:S(2)}, u32[]{:S(2)}) collective-permute-start(bf16[256,768]{1,0:T(8,128)(2,1)S(1)} %get-tuple-element.48), channel_id=1, source_target_pairs={{0,16},{1,5},{2,18},{3,7},{4,20},{5,1},{6,22},{7,3},{8,24},{9,13},... | collective-permute-start | bytes 1179656 | tf_op jit(solution)/shard_map/ppermute | solution.py:49
  41.2 12.6 %collective-permute-start.13 = (bf16[256,768]{1,0:T(8,128)(2,1)S(1)}, bf16[256,768]{1,0:T(8,128)(2,1)S(1)}, u32[]{:S(2)}, u32[]{:S(2)}) collective-permute-start(bf16[256,768]{1,0:T(8,128)(2,1)S(1)} %get-tuple-element.49), channel_id=1, source_target_pairs={{0,8},{1,3},{2,10},{3,5},{4,12},{5,7},{6,14},{7,1},{8,16},{9,11},{... | collective-permute-start | bytes 1179656 | tf_op jit(solution)/shard_map/ppermute | solution.py:49
  42.0 11.8 %collective-permute-start.14 = (bf16[256,768]{1,0:T(8,128)(2,1)S(1)}, bf16[256,768]{1,0:T(8,128)(2,1)S(1)}, u32[]{:S(2)}, u32[]{:S(2)}) collective-permute-start(bf16[256,768]{1,0:T(8,128)(2,1)S(1)} %get-tuple-element.50), channel_id=1, source_target_pairs={{0,24},{1,7},{2,26},{3,1},{4,28},{5,3},{6,30},{7,5},{8,0},{9,15},{... | collective-permute-start | bytes 1179656 | tf_op jit(solution)/shard_map/ppermute | solution.py:49
  43.9 9.9 %collective-permute-start.8 = (bf16[256,384]{1,0:T(8,128)(2,1)S(1)}, bf16[256,384]{1,0:T(8,128)(2,1)S(1)}, u32[]{:S(2)}, u32[]{:S(2)}) collective-permute-start(bf16[256,384]{1,0:T(8,128)(2,1)S(1)} %get-tuple-element.44), channel_id=1, source_target_pairs={{0,24},{1,7},{2,26},{3,1},{4,28},{5,3},{6,30},{7,5},{8,0},{9,15},{... | collective-permute-start | bytes 589832 | tf_op jit(solution)/shard_map/ppermute | solution.py:49
  54.9 26.3 %all-to-all-start = ((bf16[32,8,1152]{2,1,0:T(8,128)(2,1)}), bf16[32,8,1152]{2,1,0:T(8,128)(2,1)S(1)}, u32[]{:S(2)}, u32[]{:S(2)}) async-start(bf16[32,8,1152]{2,1,0:T(8,128)(2,1)} %bitcast.12), calls=%async_computation | async-start | bytes 1179648 | tf_op jit(solution)/shard_map/all_to_all | solution.py:55
  66.1 5.9 %collective-permute-start.15 = (bf16[3,864,128]{2,1,0:T(8,128)(2,1)S(1)}, bf16[3,864,128]{2,1,0:T(8,128)(2,1)S(1)}, u32[]{:S(2)}, u32[]{:S(2)}) collective-permute-start(bf16[3,864,128]{2,1,0:T(8,128)(2,1)S(1)} %get-tuple-element.54), channel_id=1, source_target_pairs={{0,1},{1,0},{2,3},{3,2},{4,5},{5,4},{6,7},{7,6},{8,9},{9,8},{10,11... | collective-permute-start | bytes 1990664 | tf_op jit(solution)/shard_map/ppermute | solution.py:35
  71.9 0.8 copy-start.6
  81.3 6.1 %collective-permute-start.16 = (f32[4,1152]{1,0:T(4,128)S(1)}, f32[4,1152]{1,0:T(4,128)S(1)}, u32[]{:S(2)}, u32[]{:S(2)}) collective-permute-start(f32[4,1152]{1,0:T(4,128)S(1)} %constant_dynamic-slice_fusion), channel_id=1, source_target_pairs={{0,1},{1,0},{2,3},{3,2},{4,5},{5,4},{6,7},{7,6},{8,9},{9,8},{10,11... | collective-permute-start | bytes 55304 | tf_op jit(solution)/shard_map/ppermute | solution.py:35

commit v8 on v7

--- a/solution.py
+++ b/solution.py
@@ -339,7 +339,7 @@
         (channels_in // width,),
         [pltpu.VMEM((cells, deep), BF16)],
         2 * cells * deep * channels_in,
-        60,
+        24,
     )[0]
 
 
@@ -372,14 +372,16 @@
     down = around(odd, X - 1)
 
     middle = list(middle_terms(place, even, odd, lhs, col_count))
-    weight, middle[0] = lax.optimization_barrier((weight, middle[0]))
+    side_place, middle[0] = lax.optimization_barrier((place, middle[0]))
+    middle = [middle[0]] + [crossed(middle[steps], steps) for steps in (2, 1, 3)]
+    *sides, held, sent = side_terms(side_place, even, odd, up, down, far, lhs, col_count)
+    sides[1:], sent, middle[1:] = lax.optimization_barrier((sides[1:], sent, middle[1:]))
+    got = swapped(sent)
+    weight, sides[0] = lax.optimization_barrier((weight, sides[0]))
     weight = jnp.transpose(weight, (1, 2, 0)).reshape(9 * channels_out, channels_in)
-    middle = [middle[0]] + [crossed(middle[steps], steps) for steps in (2, 1, 3)]
-    lhs, weight, middle[1], middle[2] = lax.optimization_barrier((lhs, weight, middle[1], middle[2]))
-    *sides, held, sent = side_terms(place, even, odd, up, down, far, lhs, col_count)
     sides = [sides[0]] + [crossed(sides[steps], steps) for steps in (2, 1, 3)]
+    sides, weight = lax.optimization_barrier((sides, weight))
     merged = first_sum(middle, sides)
-    got = swapped(sent)
     place, merged = lax.optimization_barrier((place, merged))
     input_grad = input_gradient(place, held, got, weight, col_count)
     merged = exchanged(merged.reshape(Z * 4, 8, 9 * half))

time: 88.5 us -> 81.1 us (0.916)
  waiting for transfers between devices: 15.5 us -> 7.11 us
  local copies, waits for them, and re-layouts: 10.6 us -> 11.9 us
    ppermute x6, waiting for transfers between devices: 11.7 us -> 2.81 us  [crossed(): return lax.ppermute(value, AXES, pairs)]
    ppermute x6, starting transfers between devices: 5.66 us -> 7.43 us  [crossed(): return lax.ppermute(value, AXES, pairs)]
    unnamed x14 -> x12, local copies, waits for them, and re-layouts: 3.9 us -> 5.28 us
    ppermute x5, starting transfers between devices: 13.3 us -> 11.9 us  [swapped(): return lax.ppermute(value, 'core', [(0, 1), (1, 0)])]
  transfers between devices with their start and end apart: 18 -> 18, of which waited for: 6 -> 7; matrix products, arithmetic and copies ran while one was open for 8% -> 8% of each run, Pallas kernels for 18% -> 24%
where the time goes in v8:
time: 81.1 us; the launch traced here: 80.6 us
  starting transfers between devices  37.9 us (47%)
  Pallas kernels  20.3 us (25%)
  local copies, waits for them, and re-layouts  11.9 us (15%)
  waiting for transfers between devices  7.11 us (9%)
  other arithmetic  2.6 us (3%)
    pallas_call x7, Pallas kernels, kernel_call(): pl.pallas_call(body, grid=grid, in_specs=in_specs, out_specs=out_specs, o...  20.3 us
    ppermute x5, starting transfers between devices, swapped(): return lax.ppermute(value, 'core', [(0, 1), (1, 0)])  11.9 us
    all_to_all x1, starting transfers between devices, exchanged(): return lax.all_to_all(value, AXES, 0, 0, axis_index_groups=groups)  11 us
    ppermute x6, starting transfers between devices, around(): lax.ppermute(value, 'x', [(source, (source + steps) % X) for source in ra...  7.51 us
    ppermute x6, starting transfers between devices, crossed(): return lax.ppermute(value, AXES, pairs)  7.43 us
    transpose x1, local copies, waits for them, and re-layouts, per_device(): jnp.transpose(weight, (1, 2, 0)).reshape(9 * channels_out, channels_in)  6.63 us
    unnamed x12, local copies, waits for them, and re-layouts  5.28 us
    ppermute x6, waiting for transfers between devices, crossed(): return lax.ppermute(value, AXES, pairs)  2.81 us
  transfers between devices with their start and end apart: 18, of which 7 were waited for; matrix products, arithmetic and copies ran while one was open for 8% of the time, Pallas kernels for 24%

profile of v8, /device:TPU:1, one launch (start us, length us, event | category | flops | bytes accessed | tf_op | source)
XLA Modules:
  0.0 80.6 jit_solution(12806882664950584741)
XLA Ops:
  0.6 1.9 %fusion.2 = (f32[2,256]{1,0:T(2,128)S(1)}, f32[2,256]{1,0:T(2,128)S(1)}, f32[2,256]{1,0:T(2,128)S(1)}, f32[2,256]{1,0:T(2,128)S(1)}) fusion(s32[2,6,72,256]{3,2,1,0:T(8,128)} %param.9, bf16[2,6,72,256]{3,2,1,0:T(8,128)(2,1)} %param.8, bf16[2,6,72,256]{3,2,1,0:T(8,128)(2,1)} %param.7), kind=kLoop, calls=%fused_computation.7 | loop fusion | flops 2209792 | bytes 1777664 | tf_op jit(solution)/shard_map/reduce_sum | solution.py:81
  2.5 3.3 %collective-permute-start = (f32[8,256]{1,0:T(8,128)S(1)}, f32[8,256]{1,0:T(8,128)S(1)}, u32[]{:S(2)}, u32[]{:S(2)}) collective-permute-start(f32[8,256]{1,0:T(8,128)S(1)} %reshape.42), channel_id=1, source_target_pairs={{0,1},{1,0},{2,3},{3,2},{4,5},{5,4},{6,7},{7,6},{8,9},{9,8},{10,11... | collective-permute-start | bytes 24584 | tf_op jit(solution)/shard_map/ppermute | solution.py:35
  5.9 2.4 %shard_map.77 = (bf16[2,864,128]{2,1,0:T(8,128)(2,1)}, bf16[2,864,128]{2,1,0:T(8,128)(2,1)}) custom-call(s32[1]{0:T(128)} %bitcast.place_ref, bf16[864,256]{1,0:T(8,128)(2,1)} %bitcast.25, bf16[864,256]{1,0:T(8,128)(2,1)} %bitcast.24, s32[864,256]{1,0:T(8,128)} %bitcast.23), custom_call_target="tpu_custom_call" | custom-call | bytes 2654212 | tf_op jit(solution)/shard_map/pallas_call | solution.py:65
  8.2 0.0 collective-permute-done
  8.2 0.1 collective-permute-start.5
  8.4 0.5 collective-permute-start.4
  8.8 1.0 %collective-permute-start.1 = (f32[8,256]{1,0:T(8,128)S(1)}, f32[8,256]{1,0:T(8,128)S(1)}, u32[]{:S(2)}, u32[]{:S(2)}) collective-permute-start(f32[8,256]{1,0:T(8,128)S(1)} %add.21.a_ref), channel_id=1, source_target_pairs={{0,4},{2,6},{4,0},{6,2},{1,5},{3,7},{5,1},{7,3},{8,12},{10,14},{12... | collective-permute-start | bytes 24584 | tf_op jit(solution)/shard_map/ppermute | solution.py:39
  9.9 0.3 collective-permute-start.2
  10.2 2.4 %collective-permute-start.3 = (f32[8,256]{1,0:T(8,128)S(1)}, f32[8,256]{1,0:T(8,128)S(1)}, u32[]{:S(2)}, u32[]{:S(2)}) collective-permute-start(f32[8,256]{1,0:T(8,128)S(1)} %add.21.a_ref), channel_id=1, source_target_pairs={{0,6},{2,0},{4,2},{6,4},{1,7},{3,1},{5,3},{7,5},{8,14},{10,8},{12,... | collective-permute-start | bytes 24584 | tf_op jit(solution)/shard_map/ppermute | solution.py:39
  12.5 0.3 collective-permute-done.1.b_ref
  12.9 0.8 %collective-permute-done.2.c_ref = f32[8,256]{1,0:T(8,128)S(1)} collective-permute-done((f32[8,256]{1,0:T(8,128)S(1)}, f32[8,256]{1,0:T(8,128)S(1)}, u32[]{:S(2)}, u32[]{:S(2)}) %collective-permute-start.2) | collective-permute-done | bytes 8224 | tf_op jit(solution)/shard_map/ppermute | solution.py:39
  13.7 0.0 collective-permute-done.3.d_ref
  13.7 0.0 collective-permute-done.4.theirs_ref
  13.7 0.0 copy-start.2
  13.7 1.0 %copy-done.2 = bf16[2,864,128]{2,1,0:T(8,128)(2,1)S(1)} copy-done((bf16[2,864,128]{2,1,0:T(8,128)(2,1)S(1)}, bf16[2,864,128]{2,1,0:T(8,128)(2,1)}, u32[]{:S(2)}) %copy-start.2) | copy-done | bytes 442392
  14.7 0.3 shard_map.78
  15.1 0.4 collective-permute-start.6
  15.5 2.4 %collective-permute-start.7 = (bf16[864,128]{1,0:T(8,128)(2,1)S(1)}, bf16[864,128]{1,0:T(8,128)(2,1)S(1)}, u32[]{:S(2)}, u32[]{:S(2)}) collective-permute-start(bf16[864,128]{1,0:T(8,128)(2,1)S(1)} %get-tuple-element.45.odd_ref), channel_id=1, source_target_pairs={{0,6},{2,0},{4,2},{6,4},{1,7},{3,1},{5,3},{7,5},{8,14},{10,8},{12,... | collective-permute-start | bytes 663560 | tf_op jit(solution)/shard_map/ppermute | solution.py:39
  17.8 1.1 %collective-permute-start.8 = (bf16[864,128]{1,0:T(8,128)(2,1)S(1)}, bf16[864,128]{1,0:T(8,128)(2,1)S(1)}, u32[]{:S(2)}, u32[]{:S(2)}) collective-permute-start(bf16[864,128]{1,0:T(8,128)(2,1)S(1)} %get-tuple-element.50), channel_id=1, source_target_pairs={{0,4},{2,6},{4,0},{6,2},{1,5},{3,7},{5,1},{7,3},{8,12},{10,14},{12... | collective-permute-start | bytes 663560 | tf_op jit(solution)/shard_map/ppermute | solution.py:39
  18.9 0.0 collective-permute-done.5.other_ref
  18.9 1.7 %shard_map.79.lhs_ref = bf16[1024,1792]{1,0:T(8,128)(2,1)S(1)} custom-call(bf16[864,1024]{1,0:T(8,128)(2,1)S(1)} %bitcast.20, bf16[864,1024]{1,0:T(8,128)(2,1)S(1)} %collective-permute-done.5.other_ref), custom_call_target="tpu_custom_call" | custom-call | bytes 7208960 | tf_op jit(solution)/shard_map/pallas_call | solution.py:65
  20.6 2.7 %shard_map.80 = (bf16[256,384]{1,0:T(8,128)(2,1)S(1)}, bf16[256,384]{1,0:T(8,128)(2,1)S(1)}, bf16[256,384]{1,0:T(8,128)(2,1)S(1)}, bf16[256,384]{1,0:T(8,128)(2,1)S(1)}) custom-call(s32[1]{0:T(128)} %bitcast.place_ref, bf16[864,128]{1,0:T(8,128)(2,1)S(1)} %get-tuple-element.44.even_ref, bf16[864,128]{1,0:T(8,128)(2,1)S(1)} %get-tuple-element.45.odd_ref, ...), custom_call_target="tpu_custom_call" | custom-call | flops 1409286144 | bytes 4898820 | tf_op jit(solution)/shard_map/pallas_call | solution.py:65
  23.3 0.9 %collective-permute-start.10 = (bf16[256,384]{1,0:T(8,128)(2,1)S(1)}, bf16[256,384]{1,0:T(8,128)(2,1)S(1)}, u32[]{:S(2)}, u32[]{:S(2)}) collective-permute-start(bf16[256,384]{1,0:T(8,128)(2,1)S(1)} %get-tuple-element.56), channel_id=1, source_target_pairs={{0,8},{1,3},{2,10},{3,5},{4,12},{5,7},{6,14},{7,1},{8,16},{9,11},{... | collective-permute-start | bytes 589832 | tf_op jit(solution)/shard_map/ppermute | solution.py:49
  24.2 1.8 %collective-permute-start.11 = (bf16[256,384]{1,0:T(8,128)(2,1)S(1)}, bf16[256,384]{1,0:T(8,128)(2,1)S(1)}, u32[]{:S(2)}, u32[]{:S(2)}) collective-permute-start(bf16[256,384]{1,0:T(8,128)(2,1)S(1)} %get-tuple-element.57), channel_id=1, source_target_pairs={{0,24},{1,7},{2,26},{3,1},{4,28},{5,3},{6,30},{7,5},{8,0},{9,15},{... | collective-permute-start | bytes 589832 | tf_op jit(solution)/shard_map/ppermute | solution.py:49
  26.0 0.0 collective-permute-done.6.up_ref
  26.0 0.7 collective-permute-start.9
  26.8 0.5 collective-permute-done.8.far_ref
  27.3 5.1 %shard_map.81 = (bf16[256,768]{1,0:T(8,128)(2,1)S(1)}, bf16[256,768]{1,0:T(8,128)(2,1)}, bf16[256,768]{1,0:T(8,128)(2,1)}, bf16[256,768]{1,0:T(8,128)(2,1)S(1)},...) custom-call(s32[1]{0:T(128)} %bitcast.place_ref, bf16[864,128]{1,0:T(8,128)(2,1)S(1)} %get-tuple-element.44.even_ref, ...), custom_call_target="tpu_custom_call" | custom-call | flops 2818572288 | bytes 7675908 | tf_op jit(solution)/shard_map/pallas_call | solution.py:65
  32.4 0.8 %copy-done.4 = bf16[3,864,128]{2,1,0:T(8,128)(2,1)} copy-done((bf16[3,864,128]{2,1,0:T(8,128)(2,1)}, bf16[3,864,128]{2,1,0:T(8,128)(2,1)S(1)}, u32[]{:S(2)}) %copy-start.4) | copy-done | bytes 663576
  33.3 0.6 collective-permute-done.9.refs_1_
  33.8 1.3 %collective-permute-start.12 = (bf16[256,768]{1,0:T(8,128)(2,1)}, bf16[256,768]{1,0:T(8,128)(2,1)S(1)}, u32[]{:S(2)}, u32[]{:S(2)}) collective-permute-start(bf16[256,768]{1,0:T(8,128)(2,1)} %get-tuple-element.63), channel_id=1, source_target_pairs={{0,16},{1,5},{2,18},{3,7},{4,20},{5,1},{6,22},{7,3},{8,24},{9,13},... | collective-permute-start | bytes 1179656 | tf_op jit(solution)/shard_map/ppermute | solution.py:49
  35.1 0.9 %collective-permute-start.13 = (bf16[256,768]{1,0:T(8,128)(2,1)}, bf16[256,768]{1,0:T(8,128)(2,1)S(1)}, u32[]{:S(2)}, u32[]{:S(2)}) collective-permute-start(bf16[256,768]{1,0:T(8,128)(2,1)} %get-tuple-element.64), channel_id=1, source_target_pairs={{0,8},{1,3},{2,10},{3,5},{4,12},{5,7},{6,14},{7,1},{8,16},{9,11},{... | collective-permute-start | bytes 1179656 | tf_op jit(solution)/shard_map/ppermute | solution.py:49
  36.0 1.8 %collective-permute-start.14 = (bf16[256,768]{1,0:T(8,128)(2,1)S(1)}, bf16[256,768]{1,0:T(8,128)(2,1)S(1)}, u32[]{:S(2)}, u32[]{:S(2)}) collective-permute-start(bf16[256,768]{1,0:T(8,128)(2,1)S(1)} %get-tuple-element.65), channel_id=1, source_target_pairs={{0,24},{1,7},{2,26},{3,1},{4,28},{5,3},{6,30},{7,5},{8,0},{9,15},{... | collective-permute-start | bytes 1179656 | tf_op jit(solution)/shard_map/ppermute | solution.py:49
  37.8 6.6 %copy.8 = bf16[9,256,1024]{2,1,0:T(8,128)(2,1)} copy(bf16[9,256,1024]{1,2,0:T(8,128)(2,1)} %bitcast.22) | data formatting | bytes 9437184 | tf_op jit(solution)/shard_map/transpose | solution.py:381
  44.4 0.0 collective-permute-done.12.refs_5_
  44.4 2.2 %collective-permute-done.13.refs_6_ = bf16[256,768]{1,0:T(8,128)(2,1)S(1)} collective-permute-done((bf16[256,768]{1,0:T(8,128)(2,1)}, bf16[256,768]{1,0:T(8,128)(2,1)S(1)}, u32[]{:S(2)}, u32[]{:S(2)}) %collective-permute-start.13) | collective-permute-done | bytes 393248 | tf_op jit(solution)/shard_map/ppermute | solution.py:49
  46.7 0.0 collective-permute-done.14.refs_7_
  46.7 1.0 %shard_map.82 = bf16[256,1152]{1,0:T(8,128)(2,1)} custom-call(bf16[256,384]{1,0:T(8,128)(2,1)S(1)} %get-tuple-element.48.refs_0_, bf16[256,384]{1,0:T(8,128)(2,1)S(1)} %collective-permute-done.9.refs_1_, bf16[256,384]{1,0:T(8,128)(2,1)S(1)} %collective-permute-done.10.refs_2_, bf16[256,384]{1,0:T(8,128)(2,1)S(1)} %collective-permute-done.11.refs_3_, ...), custom_call_target="tpu_custom_call" | custom-call | bytes 2949120 | tf_op jit(solution)/shard_map/pallas_call | solution.py:65
  47.7 11.0 %all-to-all-start = ((bf16[32,8,1152]{2,1,0:T(8,128)(2,1)}), bf16[32,8,1152]{2,1,0:T(8,128)(2,1)S(1)}, u32[]{:S(2)}, u32[]{:S(2)}) async-start(bf16[32,8,1152]{2,1,0:T(8,128)(2,1)} %bitcast.12), calls=%async_computation | async-start | bytes 1179648 | tf_op jit(solution)/shard_map/all_to_all | solution.py:55
  58.7 5.9 %collective-permute-start.15 = (bf16[3,864,128]{2,1,0:T(8,128)(2,1)S(1)}, bf16[3,864,128]{2,1,0:T(8,128)(2,1)S(1)}, u32[]{:S(2)}, u32[]{:S(2)}) collective-permute-start(bf16[3,864,128]{2,1,0:T(8,128)(2,1)S(1)} %get-tuple-element.74), channel_id=1, source_target_pairs={{0,1},{1,0},{2,3},{3,2},{4,5},{5,4},{6,7},{7,6},{8,9},{9,8},{10,11... | collective-permute-start | bytes 1990664 | tf_op jit(solution)/shard_map/ppermute | solution.py:35
  64.6 1.7 %collective-permute-done.15.got_ref = bf16[3,864,128]{2,1,0:T(8,128)(2,1)S(1)} collective-permute-done((bf16[3,864,128]{2,1,0:T(8,128)(2,1)S(1)}, bf16[3,864,128]{2,1,0:T(8,128)(2,1)S(1)}, u32[]{:S(2)}, u32[]{:S(2)}) %collective-permute-start.15) | collective-permute-done | bytes 663584 | tf_op jit(solution)/shard_map/ppermute | solution.py:35
  66.3 2.3 %copy-done = bf16[9,256,1024]{2,1,0:T(8,128)(2,1)S(1)} copy-done((bf16[9,256,1024]{2,1,0:T(8,128)(2,1)S(1)}, bf16[9,256,1024]{2,1,0:T(8,128)(2,1)}, u32[]{:S(2)}) %copy-start) | copy-done | bytes 4718616
  68.7 1.1 %copy-done.5 = bf16[3,864,128]{2,1,0:T(8,128)(2,1)S(1)} copy-done((bf16[3,864,128]{2,1,0:T(8,128)(2,1)S(1)}, bf16[3,864,128]{2,1,0:T(8,128)(2,1)}, u32[]{:S(2)}) %copy-start.5) | copy-done | bytes 663576
  69.8 7.1 %shard_map.83 = bf16[864,1024]{1,0:T(8,128)(2,1)} custom-call(s32[1]{0:T(128)} %bitcast.place_ref, bf16[3,864,128]{2,1,0:T(8,128)(2,1)S(1)} %copy-done.5, bf16[3,864,128]{2,1,0:T(8,128)(2,1)S(1)} %collective-permute-done.15.got_ref, bf16[2304,1024]{1,0:T(8,128)(2,1)S(1)} %bitcast.18), custom_call_target="tpu_custom_call" | custom-call | flops 4076863488 | bytes 7815172 | tf_op jit(solution)/shard_map/pallas_call | solution.py:65
  76.9 0.1 convert_reduce_fusion.1
  77.0 2.1 %collective-permute-start.16 = (f32[4,1152]{1,0:T(4,128)S(1)}, f32[4,1152]{1,0:T(4,128)S(1)}, u32[]{:S(2)}, u32[]{:S(2)}) collective-permute-start(f32[4,1152]{1,0:T(4,128)S(1)} %constant_dynamic-slice_fusion), channel_id=1, source_target_pairs={{0,1},{1,0},{2,3},{3,2},{4,5},{5,4},{6,7},{7,6},{8,9},{9,8},{10,11... | collective-permute-start | bytes 55304 | tf_op jit(solution)/shard_map/ppermute | solution.py:35
  79.1 0.8 %collective-permute-done.16 = f32[4,1152]{1,0:T(4,128)S(1)} collective-permute-done((f32[4,1152]{1,0:T(4,128)S(1)}, f32[4,1152]{1,0:T(4,128)S(1)}, u32[]{:S(2)}, u32[]{:S(2)}) %collective-permute-start.16) | collective-permute-done | bytes 18464 | tf_op jit(solution)/shard_map/ppermute | solution.py:35
  80.0 0.6 pad_maximum_fusion
  (17 shorter events, 0.1 us)
Async XLA Ops:
  0.6 7.6 %copy-start.1 = (bf16[2,6,72,1024]{3,2,1,0:T(8,128)(2,1)S(1)}, bf16[2,6,72,1024]{3,2,1,0:T(8,128)(2,1)}, u32[]{:S(2)}) copy-start(bf16[2,6,72,1024]{3,2,1,0:T(8,128)(2,1)} %param.6) | copy-start | bytes 5308420
  0.6 13.1 %copy-start.3 = (f32[256]{0:T(256)S(1)}, f32[256]{0:T(256)}, u32[]{:S(2)}) copy-start(f32[256]{0:T(256)} %param.10) | copy-start | bytes 3076
  2.5 5.7 %collective-permute-start = (f32[8,256]{1,0:T(8,128)S(1)}, f32[8,256]{1,0:T(8,128)S(1)}, u32[]{:S(2)}, u32[]{:S(2)}) collective-permute-start(f32[8,256]{1,0:T(8,128)S(1)} %reshape.42), channel_id=1, source_target_pairs={{0,1},{1,0},{2,3},{3,2},{4,5},{5,4},{6,7},{7,6},{8,9},{9,8},{10,11... | collective-permute-start | bytes 24584 | tf_op jit(solution)/shard_map/ppermute | solution.py:35
  8.2 10.7 %collective-permute-start.5 = (bf16[864,1024]{1,0:T(8,128)(2,1)S(1)}, bf16[864,1024]{1,0:T(8,128)(2,1)S(1)}, u32[]{:S(2)}, u32[]{:S(2)}) collective-permute-start(bf16[864,1024]{1,0:T(8,128)(2,1)S(1)} %bitcast.19), channel_id=1, source_target_pairs={{0,1},{1,0},{2,3},{3,2},{4,5},{5,4},{6,7},{7,6},{8,9},{9,8},{10,11... | collective-permute-start | bytes 5308424 | tf_op jit(solution)/shard_map/ppermute | solution.py:35
  8.4 5.3 %collective-permute-start.4 = (bf16[2,864,128]{2,1,0:T(8,128)(2,1)}, bf16[2,864,128]{2,1,0:T(8,128)(2,1)S(1)}, u32[]{:S(2)}, u32[]{:S(2)}) collective-permute-start(bf16[2,864,128]{2,1,0:T(8,128)(2,1)} %get-tuple-element.43), channel_id=1, source_target_pairs={{0,1},{1,0},{2,3},{3,2},{4,5},{5,4},{6,7},{7,6},{8,9},{9,8},{10,11... | collective-permute-start | bytes 1327112 | tf_op jit(solution)/shard_map/ppermute | solution.py:35
  8.8 4.0 %collective-permute-start.1 = (f32[8,256]{1,0:T(8,128)S(1)}, f32[8,256]{1,0:T(8,128)S(1)}, u32[]{:S(2)}, u32[]{:S(2)}) collective-permute-start(f32[8,256]{1,0:T(8,128)S(1)} %add.21.a_ref), channel_id=1, source_target_pairs={{0,4},{2,6},{4,0},{6,2},{1,5},{3,7},{5,1},{7,3},{8,12},{10,14},{12... | collective-permute-start | bytes 24584 | tf_op jit(solution)/shard_map/ppermute | solution.py:39
  9.9 3.8 %collective-permute-start.2 = (f32[8,256]{1,0:T(8,128)S(1)}, f32[8,256]{1,0:T(8,128)S(1)}, u32[]{:S(2)}, u32[]{:S(2)}) collective-permute-start(f32[8,256]{1,0:T(8,128)S(1)} %add.21.a_ref), channel_id=1, source_target_pairs={{0,2},{2,4},{4,6},{6,0},{1,3},{3,5},{5,7},{7,1},{8,10},{10,12},{12... | collective-permute-start | bytes 24584 | tf_op jit(solution)/shard_map/ppermute | solution.py:39
  10.2 3.5 %collective-permute-start.3 = (f32[8,256]{1,0:T(8,128)S(1)}, f32[8,256]{1,0:T(8,128)S(1)}, u32[]{:S(2)}, u32[]{:S(2)}) collective-permute-start(f32[8,256]{1,0:T(8,128)S(1)} %add.21.a_ref), channel_id=1, source_target_pairs={{0,6},{2,0},{4,2},{6,4},{1,7},{3,1},{5,3},{7,5},{8,14},{10,8},{12,... | collective-permute-start | bytes 24584 | tf_op jit(solution)/shard_map/ppermute | solution.py:39
  13.7 1.0 %copy-start.2 = (bf16[2,864,128]{2,1,0:T(8,128)(2,1)S(1)}, bf16[2,864,128]{2,1,0:T(8,128)(2,1)}, u32[]{:S(2)}) copy-start(bf16[2,864,128]{2,1,0:T(8,128)(2,1)} %get-tuple-element.42.mine_ref) | copy-start | bytes 1327108
  15.1 11.0 %collective-permute-start.6 = (bf16[864,128]{1,0:T(8,128)(2,1)S(1)}, bf16[864,128]{1,0:T(8,128)(2,1)S(1)}, u32[]{:S(2)}, u32[]{:S(2)}) collective-permute-start(bf16[864,128]{1,0:T(8,128)(2,1)S(1)} %get-tuple-element.44.even_ref), channel_id=1, source_target_pairs={{0,2},{2,4},{4,6},{6,0},{1,3},{3,5},{5,7},{7,1},{8,10},{10,12},{12... | collective-permute-start | bytes 663560 | tf_op jit(solution)/shard_map/ppermute | solution.py:39
  15.5 11.3 %collective-permute-start.7 = (bf16[864,128]{1,0:T(8,128)(2,1)S(1)}, bf16[864,128]{1,0:T(8,128)(2,1)S(1)}, u32[]{:S(2)}, u32[]{:S(2)}) collective-permute-start(bf16[864,128]{1,0:T(8,128)(2,1)S(1)} %get-tuple-element.45.odd_ref), channel_id=1, source_target_pairs={{0,6},{2,0},{4,2},{6,4},{1,7},{3,1},{5,3},{7,5},{8,14},{10,8},{12,... | collective-permute-start | bytes 663560 | tf_op jit(solution)/shard_map/ppermute | solution.py:39
  17.8 9.5 %collective-permute-start.8 = (bf16[864,128]{1,0:T(8,128)(2,1)S(1)}, bf16[864,128]{1,0:T(8,128)(2,1)S(1)}, u32[]{:S(2)}, u32[]{:S(2)}) collective-permute-start(bf16[864,128]{1,0:T(8,128)(2,1)S(1)} %get-tuple-element.50), channel_id=1, source_target_pairs={{0,4},{2,6},{4,0},{6,2},{1,5},{3,7},{5,1},{7,3},{8,12},{10,14},{12... | collective-permute-start | bytes 663560 | tf_op jit(solution)/shard_map/ppermute | solution.py:39
  23.3 10.0 %collective-permute-start.10 = (bf16[256,384]{1,0:T(8,128)(2,1)S(1)}, bf16[256,384]{1,0:T(8,128)(2,1)S(1)}, u32[]{:S(2)}, u32[]{:S(2)}) collective-permute-start(bf16[256,384]{1,0:T(8,128)(2,1)S(1)} %get-tuple-element.56), channel_id=1, source_target_pairs={{0,8},{1,3},{2,10},{3,5},{4,12},{5,7},{6,14},{7,1},{8,16},{9,11},{... | collective-permute-start | bytes 589832 | tf_op jit(solution)/shard_map/ppermute | solution.py:49
  24.2 9.0 %collective-permute-start.11 = (bf16[256,384]{1,0:T(8,128)(2,1)S(1)}, bf16[256,384]{1,0:T(8,128)(2,1)S(1)}, u32[]{:S(2)}, u32[]{:S(2)}) collective-permute-start(bf16[256,384]{1,0:T(8,128)(2,1)S(1)} %get-tuple-element.57), channel_id=1, source_target_pairs={{0,24},{1,7},{2,26},{3,1},{4,28},{5,3},{6,30},{7,5},{8,0},{9,15},{... | collective-permute-start | bytes 589832 | tf_op jit(solution)/shard_map/ppermute | solution.py:49
  26.0 7.8 %collective-permute-start.9 = (bf16[256,384]{1,0:T(8,128)(2,1)S(1)}, bf16[256,384]{1,0:T(8,128)(2,1)S(1)}, u32[]{:S(2)}, u32[]{:S(2)}) collective-permute-start(bf16[256,384]{1,0:T(8,128)(2,1)S(1)} %get-tuple-element.55), channel_id=1, source_target_pairs={{0,16},{1,5},{2,18},{3,7},{4,20},{5,1},{6,22},{7,3},{8,24},{9,13},... | collective-permute-start | bytes 589832 | tf_op jit(solution)/shard_map/ppermute | solution.py:49
  32.4 0.8 %copy-start.4 = (bf16[3,864,128]{2,1,0:T(8,128)(2,1)}, bf16[3,864,128]{2,1,0:T(8,128)(2,1)S(1)}, u32[]{:S(2)}) copy-start(bf16[3,864,128]{2,1,0:T(8,128)(2,1)S(1)} %get-tuple-element.73.held_ref) | copy-start | bytes 1990660
  33.8 10.6 %collective-permute-start.12 = (bf16[256,768]{1,0:T(8,128)(2,1)}, bf16[256,768]{1,0:T(8,128)(2,1)S(1)}, u32[]{:S(2)}, u32[]{:S(2)}) collective-permute-start(bf16[256,768]{1,0:T(8,128)(2,1)} %get-tuple-element.63), channel_id=1, source_target_pairs={{0,16},{1,5},{2,18},{3,7},{4,20},{5,1},{6,22},{7,3},{8,24},{9,13},... | collective-permute-start | bytes 1179656 | tf_op jit(solution)/shard_map/ppermute | solution.py:49
  35.1 11.6 %collective-permute-start.13 = (bf16[256,768]{1,0:T(8,128)(2,1)}, bf16[256,768]{1,0:T(8,128)(2,1)S(1)}, u32[]{:S(2)}, u32[]{:S(2)}) collective-permute-start(bf16[256,768]{1,0:T(8,128)(2,1)} %get-tuple-element.64), channel_id=1, source_target_pairs={{0,8},{1,3},{2,10},{3,5},{4,12},{5,7},{6,14},{7,1},{8,16},{9,11},{... | collective-permute-start | bytes 1179656 | tf_op jit(solution)/shard_map/ppermute | solution.py:49
  36.0 10.6 %collective-permute-start.14 = (bf16[256,768]{1,0:T(8,128)(2,1)S(1)}, bf16[256,768]{1,0:T(8,128)(2,1)S(1)}, u32[]{:S(2)}, u32[]{:S(2)}) collective-permute-start(bf16[256,768]{1,0:T(8,128)(2,1)S(1)} %get-tuple-element.65), channel_id=1, source_target_pairs={{0,24},{1,7},{2,26},{3,1},{4,28},{5,3},{6,30},{7,5},{8,0},{9,15},{... | collective-permute-start | bytes 1179656 | tf_op jit(solution)/shard_map/ppermute | solution.py:49
  47.7 29.2 %all-to-all-start = ((bf16[32,8,1152]{2,1,0:T(8,128)(2,1)}), bf16[32,8,1152]{2,1,0:T(8,128)(2,1)S(1)}, u32[]{:S(2)}, u32[]{:S(2)}) async-start(bf16[32,8,1152]{2,1,0:T(8,128)(2,1)} %bitcast.12), calls=%async_computation | async-start | bytes 1179648 | tf_op jit(solution)/shard_map/all_to_all | solution.py:55
  58.7 7.6 %collective-permute-start.15 = (bf16[3,864,128]{2,1,0:T(8,128)(2,1)S(1)}, bf16[3,864,128]{2,1,0:T(8,128)(2,1)S(1)}, u32[]{:S(2)}, u32[]{:S(2)}) collective-permute-start(bf16[3,864,128]{2,1,0:T(8,128)(2,1)S(1)} %get-tuple-element.74), channel_id=1, source_target_pairs={{0,1},{1,0},{2,3},{3,2},{4,5},{5,4},{6,7},{7,6},{8,9},{9,8},{10,11... | collective-permute-start | bytes 1990664 | tf_op jit(solution)/shard_map/ppermute | solution.py:35
  66.3 2.3 %copy-start = (bf16[9,256,1024]{2,1,0:T(8,128)(2,1)S(1)}, bf16[9,256,1024]{2,1,0:T(8,128)(2,1)}, u32[]{:S(2)}) copy-start(bf16[9,256,1024]{2,1,0:T(8,128)(2,1)} %copy.8) | copy-start | bytes 14155780
  68.7 1.1 %copy-start.5 = (bf16[3,864,128]{2,1,0:T(8,128)(2,1)S(1)}, bf16[3,864,128]{2,1,0:T(8,128)(2,1)}, u32[]{:S(2)}) copy-start(bf16[3,864,128]{2,1,0:T(8,128)(2,1)} %copy-done.4) | copy-start | bytes 1990660
  77.0 3.0 %collective-permute-start.16 = (f32[4,1152]{1,0:T(4,128)S(1)}, f32[4,1152]{1,0:T(4,128)S(1)}, u32[]{:S(2)}, u32[]{:S(2)}) collective-permute-start(f32[4,1152]{1,0:T(4,128)S(1)} %constant_dynamic-slice_fusion), channel_id=1, source_target_pairs={{0,1},{1,0},{2,3},{3,2},{4,5},{5,4},{6,7},{7,6},{8,9},{9,8},{10,11... | collective-permute-start | bytes 55304 | tf_op jit(solution)/shard_map/ppermute | solution.py:35

commit v9 on v8

--- a/solution.py
+++ b/solution.py
@@ -253,37 +253,60 @@
     return product_call(body, place, [even, odd], lhs, 3 * width, [])
 
 
+def tap_blocks(place_ref, even_ref, odd_ref, up_ref, down_ref, far_ref):
+    x = x_of(place_ref)
+    far_block = far_ref[...]
+    zero = jnp.zeros_like(far_block)
+    far_down = jnp.where(x < X // 2, far_block, zero)
+    far_up = jnp.where(x < X // 2, zero, far_block)
+    down_block = jnp.where(x < X - 1, down_ref[...], zero)
+    up_block = jnp.where(x > 0, up_ref[...], zero)
+    return (down_block, far_down), (even_ref[...], odd_ref[...]), (far_up, up_block)
+
+
+def own_blocks(place, even, odd, up, down, far):
+    operands = (even, odd, up, down, far)
+
+    def body(place_ref, *refs):
+        first = core_of(place_ref) == 0
+        for side, (lower, upper) in enumerate(tap_blocks(place_ref, *refs[:5])):
+            refs[5][side] = jnp.where(first, lower, upper)
+
+    out = jax.ShapeDtypeStruct((3,) + even.shape, BF16)
+    return kernel_call(
+        body,
+        (place, *operands),
+        [SMEM] + [whole(value.shape) for value in operands],
+        [out],
+        [whole(out.shape)],
+    )[0]
+
+
 def side_terms(place, even, odd, up, down, far, lhs, col_count):
     cells, width = up.shape
 
     def body(place_ref, even_ref, odd_ref, up_ref, down_ref, far_ref, lhs_ref, *rest):
-        mine_ref, theirs_ref, stacked, total = rest[4:]
+        theirs_refs = rest[4:6]
+        stacked, total = rest[6:]
 
         @pl.when(pl.program_id(0) == 0)
         def _():
             clear_padding(stacked, cells)
             first = core_of(place_ref) == 0
-            early = x_of(place_ref) < X // 2
-            far_block = far_ref[...]
-            zero = jnp.zeros_like(far_block)
-            far_down = jnp.where(early, far_block, zero)
-            far_up = jnp.where(early, zero, far_block)
-            down_block = jnp.where(x_of(place_ref) < X - 1, down_ref[...], zero)
-            up_block = jnp.where(x_of(place_ref) > 0, up_ref[...], zero)
-            pairs = ((down_block, far_down), (even_ref[...], odd_ref[...]), (far_up, up_block))
-            for side, (lower, upper) in enumerate(pairs):
-                mine = jnp.where(first, lower, upper)
+            blocks = tap_blocks(place_ref, even_ref, odd_ref, up_ref, down_ref, far_ref)
+            for side, (lower, upper) in enumerate(blocks):
                 theirs = jnp.where(first, upper, lower)
-                mine_ref[side] = mine
-                theirs_ref[side] = theirs
+                for part, ref in enumerate(theirs_refs):
+                    ref[side] = theirs[part * (cells // 2) : (part + 1) * (cells // 2)]
                 if side != 1:
+                    mine = jnp.where(first, lower, upper)
                     fill(stacked, 0, 3 * (side // 2), mine, col_count)
                     fill(stacked, 1, 3 * (side // 2), theirs, col_count)
 
         multiply(place_ref, lhs_ref, stacked, total, rest[:4])
 
-    triple = jax.ShapeDtypeStruct((3, cells, width), BF16)
-    return product_call(body, place, [even, odd, up, down, far], lhs, 6 * width, [triple, triple])
+    part = jax.ShapeDtypeStruct((3, cells // 2, width), BF16)
+    return product_call(body, place, [even, odd, up, down, far], lhs, 6 * width, [part, part])
 
 
 def first_sum(middle, sides):
@@ -314,12 +337,15 @@
     deep, channels_in = weight.shape
     width = 256
 
-    def body(place_ref, held_ref, got_ref, weight_ref, out_ref, stacked):
+    def body(place_ref, held_ref, *rest):
+        got_refs, (weight_ref, out_ref, stacked) = rest[:2], rest[2:]
+
         @pl.when(pl.program_id(0) == 0)
         def _():
             first = core_of(place_ref) == 0
             for side in range(3):
-                mine, theirs = held_ref[side], got_ref[side]
+                mine = held_ref[side]
+                theirs = jnp.concatenate([ref[side] for ref in got_refs], axis=0)
                 lower, upper = jnp.where(first, mine, theirs), jnp.where(first, theirs, mine)
                 for part, block in enumerate((lower, upper)):
                     for spot, tap in enumerate(column_taps(block, col_count)):
@@ -332,14 +358,14 @@
 
     return kernel_call(
         body,
-        (place, held, got, weight),
-        [SMEM, whole(held.shape), whole(got.shape), pl.BlockSpec((deep, width), lambda i: (0, i))],
+        (place, held, *got, weight),
+        [SMEM, whole(held.shape)] + [whole(block.shape) for block in got] + [pl.BlockSpec((deep, width), lambda i: (0, i))],
         [jax.ShapeDtypeStruct((cells, channels_in), BF16)],
         [pl.BlockSpec((cells, width), lambda i: (0, i))],
         (channels_in // width,),
         [pltpu.VMEM((cells, deep), BF16)],
         2 * cells * deep * channels_in,
-        24,
+        60,
     )[0]
 
 
@@ -374,13 +400,16 @@
     middle = list(middle_terms(place, even, odd, lhs, col_count))
     side_place, middle[0] = lax.optimization_barrier((place, middle[0]))
     middle = [middle[0]] + [crossed(middle[steps], steps) for steps in (2, 1, 3)]
-    *sides, held, sent = side_terms(side_place, even, odd, up, down, far, lhs, col_count)
+    *sides, sent_lower, sent_upper = side_terms(side_place, even, odd, up, down, far, lhs, col_count)
+    sent = [sent_lower, sent_upper]
     sides[1:], sent, middle[1:] = lax.optimization_barrier((sides[1:], sent, middle[1:]))
-    got = swapped(sent)
+    got = [swapped(block) for block in sent]
     weight, sides[0] = lax.optimization_barrier((weight, sides[0]))
     weight = jnp.transpose(weight, (1, 2, 0)).reshape(9 * channels_out, channels_in)
     sides = [sides[0]] + [crossed(sides[steps], steps) for steps in (2, 1, 3)]
-    sides, weight = lax.optimization_barrier((sides, weight))
+    held_place, weight = lax.optimization_barrier((place, weight))
+    held = own_blocks(held_place, even, odd, up, down, far)
+    sides, weight, got, held = lax.optimization_barrier((sides, weight, got, held))
     merged = first_sum(middle, sides)
     place, merged = lax.optimization_barrier((place, merged))
     input_grad = input_gradient(place, held, got, weight, col_count)

time: 81.1 us -> 84.1 us (1.037)
  local copies, waits for them, and re-layouts: 11.9 us -> 8.55 us
  starting transfers between devices: 37.9 us -> 40.2 us
  waiting for transfers between devices: 7.11 us -> 9.25 us
  Pallas kernels: 20.3 us -> 22.2 us
    all_to_all x1, waiting for transfers between devices: 0.01 us -> 6.64 us  [exchanged(): return lax.all_to_all(value, AXES, 0, 0, axis_index_groups=groups)]
    ppermute x5 -> x6, starting transfers between devices: 11.9 us -> 15.3 us  [swapped(): return lax.ppermute(value, 'core', [(0, 1), (1, 0)])]
    unnamed x12 -> x8, local copies, waits for them, and re-layouts: 5.28 us -> 1.9 us
    all_to_all x1, starting transfers between devices: 11 us -> 8.58 us  [exchanged(): return lax.all_to_all(value, AXES, 0, 0, axis_index_groups=groups)]
    ppermute x6, waiting for transfers between devices: 2.81 us -> 0.59 us  [crossed(): return lax.ppermute(value, AXES, pairs)]
    pallas_call x7 -> x8, Pallas kernels: 20.3 us -> 22.2 us  [kernel_call(): pl.pallas_call(body, grid=grid, in_specs=in_specs, out_specs=out_specs, o...]
    ppermute x5 -> x6, waiting for transfers between devices: 2.59 us -> 0.85 us  [swapped(): return lax.ppermute(value, 'core', [(0, 1), (1, 0)])]
    ppermute x6, starting transfers between devices: 7.43 us -> 8.82 us  [crossed(): return lax.ppermute(value, AXES, pairs)]
  transfers between devices with their start and end apart: 18 -> 19, of which waited for: 7 -> 5; matrix products, arithmetic and copies ran while one was open for 8% -> 8% of each run, Pallas kernels for 24% -> 25%
where the time goes in v9:
time: 84.1 us; the launch traced here: 83.6 us
  starting transfers between devices  40.2 us (48%)
  Pallas kernels  22.2 us (26%)
  waiting for transfers between devices  9.25 us (11%)
  local copies, waits for them, and re-layouts  8.55 us (10%)
  other arithmetic  2.6 us (3%)
    pallas_call x8, Pallas kernels, kernel_call(): pl.pallas_call(body, grid=grid, in_specs=in_specs, out_specs=out_specs, o...  22.2 us
    ppermute x6, starting transfers between devices, swapped(): return lax.ppermute(value, 'core', [(0, 1), (1, 0)])  15.3 us
    ppermute x6, starting transfers between devices, crossed(): return lax.ppermute(value, AXES, pairs)  8.82 us
    all_to_all x1, starting transfers between devices, exchanged(): return lax.all_to_all(value, AXES, 0, 0, axis_index_groups=groups)  8.58 us
    ppermute x6, starting transfers between devices, around(): lax.ppermute(value, 'x', [(source, (source + steps) % X) for source in ra...  7.51 us
    all_to_all x1, waiting for transfers between devices, exchanged(): return lax.all_to_all(value, AXES, 0, 0, axis_index_groups=groups)  6.64 us
    transpose x1, local copies, waits for them, and re-layouts, per_device(): jnp.transpose(weight, (1, 2, 0)).reshape(9 * channels_out, channels_in)  6.63 us
    unnamed x8, local copies, waits for them, and re-layouts  1.9 us
  transfers between devices with their start and end apart: 19, of which 5 were waited for; matrix products, arithmetic and copies ran while one was open for 8% of the time, Pallas kernels for 25%

profile of v9, /device:TPU:1, one launch (start us, length us, event | category | flops | bytes accessed | tf_op | source)
XLA Modules:
  0.0 83.6 jit_solution(14897994379275192903)
XLA Ops:
  0.6 1.9 %fusion.2 = (f32[2,256]{1,0:T(2,128)S(1)}, f32[2,256]{1,0:T(2,128)S(1)}, f32[2,256]{1,0:T(2,128)S(1)}, f32[2,256]{1,0:T(2,128)S(1)}) fusion(s32[2,6,72,256]{3,2,1,0:T(8,128)} %param.9, bf16[2,6,72,256]{3,2,1,0:T(8,128)(2,1)} %param.8, bf16[2,6,72,256]{3,2,1,0:T(8,128)(2,1)} %param.7), kind=kLoop, calls=%fused_computation.7 | loop fusion | flops 2209792 | bytes 1777664 | tf_op jit(solution)/shard_map/reduce_sum | solution.py:81
  2.5 3.3 %collective-permute-start = (f32[8,256]{1,0:T(8,128)S(1)}, f32[8,256]{1,0:T(8,128)S(1)}, u32[]{:S(2)}, u32[]{:S(2)}) collective-permute-start(f32[8,256]{1,0:T(8,128)S(1)} %reshape.42), channel_id=1, source_target_pairs={{0,1},{1,0},{2,3},{3,2},{4,5},{5,4},{6,7},{7,6},{8,9},{9,8},{10,11... | collective-permute-start | bytes 24584 | tf_op jit(solution)/shard_map/ppermute | solution.py:35
  5.9 2.4 %shard_map.77 = (bf16[2,864,128]{2,1,0:T(8,128)(2,1)}, bf16[2,864,128]{2,1,0:T(8,128)(2,1)}) custom-call(s32[1]{0:T(128)} %bitcast.place_ref, bf16[864,256]{1,0:T(8,128)(2,1)} %bitcast.25, bf16[864,256]{1,0:T(8,128)(2,1)} %bitcast.24, s32[864,256]{1,0:T(8,128)} %bitcast.23), custom_call_target="tpu_custom_call" | custom-call | bytes 2654212 | tf_op jit(solution)/shard_map/pallas_call | solution.py:65
  8.2 0.0 collective-permute-done
  8.2 0.1 collective-permute-start.5
  8.4 0.5 collective-permute-start.4
  8.8 1.0 %collective-permute-start.1 = (f32[8,256]{1,0:T(8,128)S(1)}, f32[8,256]{1,0:T(8,128)S(1)}, u32[]{:S(2)}, u32[]{:S(2)}) collective-permute-start(f32[8,256]{1,0:T(8,128)S(1)} %add.21.a_ref), channel_id=1, source_target_pairs={{0,4},{2,6},{4,0},{6,2},{1,5},{3,7},{5,1},{7,3},{8,12},{10,14},{12... | collective-permute-start | bytes 24584 | tf_op jit(solution)/shard_map/ppermute | solution.py:39
  9.9 0.3 collective-permute-start.2
  10.2 2.4 %collective-permute-start.3 = (f32[8,256]{1,0:T(8,128)S(1)}, f32[8,256]{1,0:T(8,128)S(1)}, u32[]{:S(2)}, u32[]{:S(2)}) collective-permute-start(f32[8,256]{1,0:T(8,128)S(1)} %add.21.a_ref), channel_id=1, source_target_pairs={{0,6},{2,0},{4,2},{6,4},{1,7},{3,1},{5,3},{7,5},{8,14},{10,8},{12,... | collective-permute-start | bytes 24584 | tf_op jit(solution)/shard_map/ppermute | solution.py:39
  12.5 0.3 collective-permute-done.1.b_ref
  12.9 0.8 collective-permute-done.2.c_ref
  13.7 0.0 copy-start.2
  13.7 1.0 %copy-done.2 = bf16[2,864,128]{2,1,0:T(8,128)(2,1)S(1)} copy-done((bf16[2,864,128]{2,1,0:T(8,128)(2,1)S(1)}, bf16[2,864,128]{2,1,0:T(8,128)(2,1)}, u32[]{:S(2)}) %copy-start.2) | copy-done | bytes 442392
  14.7 0.4 shard_map.78
  15.1 0.4 collective-permute-start.6
  15.5 2.4 %collective-permute-start.7 = (bf16[864,128]{1,0:T(8,128)(2,1)S(1)}, bf16[864,128]{1,0:T(8,128)(2,1)S(1)}, u32[]{:S(2)}, u32[]{:S(2)}) collective-permute-start(bf16[864,128]{1,0:T(8,128)(2,1)S(1)} %get-tuple-element.51.odd_ref.refs_1_), channel_id=1, source_target_pairs={{0,6},{2,0},{4,2},{6,4},{1,7},{3,1},{5,3},{7,5},{8,14},{10,8},{12,... | collective-permute-start | bytes 663560 | tf_op jit(solution)/shard_map/ppermute | solution.py:39
  17.8 1.1 %collective-permute-start.8 = (bf16[864,128]{1,0:T(8,128)(2,1)S(1)}, bf16[864,128]{1,0:T(8,128)(2,1)S(1)}, u32[]{:S(2)}, u32[]{:S(2)}) collective-permute-start(bf16[864,128]{1,0:T(8,128)(2,1)S(1)} %get-tuple-element.56), channel_id=1, source_target_pairs={{0,4},{2,6},{4,0},{6,2},{1,5},{3,7},{5,1},{7,3},{8,12},{10,14},{12... | collective-permute-start | bytes 663560 | tf_op jit(solution)/shard_map/ppermute | solution.py:39
  18.9 0.0 collective-permute-done.5.other_ref
  18.9 1.7 %shard_map.79.lhs_ref = bf16[1024,1792]{1,0:T(8,128)(2,1)S(1)} custom-call(bf16[864,1024]{1,0:T(8,128)(2,1)S(1)} %bitcast.19, bf16[864,1024]{1,0:T(8,128)(2,1)S(1)} %collective-permute-done.5.other_ref), custom_call_target="tpu_custom_call" | custom-call | bytes 7208960 | tf_op jit(solution)/shard_map/pallas_call | solution.py:65
  20.6 2.7 %shard_map.80 = (bf16[256,384]{1,0:T(8,128)(2,1)S(1)}, bf16[256,384]{1,0:T(8,128)(2,1)S(1)}, bf16[256,384]{1,0:T(8,128)(2,1)S(1)}, bf16[256,384]{1,0:T(8,128)(2,1)S(1)}) custom-call(s32[1]{0:T(128)} %bitcast.place_ref, bf16[864,128]{1,0:T(8,128)(2,1)S(1)} %get-tuple-element.50.even_ref.refs_0_, bf16[864,128]{1,0:T(8,128)(2,1)S(1)} %get-tuple-element.51.odd_ref.refs_1_, ...), custom_call_target="tpu_custom_call" | custom-call | flops 1409286144 | bytes 4898820 | tf_op jit(solution)/shard_map/pallas_call | solution.py:65
  23.3 2.0 %collective-permute-start.9 = (bf16[256,384]{1,0:T(8,128)(2,1)S(1)}, bf16[256,384]{1,0:T(8,128)(2,1)S(1)}, u32[]{:S(2)}, u32[]{:S(2)}) collective-permute-start(bf16[256,384]{1,0:T(8,128)(2,1)S(1)} %get-tuple-element.62), channel_id=1, source_target_pairs={{0,16},{1,5},{2,18},{3,7},{4,20},{5,1},{6,22},{7,3},{8,24},{9,13},... | collective-permute-start | bytes 589832 | tf_op jit(solution)/shard_map/ppermute | solution.py:49
  25.3 0.0 collective-permute-done.6.up_ref.refs_2_
  25.3 2.7 %collective-permute-start.11 = (bf16[256,384]{1,0:T(8,128)(2,1)S(1)}, bf16[256,384]{1,0:T(8,128)(2,1)S(1)}, u32[]{:S(2)}, u32[]{:S(2)}) collective-permute-start(bf16[256,384]{1,0:T(8,128)(2,1)S(1)} %get-tuple-element.64), channel_id=1, source_target_pairs={{0,24},{1,7},{2,26},{3,1},{4,28},{5,3},{6,30},{7,5},{8,0},{9,15},{... | collective-permute-start | bytes 589832 | tf_op jit(solution)/shard_map/ppermute | solution.py:49
  28.0 0.0 collective-permute-done.7.down_ref.refs_3_
  28.0 0.0 collective-permute-done.8.far_ref.refs_4_
  28.0 5.3 %shard_map.81 = (bf16[256,768]{1,0:T(8,128)(2,1)S(1)}, bf16[256,768]{1,0:T(8,128)(2,1)}, bf16[256,768]{1,0:T(8,128)(2,1)}, bf16[256,768]{1,0:T(8,128)(2,1)}, bf1...) custom-call(s32[1]{0:T(128)} %bitcast.place_ref, bf16[864,128]{1,0:T(8,128)(2,1)S(1)} %get-tuple-element.50.even_ref.refs_0_, ...), custom_call_target="tpu_custom_call" | custom-call | flops 2818572288 | bytes 7012356 | tf_op jit(solution)/shard_map/pallas_call | solution.py:65
  33.2 0.0 collective-permute-done.9.refs_1_
  33.2 0.6 collective-permute-done.10.refs_2_
  33.8 0.0 collective-permute-done.11.refs_3_
  33.8 1.5 %collective-permute-start.12 = (bf16[256,768]{1,0:T(8,128)(2,1)}, bf16[256,768]{1,0:T(8,128)(2,1)S(1)}, u32[]{:S(2)}, u32[]{:S(2)}) collective-permute-start(bf16[256,768]{1,0:T(8,128)(2,1)} %get-tuple-element.70), channel_id=1, source_target_pairs={{0,16},{1,5},{2,18},{3,7},{4,20},{5,1},{6,22},{7,3},{8,24},{9,13},... | collective-permute-start | bytes 1179656 | tf_op jit(solution)/shard_map/ppermute | solution.py:49
  35.3 0.7 collective-permute-start.13
  36.0 1.9 %collective-permute-start.14 = (bf16[256,768]{1,0:T(8,128)(2,1)}, bf16[256,768]{1,0:T(8,128)(2,1)S(1)}, u32[]{:S(2)}, u32[]{:S(2)}) collective-permute-start(bf16[256,768]{1,0:T(8,128)(2,1)} %get-tuple-element.72), channel_id=1, source_target_pairs={{0,24},{1,7},{2,26},{3,1},{4,28},{5,3},{6,30},{7,5},{8,0},{9,15},{... | collective-permute-start | bytes 1179656 | tf_op jit(solution)/shard_map/ppermute | solution.py:49
  38.0 5.9 %collective-permute-start.15 = (bf16[3,432,128]{2,1,0:T(8,128)(2,1)}, bf16[3,432,128]{2,1,0:T(8,128)(2,1)}, u32[]{:S(2)}, u32[]{:S(2)}) collective-permute-start(bf16[3,432,128]{2,1,0:T(8,128)(2,1)} %get-tuple-element.75), channel_id=1, source_target_pairs={{0,1},{1,0},{2,3},{3,2},{4,5},{5,4},{6,7},{7,6},{8,9},{9,8},{10,11... | collective-permute-start | bytes 995336 | tf_op jit(solution)/shard_map/ppermute | solution.py:35
  43.8 0.0 collective-permute-start.16
  43.8 6.6 %copy.8 = bf16[9,256,1024]{2,1,0:T(8,128)(2,1)} copy(bf16[9,256,1024]{1,2,0:T(8,128)(2,1)} %bitcast.21) | data formatting | bytes 9437184 | tf_op jit(solution)/shard_map/transpose | solution.py:408
  50.5 0.2 shard_map.82.held_ref
  50.7 0.9 %copy-done.1 = bf16[3,864,128]{2,1,0:T(8,128)(2,1)} copy-done((bf16[3,864,128]{2,1,0:T(8,128)(2,1)}, bf16[3,864,128]{2,1,0:T(8,128)(2,1)S(1)}, u32[]{:S(2)}) %copy-start.1) | copy-done | bytes 663576
  51.6 0.0 collective-permute-done.12.refs_5_
  51.6 0.0 collective-permute-done.13.refs_6_
  51.6 0.0 collective-permute-done.14.refs_7_
  51.6 1.1 %shard_map.83 = bf16[256,1152]{1,0:T(8,128)(2,1)} custom-call(bf16[256,384]{1,0:T(8,128)(2,1)S(1)} %get-tuple-element.54.refs_0_, bf16[256,384]{1,0:T(8,128)(2,1)S(1)} %collective-permute-done.9.refs_1_, bf16[256,384]{1,0:T(8,128)(2,1)S(1)} %collective-permute-done.10.refs_2_, bf16[256,384]{1,0:T(8,128)(2,1)S(1)} %collective-permute-done.11.refs_3_, ...), custom_call_target="tpu_custom_call" | custom-call | bytes 2949120 | tf_op jit(solution)/shard_map/pallas_call | solution.py:65
  52.7 8.6 %all-to-all-start = ((bf16[32,8,1152]{2,1,0:T(8,128)(2,1)}), bf16[32,8,1152]{2,1,0:T(8,128)(2,1)S(1)}, u32[]{:S(2)}, u32[]{:S(2)}) async-start(bf16[32,8,1152]{2,1,0:T(8,128)(2,1)} %bitcast.12), calls=%async_computation | async-start | bytes 1179648 | tf_op jit(solution)/shard_map/all_to_all | solution.py:55
  61.3 8.6 %shard_map.84 = bf16[864,1024]{1,0:T(8,128)(2,1)} custom-call(s32[1]{0:T(128)} %bitcast.place_ref, bf16[3,864,128]{2,1,0:T(8,128)(2,1)} %copy-done.1, bf16[3,432,128]{2,1,0:T(8,128)(2,1)} %collective-permute-done.15.rest_0_, bf16[3,432,128]{2,1,0:T(8,128)(2,1)} %collective-permute-done.16.rest_1_, bf16[2304,1024]{1,0:T(8,128)(2,1)} %bitcast.22), custom_call_target="tpu_custom_call" | custom-call | flops 4076863488 | bytes 7815172 | tf_op jit(solution)/shard_map/pallas_call | solution.py:65
  69.8 6.6 %all-to-all-done = bf16[32,8,1152]{2,1,0:T(8,128)(2,1)S(1)} async-done(((bf16[32,8,1152]{2,1,0:T(8,128)(2,1)}), bf16[32,8,1152]{2,1,0:T(8,128)(2,1)S(1)}, u32[]{:S(2)}, u32[]{:S(2)}) %all-to-all-start) | async-done | bytes 589856 | tf_op jit(solution)/shard_map/all_to_all | solution.py:55
  76.5 0.1 convert_reduce_fusion.1
  76.6 5.5 %collective-permute-start.17 = (f32[4,1152]{1,0:T(4,128)S(1)}, f32[4,1152]{1,0:T(4,128)S(1)}, u32[]{:S(2)}, u32[]{:S(2)}) collective-permute-start(f32[4,1152]{1,0:T(4,128)S(1)} %constant_dynamic-slice_fusion), channel_id=1, source_target_pairs={{0,1},{1,0},{2,3},{3,2},{4,5},{5,4},{6,7},{7,6},{8,9},{9,8},{10,11... | collective-permute-start | bytes 55304 | tf_op jit(solution)/shard_map/ppermute | solution.py:35
  82.1 0.8 %collective-permute-done.17 = f32[4,1152]{1,0:T(4,128)S(1)} collective-permute-done((f32[4,1152]{1,0:T(4,128)S(1)}, f32[4,1152]{1,0:T(4,128)S(1)}, u32[]{:S(2)}, u32[]{:S(2)}) %collective-permute-start.17) | collective-permute-done | bytes 18464 | tf_op jit(solution)/shard_map/ppermute | solution.py:35
  83.0 0.6 pad_maximum_fusion
  (16 shorter events, 0.1 us)
Async XLA Ops:
  0.6 7.6 %copy-start = (bf16[2,6,72,1024]{3,2,1,0:T(8,128)(2,1)S(1)}, bf16[2,6,72,1024]{3,2,1,0:T(8,128)(2,1)}, u32[]{:S(2)}) copy-start(bf16[2,6,72,1024]{3,2,1,0:T(8,128)(2,1)} %param.6) | copy-start | bytes 5308420
  0.6 13.1 %copy-start.3 = (f32[256]{0:T(256)S(1)}, f32[256]{0:T(256)}, u32[]{:S(2)}) copy-start(f32[256]{0:T(256)} %param.10) | copy-start | bytes 3076
  2.5 5.7 %collective-permute-start = (f32[8,256]{1,0:T(8,128)S(1)}, f32[8,256]{1,0:T(8,128)S(1)}, u32[]{:S(2)}, u32[]{:S(2)}) collective-permute-start(f32[8,256]{1,0:T(8,128)S(1)} %reshape.42), channel_id=1, source_target_pairs={{0,1},{1,0},{2,3},{3,2},{4,5},{5,4},{6,7},{7,6},{8,9},{9,8},{10,11... | collective-permute-start | bytes 24584 | tf_op jit(solution)/shard_map/ppermute | solution.py:35
  8.2 10.7 %collective-permute-start.5 = (bf16[864,1024]{1,0:T(8,128)(2,1)S(1)}, bf16[864,1024]{1,0:T(8,128)(2,1)S(1)}, u32[]{:S(2)}, u32[]{:S(2)}) collective-permute-start(bf16[864,1024]{1,0:T(8,128)(2,1)S(1)} %bitcast.18), channel_id=1, source_target_pairs={{0,1},{1,0},{2,3},{3,2},{4,5},{5,4},{6,7},{7,6},{8,9},{9,8},{10,11... | collective-permute-start | bytes 5308424 | tf_op jit(solution)/shard_map/ppermute | solution.py:35
  8.4 5.3 %collective-permute-start.4 = (bf16[2,864,128]{2,1,0:T(8,128)(2,1)}, bf16[2,864,128]{2,1,0:T(8,128)(2,1)S(1)}, u32[]{:S(2)}, u32[]{:S(2)}) collective-permute-start(bf16[2,864,128]{2,1,0:T(8,128)(2,1)} %get-tuple-element.49), channel_id=1, source_target_pairs={{0,1},{1,0},{2,3},{3,2},{4,5},{5,4},{6,7},{7,6},{8,9},{9,8},{10,11... | collective-permute-start | bytes 1327112 | tf_op jit(solution)/shard_map/ppermute | solution.py:35
  8.8 4.0 %collective-permute-start.1 = (f32[8,256]{1,0:T(8,128)S(1)}, f32[8,256]{1,0:T(8,128)S(1)}, u32[]{:S(2)}, u32[]{:S(2)}) collective-permute-start(f32[8,256]{1,0:T(8,128)S(1)} %add.21.a_ref), channel_id=1, source_target_pairs={{0,4},{2,6},{4,0},{6,2},{1,5},{3,7},{5,1},{7,3},{8,12},{10,14},{12... | collective-permute-start | bytes 24584 | tf_op jit(solution)/shard_map/ppermute | solution.py:39
  9.9 3.8 %collective-permute-start.2 = (f32[8,256]{1,0:T(8,128)S(1)}, f32[8,256]{1,0:T(8,128)S(1)}, u32[]{:S(2)}, u32[]{:S(2)}) collective-permute-start(f32[8,256]{1,0:T(8,128)S(1)} %add.21.a_ref), channel_id=1, source_target_pairs={{0,2},{2,4},{4,6},{6,0},{1,3},{3,5},{5,7},{7,1},{8,10},{10,12},{12... | collective-permute-start | bytes 24584 | tf_op jit(solution)/shard_map/ppermute | solution.py:39
  10.2 3.5 %collective-permute-start.3 = (f32[8,256]{1,0:T(8,128)S(1)}, f32[8,256]{1,0:T(8,128)S(1)}, u32[]{:S(2)}, u32[]{:S(2)}) collective-permute-start(f32[8,256]{1,0:T(8,128)S(1)} %add.21.a_ref), channel_id=1, source_target_pairs={{0,6},{2,0},{4,2},{6,4},{1,7},{3,1},{5,3},{7,5},{8,14},{10,8},{12,... | collective-permute-start | bytes 24584 | tf_op jit(solution)/shard_map/ppermute | solution.py:39
  13.7 1.0 %copy-start.2 = (bf16[2,864,128]{2,1,0:T(8,128)(2,1)S(1)}, bf16[2,864,128]{2,1,0:T(8,128)(2,1)}, u32[]{:S(2)}) copy-start(bf16[2,864,128]{2,1,0:T(8,128)(2,1)} %get-tuple-element.48.mine_ref) | copy-start | bytes 1327108
  15.1 10.2 %collective-permute-start.6 = (bf16[864,128]{1,0:T(8,128)(2,1)S(1)}, bf16[864,128]{1,0:T(8,128)(2,1)S(1)}, u32[]{:S(2)}, u32[]{:S(2)}) collective-permute-start(bf16[864,128]{1,0:T(8,128)(2,1)S(1)} %get-tuple-element.50.even_ref.refs_0_), channel_id=1, source_target_pairs={{0,2},{2,4},{4,6},{6,0},{1,3},{3,5},{5,7},{7,1},{8,10},{10,12},{12... | collective-permute-start | bytes 663560 | tf_op jit(solution)/shard_map/ppermute | solution.py:39
  15.5 12.5 %collective-permute-start.7 = (bf16[864,128]{1,0:T(8,128)(2,1)S(1)}, bf16[864,128]{1,0:T(8,128)(2,1)S(1)}, u32[]{:S(2)}, u32[]{:S(2)}) collective-permute-start(bf16[864,128]{1,0:T(8,128)(2,1)S(1)} %get-tuple-element.51.odd_ref.refs_1_), channel_id=1, source_target_pairs={{0,6},{2,0},{4,2},{6,4},{1,7},{3,1},{5,3},{7,5},{8,14},{10,8},{12,... | collective-permute-start | bytes 663560 | tf_op jit(solution)/shard_map/ppermute | solution.py:39
  17.8 10.1 %collective-permute-start.8 = (bf16[864,128]{1,0:T(8,128)(2,1)S(1)}, bf16[864,128]{1,0:T(8,128)(2,1)S(1)}, u32[]{:S(2)}, u32[]{:S(2)}) collective-permute-start(bf16[864,128]{1,0:T(8,128)(2,1)S(1)} %get-tuple-element.56), channel_id=1, source_target_pairs={{0,4},{2,6},{4,0},{6,2},{1,5},{3,7},{5,1},{7,3},{8,12},{10,14},{12... | collective-permute-start | bytes 663560 | tf_op jit(solution)/shard_map/ppermute | solution.py:39
  23.3 9.9 %collective-permute-start.9 = (bf16[256,384]{1,0:T(8,128)(2,1)S(1)}, bf16[256,384]{1,0:T(8,128)(2,1)S(1)}, u32[]{:S(2)}, u32[]{:S(2)}) collective-permute-start(bf16[256,384]{1,0:T(8,128)(2,1)S(1)} %get-tuple-element.62), channel_id=1, source_target_pairs={{0,16},{1,5},{2,18},{3,7},{4,20},{5,1},{6,22},{7,3},{8,24},{9,13},... | collective-permute-start | bytes 589832 | tf_op jit(solution)/shard_map/ppermute | solution.py:49
  25.3 8.5 %collective-permute-start.10 = (bf16[256,384]{1,0:T(8,128)(2,1)S(1)}, bf16[256,384]{1,0:T(8,128)(2,1)S(1)}, u32[]{:S(2)}, u32[]{:S(2)}) collective-permute-start(bf16[256,384]{1,0:T(8,128)(2,1)S(1)} %get-tuple-element.63), channel_id=1, source_target_pairs={{0,8},{1,3},{2,10},{3,5},{4,12},{5,7},{6,14},{7,1},{8,16},{9,11},{... | collective-permute-start | bytes 589832 | tf_op jit(solution)/shard_map/ppermute | solution.py:49
  25.3 8.5 %collective-permute-start.11 = (bf16[256,384]{1,0:T(8,128)(2,1)S(1)}, bf16[256,384]{1,0:T(8,128)(2,1)S(1)}, u32[]{:S(2)}, u32[]{:S(2)}) collective-permute-start(bf16[256,384]{1,0:T(8,128)(2,1)S(1)} %get-tuple-element.64), channel_id=1, source_target_pairs={{0,24},{1,7},{2,26},{3,1},{4,28},{5,3},{6,30},{7,5},{8,0},{9,15},{... | collective-permute-start | bytes 589832 | tf_op jit(solution)/shard_map/ppermute | solution.py:49
  33.8 17.7 %collective-permute-start.12 = (bf16[256,768]{1,0:T(8,128)(2,1)}, bf16[256,768]{1,0:T(8,128)(2,1)S(1)}, u32[]{:S(2)}, u32[]{:S(2)}) collective-permute-start(bf16[256,768]{1,0:T(8,128)(2,1)} %get-tuple-element.70), channel_id=1, source_target_pairs={{0,16},{1,5},{2,18},{3,7},{4,20},{5,1},{6,22},{7,3},{8,24},{9,13},... | collective-permute-start | bytes 1179656 | tf_op jit(solution)/shard_map/ppermute | solution.py:49
  35.3 16.3 %collective-permute-start.13 = (bf16[256,768]{1,0:T(8,128)(2,1)}, bf16[256,768]{1,0:T(8,128)(2,1)S(1)}, u32[]{:S(2)}, u32[]{:S(2)}) collective-permute-start(bf16[256,768]{1,0:T(8,128)(2,1)} %get-tuple-element.71), channel_id=1, source_target_pairs={{0,8},{1,3},{2,10},{3,5},{4,12},{5,7},{6,14},{7,1},{8,16},{9,11},{... | collective-permute-start | bytes 1179656 | tf_op jit(solution)/shard_map/ppermute | solution.py:49
  36.0 15.6 %collective-permute-start.14 = (bf16[256,768]{1,0:T(8,128)(2,1)}, bf16[256,768]{1,0:T(8,128)(2,1)S(1)}, u32[]{:S(2)}, u32[]{:S(2)}) collective-permute-start(bf16[256,768]{1,0:T(8,128)(2,1)} %get-tuple-element.72), channel_id=1, source_target_pairs={{0,24},{1,7},{2,26},{3,1},{4,28},{5,3},{6,30},{7,5},{8,0},{9,15},{... | collective-permute-start | bytes 1179656 | tf_op jit(solution)/shard_map/ppermute | solution.py:49
  38.0 13.6 %collective-permute-start.15 = (bf16[3,432,128]{2,1,0:T(8,128)(2,1)}, bf16[3,432,128]{2,1,0:T(8,128)(2,1)}, u32[]{:S(2)}, u32[]{:S(2)}) collective-permute-start(bf16[3,432,128]{2,1,0:T(8,128)(2,1)} %get-tuple-element.75), channel_id=1, source_target_pairs={{0,1},{1,0},{2,3},{3,2},{4,5},{5,4},{6,7},{7,6},{8,9},{9,8},{10,11... | collective-permute-start | bytes 995336 | tf_op jit(solution)/shard_map/ppermute | solution.py:35
  43.8 7.8 %collective-permute-start.16 = (bf16[3,432,128]{2,1,0:T(8,128)(2,1)}, bf16[3,432,128]{2,1,0:T(8,128)(2,1)}, u32[]{:S(2)}, u32[]{:S(2)}) collective-permute-start(bf16[3,432,128]{2,1,0:T(8,128)(2,1)} %get-tuple-element.76), channel_id=1, source_target_pairs={{0,1},{1,0},{2,3},{3,2},{4,5},{5,4},{6,7},{7,6},{8,9},{9,8},{10,11... | collective-permute-start | bytes 995336 | tf_op jit(solution)/shard_map/ppermute | solution.py:35
  50.7 0.9 %copy-start.1 = (bf16[3,864,128]{2,1,0:T(8,128)(2,1)}, bf16[3,864,128]{2,1,0:T(8,128)(2,1)S(1)}, u32[]{:S(2)}) copy-start(bf16[3,864,128]{2,1,0:T(8,128)(2,1)S(1)} %shard_map.82.held_ref) | copy-start | bytes 1990660
  52.7 23.8 %all-to-all-start = ((bf16[32,8,1152]{2,1,0:T(8,128)(2,1)}), bf16[32,8,1152]{2,1,0:T(8,128)(2,1)S(1)}, u32[]{:S(2)}, u32[]{:S(2)}) async-start(bf16[32,8,1152]{2,1,0:T(8,128)(2,1)} %bitcast.12), calls=%async_computation | async-start | bytes 1179648 | tf_op jit(solution)/shard_map/all_to_all | solution.py:55
  76.6 6.4 %collective-permute-start.17 = (f32[4,1152]{1,0:T(4,128)S(1)}, f32[4,1152]{1,0:T(4,128)S(1)}, u32[]{:S(2)}, u32[]{:S(2)}) collective-permute-start(f32[4,1152]{1,0:T(4,128)S(1)} %constant_dynamic-slice_fusion), channel_id=1, source_target_pairs={{0,1},{1,0},{2,3},{3,2},{4,5},{5,4},{6,7},{7,6},{8,9},{9,8},{10,11... | collective-permute-start | bytes 55304 | tf_op jit(solution)/shard_map/ppermute | solution.py:35

commit v10 on v9

--- a/solution.py
+++ b/solution.py
@@ -53,6 +53,9 @@
     groups = [[device(z, y, x, 0) for z in range(Z) for x in range(X)] for y in range(Y)]
     groups += [[device(z, y, x, 1) for z in range(Z) for y in range(Y)] for x in range(X)]
     return lax.all_to_all(value, AXES, 0, 0, axis_index_groups=groups)
+
+
+VMEM = pl.BlockSpec(memory_space=pltpu.VMEM)
 
 
 def whole(shape):
@@ -200,35 +203,37 @@
 
 def multiply(place_ref, lhs_ref, stacked, total, out_refs):
     columns = stacked.shape[1]
-    product = jnp.dot(lhs_ref[...], stacked[...], preferred_element_type=F32)
-    total[...] = product.reshape(total.shape)
-    tall = total.shape[0] * 32
-
-    @pl.when(core_of(place_ref) == 0)
-    def _():
-        for steps in range(Y):
-            chunk = total[:, lax.rem(y_of(place_ref) + steps, Y), :, :, :]
-            out_refs[steps][...] = chunk.reshape(tall, columns).astype(BF16)
-
-    @pl.when(core_of(place_ref) != 0)
-    def _():
-        for steps in range(X):
-            chunk = total[:, :, lax.rem(x_of(place_ref) + steps, X), :, :]
-            out_refs[steps][...] = chunk.reshape(tall, columns).astype(BF16)
+    groups = total.shape[0]
+    for part in range(lhs_ref.shape[0] // (groups * 128)):
+        rows = slice(part * groups * 128, (part + 1) * groups * 128)
+        out_rows = slice(part * groups * 32, (part + 1) * groups * 32)
+        product = jnp.dot(lhs_ref[rows, :], stacked[...], preferred_element_type=F32)
+        total[...] = product.reshape(total.shape)
+
+        @pl.when(core_of(place_ref) == 0)
+        def _():
+            for steps in range(Y):
+                chunk = total[:, lax.rem(y_of(place_ref) + steps, Y), :, :, :]
+                out_refs[steps][out_rows, :] = chunk.reshape(groups * 32, columns).astype(BF16)
+
+        @pl.when(core_of(place_ref) != 0)
+        def _():
+            for steps in range(X):
+                chunk = total[:, :, lax.rem(x_of(place_ref) + steps, X), :, :]
+                out_refs[steps][out_rows, :] = chunk.reshape(groups * 32, columns).astype(BF16)
 
 
 def product_call(body, place, fixed, lhs, columns, extra):
     channels_in, deep = lhs.shape
-    steps = 2
-    tall = channels_in // steps
+    groups = 4
     return kernel_call(
         body,
         (place, *fixed, lhs),
-        [SMEM] + [whole(value.shape) for value in fixed] + [pl.BlockSpec((tall, deep), lambda i: (i, 0))],
+        [SMEM] + [VMEM] * (len(fixed) + 1),
         [jax.ShapeDtypeStruct((channels_in // 4, columns), BF16)] * 4 + extra,
-        [pl.BlockSpec((tall // 4, columns), lambda i: (i, 0))] * 4 + [whole(value.shape) for value in extra],
-        (steps,),
-        [pltpu.VMEM((deep, columns), BF16), pltpu.VMEM((tall // 128, Y, X, 8, columns), F32)],
+        [VMEM] * (4 + len(extra)),
+        (),
+        [pltpu.VMEM((deep, columns), BF16), pltpu.VMEM((groups, Y, X, 8, columns), F32)],
         flops=2 * channels_in * deep * columns,
         vmem=24,
     )
@@ -239,15 +244,11 @@
 
     def body(place_ref, even_ref, odd_ref, lhs_ref, *rest):
         stacked, total = rest[4:]
-
-        @pl.when(pl.program_id(0) == 0)
-        def _():
-            clear_padding(stacked, cells)
-            first = core_of(place_ref) == 0
-            even_block, odd_block = even_ref[...], odd_ref[...]
-            fill(stacked, 0, 0, jnp.where(first, even_block, odd_block), col_count)
-            fill(stacked, 1, 0, jnp.where(first, odd_block, even_block), col_count)
-
+        clear_padding(stacked, cells)
+        first = core_of(place_ref) == 0
+        even_block, odd_block = even_ref[...], odd_ref[...]
+        fill(stacked, 0, 0, jnp.where(first, even_block, odd_block), col_count)
+        fill(stacked, 1, 0, jnp.where(first, odd_block, even_block), col_count)
         multiply(place_ref, lhs_ref, stacked, total, rest[:4])
 
     return product_call(body, place, [even, odd], lhs, 3 * width, [])
@@ -289,20 +290,17 @@
         theirs_refs = rest[4:6]
         stacked, total = rest[6:]
 
-        @pl.when(pl.program_id(0) == 0)
-        def _():
-            clear_padding(stacked, cells)
-            first = core_of(place_ref) == 0
-            blocks = tap_blocks(place_ref, even_ref, odd_ref, up_ref, down_ref, far_ref)
-            for side, (lower, upper) in enumerate(blocks):
-                theirs = jnp.where(first, upper, lower)
-                for part, ref in enumerate(theirs_refs):
-                    ref[side] = theirs[part * (cells // 2) : (part + 1) * (cells // 2)]
-                if side != 1:
-                    mine = jnp.where(first, lower, upper)
-                    fill(stacked, 0, 3 * (side // 2), mine, col_count)
-                    fill(stacked, 1, 3 * (side // 2), theirs, col_count)
-
+        clear_padding(stacked, cells)
+        first = core_of(place_ref) == 0
+        blocks = tap_blocks(place_ref, even_ref, odd_ref, up_ref, down_ref, far_ref)
+        for side, (lower, upper) in enumerate(blocks):
+            theirs = jnp.where(first, upper, lower)
+            for part, ref in enumerate(theirs_refs):
+                ref[side] = theirs[part * (cells // 2) : (part + 1) * (cells // 2)]
+            if side != 1:
+                mine = jnp.where(first, lower, upper)
+                fill(stacked, 0, 3 * (side // 2), mine, col_count)
+                fill(stacked, 1, 3 * (side // 2), theirs, col_count)
         multiply(place_ref, lhs_ref, stacked, total, rest[:4])
 
     part = jax.ShapeDtypeStruct((3, cells // 2, width), BF16)

time: 84.1 us -> 84.7 us (level)
  transfers between devices with their start and end apart: 19 -> 19, of which waited for: 5 -> 5; matrix products, arithmetic and copies ran while one was open for 8% -> 8% of each run, Pallas kernels for 25% -> 26%
where the time goes in v10:
time: 84.7 us; the launch traced here: 84.3 us
  starting transfers between devices  40.8 us (48%)
  Pallas kernels  22.7 us (27%)
  waiting for transfers between devices  8.91 us (11%)
  local copies, waits for them, and re-layouts  8.55 us (10%)
  other arithmetic  2.6 us (3%)
    pallas_call x8, Pallas kernels, kernel_call(): pl.pallas_call(body, grid=grid, in_specs=in_specs, out_specs=out_specs, o...  22.7 us
    ppermute x6, starting transfers between devices, swapped(): return lax.ppermute(value, 'core', [(0, 1), (1, 0)])  15.9 us
    ppermute x6, starting transfers between devices, crossed(): return lax.ppermute(value, AXES, pairs)  8.81 us
    all_to_all x1, starting transfers between devices, exchanged(): return lax.all_to_all(value, AXES, 0, 0, axis_index_groups=groups)  8.58 us
    ppermute x6, starting transfers between devices, around(): lax.ppermute(value, 'x', [(source, (source + steps) % X) for source in ra...  7.51 us
    all_to_all x1, waiting for transfers between devices, exchanged(): return lax.all_to_all(value, AXES, 0, 0, axis_index_groups=groups)  6.74 us
    transpose x1, local copies, waits for them, and re-layouts, per_device(): jnp.transpose(weight, (1, 2, 0)).reshape(9 * channels_out, channels_in)  6.63 us
    unnamed x8, local copies, waits for them, and re-layouts  1.9 us
  transfers between devices with their start and end apart: 19, of which 5 were waited for; matrix products, arithmetic and copies ran while one was open for 8% of the time, Pallas kernels for 26%

profile of v10, /device:TPU:1, one launch (start us, length us, event | category | flops | bytes accessed | tf_op | source)
XLA Modules:
  0.0 84.3 jit_solution(11807804833766991157)
XLA Ops:
  0.6 1.9 %fusion.2 = (f32[2,256]{1,0:T(2,128)S(1)}, f32[2,256]{1,0:T(2,128)S(1)}, f32[2,256]{1,0:T(2,128)S(1)}, f32[2,256]{1,0:T(2,128)S(1)}) fusion(s32[2,6,72,256]{3,2,1,0:T(8,128)} %param.9, bf16[2,6,72,256]{3,2,1,0:T(8,128)(2,1)} %param.8, bf16[2,6,72,256]{3,2,1,0:T(8,128)(2,1)} %param.7), kind=kLoop, calls=%fused_computation.7 | loop fusion | flops 2209792 | bytes 1777664 | tf_op jit(solution)/shard_map/reduce_sum | solution.py:84
  2.5 3.3 %collective-permute-start = (f32[8,256]{1,0:T(8,128)S(1)}, f32[8,256]{1,0:T(8,128)S(1)}, u32[]{:S(2)}, u32[]{:S(2)}) collective-permute-start(f32[8,256]{1,0:T(8,128)S(1)} %reshape.42), channel_id=1, source_target_pairs={{0,1},{1,0},{2,3},{3,2},{4,5},{5,4},{6,7},{7,6},{8,9},{9,8},{10,11... | collective-permute-start | bytes 24584 | tf_op jit(solution)/shard_map/ppermute | solution.py:35
  5.9 2.4 %shard_map.77 = (bf16[2,864,128]{2,1,0:T(8,128)(2,1)}, bf16[2,864,128]{2,1,0:T(8,128)(2,1)}) custom-call(s32[1]{0:T(128)} %bitcast.place_ref, bf16[864,256]{1,0:T(8,128)(2,1)} %bitcast.25, bf16[864,256]{1,0:T(8,128)(2,1)} %bitcast.24, s32[864,256]{1,0:T(8,128)} %bitcast.23), custom_call_target="tpu_custom_call" | custom-call | bytes 2654212 | tf_op jit(solution)/shard_map/pallas_call | solution.py:68
  8.2 0.0 collective-permute-done
  8.2 0.1 collective-permute-start.5
  8.4 0.5 collective-permute-start.4
  8.8 1.0 %collective-permute-start.1 = (f32[8,256]{1,0:T(8,128)S(1)}, f32[8,256]{1,0:T(8,128)S(1)}, u32[]{:S(2)}, u32[]{:S(2)}) collective-permute-start(f32[8,256]{1,0:T(8,128)S(1)} %add.21.a_ref), channel_id=1, source_target_pairs={{0,4},{2,6},{4,0},{6,2},{1,5},{3,7},{5,1},{7,3},{8,12},{10,14},{12... | collective-permute-start | bytes 24584 | tf_op jit(solution)/shard_map/ppermute | solution.py:39
  9.9 0.3 collective-permute-start.2
  10.2 2.4 %collective-permute-start.3 = (f32[8,256]{1,0:T(8,128)S(1)}, f32[8,256]{1,0:T(8,128)S(1)}, u32[]{:S(2)}, u32[]{:S(2)}) collective-permute-start(f32[8,256]{1,0:T(8,128)S(1)} %add.21.a_ref), channel_id=1, source_target_pairs={{0,6},{2,0},{4,2},{6,4},{1,7},{3,1},{5,3},{7,5},{8,14},{10,8},{12,... | collective-permute-start | bytes 24584 | tf_op jit(solution)/shard_map/ppermute | solution.py:39
  12.5 0.3 collective-permute-done.1.b_ref
  12.9 0.8 collective-permute-done.2.c_ref
  13.7 0.0 collective-permute-done.3.d_ref
  13.7 0.0 copy-start.2
  13.7 1.0 %copy-done.2 = bf16[2,864,128]{2,1,0:T(8,128)(2,1)S(1)} copy-done((bf16[2,864,128]{2,1,0:T(8,128)(2,1)S(1)}, bf16[2,864,128]{2,1,0:T(8,128)(2,1)}, u32[]{:S(2)}) %copy-start.2) | copy-done | bytes 442392
  14.7 0.4 shard_map.78
  15.1 0.4 collective-permute-start.6
  15.5 2.4 %collective-permute-start.7 = (bf16[864,128]{1,0:T(8,128)(2,1)S(1)}, bf16[864,128]{1,0:T(8,128)(2,1)S(1)}, u32[]{:S(2)}, u32[]{:S(2)}) collective-permute-start(bf16[864,128]{1,0:T(8,128)(2,1)S(1)} %get-tuple-element.51.odd_ref.refs_1_), channel_id=1, source_target_pairs={{0,6},{2,0},{4,2},{6,4},{1,7},{3,1},{5,3},{7,5},{8,14},{10,8},{12,... | collective-permute-start | bytes 663560 | tf_op jit(solution)/shard_map/ppermute | solution.py:39
  17.8 1.1 %collective-permute-start.8 = (bf16[864,128]{1,0:T(8,128)(2,1)S(1)}, bf16[864,128]{1,0:T(8,128)(2,1)S(1)}, u32[]{:S(2)}, u32[]{:S(2)}) collective-permute-start(bf16[864,128]{1,0:T(8,128)(2,1)S(1)} %get-tuple-element.56), channel_id=1, source_target_pairs={{0,4},{2,6},{4,0},{6,2},{1,5},{3,7},{5,1},{7,3},{8,12},{10,14},{12... | collective-permute-start | bytes 663560 | tf_op jit(solution)/shard_map/ppermute | solution.py:39
  18.9 0.0 collective-permute-done.5.other_ref
  18.9 1.7 %shard_map.79.lhs_ref = bf16[1024,1792]{1,0:T(8,128)(2,1)S(1)} custom-call(bf16[864,1024]{1,0:T(8,128)(2,1)S(1)} %bitcast.19, bf16[864,1024]{1,0:T(8,128)(2,1)S(1)} %collective-permute-done.5.other_ref), custom_call_target="tpu_custom_call" | custom-call | bytes 7208960 | tf_op jit(solution)/shard_map/pallas_call | solution.py:68
  20.6 2.5 %shard_map.80 = (bf16[256,384]{1,0:T(8,128)(2,1)S(1)}, bf16[256,384]{1,0:T(8,128)(2,1)S(1)}, bf16[256,384]{1,0:T(8,128)(2,1)S(1)}, bf16[256,384]{1,0:T(8,128)(2,1)S(1)}) custom-call(s32[1]{0:T(128)} %bitcast.place_ref, bf16[864,128]{1,0:T(8,128)(2,1)S(1)} %get-tuple-element.50.even_ref.refs_0_, bf16[864,128]{1,0:T(8,128)(2,1)S(1)} %get-tuple-element.51.odd_ref.refs_1_, ...), custom_call_target="tpu_custom_call" | custom-call | flops 1409286144 | bytes 4898820 | tf_op jit(solution)/shard_map/pallas_call | solution.py:68
  23.1 2.0 %collective-permute-start.9 = (bf16[256,384]{1,0:T(8,128)(2,1)S(1)}, bf16[256,384]{1,0:T(8,128)(2,1)S(1)}, u32[]{:S(2)}, u32[]{:S(2)}) collective-permute-start(bf16[256,384]{1,0:T(8,128)(2,1)S(1)} %get-tuple-element.62), channel_id=1, source_target_pairs={{0,16},{1,5},{2,18},{3,7},{4,20},{5,1},{6,22},{7,3},{8,24},{9,13},... | collective-permute-start | bytes 589832 | tf_op jit(solution)/shard_map/ppermute | solution.py:49
  25.1 0.0 collective-permute-start.10
  25.1 0.0 collective-permute-done.6.up_ref.refs_2_
  25.1 2.7 %collective-permute-start.11 = (bf16[256,384]{1,0:T(8,128)(2,1)S(1)}, bf16[256,384]{1,0:T(8,128)(2,1)S(1)}, u32[]{:S(2)}, u32[]{:S(2)}) collective-permute-start(bf16[256,384]{1,0:T(8,128)(2,1)S(1)} %get-tuple-element.64), channel_id=1, source_target_pairs={{0,24},{1,7},{2,26},{3,1},{4,28},{5,3},{6,30},{7,5},{8,0},{9,15},{... | collective-permute-start | bytes 589832 | tf_op jit(solution)/shard_map/ppermute | solution.py:49
  27.8 0.0 collective-permute-done.7.down_ref.refs_3_
  27.8 0.0 collective-permute-done.8.far_ref.refs_4_
  27.8 5.9 %shard_map.81 = (bf16[256,768]{1,0:T(8,128)(2,1)S(1)}, bf16[256,768]{1,0:T(8,128)(2,1)}, bf16[256,768]{1,0:T(8,128)(2,1)}, bf16[256,768]{1,0:T(8,128)(2,1)}, bf1...) custom-call(s32[1]{0:T(128)} %bitcast.place_ref, bf16[864,128]{1,0:T(8,128)(2,1)S(1)} %get-tuple-element.50.even_ref.refs_0_, ...), custom_call_target="tpu_custom_call" | custom-call | flops 2818572288 | bytes 7012356 | tf_op jit(solution)/shard_map/pallas_call | solution.py:68
  33.7 0.1 collective-permute-done.10.refs_2_
  33.8 0.0 collective-permute-done.11.refs_3_
  33.8 1.5 %collective-permute-start.12 = (bf16[256,768]{1,0:T(8,128)(2,1)}, bf16[256,768]{1,0:T(8,128)(2,1)S(1)}, u32[]{:S(2)}, u32[]{:S(2)}) collective-permute-start(bf16[256,768]{1,0:T(8,128)(2,1)} %get-tuple-element.70), channel_id=1, source_target_pairs={{0,16},{1,5},{2,18},{3,7},{4,20},{5,1},{6,22},{7,3},{8,24},{9,13},... | collective-permute-start | bytes 1179656 | tf_op jit(solution)/shard_map/ppermute | solution.py:49
  35.3 0.7 collective-permute-start.13
  36.0 1.9 %collective-permute-start.14 = (bf16[256,768]{1,0:T(8,128)(2,1)}, bf16[256,768]{1,0:T(8,128)(2,1)S(1)}, u32[]{:S(2)}, u32[]{:S(2)}) collective-permute-start(bf16[256,768]{1,0:T(8,128)(2,1)} %get-tuple-element.72), channel_id=1, source_target_pairs={{0,24},{1,7},{2,26},{3,1},{4,28},{5,3},{6,30},{7,5},{8,0},{9,15},{... | collective-permute-start | bytes 1179656 | tf_op jit(solution)/shard_map/ppermute | solution.py:49
  38.0 6.7 %collective-permute-start.15 = (bf16[3,432,128]{2,1,0:T(8,128)(2,1)}, bf16[3,432,128]{2,1,0:T(8,128)(2,1)}, u32[]{:S(2)}, u32[]{:S(2)}) collective-permute-start(bf16[3,432,128]{2,1,0:T(8,128)(2,1)} %get-tuple-element.75), channel_id=1, source_target_pairs={{0,1},{1,0},{2,3},{3,2},{4,5},{5,4},{6,7},{7,6},{8,9},{9,8},{10,11... | collective-permute-start | bytes 995336 | tf_op jit(solution)/shard_map/ppermute | solution.py:35
  44.6 0.0 collective-permute-start.16
  44.6 6.6 %copy.8 = bf16[9,256,1024]{2,1,0:T(8,128)(2,1)} copy(bf16[9,256,1024]{1,2,0:T(8,128)(2,1)} %bitcast.21) | data formatting | bytes 9437184 | tf_op jit(solution)/shard_map/transpose | solution.py:406
  51.3 0.2 shard_map.82.held_ref
  51.5 0.9 %copy-done.1 = bf16[3,864,128]{2,1,0:T(8,128)(2,1)} copy-done((bf16[3,864,128]{2,1,0:T(8,128)(2,1)}, bf16[3,864,128]{2,1,0:T(8,128)(2,1)S(1)}, u32[]{:S(2)}) %copy-start.1) | copy-done | bytes 663576
  52.4 0.0 collective-permute-done.15.rest_0_
  52.4 0.0 collective-permute-done.13.refs_6_
  52.4 1.1 %shard_map.83 = bf16[256,1152]{1,0:T(8,128)(2,1)} custom-call(bf16[256,384]{1,0:T(8,128)(2,1)S(1)} %get-tuple-element.54.refs_0_, bf16[256,384]{1,0:T(8,128)(2,1)S(1)} %collective-permute-done.9.refs_1_, bf16[256,384]{1,0:T(8,128)(2,1)S(1)} %collective-permute-done.10.refs_2_, bf16[256,384]{1,0:T(8,128)(2,1)S(1)} %collective-permute-done.11.refs_3_, ...), custom_call_target="tpu_custom_call" | custom-call | bytes 2949120 | tf_op jit(solution)/shard_map/pallas_call | solution.py:68
  53.5 8.6 %all-to-all-start = ((bf16[32,8,1152]{2,1,0:T(8,128)(2,1)}), bf16[32,8,1152]{2,1,0:T(8,128)(2,1)S(1)}, u32[]{:S(2)}, u32[]{:S(2)}) async-start(bf16[32,8,1152]{2,1,0:T(8,128)(2,1)} %bitcast.12), calls=%async_computation | async-start | bytes 1179648 | tf_op jit(solution)/shard_map/all_to_all | solution.py:55
  62.1 8.6 %shard_map.84 = bf16[864,1024]{1,0:T(8,128)(2,1)} custom-call(s32[1]{0:T(128)} %bitcast.place_ref, bf16[3,864,128]{2,1,0:T(8,128)(2,1)} %copy-done.1, bf16[3,432,128]{2,1,0:T(8,128)(2,1)} %collective-permute-done.15.rest_0_, bf16[3,432,128]{2,1,0:T(8,128)(2,1)} %collective-permute-done.16.rest_1_, bf16[2304,1024]{1,0:T(8,128)(2,1)} %bitcast.22), custom_call_target="tpu_custom_call" | custom-call | flops 4076863488 | bytes 7815172 | tf_op jit(solution)/shard_map/pallas_call | solution.py:68
  70.6 6.7 %all-to-all-done = bf16[32,8,1152]{2,1,0:T(8,128)(2,1)S(1)} async-done(((bf16[32,8,1152]{2,1,0:T(8,128)(2,1)}), bf16[32,8,1152]{2,1,0:T(8,128)(2,1)S(1)}, u32[]{:S(2)}, u32[]{:S(2)}) %all-to-all-start) | async-done | bytes 589856 | tf_op jit(solution)/shard_map/all_to_all | solution.py:55
  77.4 0.1 convert_reduce_fusion.1
  77.5 5.3 %collective-permute-start.17 = (f32[4,1152]{1,0:T(4,128)S(1)}, f32[4,1152]{1,0:T(4,128)S(1)}, u32[]{:S(2)}, u32[]{:S(2)}) collective-permute-start(f32[4,1152]{1,0:T(4,128)S(1)} %constant_dynamic-slice_fusion), channel_id=1, source_target_pairs={{0,1},{1,0},{2,3},{3,2},{4,5},{5,4},{6,7},{7,6},{8,9},{9,8},{10,11... | collective-permute-start | bytes 55304 | tf_op jit(solution)/shard_map/ppermute | solution.py:35
  82.8 0.8 collective-permute-done.17
  83.6 0.6 pad_maximum_fusion
  (16 shorter events, 0.1 us)
Async XLA Ops:
  0.6 7.6 %copy-start = (bf16[2,6,72,1024]{3,2,1,0:T(8,128)(2,1)S(1)}, bf16[2,6,72,1024]{3,2,1,0:T(8,128)(2,1)}, u32[]{:S(2)}) copy-start(bf16[2,6,72,1024]{3,2,1,0:T(8,128)(2,1)} %param.6) | copy-start | bytes 5308420
  0.6 13.1 %copy-start.3 = (f32[256]{0:T(256)S(1)}, f32[256]{0:T(256)}, u32[]{:S(2)}) copy-start(f32[256]{0:T(256)} %param.10) | copy-start | bytes 3076
  2.5 5.7 %collective-permute-start = (f32[8,256]{1,0:T(8,128)S(1)}, f32[8,256]{1,0:T(8,128)S(1)}, u32[]{:S(2)}, u32[]{:S(2)}) collective-permute-start(f32[8,256]{1,0:T(8,128)S(1)} %reshape.42), channel_id=1, source_target_pairs={{0,1},{1,0},{2,3},{3,2},{4,5},{5,4},{6,7},{7,6},{8,9},{9,8},{10,11... | collective-permute-start | bytes 24584 | tf_op jit(solution)/shard_map/ppermute | solution.py:35
  8.2 10.7 %collective-permute-start.5 = (bf16[864,1024]{1,0:T(8,128)(2,1)S(1)}, bf16[864,1024]{1,0:T(8,128)(2,1)S(1)}, u32[]{:S(2)}, u32[]{:S(2)}) collective-permute-start(bf16[864,1024]{1,0:T(8,128)(2,1)S(1)} %bitcast.18), channel_id=1, source_target_pairs={{0,1},{1,0},{2,3},{3,2},{4,5},{5,4},{6,7},{7,6},{8,9},{9,8},{10,11... | collective-permute-start | bytes 5308424 | tf_op jit(solution)/shard_map/ppermute | solution.py:35
  8.4 5.3 %collective-permute-start.4 = (bf16[2,864,128]{2,1,0:T(8,128)(2,1)}, bf16[2,864,128]{2,1,0:T(8,128)(2,1)S(1)}, u32[]{:S(2)}, u32[]{:S(2)}) collective-permute-start(bf16[2,864,128]{2,1,0:T(8,128)(2,1)} %get-tuple-element.49), channel_id=1, source_target_pairs={{0,1},{1,0},{2,3},{3,2},{4,5},{5,4},{6,7},{7,6},{8,9},{9,8},{10,11... | collective-permute-start | bytes 1327112 | tf_op jit(solution)/shard_map/ppermute | solution.py:35
  8.8 4.0 %collective-permute-start.1 = (f32[8,256]{1,0:T(8,128)S(1)}, f32[8,256]{1,0:T(8,128)S(1)}, u32[]{:S(2)}, u32[]{:S(2)}) collective-permute-start(f32[8,256]{1,0:T(8,128)S(1)} %add.21.a_ref), channel_id=1, source_target_pairs={{0,4},{2,6},{4,0},{6,2},{1,5},{3,7},{5,1},{7,3},{8,12},{10,14},{12... | collective-permute-start | bytes 24584 | tf_op jit(solution)/shard_map/ppermute | solution.py:39
  9.9 3.8 %collective-permute-start.2 = (f32[8,256]{1,0:T(8,128)S(1)}, f32[8,256]{1,0:T(8,128)S(1)}, u32[]{:S(2)}, u32[]{:S(2)}) collective-permute-start(f32[8,256]{1,0:T(8,128)S(1)} %add.21.a_ref), channel_id=1, source_target_pairs={{0,2},{2,4},{4,6},{6,0},{1,3},{3,5},{5,7},{7,1},{8,10},{10,12},{12... | collective-permute-start | bytes 24584 | tf_op jit(solution)/shard_map/ppermute | solution.py:39
  10.2 3.5 %collective-permute-start.3 = (f32[8,256]{1,0:T(8,128)S(1)}, f32[8,256]{1,0:T(8,128)S(1)}, u32[]{:S(2)}, u32[]{:S(2)}) collective-permute-start(f32[8,256]{1,0:T(8,128)S(1)} %add.21.a_ref), channel_id=1, source_target_pairs={{0,6},{2,0},{4,2},{6,4},{1,7},{3,1},{5,3},{7,5},{8,14},{10,8},{12,... | collective-permute-start | bytes 24584 | tf_op jit(solution)/shard_map/ppermute | solution.py:39
  13.7 1.0 %copy-start.2 = (bf16[2,864,128]{2,1,0:T(8,128)(2,1)S(1)}, bf16[2,864,128]{2,1,0:T(8,128)(2,1)}, u32[]{:S(2)}) copy-start(bf16[2,864,128]{2,1,0:T(8,128)(2,1)} %get-tuple-element.48.mine_ref) | copy-start | bytes 1327108
  15.1 10.0 %collective-permute-start.6 = (bf16[864,128]{1,0:T(8,128)(2,1)S(1)}, bf16[864,128]{1,0:T(8,128)(2,1)S(1)}, u32[]{:S(2)}, u32[]{:S(2)}) collective-permute-start(bf16[864,128]{1,0:T(8,128)(2,1)S(1)} %get-tuple-element.50.even_ref.refs_0_), channel_id=1, source_target_pairs={{0,2},{2,4},{4,6},{6,0},{1,3},{3,5},{5,7},{7,1},{8,10},{10,12},{12... | collective-permute-start | bytes 663560 | tf_op jit(solution)/shard_map/ppermute | solution.py:39
  15.5 12.3 %collective-permute-start.7 = (bf16[864,128]{1,0:T(8,128)(2,1)S(1)}, bf16[864,128]{1,0:T(8,128)(2,1)S(1)}, u32[]{:S(2)}, u32[]{:S(2)}) collective-permute-start(bf16[864,128]{1,0:T(8,128)(2,1)S(1)} %get-tuple-element.51.odd_ref.refs_1_), channel_id=1, source_target_pairs={{0,6},{2,0},{4,2},{6,4},{1,7},{3,1},{5,3},{7,5},{8,14},{10,8},{12,... | collective-permute-start | bytes 663560 | tf_op jit(solution)/shard_map/ppermute | solution.py:39
  17.8 10.0 %collective-permute-start.8 = (bf16[864,128]{1,0:T(8,128)(2,1)S(1)}, bf16[864,128]{1,0:T(8,128)(2,1)S(1)}, u32[]{:S(2)}, u32[]{:S(2)}) collective-permute-start(bf16[864,128]{1,0:T(8,128)(2,1)S(1)} %get-tuple-element.56), channel_id=1, source_target_pairs={{0,4},{2,6},{4,0},{6,2},{1,5},{3,7},{5,1},{7,3},{8,12},{10,14},{12... | collective-permute-start | bytes 663560 | tf_op jit(solution)/shard_map/ppermute | solution.py:39
  23.1 10.6 %collective-permute-start.9 = (bf16[256,384]{1,0:T(8,128)(2,1)S(1)}, bf16[256,384]{1,0:T(8,128)(2,1)S(1)}, u32[]{:S(2)}, u32[]{:S(2)}) collective-permute-start(bf16[256,384]{1,0:T(8,128)(2,1)S(1)} %get-tuple-element.62), channel_id=1, source_target_pairs={{0,16},{1,5},{2,18},{3,7},{4,20},{5,1},{6,22},{7,3},{8,24},{9,13},... | collective-permute-start | bytes 589832 | tf_op jit(solution)/shard_map/ppermute | solution.py:49
  25.1 8.7 %collective-permute-start.10 = (bf16[256,384]{1,0:T(8,128)(2,1)S(1)}, bf16[256,384]{1,0:T(8,128)(2,1)S(1)}, u32[]{:S(2)}, u32[]{:S(2)}) collective-permute-start(bf16[256,384]{1,0:T(8,128)(2,1)S(1)} %get-tuple-element.63), channel_id=1, source_target_pairs={{0,8},{1,3},{2,10},{3,5},{4,12},{5,7},{6,14},{7,1},{8,16},{9,11},{... | collective-permute-start | bytes 589832 | tf_op jit(solution)/shard_map/ppermute | solution.py:49
  25.1 8.7 %collective-permute-start.11 = (bf16[256,384]{1,0:T(8,128)(2,1)S(1)}, bf16[256,384]{1,0:T(8,128)(2,1)S(1)}, u32[]{:S(2)}, u32[]{:S(2)}) collective-permute-start(bf16[256,384]{1,0:T(8,128)(2,1)S(1)} %get-tuple-element.64), channel_id=1, source_target_pairs={{0,24},{1,7},{2,26},{3,1},{4,28},{5,3},{6,30},{7,5},{8,0},{9,15},{... | collective-permute-start | bytes 589832 | tf_op jit(solution)/shard_map/ppermute | solution.py:49
  33.8 18.6 %collective-permute-start.12 = (bf16[256,768]{1,0:T(8,128)(2,1)}, bf16[256,768]{1,0:T(8,128)(2,1)S(1)}, u32[]{:S(2)}, u32[]{:S(2)}) collective-permute-start(bf16[256,768]{1,0:T(8,128)(2,1)} %get-tuple-element.70), channel_id=1, source_target_pairs={{0,16},{1,5},{2,18},{3,7},{4,20},{5,1},{6,22},{7,3},{8,24},{9,13},... | collective-permute-start | bytes 1179656 | tf_op jit(solution)/shard_map/ppermute | solution.py:49
  35.3 17.1 %collective-permute-start.13 = (bf16[256,768]{1,0:T(8,128)(2,1)}, bf16[256,768]{1,0:T(8,128)(2,1)S(1)}, u32[]{:S(2)}, u32[]{:S(2)}) collective-permute-start(bf16[256,768]{1,0:T(8,128)(2,1)} %get-tuple-element.71), channel_id=1, source_target_pairs={{0,8},{1,3},{2,10},{3,5},{4,12},{5,7},{6,14},{7,1},{8,16},{9,11},{... | collective-permute-start | bytes 1179656 | tf_op jit(solution)/shard_map/ppermute | solution.py:49
  36.0 16.4 %collective-permute-start.14 = (bf16[256,768]{1,0:T(8,128)(2,1)}, bf16[256,768]{1,0:T(8,128)(2,1)S(1)}, u32[]{:S(2)}, u32[]{:S(2)}) collective-permute-start(bf16[256,768]{1,0:T(8,128)(2,1)} %get-tuple-element.72), channel_id=1, source_target_pairs={{0,24},{1,7},{2,26},{3,1},{4,28},{5,3},{6,30},{7,5},{8,0},{9,15},{... | collective-permute-start | bytes 1179656 | tf_op jit(solution)/shard_map/ppermute | solution.py:49
  38.0 14.4 %collective-permute-start.15 = (bf16[3,432,128]{2,1,0:T(8,128)(2,1)}, bf16[3,432,128]{2,1,0:T(8,128)(2,1)}, u32[]{:S(2)}, u32[]{:S(2)}) collective-permute-start(bf16[3,432,128]{2,1,0:T(8,128)(2,1)} %get-tuple-element.75), channel_id=1, source_target_pairs={{0,1},{1,0},{2,3},{3,2},{4,5},{5,4},{6,7},{7,6},{8,9},{9,8},{10,11... | collective-permute-start | bytes 995336 | tf_op jit(solution)/shard_map/ppermute | solution.py:35
  44.6 7.8 %collective-permute-start.16 = (bf16[3,432,128]{2,1,0:T(8,128)(2,1)}, bf16[3,432,128]{2,1,0:T(8,128)(2,1)}, u32[]{:S(2)}, u32[]{:S(2)}) collective-permute-start(bf16[3,432,128]{2,1,0:T(8,128)(2,1)} %get-tuple-element.76), channel_id=1, source_target_pairs={{0,1},{1,0},{2,3},{3,2},{4,5},{5,4},{6,7},{7,6},{8,9},{9,8},{10,11... | collective-permute-start | bytes 995336 | tf_op jit(solution)/shard_map/ppermute | solution.py:35
  51.5 0.9 %copy-start.1 = (bf16[3,864,128]{2,1,0:T(8,128)(2,1)}, bf16[3,864,128]{2,1,0:T(8,128)(2,1)S(1)}, u32[]{:S(2)}) copy-start(bf16[3,864,128]{2,1,0:T(8,128)(2,1)S(1)} %shard_map.82.held_ref) | copy-start | bytes 1990660
  53.5 23.9 %all-to-all-start = ((bf16[32,8,1152]{2,1,0:T(8,128)(2,1)}), bf16[32,8,1152]{2,1,0:T(8,128)(2,1)S(1)}, u32[]{:S(2)}, u32[]{:S(2)}) async-start(bf16[32,8,1152]{2,1,0:T(8,128)(2,1)} %bitcast.12), calls=%async_computation | async-start | bytes 1179648 | tf_op jit(solution)/shard_map/all_to_all | solution.py:55
  77.5 6.1 %collective-permute-start.17 = (f32[4,1152]{1,0:T(4,128)S(1)}, f32[4,1152]{1,0:T(4,128)S(1)}, u32[]{:S(2)}, u32[]{:S(2)}) collective-permute-start(f32[4,1152]{1,0:T(4,128)S(1)} %constant_dynamic-slice_fusion), channel_id=1, source_target_pairs={{0,1},{1,0},{2,3},{3,2},{4,5},{5,4},{6,7},{7,6},{8,9},{9,8},{10,11... | collective-permute-start | bytes 55304 | tf_op jit(solution)/shard_map/ppermute | solution.py:35

commit v11 on v9

--- a/solution.py
+++ b/solution.py
@@ -87,33 +87,29 @@
     steps = 2
     tall = cells // steps
 
-    def body(place_ref, conv_ref, grad_ref, mask_ref, mine_ref, sent_ref):
+    def body(place_ref, conv_ref, grad_ref, mask_ref, sent_ref):
         first = core_of(place_ref) == 0
         passed = (grad_ref[...].astype(F32) * mask_ref[...].astype(F32)).astype(BF16)
         for which, value in enumerate((conv_ref[...], passed)):
-            lower, upper = value[:, :half], value[:, half:]
-            mine_ref[which] = jnp.where(first, lower, upper)
-            sent_ref[which] = jnp.where(first, upper, lower)
+            sent_ref[which] = jnp.where(first, value[:, half:], value[:, :half])
 
     rows = pl.BlockSpec((tall, channels), lambda i: (i, 0))
-    out = jax.ShapeDtypeStruct((2, cells, half), BF16)
-    spec = pl.BlockSpec((2, tall, half), lambda i: (0, i, 0))
     return kernel_call(
         body,
         (place, conv, grad, mask),
         [SMEM, rows, rows, rows],
-        [out, out],
-        [spec, spec],
+        [jax.ShapeDtypeStruct((2, cells, half), BF16)],
+        [pl.BlockSpec((2, tall, half), lambda i: (0, i, 0))],
         (steps,),
         vmem=60,
-    )
+    )[0]
 
 
 def pre_gradient(place, gain, sums, mine, theirs, images, cell_count):
-    _, cells, half = mine.shape
+    _, cells, half = theirs.shape
     each = cells // images
 
-    def body(place_ref, gain_ref, a_ref, b_ref, c_ref, d_ref, mine_ref, theirs_ref, even_ref, odd_ref, far_ref):
+    def body(place_ref, gain_ref, a_ref, b_ref, c_ref, d_ref, conv_ref, passed_ref, theirs_ref, even_ref, odd_ref, far_ref):
         first = core_of(place_ref) == 0
         early = x_of(place_ref) < X // 2
         means = (a_ref[...] + b_ref[...] + c_ref[...] + d_ref[...]) / cell_count
@@ -128,8 +124,8 @@
             grad_mean = gain_row * passed_mean
             cross_mean = gain_row * (product_mean - chan_mean * passed_mean) * inv_std
             blocks = []
-            for ref in (mine_ref, theirs_ref):
-                values, passed = ref[0, rows, :].astype(F32), ref[1, rows, :].astype(F32)
+            for conv, grad in ((conv_ref, passed_ref), (theirs_ref.at[0], theirs_ref.at[1])):
+                values, passed = conv[rows, :].astype(F32), grad[rows, :].astype(F32)
                 normed = (values - chan_mean) * inv_std
                 blocks.append(inv_std * (gain_row * passed - grad_mean - normed * cross_mean))
             even = jnp.where(first, blocks[0], blocks[1])
@@ -141,8 +137,9 @@
     out = jax.ShapeDtypeStruct((cells, half), BF16)
     return kernel_call(
         body,
-        (place, gain, *sums, mine, theirs),
-        [SMEM, whole(gain.shape)] + [whole(sums[0].shape)] * 4 + [whole(mine.shape)] * 2,
+        (place, gain, *sums, *mine, theirs),
+        [SMEM, whole(gain.shape)] + [whole(sums[0].shape)] * 4 + [whole((cells, half))] * 2
+        + [whole(theirs.shape)],
         [out] * 3,
         [whole(out.shape)] * 3,
     )
@@ -286,8 +283,7 @@
     cells, width = up.shape
 
     def body(place_ref, even_ref, odd_ref, up_ref, down_ref, far_ref, lhs_ref, *rest):
-        theirs_refs = rest[4:6]
-        stacked, total = rest[6:]
+        theirs_ref, stacked, total = rest[4:]
 
         @pl.when(pl.program_id(0) == 0)
         def _():
@@ -296,8 +292,7 @@
             blocks = tap_blocks(place_ref, even_ref, odd_ref, up_ref, down_ref, far_ref)
             for side, (lower, upper) in enumerate(blocks):
                 theirs = jnp.where(first, upper, lower)
-                for part, ref in enumerate(theirs_refs):
-                    ref[side] = theirs[part * (cells // 2) : (part + 1) * (cells // 2)]
+                theirs_ref[side] = theirs
                 if side != 1:
                     mine = jnp.where(first, lower, upper)
                     fill(stacked, 0, 3 * (side // 2), mine, col_count)
@@ -305,8 +300,8 @@
 
         multiply(place_ref, lhs_ref, stacked, total, rest[:4])
 
-    part = jax.ShapeDtypeStruct((3, cells // 2, width), BF16)
-    return product_call(body, place, [even, odd, up, down, far], lhs, 6 * width, [part, part])
+    triple = jax.ShapeDtypeStruct((3, cells, width), BF16)
+    return product_call(body, place, [even, odd, up, down, far], lhs, 6 * width, [triple])
 
 
 def first_sum(middle, sides):
@@ -337,15 +332,13 @@
     deep, channels_in = weight.shape
     width = 256
 
-    def body(place_ref, held_ref, *rest):
-        got_refs, (weight_ref, out_ref, stacked) = rest[:2], rest[2:]
+    def body(place_ref, held_ref, got_ref, weight_ref, out_ref, stacked):
 
         @pl.when(pl.program_id(0) == 0)
         def _():
             first = core_of(place_ref) == 0
             for side in range(3):
-                mine = held_ref[side]
-                theirs = jnp.concatenate([ref[side] for ref in got_refs], axis=0)
+                mine, theirs = held_ref[side], got_ref[side]
                 lower, upper = jnp.where(first, mine, theirs), jnp.where(first, theirs, mine)
                 for part, block in enumerate((lower, upper)):
                     for spot, tap in enumerate(column_taps(block, col_count)):
@@ -358,8 +351,8 @@
 
     return kernel_call(
         body,
-        (place, held, *got, weight),
-        [SMEM, whole(held.shape)] + [whole(block.shape) for block in got] + [pl.BlockSpec((deep, width), lambda i: (0, i))],
+        (place, held, got, weight),
+        [SMEM, whole(held.shape), whole(got.shape)] + [pl.BlockSpec((deep, width), lambda i: (0, i))],
         [jax.ShapeDtypeStruct((cells, channels_in), BF16)],
         [pl.BlockSpec((cells, width), lambda i: (0, i))],
         (channels_in // width,),
@@ -381,14 +374,16 @@
     input_flat = inputs.reshape(cells, channels_in)
     sums = channel_sums(conv_out, grad_out, relu_mask)
     got_sums = swapped(sums)
-    mine, sent = prepare(
-        place,
-        *(value.reshape(cells, channels_out) for value in (conv_out, grad_out, relu_mask)),
-    )
+    flat = [value.reshape(cells, channels_out) for value in (conv_out, grad_out, relu_mask)]
+    sent = prepare(place, *flat)
     input_flat, sent, got_sums = lax.optimization_barrier((input_flat, sent, got_sums))
     theirs = swapped(sent)
     input_other = swapped(input_flat)
     sums = sums + got_sums
+    conv_half, grad_half, mask_half = (
+        lax.dynamic_slice_in_dim(value, core * half, half, axis=1) for value in flat
+    )
+    mine = [conv_half, (grad_half.astype(F32) * mask_half.astype(F32)).astype(BF16)]
     sums = [sums] + [around(sums, steps) for steps in (2, 1, 3)]
     lhs = transposed(input_flat, input_other)
     gain = norm_gain.reshape(1, channels_out)
@@ -400,16 +395,15 @@
     middle = list(middle_terms(place, even, odd, lhs, col_count))
     side_place, middle[0] = lax.optimization_barrier((place, middle[0]))
     middle = [middle[0]] + [crossed(middle[steps], steps) for steps in (2, 1, 3)]
-    *sides, sent_lower, sent_upper = side_terms(side_place, even, odd, up, down, far, lhs, col_count)
-    sent = [sent_lower, sent_upper]
+    *sides, sent = side_terms(side_place, even, odd, up, down, far, lhs, col_count)
     sides[1:], sent, middle[1:] = lax.optimization_barrier((sides[1:], sent, middle[1:]))
-    got = [swapped(block) for block in sent]
+    got = swapped(sent)
     weight, sides[0] = lax.optimization_barrier((weight, sides[0]))
     weight = jnp.transpose(weight, (1, 2, 0)).reshape(9 * channels_out, channels_in)
     sides = [sides[0]] + [crossed(sides[steps], steps) for steps in (2, 1, 3)]
     held_place, weight = lax.optimization_barrier((place, weight))
     held = own_blocks(held_place, even, odd, up, down, far)
-    sides, weight, got, held = lax.optimization_barrier((sides, weight, got, held))
+    sides, weight, held = lax.optimization_barrier((sides, weight, held))
     merged = first_sum(middle, sides)
     place, merged = lax.optimization_barrier((place, merged))
     input_grad = input_gradient(place, held, got, weight, col_count)

time: 84.1 us -> 83.7 us (level)
  waiting for transfers between devices: 9.25 us -> 3.67 us
  local copies, waits for them, and re-layouts: 8.55 us -> 10.8 us
  other arithmetic: 2.6 us -> 4.43 us
    all_to_all x1, waiting for transfers between devices: 6.64 us -> 0.01 us  [exchanged(): return lax.all_to_all(value, AXES, 0, 0, axis_index_groups=groups)]
    all_to_all x1, starting transfers between devices: 8.58 us -> 11 us  [exchanged(): return lax.all_to_all(value, AXES, 0, 0, axis_index_groups=groups)]
    ppermute x6 -> x5, starting transfers between devices: 15.3 us -> 13.3 us  [swapped(): return lax.ppermute(value, 'core', [(0, 1), (1, 0)])]
    ppermute x6 -> x5, waiting for transfers between devices: 0.85 us -> 2.59 us  [swapped(): return lax.ppermute(value, 'core', [(0, 1), (1, 0)])]
    unnamed x8 -> x34, local copies, waits for them, and re-layouts: 1.9 us -> 3.17 us
    ppermute x6, waiting for transfers between devices: 1.17 us -> 0.02 us  [around(): lax.ppermute(value, 'x', [(source, (source + steps) % X) for source in ra...]
    convert_element_type x0 -> x1, other arithmetic: none -> 1.13 us  [per_device(): (grad_half.astype(F32) * mask_half.astype(F32)).astype(BF16)]
    dynamic_slice x0 -> x1, local copies, waits for them, and re-layouts: none -> 0.95 us  [per_device(): lax.dynamic_slice_in_dim(value, core * half, half, axis=1)]
  transfers between devices with their start and end apart: 19 -> 18, of which waited for: 5 -> 3; matrix products, arithmetic and copies ran while one was open for 8% -> 11% of each run, Pallas kernels for 25% -> 26%
where the time goes in v11:
time: 83.7 us; the launch traced here: 83.1 us
  starting transfers between devices  40.6 us (49%)
  Pallas kernels  22.7 us (27%)
  local copies, waits for them, and re-layouts  10.8 us (13%)
  other arithmetic  4.43 us (5%)
  waiting for transfers between devices  3.67 us (4%)
  between operations  0.88 us (1%)
    pallas_call x8, Pallas kernels, kernel_call(): pl.pallas_call(body, grid=grid, in_specs=in_specs, out_specs=out_specs, o...  22.7 us
    ppermute x5, starting transfers between devices, swapped(): return lax.ppermute(value, 'core', [(0, 1), (1, 0)])  13.3 us
    all_to_all x1, starting transfers between devices, exchanged(): return lax.all_to_all(value, AXES, 0, 0, axis_index_groups=groups)  11 us
    ppermute x6, starting transfers between devices, crossed(): return lax.ppermute(value, AXES, pairs)  8.74 us
    ppermute x6, starting transfers between devices, around(): lax.ppermute(value, 'x', [(source, (source + steps) % X) for source in ra...  7.48 us
    transpose x1, local copies, waits for them, and re-layouts, per_device(): jnp.transpose(weight, (1, 2, 0)).reshape(9 * channels_out, channels_in)  6.7 us
    unnamed x34, local copies, waits for them, and re-layouts  3.17 us
    ppermute x5, waiting for transfers between devices, swapped(): return lax.ppermute(value, 'core', [(0, 1), (1, 0)])  2.59 us
  transfers between devices with their start and end apart: 18, of which 3 were waited for; matrix products, arithmetic and copies ran while one was open for 11% of the time, Pallas kernels for 26%

profile of v11, /device:TPU:1, one launch (start us, length us, event | category | flops | bytes accessed | tf_op | source)
XLA Modules:
  0.0 83.1 jit_solution(1672793293798675479)
XLA Ops:
  0.6 1.9 %fusion.2 = (f32[2,256]{1,0:T(2,128)S(1)}, f32[2,256]{1,0:T(2,128)S(1)}, f32[2,256]{1,0:T(2,128)S(1)}, f32[2,256]{1,0:T(2,128)S(1)}) fusion(s32[2,6,72,256]{3,2,1,0:T(8,128)} %param.9, bf16[2,6,72,256]{3,2,1,0:T(8,128)(2,1)} %param.8, bf16[2,6,72,256]{3,2,1,0:T(8,128)(2,1)} %param.7), kind=kLoop, calls=%fused_computation.7 | loop fusion | flops 2209792 | bytes 1777664 | tf_op jit(solution)/shard_map/reduce_sum | solution.py:81
  2.5 3.3 %collective-permute-start = (f32[8,256]{1,0:T(8,128)S(1)}, f32[8,256]{1,0:T(8,128)S(1)}, u32[]{:S(2)}, u32[]{:S(2)}) collective-permute-start(f32[8,256]{1,0:T(8,128)S(1)} %reshape.42), channel_id=1, source_target_pairs={{0,1},{1,0},{2,3},{3,2},{4,5},{5,4},{6,7},{7,6},{8,9},{9,8},{10,11... | collective-permute-start | bytes 24584 | tf_op jit(solution)/shard_map/ppermute | solution.py:35
  5.9 2.3 %shard_map.77 = bf16[2,864,128]{2,1,0:T(8,128)(2,1)} custom-call(s32[1]{0:T(128)} %bitcast.place_ref, bf16[864,256]{1,0:T(8,128)(2,1)} %bitcast.25, bf16[864,256]{1,0:T(8,128)(2,1)} %bitcast.27, s32[864,256]{1,0:T(8,128)} %bitcast.21), custom_call_target="tpu_custom_call" | custom-call | bytes 2211844 | tf_op jit(solution)/shard_map/pallas_call | solution.py:65
  8.1 0.0 collective-permute-done
  8.1 0.6 copy-done.15
  8.7 0.1 collective-permute-start.5
  8.8 0.5 collective-permute-start.4
  9.3 0.9 %constant_dynamic-slice_fusion.1.conv_ref = bf16[864,128]{1,0:T(8,128)(2,1)S(1)} fusion(bf16[864,256]{1,0:T(8,128)(2,1)} %bitcast.26, s32[]{:T(128)S(6)} %select_n.29), kind=kLoop, calls=%fused_computation.15 | loop fusion | bytes 442372 | tf_op jit(solution)/shard_map/dynamic_slice | solution.py:384
  10.2 0.7 add.26.a_ref
  10.9 1.0 %collective-permute-start.1 = (f32[8,256]{1,0:T(8,128)S(1)}, f32[8,256]{1,0:T(8,128)S(1)}, u32[]{:S(2)}, u32[]{:S(2)}) collective-permute-start(f32[8,256]{1,0:T(8,128)S(1)} %add.26.a_ref), channel_id=1, source_target_pairs={{0,4},{2,6},{4,0},{6,2},{1,5},{3,7},{5,1},{7,3},{8,12},{10,14},{12... | collective-permute-start | bytes 24584 | tf_op jit(solution)/shard_map/ppermute | solution.py:39
  11.9 0.3 collective-permute-start.2
  12.2 2.4 %collective-permute-start.3 = (f32[8,256]{1,0:T(8,128)S(1)}, f32[8,256]{1,0:T(8,128)S(1)}, u32[]{:S(2)}, u32[]{:S(2)}) collective-permute-start(f32[8,256]{1,0:T(8,128)S(1)} %add.26.a_ref), channel_id=1, source_target_pairs={{0,6},{2,0},{4,2},{6,4},{1,7},{3,1},{5,3},{7,5},{8,14},{10,8},{12,... | collective-permute-start | bytes 24584 | tf_op jit(solution)/shard_map/ppermute | solution.py:39
  14.6 1.1 %multiply_convert_fusion.passed_ref = bf16[864,128]{1,0:T(8,128)(2,1)S(1)} fusion(s32[864,256]{1,0:T(8,128)} %bitcast.22, s32[]{:T(128)S(6)} %select_n.29, bf16[864,256]{1,0:T(8,128)(2,1)} %bitcast.28), kind=kLoop, calls=%fused_computation.8 | loop fusion | flops 442368 | bytes 884740 | tf_op jit(solution)/shard_map/convert_element_type | solution.py:386
  15.7 0.0 collective-permute-done.3.d_ref
  15.8 1.4 %shard_map.78 = (bf16[864,128]{1,0:T(8,128)(2,1)S(1)}, bf16[864,128]{1,0:T(8,128)(2,1)S(1)}, bf16[864,128]{1,0:T(8,128)(2,1)S(1)}) custom-call(s32[1]{0:T(128)} %bitcast.place_ref, f32[1,256]{1,0:T(1,128)S(1)} %bitcast.20, f32[8,256]{1,0:T(8,128)S(1)} %add.26.a_ref, f32[8,256]{1,0:T(8,128)S(1)} %collective-permute-done.1.b_ref, ...), custom_call_target="tpu_custom_call" | custom-call | bytes 1582084 | tf_op jit(solution)/shard_map/pallas_call | solution.py:65
  17.2 0.4 collective-permute-start.6
  17.5 2.4 %collective-permute-start.7 = (bf16[864,128]{1,0:T(8,128)(2,1)S(1)}, bf16[864,128]{1,0:T(8,128)(2,1)S(1)}, u32[]{:S(2)}, u32[]{:S(2)}) collective-permute-start(bf16[864,128]{1,0:T(8,128)(2,1)S(1)} %get-tuple-element.43.odd_ref.refs_1_), channel_id=1, source_target_pairs={{0,6},{2,0},{4,2},{6,4},{1,7},{3,1},{5,3},{7,5},{8,14},{10,8},{12,... | collective-permute-start | bytes 663560 | tf_op jit(solution)/shard_map/ppermute | solution.py:39
  19.9 1.0 %collective-permute-start.8 = (bf16[864,128]{1,0:T(8,128)(2,1)S(1)}, bf16[864,128]{1,0:T(8,128)(2,1)S(1)}, u32[]{:S(2)}, u32[]{:S(2)}) collective-permute-start(bf16[864,128]{1,0:T(8,128)(2,1)S(1)} %get-tuple-element.48), channel_id=1, source_target_pairs={{0,4},{2,6},{4,0},{6,2},{1,5},{3,7},{5,1},{7,3},{8,12},{10,14},{12... | collective-permute-start | bytes 663560 | tf_op jit(solution)/shard_map/ppermute | solution.py:39
  21.0 1.7 %shard_map.79.lhs_ref = bf16[1024,1792]{1,0:T(8,128)(2,1)S(1)} custom-call(bf16[864,1024]{1,0:T(8,128)(2,1)S(1)} %bitcast.19, bf16[864,1024]{1,0:T(8,128)(2,1)S(1)} %collective-permute-done.5.other_ref), custom_call_target="tpu_custom_call" | custom-call | bytes 7208960 | tf_op jit(solution)/shard_map/pallas_call | solution.py:65
  22.7 2.7 %shard_map.80 = (bf16[256,384]{1,0:T(8,128)(2,1)S(1)}, bf16[256,384]{1,0:T(8,128)(2,1)S(1)}, bf16[256,384]{1,0:T(8,128)(2,1)S(1)}, bf16[256,384]{1,0:T(8,128)(2,1)S(1)}) custom-call(s32[1]{0:T(128)} %bitcast.place_ref, bf16[864,128]{1,0:T(8,128)(2,1)S(1)} %get-tuple-element.42.even_ref.refs_0_, bf16[864,128]{1,0:T(8,128)(2,1)S(1)} %get-tuple-element.43.odd_ref.refs_1_, ...), custom_call_target="tpu_custom_call" | custom-call | flops 1409286144 | bytes 4898820 | tf_op jit(solution)/shard_map/pallas_call | solution.py:65
  25.4 2.0 %collective-permute-start.9 = (bf16[256,384]{1,0:T(8,128)(2,1)S(1)}, bf16[256,384]{1,0:T(8,128)(2,1)S(1)}, u32[]{:S(2)}, u32[]{:S(2)}) collective-permute-start(bf16[256,384]{1,0:T(8,128)(2,1)S(1)} %get-tuple-element.53), channel_id=1, source_target_pairs={{0,16},{1,5},{2,18},{3,7},{4,20},{5,1},{6,22},{7,3},{8,24},{9,13},... | collective-permute-start | bytes 589832 | tf_op jit(solution)/shard_map/ppermute | solution.py:49
  27.4 0.0 collective-permute-start.10
  27.4 0.0 collective-permute-done.6.up_ref.refs_2_
  27.4 2.7 %collective-permute-start.11 = (bf16[256,384]{1,0:T(8,128)(2,1)S(1)}, bf16[256,384]{1,0:T(8,128)(2,1)S(1)}, u32[]{:S(2)}, u32[]{:S(2)}) collective-permute-start(bf16[256,384]{1,0:T(8,128)(2,1)S(1)} %get-tuple-element.55), channel_id=1, source_target_pairs={{0,24},{1,7},{2,26},{3,1},{4,28},{5,3},{6,30},{7,5},{8,0},{9,15},{... | collective-permute-start | bytes 589832 | tf_op jit(solution)/shard_map/ppermute | solution.py:49
  30.1 0.0 collective-permute-done.7.down_ref.refs_3_
  30.1 0.0 collective-permute-done.8.far_ref.refs_4_
  30.1 5.0 %shard_map.81 = (bf16[256,768]{1,0:T(8,128)(2,1)S(1)}, bf16[256,768]{1,0:T(8,128)(2,1)}, bf16[256,768]{1,0:T(8,128)(2,1)}, bf16[256,768]{1,0:T(8,128)(2,1)}, bf16[3,864,128]{2,1,0:T(8,128)(2,1)S(1)}) custom-call(s32[1]{0:T(128)} %bitcast.place_ref, bf16[864,128]{1,0:T(8,128)(2,1)S(1)} %get-tuple-element.42.even_ref.refs_0_, ...), custom_call_target="tpu_custom_call" | custom-call | flops 2818572288 | bytes 7012356 | tf_op jit(solution)/shard_map/pallas_call | solution.py:65
  35.1 0.0 copy-start.13
  35.2 0.8 copy-done.13
  36.0 0.0 collective-permute-done.9.refs_1_
  36.0 0.0 collective-permute-done.10.refs_2_
  36.0 1.4 %collective-permute-start.12 = (bf16[256,768]{1,0:T(8,128)(2,1)}, bf16[256,768]{1,0:T(8,128)(2,1)S(1)}, u32[]{:S(2)}, u32[]{:S(2)}) collective-permute-start(bf16[256,768]{1,0:T(8,128)(2,1)} %get-tuple-element.61), channel_id=1, source_target_pairs={{0,16},{1,5},{2,18},{3,7},{4,20},{5,1},{6,22},{7,3},{8,24},{9,13},... | collective-permute-start | bytes 1179656 | tf_op jit(solution)/shard_map/ppermute | solution.py:49
  37.4 0.8 collective-permute-start.13
  38.1 1.9 %collective-permute-start.14 = (bf16[256,768]{1,0:T(8,128)(2,1)}, bf16[256,768]{1,0:T(8,128)(2,1)S(1)}, u32[]{:S(2)}, u32[]{:S(2)}) collective-permute-start(bf16[256,768]{1,0:T(8,128)(2,1)} %get-tuple-element.63), channel_id=1, source_target_pairs={{0,24},{1,7},{2,26},{3,1},{4,28},{5,3},{6,30},{7,5},{8,0},{9,15},{... | collective-permute-start | bytes 1179656 | tf_op jit(solution)/shard_map/ppermute | solution.py:49
  40.1 6.7 %copy.8 = bf16[9,256,1024]{2,1,0:T(8,128)(2,1)} copy(bf16[9,256,1024]{1,2,0:T(8,128)(2,1)} %bitcast.23) | data formatting | bytes 9437184 | tf_op jit(solution)/shard_map/transpose | solution.py:402
  46.8 0.2 shard_map.82.held_ref
  47.0 0.8 %copy-done.1 = bf16[3,864,128]{2,1,0:T(8,128)(2,1)} copy-done((bf16[3,864,128]{2,1,0:T(8,128)(2,1)}, bf16[3,864,128]{2,1,0:T(8,128)(2,1)S(1)}, u32[]{:S(2)}) %copy-start.1) | copy-done | bytes 663576
  47.9 1.0 %collective-permute-done.13.refs_6_ = bf16[256,768]{1,0:T(8,128)(2,1)S(1)} collective-permute-done((bf16[256,768]{1,0:T(8,128)(2,1)}, bf16[256,768]{1,0:T(8,128)(2,1)S(1)}, u32[]{:S(2)}, u32[]{:S(2)}) %collective-permute-start.13) | collective-permute-done | bytes 393248 | tf_op jit(solution)/shard_map/ppermute | solution.py:49
  48.9 1.1 %shard_map.83 = bf16[256,1152]{1,0:T(8,128)(2,1)} custom-call(bf16[256,384]{1,0:T(8,128)(2,1)S(1)} %get-tuple-element.46.refs_0_, bf16[256,384]{1,0:T(8,128)(2,1)S(1)} %collective-permute-done.9.refs_1_, bf16[256,384]{1,0:T(8,128)(2,1)S(1)} %collective-permute-done.10.refs_2_, bf16[256,384]{1,0:T(8,128)(2,1)S(1)} %collective-permute-done.11.refs_3_, ...), custom_call_target="tpu_custom_call" | custom-call | bytes 2949120 | tf_op jit(solution)/shard_map/pallas_call | solution.py:65
  50.0 11.0 %all-to-all-start = ((bf16[32,8,1152]{2,1,0:T(8,128)(2,1)}), bf16[32,8,1152]{2,1,0:T(8,128)(2,1)S(1)}, u32[]{:S(2)}, u32[]{:S(2)}) async-start(bf16[32,8,1152]{2,1,0:T(8,128)(2,1)} %bitcast.12), calls=%async_computation | async-start | bytes 1179648 | tf_op jit(solution)/shard_map/all_to_all | solution.py:55
  61.1 6.1 %collective-permute-start.15 = (bf16[3,864,128]{2,1,0:T(8,128)(2,1)S(1)}, bf16[3,864,128]{2,1,0:T(8,128)(2,1)S(1)}, u32[]{:S(2)}, u32[]{:S(2)}) collective-permute-start(bf16[3,864,128]{2,1,0:T(8,128)(2,1)S(1)} %copy-done.14), channel_id=1, source_target_pairs={{0,1},{1,0},{2,3},{3,2},{4,5},{5,4},{6,7},{7,6},{8,9},{9,8},{10,11... | collective-permute-start | bytes 1990664 | tf_op jit(solution)/shard_map/ppermute | solution.py:35
  67.1 1.7 %collective-permute-done.15.got_ref = bf16[3,864,128]{2,1,0:T(8,128)(2,1)S(1)} collective-permute-done((bf16[3,864,128]{2,1,0:T(8,128)(2,1)S(1)}, bf16[3,864,128]{2,1,0:T(8,128)(2,1)S(1)}, u32[]{:S(2)}, u32[]{:S(2)}) %collective-permute-start.15) | collective-permute-done | bytes 663584 | tf_op jit(solution)/shard_map/ppermute | solution.py:35
  68.9 0.8 %copy-done.16 = bf16[3,864,128]{2,1,0:T(8,128)(2,1)} copy-done((bf16[3,864,128]{2,1,0:T(8,128)(2,1)}, bf16[3,864,128]{2,1,0:T(8,128)(2,1)S(1)}, u32[]{:S(2)}) %copy-start.16) | copy-done | bytes 663576
  69.7 8.4 %shard_map.84 = bf16[864,1024]{1,0:T(8,128)(2,1)} custom-call(s32[1]{0:T(128)} %bitcast.place_ref, bf16[3,864,128]{2,1,0:T(8,128)(2,1)} %copy-done.1, bf16[3,864,128]{2,1,0:T(8,128)(2,1)} %copy-done.16, bf16[2304,1024]{1,0:T(8,128)(2,1)} %bitcast.24), custom_call_target="tpu_custom_call" | custom-call | flops 4076863488 | bytes 7815172 | tf_op jit(solution)/shard_map/pallas_call | solution.py:65
  78.1 0.1 convert_reduce_fusion.1
  78.3 3.4 %collective-permute-start.16 = (f32[4,1152]{1,0:T(4,128)S(1)}, f32[4,1152]{1,0:T(4,128)S(1)}, u32[]{:S(2)}, u32[]{:S(2)}) collective-permute-start(f32[4,1152]{1,0:T(4,128)S(1)} %constant_dynamic-slice_fusion), channel_id=1, source_target_pairs={{0,1},{1,0},{2,3},{3,2},{4,5},{5,4},{6,7},{7,6},{8,9},{9,8},{10,11... | collective-permute-start | bytes 55304 | tf_op jit(solution)/shard_map/ppermute | solution.py:35
  81.6 0.8 %collective-permute-done.16 = f32[4,1152]{1,0:T(4,128)S(1)} collective-permute-done((f32[4,1152]{1,0:T(4,128)S(1)}, f32[4,1152]{1,0:T(4,128)S(1)}, u32[]{:S(2)}, u32[]{:S(2)}) %collective-permute-start.16) | collective-permute-done | bytes 18464 | tf_op jit(solution)/shard_map/ppermute | solution.py:35
  82.5 0.6 pad_maximum_fusion
  (42 shorter events, 0.1 us)
Async XLA Ops:
  0.6 8.1 %copy-start = (bf16[2,6,72,1024]{3,2,1,0:T(8,128)(2,1)S(1)}, bf16[2,6,72,1024]{3,2,1,0:T(8,128)(2,1)}, u32[]{:S(2)}) copy-start(bf16[2,6,72,1024]{3,2,1,0:T(8,128)(2,1)} %param.6) | copy-start | bytes 5308420
  2.5 5.6 %collective-permute-start = (f32[8,256]{1,0:T(8,128)S(1)}, f32[8,256]{1,0:T(8,128)S(1)}, u32[]{:S(2)}, u32[]{:S(2)}) collective-permute-start(f32[8,256]{1,0:T(8,128)S(1)} %reshape.42), channel_id=1, source_target_pairs={{0,1},{1,0},{2,3},{3,2},{4,5},{5,4},{6,7},{7,6},{8,9},{9,8},{10,11... | collective-permute-start | bytes 24584 | tf_op jit(solution)/shard_map/ppermute | solution.py:35
  5.8 9.9 %copy-start.12 = (f32[256]{0:T(256)S(1)}, f32[256]{0:T(256)}, u32[]{:S(2)}) copy-start(f32[256]{0:T(256)} %param.10) | copy-start | bytes 3076
  8.1 0.6 copy-start.15
  8.7 12.2 %collective-permute-start.5 = (bf16[864,1024]{1,0:T(8,128)(2,1)S(1)}, bf16[864,1024]{1,0:T(8,128)(2,1)S(1)}, u32[]{:S(2)}, u32[]{:S(2)}) collective-permute-start(bf16[864,1024]{1,0:T(8,128)(2,1)S(1)} %bitcast.18), channel_id=1, source_target_pairs={{0,1},{1,0},{2,3},{3,2},{4,5},{5,4},{6,7},{7,6},{8,9},{9,8},{10,11... | collective-permute-start | bytes 5308424 | tf_op jit(solution)/shard_map/ppermute | solution.py:35
  8.8 7.0 %collective-permute-start.4 = (bf16[2,864,128]{2,1,0:T(8,128)(2,1)}, bf16[2,864,128]{2,1,0:T(8,128)(2,1)}, u32[]{:S(2)}, u32[]{:S(2)}) collective-permute-start(bf16[2,864,128]{2,1,0:T(8,128)(2,1)} %shard_map.77), channel_id=1, source_target_pairs={{0,1},{1,0},{2,3},{3,2},{4,5},{5,4},{6,7},{7,6},{8,9},{9,8},{10,11... | collective-permute-start | bytes 1327112 | tf_op jit(solution)/shard_map/ppermute | solution.py:35
  10.9 4.8 %collective-permute-start.1 = (f32[8,256]{1,0:T(8,128)S(1)}, f32[8,256]{1,0:T(8,128)S(1)}, u32[]{:S(2)}, u32[]{:S(2)}) collective-permute-start(f32[8,256]{1,0:T(8,128)S(1)} %add.26.a_ref), channel_id=1, source_target_pairs={{0,4},{2,6},{4,0},{6,2},{1,5},{3,7},{5,1},{7,3},{8,12},{10,14},{12... | collective-permute-start | bytes 24584 | tf_op jit(solution)/shard_map/ppermute | solution.py:39
  11.9 3.8 %collective-permute-start.2 = (f32[8,256]{1,0:T(8,128)S(1)}, f32[8,256]{1,0:T(8,128)S(1)}, u32[]{:S(2)}, u32[]{:S(2)}) collective-permute-start(f32[8,256]{1,0:T(8,128)S(1)} %add.26.a_ref), channel_id=1, source_target_pairs={{0,2},{2,4},{4,6},{6,0},{1,3},{3,5},{5,7},{7,1},{8,10},{10,12},{12... | collective-permute-start | bytes 24584 | tf_op jit(solution)/shard_map/ppermute | solution.py:39
  12.2 3.5 %collective-permute-start.3 = (f32[8,256]{1,0:T(8,128)S(1)}, f32[8,256]{1,0:T(8,128)S(1)}, u32[]{:S(2)}, u32[]{:S(2)}) collective-permute-start(f32[8,256]{1,0:T(8,128)S(1)} %add.26.a_ref), channel_id=1, source_target_pairs={{0,6},{2,0},{4,2},{6,4},{1,7},{3,1},{5,3},{7,5},{8,14},{10,8},{12,... | collective-permute-start | bytes 24584 | tf_op jit(solution)/shard_map/ppermute | solution.py:39
  17.1 12.9 %copy-start.2 = (bf16[864,128]{1,0:T(8,128)(2,1)}, bf16[864,128]{1,0:T(8,128)(2,1)S(1)}, u32[]{:S(2)}) copy-start(bf16[864,128]{1,0:T(8,128)(2,1)S(1)} %get-tuple-element.42.even_ref.refs_0_) | copy-start | bytes 663556
  17.2 12.9 %copy-start.4 = (bf16[864,128]{1,0:T(8,128)(2,1)}, bf16[864,128]{1,0:T(8,128)(2,1)S(1)}, u32[]{:S(2)}) copy-start(bf16[864,128]{1,0:T(8,128)(2,1)S(1)} %get-tuple-element.43.odd_ref.refs_1_) | copy-start | bytes 663556
  17.2 10.2 %collective-permute-start.6 = (bf16[864,128]{1,0:T(8,128)(2,1)S(1)}, bf16[864,128]{1,0:T(8,128)(2,1)S(1)}, u32[]{:S(2)}, u32[]{:S(2)}) collective-permute-start(bf16[864,128]{1,0:T(8,128)(2,1)S(1)} %get-tuple-element.42.even_ref.refs_0_), channel_id=1, source_target_pairs={{0,2},{2,4},{4,6},{6,0},{1,3},{3,5},{5,7},{7,1},{8,10},{10,12},{12... | collective-permute-start | bytes 663560 | tf_op jit(solution)/shard_map/ppermute | solution.py:39
  17.5 12.5 %collective-permute-start.7 = (bf16[864,128]{1,0:T(8,128)(2,1)S(1)}, bf16[864,128]{1,0:T(8,128)(2,1)S(1)}, u32[]{:S(2)}, u32[]{:S(2)}) collective-permute-start(bf16[864,128]{1,0:T(8,128)(2,1)S(1)} %get-tuple-element.43.odd_ref.refs_1_), channel_id=1, source_target_pairs={{0,6},{2,0},{4,2},{6,4},{1,7},{3,1},{5,3},{7,5},{8,14},{10,8},{12,... | collective-permute-start | bytes 663560 | tf_op jit(solution)/shard_map/ppermute | solution.py:39
  19.9 10.1 %collective-permute-start.8 = (bf16[864,128]{1,0:T(8,128)(2,1)S(1)}, bf16[864,128]{1,0:T(8,128)(2,1)S(1)}, u32[]{:S(2)}, u32[]{:S(2)}) collective-permute-start(bf16[864,128]{1,0:T(8,128)(2,1)S(1)} %get-tuple-element.48), channel_id=1, source_target_pairs={{0,4},{2,6},{4,0},{6,2},{1,5},{3,7},{5,1},{7,3},{8,12},{10,14},{12... | collective-permute-start | bytes 663560 | tf_op jit(solution)/shard_map/ppermute | solution.py:39
  25.4 10.6 %collective-permute-start.9 = (bf16[256,384]{1,0:T(8,128)(2,1)S(1)}, bf16[256,384]{1,0:T(8,128)(2,1)S(1)}, u32[]{:S(2)}, u32[]{:S(2)}) collective-permute-start(bf16[256,384]{1,0:T(8,128)(2,1)S(1)} %get-tuple-element.53), channel_id=1, source_target_pairs={{0,16},{1,5},{2,18},{3,7},{4,20},{5,1},{6,22},{7,3},{8,24},{9,13},... | collective-permute-start | bytes 589832 | tf_op jit(solution)/shard_map/ppermute | solution.py:49
  27.4 8.6 %collective-permute-start.10 = (bf16[256,384]{1,0:T(8,128)(2,1)S(1)}, bf16[256,384]{1,0:T(8,128)(2,1)S(1)}, u32[]{:S(2)}, u32[]{:S(2)}) collective-permute-start(bf16[256,384]{1,0:T(8,128)(2,1)S(1)} %get-tuple-element.54), channel_id=1, source_target_pairs={{0,8},{1,3},{2,10},{3,5},{4,12},{5,7},{6,14},{7,1},{8,16},{9,11},{... | collective-permute-start | bytes 589832 | tf_op jit(solution)/shard_map/ppermute | solution.py:49
  27.4 7.8 %copy-start.6 = (bf16[864,128]{1,0:T(8,128)(2,1)}, bf16[864,128]{1,0:T(8,128)(2,1)S(1)}, u32[]{:S(2)}) copy-start(bf16[864,128]{1,0:T(8,128)(2,1)S(1)} %collective-permute-done.6.up_ref.refs_2_) | copy-start | bytes 663556
  27.4 8.6 %collective-permute-start.11 = (bf16[256,384]{1,0:T(8,128)(2,1)S(1)}, bf16[256,384]{1,0:T(8,128)(2,1)S(1)}, u32[]{:S(2)}, u32[]{:S(2)}) collective-permute-start(bf16[256,384]{1,0:T(8,128)(2,1)S(1)} %get-tuple-element.55), channel_id=1, source_target_pairs={{0,24},{1,7},{2,26},{3,1},{4,28},{5,3},{6,30},{7,5},{8,0},{9,15},{... | collective-permute-start | bytes 589832 | tf_op jit(solution)/shard_map/ppermute | solution.py:49
  30.1 5.1 %copy-start.8 = (bf16[864,128]{1,0:T(8,128)(2,1)}, bf16[864,128]{1,0:T(8,128)(2,1)S(1)}, u32[]{:S(2)}) copy-start(bf16[864,128]{1,0:T(8,128)(2,1)S(1)} %collective-permute-done.7.down_ref.refs_3_) | copy-start | bytes 663556
  30.1 5.0 %copy-start.10 = (bf16[864,128]{1,0:T(8,128)(2,1)}, bf16[864,128]{1,0:T(8,128)(2,1)S(1)}, u32[]{:S(2)}) copy-start(bf16[864,128]{1,0:T(8,128)(2,1)S(1)} %collective-permute-done.8.far_ref.refs_4_) | copy-start | bytes 663556
  35.1 0.8 %copy-start.13 = (bf16[3,864,128]{2,1,0:T(8,128)(2,1)}, bf16[3,864,128]{2,1,0:T(8,128)(2,1)S(1)}, u32[]{:S(2)}) copy-start(bf16[3,864,128]{2,1,0:T(8,128)(2,1)S(1)} %get-tuple-element.74) | copy-start | bytes 1990660
  36.0 11.9 %collective-permute-start.12 = (bf16[256,768]{1,0:T(8,128)(2,1)}, bf16[256,768]{1,0:T(8,128)(2,1)S(1)}, u32[]{:S(2)}, u32[]{:S(2)}) collective-permute-start(bf16[256,768]{1,0:T(8,128)(2,1)} %get-tuple-element.61), channel_id=1, source_target_pairs={{0,16},{1,5},{2,18},{3,7},{4,20},{5,1},{6,22},{7,3},{8,24},{9,13},... | collective-permute-start | bytes 1179656 | tf_op jit(solution)/shard_map/ppermute | solution.py:49
  37.4 11.6 %collective-permute-start.13 = (bf16[256,768]{1,0:T(8,128)(2,1)}, bf16[256,768]{1,0:T(8,128)(2,1)S(1)}, u32[]{:S(2)}, u32[]{:S(2)}) collective-permute-start(bf16[256,768]{1,0:T(8,128)(2,1)} %get-tuple-element.62), channel_id=1, source_target_pairs={{0,8},{1,3},{2,10},{3,5},{4,12},{5,7},{6,14},{7,1},{8,16},{9,11},{... | collective-permute-start | bytes 1179656 | tf_op jit(solution)/shard_map/ppermute | solution.py:49
  38.1 10.8 %collective-permute-start.14 = (bf16[256,768]{1,0:T(8,128)(2,1)}, bf16[256,768]{1,0:T(8,128)(2,1)S(1)}, u32[]{:S(2)}, u32[]{:S(2)}) collective-permute-start(bf16[256,768]{1,0:T(8,128)(2,1)} %get-tuple-element.63), channel_id=1, source_target_pairs={{0,24},{1,7},{2,26},{3,1},{4,28},{5,3},{6,30},{7,5},{8,0},{9,15},{... | collective-permute-start | bytes 1179656 | tf_op jit(solution)/shard_map/ppermute | solution.py:49
  40.0 6.7 %copy-start.3 = (bf16[864,128]{1,0:T(8,128)(2,1)S(1)}, bf16[864,128]{1,0:T(8,128)(2,1)}, u32[]{:S(2)}) copy-start(bf16[864,128]{1,0:T(8,128)(2,1)} %copy-done.2) | copy-start | bytes 663556
  40.0 6.7 %copy-start.5 = (bf16[864,128]{1,0:T(8,128)(2,1)S(1)}, bf16[864,128]{1,0:T(8,128)(2,1)}, u32[]{:S(2)}) copy-start(bf16[864,128]{1,0:T(8,128)(2,1)} %copy-done.4) | copy-start | bytes 663556
  40.0 6.7 %copy-start.7 = (bf16[864,128]{1,0:T(8,128)(2,1)S(1)}, bf16[864,128]{1,0:T(8,128)(2,1)}, u32[]{:S(2)}) copy-start(bf16[864,128]{1,0:T(8,128)(2,1)} %copy-done.6) | copy-start | bytes 663556
  40.0 6.7 %copy-start.9 = (bf16[864,128]{1,0:T(8,128)(2,1)S(1)}, bf16[864,128]{1,0:T(8,128)(2,1)}, u32[]{:S(2)}) copy-start(bf16[864,128]{1,0:T(8,128)(2,1)} %copy-done.8) | copy-start | bytes 663556
  40.1 6.7 %copy-start.11 = (bf16[864,128]{1,0:T(8,128)(2,1)S(1)}, bf16[864,128]{1,0:T(8,128)(2,1)}, u32[]{:S(2)}) copy-start(bf16[864,128]{1,0:T(8,128)(2,1)} %copy-done.10) | copy-start | bytes 663556
  47.0 0.9 %copy-start.1 = (bf16[3,864,128]{2,1,0:T(8,128)(2,1)}, bf16[3,864,128]{2,1,0:T(8,128)(2,1)S(1)}, u32[]{:S(2)}) copy-start(bf16[3,864,128]{2,1,0:T(8,128)(2,1)S(1)} %shard_map.82.held_ref) | copy-start | bytes 1990660
  47.9 13.2 %copy-start.14 = (bf16[3,864,128]{2,1,0:T(8,128)(2,1)S(1)}, bf16[3,864,128]{2,1,0:T(8,128)(2,1)}, u32[]{:S(2)}) copy-start(bf16[3,864,128]{2,1,0:T(8,128)(2,1)} %copy-done.13) | copy-start | bytes 1990660
  50.0 28.1 %all-to-all-start = ((bf16[32,8,1152]{2,1,0:T(8,128)(2,1)}), bf16[32,8,1152]{2,1,0:T(8,128)(2,1)S(1)}, u32[]{:S(2)}, u32[]{:S(2)}) async-start(bf16[32,8,1152]{2,1,0:T(8,128)(2,1)} %bitcast.12), calls=%async_computation | async-start | bytes 1179648 | tf_op jit(solution)/shard_map/all_to_all | solution.py:55
  61.1 7.8 %collective-permute-start.15 = (bf16[3,864,128]{2,1,0:T(8,128)(2,1)S(1)}, bf16[3,864,128]{2,1,0:T(8,128)(2,1)S(1)}, u32[]{:S(2)}, u32[]{:S(2)}) collective-permute-start(bf16[3,864,128]{2,1,0:T(8,128)(2,1)S(1)} %copy-done.14), channel_id=1, source_target_pairs={{0,1},{1,0},{2,3},{3,2},{4,5},{5,4},{6,7},{7,6},{8,9},{9,8},{10,11... | collective-permute-start | bytes 1990664 | tf_op jit(solution)/shard_map/ppermute | solution.py:35
  68.9 0.8 %copy-start.16 = (bf16[3,864,128]{2,1,0:T(8,128)(2,1)}, bf16[3,864,128]{2,1,0:T(8,128)(2,1)S(1)}, u32[]{:S(2)}) copy-start(bf16[3,864,128]{2,1,0:T(8,128)(2,1)S(1)} %collective-permute-done.15.got_ref) | copy-start | bytes 1990660
  78.3 4.2 %collective-permute-start.16 = (f32[4,1152]{1,0:T(4,128)S(1)}, f32[4,1152]{1,0:T(4,128)S(1)}, u32[]{:S(2)}, u32[]{:S(2)}) collective-permute-start(f32[4,1152]{1,0:T(4,128)S(1)} %constant_dynamic-slice_fusion), channel_id=1, source_target_pairs={{0,1},{1,0},{2,3},{3,2},{4,5},{5,4},{6,7},{7,6},{8,9},{9,8},{10,11... | collective-permute-start | bytes 55304 | tf_op jit(solution)/shard_map/ppermute | solution.py:35

commit v12 on v9

--- a/solution.py
+++ b/solution.py
@@ -109,11 +109,11 @@
     )
 
 
-def pre_gradient(place, gain, sums, mine, theirs, images, cell_count):
+def pre_gradient(token, place, gain, sums, mine, theirs, images, cell_count):
     _, cells, half = mine.shape
     each = cells // images
 
-    def body(place_ref, gain_ref, a_ref, b_ref, c_ref, d_ref, mine_ref, theirs_ref, even_ref, odd_ref, far_ref):
+    def body(_, place_ref, gain_ref, a_ref, b_ref, c_ref, d_ref, mine_ref, theirs_ref, even_ref, odd_ref, far_ref):
         first = core_of(place_ref) == 0
         early = x_of(place_ref) < X // 2
         means = (a_ref[...] + b_ref[...] + c_ref[...] + d_ref[...]) / cell_count
@@ -141,8 +141,8 @@
     out = jax.ShapeDtypeStruct((cells, half), BF16)
     return kernel_call(
         body,
-        (place, gain, *sums, mine, theirs),
-        [SMEM, whole(gain.shape)] + [whole(sums[0].shape)] * 4 + [whole(mine.shape)] * 2,
+        (token, place, gain, *sums, mine, theirs),
+        [whole(token.shape), SMEM, whole(gain.shape)] + [whole(sums[0].shape)] * 4 + [whole(mine.shape)] * 2,
         [out] * 3,
         [whole(out.shape)] * 3,
     )
@@ -157,7 +157,8 @@
     deep = padded_count(cells)
     width = 256
 
-    def body(own_ref, other_ref, out_ref):
+    def body(own_ref, other_ref, out_ref, token_ref):
+        token_ref[...] = jnp.zeros_like(token_ref)
         for which, ref in enumerate((own_ref, other_ref)):
             block = jnp.concatenate([ref[...], jnp.zeros((deep - cells, width), BF16)], axis=0)
             out_ref[:, which * deep : (which + 1) * deep] = block.T
@@ -167,10 +168,10 @@
         body,
         (own, other),
         [spec, spec],
-        [jax.ShapeDtypeStruct((channels, 2 * deep), BF16)],
-        [pl.BlockSpec((width, 2 * deep), lambda i: (i, 0))],
+        [jax.ShapeDtypeStruct((channels, 2 * deep), BF16), jax.ShapeDtypeStruct((8, 128), F32)],
+        [pl.BlockSpec((width, 2 * deep), lambda i: (i, 0)), whole((8, 128))],
         (channels // width,),
-    )[0]
+    )
 
 
 def column_taps(block, col_count):
@@ -253,7 +254,7 @@
     return product_call(body, place, [even, odd], lhs, 3 * width, [])
 
 
-def tap_blocks(place_ref, even_ref, odd_ref, up_ref, down_ref, far_ref):
+def tap_blocks(place_ref, even_ref, odd_ref, far_ref, up_ref, down_ref):
     x = x_of(place_ref)
     far_block = far_ref[...]
     zero = jnp.zeros_like(far_block)
@@ -264,8 +265,8 @@
     return (down_block, far_down), (even_ref[...], odd_ref[...]), (far_up, up_block)
 
 
-def own_blocks(place, even, odd, up, down, far):
-    operands = (even, odd, up, down, far)
+def own_blocks(place, even, odd, far, up, down):
+    operands = (even, odd, far, up, down)
 
     def body(place_ref, *refs):
         first = core_of(place_ref) == 0
@@ -282,10 +283,10 @@
     )[0]
 
 
-def side_terms(place, even, odd, up, down, far, lhs, col_count):
+def side_terms(place, even, odd, far, up, down, lhs, col_count):
     cells, width = up.shape
 
-    def body(place_ref, even_ref, odd_ref, up_ref, down_ref, far_ref, lhs_ref, *rest):
+    def body(place_ref, even_ref, odd_ref, far_ref, up_ref, down_ref, lhs_ref, *rest):
         theirs_refs = rest[4:6]
         stacked, total = rest[6:]
 
@@ -293,7 +294,7 @@
         def _():
             clear_padding(stacked, cells)
             first = core_of(place_ref) == 0
-            blocks = tap_blocks(place_ref, even_ref, odd_ref, up_ref, down_ref, far_ref)
+            blocks = tap_blocks(place_ref, even_ref, odd_ref, far_ref, up_ref, down_ref)
             for side, (lower, upper) in enumerate(blocks):
                 theirs = jnp.where(first, upper, lower)
                 for part, ref in enumerate(theirs_refs):
@@ -306,7 +307,7 @@
         multiply(place_ref, lhs_ref, stacked, total, rest[:4])
 
     part = jax.ShapeDtypeStruct((3, cells // 2, width), BF16)
-    return product_call(body, place, [even, odd, up, down, far], lhs, 6 * width, [part, part])
+    return product_call(body, place, [even, odd, far, up, down], lhs, 6 * width, [part, part])
 
 
 def first_sum(middle, sides):
@@ -390,9 +391,9 @@
     input_other = swapped(input_flat)
     sums = sums + got_sums
     sums = [sums] + [around(sums, steps) for steps in (2, 1, 3)]
-    lhs = transposed(input_flat, input_other)
+    lhs, token = transposed(input_flat, input_other)
     gain = norm_gain.reshape(1, channels_out)
-    even, odd, far = pre_gradient(place, gain, sums, mine, theirs, image_count, cell_count)
+    even, odd, far = pre_gradient(token, place, gain, sums, mine, theirs, image_count, cell_count)
     far = around(far, 2)
     up = around(even, 1)
     down = around(odd, X - 1)
@@ -400,7 +401,7 @@
     middle = list(middle_terms(place, even, odd, lhs, col_count))
     side_place, middle[0] = lax.optimization_barrier((place, middle[0]))
     middle = [middle[0]] + [crossed(middle[steps], steps) for steps in (2, 1, 3)]
-    *sides, sent_lower, sent_upper = side_terms(side_place, even, odd, up, down, far, lhs, col_count)
+    *sides, sent_lower, sent_upper = side_terms(side_place, even, odd, far, up, down, lhs, col_count)
     sent = [sent_lower, sent_upper]
     sides[1:], sent, middle[1:] = lax.optimization_barrier((sides[1:], sent, middle[1:]))
     got = [swapped(block) for block in sent]
@@ -408,7 +409,7 @@
     weight = jnp.transpose(weight, (1, 2, 0)).reshape(9 * channels_out, channels_in)
     sides = [sides[0]] + [crossed(sides[steps], steps) for steps in (2, 1, 3)]
     held_place, weight = lax.optimization_barrier((place, weight))
-    held = own_blocks(held_place, even, odd, up, down, far)
+    held = own_blocks(held_place, even, odd, far, up, down)
     sides, weight, got, held = lax.optimization_barrier((sides, weight, got, held))
     merged = first_sum(middle, sides)
     place, merged = lax.optimization_barrier((place, merged))

time: 84.1 us -> 82.5 us (0.981)
  starting transfers between devices: 40.2 us -> 35.6 us
  waiting for transfers between devices: 9.25 us -> 13.4 us
  local copies, waits for them, and re-layouts: 8.55 us -> 7.53 us
    ppermute x6, waiting for transfers between devices: 1.17 us -> 5.39 us  [around(): lax.ppermute(value, 'x', [(source, (source + steps) % X) for source in ra...]
    ppermute x6, starting transfers between devices: 15.3 us -> 12.6 us  [swapped(): return lax.ppermute(value, 'core', [(0, 1), (1, 0)])]
    ppermute x6, starting transfers between devices: 8.82 us -> 6.94 us  [crossed(): return lax.ppermute(value, AXES, pairs)]
    unnamed x8, local copies, waits for them, and re-layouts: 1.9 us -> 0.87 us
where the time goes in v12:
time: 82.5 us; the launch traced here: 82.1 us
  starting transfers between devices  35.6 us (43%)
  Pallas kernels  22.2 us (27%)
  waiting for transfers between devices  13.4 us (16%)
  local copies, waits for them, and re-layouts  7.53 us (9%)
  other arithmetic  2.6 us (3%)
    pallas_call x8, Pallas kernels, kernel_call(): pl.pallas_call(body, grid=grid, in_specs=in_specs, out_specs=out_specs, o...  22.2 us
    ppermute x6, starting transfers between devices, swapped(): return lax.ppermute(value, 'core', [(0, 1), (1, 0)])  12.6 us
    all_to_all x1, starting transfers between devices, exchanged(): return lax.all_to_all(value, AXES, 0, 0, axis_index_groups=groups)  8.58 us
    ppermute x6, starting transfers between devices, around(): lax.ppermute(value, 'x', [(source, (source + steps) % X) for source in ra...  7.46 us
    all_to_all x1, waiting for transfers between devices, exchanged(): return lax.all_to_all(value, AXES, 0, 0, axis_index_groups=groups)  7.05 us
    ppermute x6, starting transfers between devices, crossed(): return lax.ppermute(value, AXES, pairs)  6.94 us
    transpose x1, local copies, waits for them, and re-layouts, per_device(): jnp.transpose(weight, (1, 2, 0)).reshape(9 * channels_out, channels_in)  6.63 us
    ppermute x6, waiting for transfers between devices, around(): lax.ppermute(value, 'x', [(source, (source + steps) % X) for source in ra...  5.39 us
  transfers between devices with their start and end apart: 19, of which 5 were waited for; matrix products, arithmetic and copies ran while one was open for 8% of the time, Pallas kernels for 25%

profile of v12, /device:TPU:1, one launch (start us, length us, event | category | flops | bytes accessed | tf_op | source)
XLA Modules:
  0.0 82.1 jit_solution(4741319973018757837)
XLA Ops:
  0.6 1.9 %fusion.2 = (f32[2,256]{1,0:T(2,128)S(1)}, f32[2,256]{1,0:T(2,128)S(1)}, f32[2,256]{1,0:T(2,128)S(1)}, f32[2,256]{1,0:T(2,128)S(1)}) fusion(s32[2,6,72,256]{3,2,1,0:T(8,128)} %param.9, bf16[2,6,72,256]{3,2,1,0:T(8,128)(2,1)} %param.8, bf16[2,6,72,256]{3,2,1,0:T(8,128)(2,1)} %param.7), kind=kLoop, calls=%fused_computation.7 | loop fusion | flops 2209792 | bytes 1777664 | tf_op jit(solution)/shard_map/reduce_sum | solution.py:81
  2.5 3.3 %collective-permute-start = (f32[8,256]{1,0:T(8,128)S(1)}, f32[8,256]{1,0:T(8,128)S(1)}, u32[]{:S(2)}, u32[]{:S(2)}) collective-permute-start(f32[8,256]{1,0:T(8,128)S(1)} %reshape.45), channel_id=1, source_target_pairs={{0,1},{1,0},{2,3},{3,2},{4,5},{5,4},{6,7},{7,6},{8,9},{9,8},{10,11... | collective-permute-start | bytes 24584 | tf_op jit(solution)/shard_map/ppermute | solution.py:35
  5.8 2.4 %shard_map.77 = (bf16[2,864,128]{2,1,0:T(8,128)(2,1)}, bf16[2,864,128]{2,1,0:T(8,128)(2,1)}) custom-call(s32[1]{0:T(128)} %bitcast.place_ref, bf16[864,256]{1,0:T(8,128)(2,1)} %bitcast.25, bf16[864,256]{1,0:T(8,128)(2,1)} %bitcast.24, s32[864,256]{1,0:T(8,128)} %bitcast.23), custom_call_target="tpu_custom_call" | custom-call | bytes 2654212 | tf_op jit(solution)/shard_map/pallas_call | solution.py:65
  8.2 0.0 collective-permute-done
  8.2 0.1 collective-permute-start.1
  8.4 0.5 collective-permute-start.5
  8.8 1.0 %collective-permute-start.2 = (f32[8,256]{1,0:T(8,128)S(1)}, f32[8,256]{1,0:T(8,128)S(1)}, u32[]{:S(2)}, u32[]{:S(2)}) collective-permute-start(f32[8,256]{1,0:T(8,128)S(1)} %add.21.a_ref), channel_id=1, source_target_pairs={{0,4},{2,6},{4,0},{6,2},{1,5},{3,7},{5,1},{7,3},{8,12},{10,14},{12... | collective-permute-start | bytes 24584 | tf_op jit(solution)/shard_map/ppermute | solution.py:39
  9.8 0.3 collective-permute-start.3
  10.2 2.4 %collective-permute-start.4 = (f32[8,256]{1,0:T(8,128)S(1)}, f32[8,256]{1,0:T(8,128)S(1)}, u32[]{:S(2)}, u32[]{:S(2)}) collective-permute-start(f32[8,256]{1,0:T(8,128)S(1)} %add.21.a_ref), channel_id=1, source_target_pairs={{0,6},{2,0},{4,2},{6,4},{1,7},{3,1},{5,3},{7,5},{8,14},{10,8},{12,... | collective-permute-start | bytes 24584 | tf_op jit(solution)/shard_map/ppermute | solution.py:39
  12.5 0.1 collective-permute-done.1.other_ref
  12.6 1.7 %shard_map.78 = (bf16[1024,1792]{1,0:T(8,128)(2,1)S(1)}, f32[8,128]{1,0:T(8,128)S(1)}) custom-call(bf16[864,1024]{1,0:T(8,128)(2,1)S(1)} %bitcast.19, bf16[864,1024]{1,0:T(8,128)(2,1)S(1)} %collective-permute-done.1.other_ref), custom_call_target="tpu_custom_call" | custom-call | bytes 7213056 | tf_op jit(solution)/shard_map/pallas_call | solution.py:65
  14.3 0.0 collective-permute-done.2.b_ref
  14.4 0.0 collective-permute-done.3.c_ref
  14.4 0.0 collective-permute-done.4.d_ref
  14.4 0.0 collective-permute-done.5.theirs_ref
  14.4 0.4 shard_map.79
  14.8 1.1 %collective-permute-start.6 = (bf16[864,128]{1,0:T(8,128)(2,1)S(1)}, bf16[864,128]{1,0:T(8,128)(2,1)S(1)}, u32[]{:S(2)}, u32[]{:S(2)}) collective-permute-start(bf16[864,128]{1,0:T(8,128)(2,1)S(1)} %get-tuple-element.60), channel_id=1, source_target_pairs={{0,4},{2,6},{4,0},{6,2},{1,5},{3,7},{5,1},{7,3},{8,12},{10,14},{12... | collective-permute-start | bytes 663560 | tf_op jit(solution)/shard_map/ppermute | solution.py:39
  15.9 1.4 %collective-permute-start.7 = (bf16[864,128]{1,0:T(8,128)(2,1)S(1)}, bf16[864,128]{1,0:T(8,128)(2,1)S(1)}, u32[]{:S(2)}, u32[]{:S(2)}) collective-permute-start(bf16[864,128]{1,0:T(8,128)(2,1)S(1)} %get-tuple-element.54.even_ref.refs_0_), channel_id=1, source_target_pairs={{0,2},{2,4},{4,6},{6,0},{1,3},{3,5},{5,7},{7,1},{8,10},{10,12},{12... | collective-permute-start | bytes 663560 | tf_op jit(solution)/shard_map/ppermute | solution.py:39
  17.3 1.3 %collective-permute-start.8 = (bf16[864,128]{1,0:T(8,128)(2,1)S(1)}, bf16[864,128]{1,0:T(8,128)(2,1)S(1)}, u32[]{:S(2)}, u32[]{:S(2)}) collective-permute-start(bf16[864,128]{1,0:T(8,128)(2,1)S(1)} %get-tuple-element.55.odd_ref.refs_1_), channel_id=1, source_target_pairs={{0,6},{2,0},{4,2},{6,4},{1,7},{3,1},{5,3},{7,5},{8,14},{10,8},{12,... | collective-permute-start | bytes 663560 | tf_op jit(solution)/shard_map/ppermute | solution.py:39
  18.5 2.7 %shard_map.80 = (bf16[256,384]{1,0:T(8,128)(2,1)S(1)}, bf16[256,384]{1,0:T(8,128)(2,1)S(1)}, bf16[256,384]{1,0:T(8,128)(2,1)S(1)}, bf16[256,384]{1,0:T(8,128)(2,1)S(1)}) custom-call(s32[1]{0:T(128)} %bitcast.place_ref, bf16[864,128]{1,0:T(8,128)(2,1)S(1)} %get-tuple-element.54.even_ref.refs_0_, bf16[864,128]{1,0:T(8,128)(2,1)S(1)} %get-tuple-element.55.odd_ref.refs_1_, ...), custom_call_target="tpu_custom_call" | custom-call | flops 1409286144 | bytes 4898820 | tf_op jit(solution)/shard_map/pallas_call | solution.py:65
  21.2 0.8 %collective-permute-start.9 = (bf16[256,384]{1,0:T(8,128)(2,1)S(1)}, bf16[256,384]{1,0:T(8,128)(2,1)S(1)}, u32[]{:S(2)}, u32[]{:S(2)}) collective-permute-start(bf16[256,384]{1,0:T(8,128)(2,1)S(1)} %get-tuple-element.66), channel_id=1, source_target_pairs={{0,16},{1,5},{2,18},{3,7},{4,20},{5,1},{6,22},{7,3},{8,24},{9,13},... | collective-permute-start | bytes 589832 | tf_op jit(solution)/shard_map/ppermute | solution.py:49
  22.0 0.0 collective-permute-start.10
  22.0 0.4 collective-permute-done.6.far_ref.refs_2_
  22.5 2.3 %collective-permute-start.11 = (bf16[256,384]{1,0:T(8,128)(2,1)S(1)}, bf16[256,384]{1,0:T(8,128)(2,1)S(1)}, u32[]{:S(2)}, u32[]{:S(2)}) collective-permute-start(bf16[256,384]{1,0:T(8,128)(2,1)S(1)} %get-tuple-element.68), channel_id=1, source_target_pairs={{0,24},{1,7},{2,26},{3,1},{4,28},{5,3},{6,30},{7,5},{8,0},{9,15},{... | collective-permute-start | bytes 589832 | tf_op jit(solution)/shard_map/ppermute | solution.py:49
  24.7 5.0 %collective-permute-done.7.up_ref.refs_3_ = bf16[864,128]{1,0:T(8,128)(2,1)S(1)} collective-permute-done((bf16[864,128]{1,0:T(8,128)(2,1)S(1)}, bf16[864,128]{1,0:T(8,128)(2,1)S(1)}, u32[]{:S(2)}, u32[]{:S(2)}) %collective-permute-start.7) | collective-permute-done | bytes 221216 | tf_op jit(solution)/shard_map/ppermute | solution.py:39
  29.7 0.0 collective-permute-done.8.down_ref.refs_4_
  29.7 5.2 %shard_map.81 = (bf16[256,768]{1,0:T(8,128)(2,1)S(1)}, bf16[256,768]{1,0:T(8,128)(2,1)}, bf16[256,768]{1,0:T(8,128)(2,1)}, bf16[256,768]{1,0:T(8,128)(2,1)}, bf1...) custom-call(s32[1]{0:T(128)} %bitcast.place_ref, bf16[864,128]{1,0:T(8,128)(2,1)S(1)} %get-tuple-element.54.even_ref.refs_0_, ...), custom_call_target="tpu_custom_call" | custom-call | flops 2818572288 | bytes 7012356 | tf_op jit(solution)/shard_map/pallas_call | solution.py:65
  34.9 0.0 collective-permute-done.9.refs_1_
  34.9 0.0 collective-permute-done.10.refs_2_
  34.9 1.2 %collective-permute-start.12 = (bf16[256,768]{1,0:T(8,128)(2,1)}, bf16[256,768]{1,0:T(8,128)(2,1)S(1)}, u32[]{:S(2)}, u32[]{:S(2)}) collective-permute-start(bf16[256,768]{1,0:T(8,128)(2,1)} %get-tuple-element.74), channel_id=1, source_target_pairs={{0,16},{1,5},{2,18},{3,7},{4,20},{5,1},{6,22},{7,3},{8,24},{9,13},... | collective-permute-start | bytes 1179656 | tf_op jit(solution)/shard_map/ppermute | solution.py:49
  36.1 1.3 %collective-permute-start.13 = (bf16[256,768]{1,0:T(8,128)(2,1)}, bf16[256,768]{1,0:T(8,128)(2,1)S(1)}, u32[]{:S(2)}, u32[]{:S(2)}) collective-permute-start(bf16[256,768]{1,0:T(8,128)(2,1)} %get-tuple-element.75), channel_id=1, source_target_pairs={{0,8},{1,3},{2,10},{3,5},{4,12},{5,7},{6,14},{7,1},{8,16},{9,11},{... | collective-permute-start | bytes 1179656 | tf_op jit(solution)/shard_map/ppermute | solution.py:49
  37.4 1.4 %collective-permute-start.14 = (bf16[256,768]{1,0:T(8,128)(2,1)}, bf16[256,768]{1,0:T(8,128)(2,1)S(1)}, u32[]{:S(2)}, u32[]{:S(2)}) collective-permute-start(bf16[256,768]{1,0:T(8,128)(2,1)} %get-tuple-element.76), channel_id=1, source_target_pairs={{0,24},{1,7},{2,26},{3,1},{4,28},{5,3},{6,30},{7,5},{8,0},{9,15},{... | collective-permute-start | bytes 1179656 | tf_op jit(solution)/shard_map/ppermute | solution.py:49
  38.8 3.8 %collective-permute-start.15 = (bf16[3,432,128]{2,1,0:T(8,128)(2,1)}, bf16[3,432,128]{2,1,0:T(8,128)(2,1)}, u32[]{:S(2)}, u32[]{:S(2)}) collective-permute-start(bf16[3,432,128]{2,1,0:T(8,128)(2,1)} %get-tuple-element.79), channel_id=1, source_target_pairs={{0,1},{1,0},{2,3},{3,2},{4,5},{5,4},{6,7},{7,6},{8,9},{9,8},{10,11... | collective-permute-start | bytes 995336 | tf_op jit(solution)/shard_map/ppermute | solution.py:35
  42.5 0.0 collective-permute-start.16
  42.5 6.6 %copy.8 = bf16[9,256,1024]{2,1,0:T(8,128)(2,1)} copy(bf16[9,256,1024]{1,2,0:T(8,128)(2,1)} %bitcast.21) | data formatting | bytes 9437184 | tf_op jit(solution)/shard_map/transpose | solution.py:409
  49.2 0.2 shard_map.82.held_ref
  49.4 0.9 %copy-done.1 = bf16[3,864,128]{2,1,0:T(8,128)(2,1)} copy-done((bf16[3,864,128]{2,1,0:T(8,128)(2,1)}, bf16[3,864,128]{2,1,0:T(8,128)(2,1)S(1)}, u32[]{:S(2)}) %copy-start.1) | copy-done | bytes 663576
  50.3 0.0 collective-permute-done.15.rest_0_
  50.3 0.0 collective-permute-done.16.rest_1_
  50.3 0.0 collective-permute-done.12.refs_5_
  50.3 1.1 %shard_map.83 = bf16[256,1152]{1,0:T(8,128)(2,1)} custom-call(bf16[256,384]{1,0:T(8,128)(2,1)S(1)} %get-tuple-element.58.refs_0_, bf16[256,384]{1,0:T(8,128)(2,1)S(1)} %collective-permute-done.9.refs_1_, bf16[256,384]{1,0:T(8,128)(2,1)S(1)} %collective-permute-done.10.refs_2_, bf16[256,384]{1,0:T(8,128)(2,1)S(1)} %collective-permute-done.11.refs_3_, ...), custom_call_target="tpu_custom_call" | custom-call | bytes 2949120 | tf_op jit(solution)/shard_map/pallas_call | solution.py:65
  51.4 8.6 %all-to-all-start = ((bf16[32,8,1152]{2,1,0:T(8,128)(2,1)}), bf16[32,8,1152]{2,1,0:T(8,128)(2,1)S(1)}, u32[]{:S(2)}, u32[]{:S(2)}) async-start(bf16[32,8,1152]{2,1,0:T(8,128)(2,1)} %bitcast.12), calls=%async_computation | async-start | bytes 1179648 | tf_op jit(solution)/shard_map/all_to_all | solution.py:55
  60.0 8.6 %shard_map.84 = bf16[864,1024]{1,0:T(8,128)(2,1)} custom-call(s32[1]{0:T(128)} %bitcast.place_ref, bf16[3,864,128]{2,1,0:T(8,128)(2,1)} %copy-done.1, bf16[3,432,128]{2,1,0:T(8,128)(2,1)} %collective-permute-done.15.rest_0_, bf16[3,432,128]{2,1,0:T(8,128)(2,1)} %collective-permute-done.16.rest_1_, bf16[2304,1024]{1,0:T(8,128)(2,1)} %bitcast.22), custom_call_target="tpu_custom_call" | custom-call | flops 4076863488 | bytes 7815172 | tf_op jit(solution)/shard_map/pallas_call | solution.py:65
  68.6 7.1 %all-to-all-done = bf16[32,8,1152]{2,1,0:T(8,128)(2,1)S(1)} async-done(((bf16[32,8,1152]{2,1,0:T(8,128)(2,1)}), bf16[32,8,1152]{2,1,0:T(8,128)(2,1)S(1)}, u32[]{:S(2)}, u32[]{:S(2)}) %all-to-all-start) | async-done | bytes 589856 | tf_op jit(solution)/shard_map/all_to_all | solution.py:55
  75.6 0.1 convert_reduce_fusion.1
  75.7 4.9 %collective-permute-start.17 = (f32[4,1152]{1,0:T(4,128)S(1)}, f32[4,1152]{1,0:T(4,128)S(1)}, u32[]{:S(2)}, u32[]{:S(2)}) collective-permute-start(f32[4,1152]{1,0:T(4,128)S(1)} %constant_dynamic-slice_fusion), channel_id=1, source_target_pairs={{0,1},{1,0},{2,3},{3,2},{4,5},{5,4},{6,7},{7,6},{8,9},{9,8},{10,11... | collective-permute-start | bytes 55304 | tf_op jit(solution)/shard_map/ppermute | solution.py:35
  80.6 0.8 %collective-permute-done.17 = f32[4,1152]{1,0:T(4,128)S(1)} collective-permute-done((f32[4,1152]{1,0:T(4,128)S(1)}, f32[4,1152]{1,0:T(4,128)S(1)}, u32[]{:S(2)}, u32[]{:S(2)}) %collective-permute-start.17) | collective-permute-done | bytes 18464 | tf_op jit(solution)/shard_map/ppermute | solution.py:35
  81.5 0.6 pad_maximum_fusion
  (16 shorter events, 0.1 us)
Async XLA Ops:
  0.6 7.6 %copy-start = (bf16[2,6,72,1024]{3,2,1,0:T(8,128)(2,1)S(1)}, bf16[2,6,72,1024]{3,2,1,0:T(8,128)(2,1)}, u32[]{:S(2)}) copy-start(bf16[2,6,72,1024]{3,2,1,0:T(8,128)(2,1)} %param.6) | copy-start | bytes 5308420
  2.5 5.7 %collective-permute-start = (f32[8,256]{1,0:T(8,128)S(1)}, f32[8,256]{1,0:T(8,128)S(1)}, u32[]{:S(2)}, u32[]{:S(2)}) collective-permute-start(f32[8,256]{1,0:T(8,128)S(1)} %reshape.45), channel_id=1, source_target_pairs={{0,1},{1,0},{2,3},{3,2},{4,5},{5,4},{6,7},{7,6},{8,9},{9,8},{10,11... | collective-permute-start | bytes 24584 | tf_op jit(solution)/shard_map/ppermute | solution.py:35
  8.2 4.4 %collective-permute-start.1 = (bf16[864,1024]{1,0:T(8,128)(2,1)S(1)}, bf16[864,1024]{1,0:T(8,128)(2,1)S(1)}, u32[]{:S(2)}, u32[]{:S(2)}) collective-permute-start(bf16[864,1024]{1,0:T(8,128)(2,1)S(1)} %bitcast.18), channel_id=1, source_target_pairs={{0,1},{1,0},{2,3},{3,2},{4,5},{5,4},{6,7},{7,6},{8,9},{9,8},{10,11... | collective-permute-start | bytes 5308424 | tf_op jit(solution)/shard_map/ppermute | solution.py:35
  8.4 6.0 %collective-permute-start.5 = (bf16[2,864,128]{2,1,0:T(8,128)(2,1)}, bf16[2,864,128]{2,1,0:T(8,128)(2,1)S(1)}, u32[]{:S(2)}, u32[]{:S(2)}) collective-permute-start(bf16[2,864,128]{2,1,0:T(8,128)(2,1)} %get-tuple-element.53), channel_id=1, source_target_pairs={{0,1},{1,0},{2,3},{3,2},{4,5},{5,4},{6,7},{7,6},{8,9},{9,8},{10,11... | collective-permute-start | bytes 1327112 | tf_op jit(solution)/shard_map/ppermute | solution.py:35
  8.8 5.6 %copy-start.2 = (bf16[2,864,128]{2,1,0:T(8,128)(2,1)S(1)}, bf16[2,864,128]{2,1,0:T(8,128)(2,1)}, u32[]{:S(2)}) copy-start(bf16[2,864,128]{2,1,0:T(8,128)(2,1)} %get-tuple-element.52.mine_ref) | copy-start | bytes 1327108
  8.8 5.6 %copy-start.3 = (f32[256]{0:T(256)S(1)}, f32[256]{0:T(256)}, u32[]{:S(2)}) copy-start(f32[256]{0:T(256)} %param.10) | copy-start | bytes 3076
  8.8 5.5 %collective-permute-start.2 = (f32[8,256]{1,0:T(8,128)S(1)}, f32[8,256]{1,0:T(8,128)S(1)}, u32[]{:S(2)}, u32[]{:S(2)}) collective-permute-start(f32[8,256]{1,0:T(8,128)S(1)} %add.21.a_ref), channel_id=1, source_target_pairs={{0,4},{2,6},{4,0},{6,2},{1,5},{3,7},{5,1},{7,3},{8,12},{10,14},{12... | collective-permute-start | bytes 24584 | tf_op jit(solution)/shard_map/ppermute | solution.py:39
  9.8 4.5 %collective-permute-start.3 = (f32[8,256]{1,0:T(8,128)S(1)}, f32[8,256]{1,0:T(8,128)S(1)}, u32[]{:S(2)}, u32[]{:S(2)}) collective-permute-start(f32[8,256]{1,0:T(8,128)S(1)} %add.21.a_ref), channel_id=1, source_target_pairs={{0,2},{2,4},{4,6},{6,0},{1,3},{3,5},{5,7},{7,1},{8,10},{10,12},{12... | collective-permute-start | bytes 24584 | tf_op jit(solution)/shard_map/ppermute | solution.py:39
  10.2 4.2 %collective-permute-start.4 = (f32[8,256]{1,0:T(8,128)S(1)}, f32[8,256]{1,0:T(8,128)S(1)}, u32[]{:S(2)}, u32[]{:S(2)}) collective-permute-start(f32[8,256]{1,0:T(8,128)S(1)} %add.21.a_ref), channel_id=1, source_target_pairs={{0,6},{2,0},{4,2},{6,4},{1,7},{3,1},{5,3},{7,5},{8,14},{10,8},{12,... | collective-permute-start | bytes 24584 | tf_op jit(solution)/shard_map/ppermute | solution.py:39
  14.8 7.7 %collective-permute-start.6 = (bf16[864,128]{1,0:T(8,128)(2,1)S(1)}, bf16[864,128]{1,0:T(8,128)(2,1)S(1)}, u32[]{:S(2)}, u32[]{:S(2)}) collective-permute-start(bf16[864,128]{1,0:T(8,128)(2,1)S(1)} %get-tuple-element.60), channel_id=1, source_target_pairs={{0,4},{2,6},{4,0},{6,2},{1,5},{3,7},{5,1},{7,3},{8,12},{10,14},{12... | collective-permute-start | bytes 663560 | tf_op jit(solution)/shard_map/ppermute | solution.py:39
  15.9 13.8 %collective-permute-start.7 = (bf16[864,128]{1,0:T(8,128)(2,1)S(1)}, bf16[864,128]{1,0:T(8,128)(2,1)S(1)}, u32[]{:S(2)}, u32[]{:S(2)}) collective-permute-start(bf16[864,128]{1,0:T(8,128)(2,1)S(1)} %get-tuple-element.54.even_ref.refs_0_), channel_id=1, source_target_pairs={{0,2},{2,4},{4,6},{6,0},{1,3},{3,5},{5,7},{7,1},{8,10},{10,12},{12... | collective-permute-start | bytes 663560 | tf_op jit(solution)/shard_map/ppermute | solution.py:39
  17.3 12.4 %collective-permute-start.8 = (bf16[864,128]{1,0:T(8,128)(2,1)S(1)}, bf16[864,128]{1,0:T(8,128)(2,1)S(1)}, u32[]{:S(2)}, u32[]{:S(2)}) collective-permute-start(bf16[864,128]{1,0:T(8,128)(2,1)S(1)} %get-tuple-element.55.odd_ref.refs_1_), channel_id=1, source_target_pairs={{0,6},{2,0},{4,2},{6,4},{1,7},{3,1},{5,3},{7,5},{8,14},{10,8},{12,... | collective-permute-start | bytes 663560 | tf_op jit(solution)/shard_map/ppermute | solution.py:39
  21.2 13.7 %collective-permute-start.9 = (bf16[256,384]{1,0:T(8,128)(2,1)S(1)}, bf16[256,384]{1,0:T(8,128)(2,1)S(1)}, u32[]{:S(2)}, u32[]{:S(2)}) collective-permute-start(bf16[256,384]{1,0:T(8,128)(2,1)S(1)} %get-tuple-element.66), channel_id=1, source_target_pairs={{0,16},{1,5},{2,18},{3,7},{4,20},{5,1},{6,22},{7,3},{8,24},{9,13},... | collective-permute-start | bytes 589832 | tf_op jit(solution)/shard_map/ppermute | solution.py:49
  22.0 12.9 %collective-permute-start.10 = (bf16[256,384]{1,0:T(8,128)(2,1)S(1)}, bf16[256,384]{1,0:T(8,128)(2,1)S(1)}, u32[]{:S(2)}, u32[]{:S(2)}) collective-permute-start(bf16[256,384]{1,0:T(8,128)(2,1)S(1)} %get-tuple-element.67), channel_id=1, source_target_pairs={{0,8},{1,3},{2,10},{3,5},{4,12},{5,7},{6,14},{7,1},{8,16},{9,11},{... | collective-permute-start | bytes 589832 | tf_op jit(solution)/shard_map/ppermute | solution.py:49
  22.5 12.5 %collective-permute-start.11 = (bf16[256,384]{1,0:T(8,128)(2,1)S(1)}, bf16[256,384]{1,0:T(8,128)(2,1)S(1)}, u32[]{:S(2)}, u32[]{:S(2)}) collective-permute-start(bf16[256,384]{1,0:T(8,128)(2,1)S(1)} %get-tuple-element.68), channel_id=1, source_target_pairs={{0,24},{1,7},{2,26},{3,1},{4,28},{5,3},{6,30},{7,5},{8,0},{9,15},{... | collective-permute-start | bytes 589832 | tf_op jit(solution)/shard_map/ppermute | solution.py:49
  34.9 15.4 %collective-permute-start.12 = (bf16[256,768]{1,0:T(8,128)(2,1)}, bf16[256,768]{1,0:T(8,128)(2,1)S(1)}, u32[]{:S(2)}, u32[]{:S(2)}) collective-permute-start(bf16[256,768]{1,0:T(8,128)(2,1)} %get-tuple-element.74), channel_id=1, source_target_pairs={{0,16},{1,5},{2,18},{3,7},{4,20},{5,1},{6,22},{7,3},{8,24},{9,13},... | collective-permute-start | bytes 1179656 | tf_op jit(solution)/shard_map/ppermute | solution.py:49
  36.1 14.2 %collective-permute-start.13 = (bf16[256,768]{1,0:T(8,128)(2,1)}, bf16[256,768]{1,0:T(8,128)(2,1)S(1)}, u32[]{:S(2)}, u32[]{:S(2)}) collective-permute-start(bf16[256,768]{1,0:T(8,128)(2,1)} %get-tuple-element.75), channel_id=1, source_target_pairs={{0,8},{1,3},{2,10},{3,5},{4,12},{5,7},{6,14},{7,1},{8,16},{9,11},{... | collective-permute-start | bytes 1179656 | tf_op jit(solution)/shard_map/ppermute | solution.py:49
  37.4 12.9 %collective-permute-start.14 = (bf16[256,768]{1,0:T(8,128)(2,1)}, bf16[256,768]{1,0:T(8,128)(2,1)S(1)}, u32[]{:S(2)}, u32[]{:S(2)}) collective-permute-start(bf16[256,768]{1,0:T(8,128)(2,1)} %get-tuple-element.76), channel_id=1, source_target_pairs={{0,24},{1,7},{2,26},{3,1},{4,28},{5,3},{6,30},{7,5},{8,0},{9,15},{... | collective-permute-start | bytes 1179656 | tf_op jit(solution)/shard_map/ppermute | solution.py:49
  38.8 11.5 %collective-permute-start.15 = (bf16[3,432,128]{2,1,0:T(8,128)(2,1)}, bf16[3,432,128]{2,1,0:T(8,128)(2,1)}, u32[]{:S(2)}, u32[]{:S(2)}) collective-permute-start(bf16[3,432,128]{2,1,0:T(8,128)(2,1)} %get-tuple-element.79), channel_id=1, source_target_pairs={{0,1},{1,0},{2,3},{3,2},{4,5},{5,4},{6,7},{7,6},{8,9},{9,8},{10,11... | collective-permute-start | bytes 995336 | tf_op jit(solution)/shard_map/ppermute | solution.py:35
  42.5 7.8 %collective-permute-start.16 = (bf16[3,432,128]{2,1,0:T(8,128)(2,1)}, bf16[3,432,128]{2,1,0:T(8,128)(2,1)}, u32[]{:S(2)}, u32[]{:S(2)}) collective-permute-start(bf16[3,432,128]{2,1,0:T(8,128)(2,1)} %get-tuple-element.80), channel_id=1, source_target_pairs={{0,1},{1,0},{2,3},{3,2},{4,5},{5,4},{6,7},{7,6},{8,9},{9,8},{10,11... | collective-permute-start | bytes 995336 | tf_op jit(solution)/shard_map/ppermute | solution.py:35
  49.4 0.9 %copy-start.1 = (bf16[3,864,128]{2,1,0:T(8,128)(2,1)}, bf16[3,864,128]{2,1,0:T(8,128)(2,1)S(1)}, u32[]{:S(2)}) copy-start(bf16[3,864,128]{2,1,0:T(8,128)(2,1)S(1)} %shard_map.82.held_ref) | copy-start | bytes 1990660
  51.4 24.2 %all-to-all-start = ((bf16[32,8,1152]{2,1,0:T(8,128)(2,1)}), bf16[32,8,1152]{2,1,0:T(8,128)(2,1)S(1)}, u32[]{:S(2)}, u32[]{:S(2)}) async-start(bf16[32,8,1152]{2,1,0:T(8,128)(2,1)} %bitcast.12), calls=%async_computation | async-start | bytes 1179648 | tf_op jit(solution)/shard_map/all_to_all | solution.py:55
  75.7 5.7 %collective-permute-start.17 = (f32[4,1152]{1,0:T(4,128)S(1)}, f32[4,1152]{1,0:T(4,128)S(1)}, u32[]{:S(2)}, u32[]{:S(2)}) collective-permute-start(f32[4,1152]{1,0:T(4,128)S(1)} %constant_dynamic-slice_fusion), channel_id=1, source_target_pairs={{0,1},{1,0},{2,3},{3,2},{4,5},{5,4},{6,7},{7,6},{8,9},{9,8},{10,11... | collective-permute-start | bytes 55304 | tf_op jit(solution)/shard_map/ppermute | solution.py:35

commit v13 on v12

--- a/solution.py
+++ b/solution.py
@@ -254,7 +254,7 @@
     return product_call(body, place, [even, odd], lhs, 3 * width, [])
 
 
-def tap_blocks(place_ref, even_ref, odd_ref, far_ref, up_ref, down_ref):
+def tap_blocks(place_ref, even_ref, odd_ref, up_ref, down_ref, far_ref):
     x = x_of(place_ref)
     far_block = far_ref[...]
     zero = jnp.zeros_like(far_block)
@@ -265,8 +265,8 @@
     return (down_block, far_down), (even_ref[...], odd_ref[...]), (far_up, up_block)
 
 
-def own_blocks(place, even, odd, far, up, down):
-    operands = (even, odd, far, up, down)
+def own_blocks(place, even, odd, up, down, far):
+    operands = (even, odd, up, down, far)
 
     def body(place_ref, *refs):
         first = core_of(place_ref) == 0
@@ -283,10 +283,10 @@
     )[0]
 
 
-def side_terms(place, even, odd, far, up, down, lhs, col_count):
+def side_terms(place, even, odd, up, down, far, lhs, col_count):
     cells, width = up.shape
 
-    def body(place_ref, even_ref, odd_ref, far_ref, up_ref, down_ref, lhs_ref, *rest):
+    def body(place_ref, even_ref, odd_ref, up_ref, down_ref, far_ref, lhs_ref, *rest):
         theirs_refs = rest[4:6]
         stacked, total = rest[6:]
 
@@ -294,7 +294,7 @@
         def _():
             clear_padding(stacked, cells)
             first = core_of(place_ref) == 0
-            blocks = tap_blocks(place_ref, even_ref, odd_ref, far_ref, up_ref, down_ref)
+            blocks = tap_blocks(place_ref, even_ref, odd_ref, up_ref, down_ref, far_ref)
             for side, (lower, upper) in enumerate(blocks):
                 theirs = jnp.where(first, upper, lower)
                 for part, ref in enumerate(theirs_refs):
@@ -307,7 +307,7 @@
         multiply(place_ref, lhs_ref, stacked, total, rest[:4])
 
     part = jax.ShapeDtypeStruct((3, cells // 2, width), BF16)
-    return product_call(body, place, [even, odd, far, up, down], lhs, 6 * width, [part, part])
+    return product_call(body, place, [even, odd, up, down, far], lhs, 6 * width, [part, part])
 
 
 def first_sum(middle, sides):
@@ -401,7 +401,7 @@
     middle = list(middle_terms(place, even, odd, lhs, col_count))
     side_place, middle[0] = lax.optimization_barrier((place, middle[0]))
     middle = [middle[0]] + [crossed(middle[steps], steps) for steps in (2, 1, 3)]
-    *sides, sent_lower, sent_upper = side_terms(side_place, even, odd, far, up, down, lhs, col_count)
+    *sides, sent_lower, sent_upper = side_terms(side_place, even, odd, up, down, far, lhs, col_count)
     sent = [sent_lower, sent_upper]
     sides[1:], sent, middle[1:] = lax.optimization_barrier((sides[1:], sent, middle[1:]))
     got = [swapped(block) for block in sent]
@@ -409,7 +409,7 @@
     weight = jnp.transpose(weight, (1, 2, 0)).reshape(9 * channels_out, channels_in)
     sides = [sides[0]] + [crossed(sides[steps], steps) for steps in (2, 1, 3)]
     held_place, weight = lax.optimization_barrier((place, weight))
-    held = own_blocks(held_place, even, odd, far, up, down)
+    held = own_blocks(held_place, even, odd, up, down, far)
     sides, weight, got, held = lax.optimization_barrier((sides, weight, got, held))
     merged = first_sum(middle, sides)
     place, merged = lax.optimization_barrier((place, merged))

time: 82.5 us -> 83.5 us (1.012)
  starting transfers between devices: 35.6 us -> 41.6 us
  waiting for transfers between devices: 13.4 us -> 8.46 us
    ppermute x6, waiting for transfers between devices: 5.39 us -> 0.56 us  [around(): lax.ppermute(value, 'x', [(source, (source + steps) % X) for source in ra...]
    ppermute x6, starting transfers between devices: 12.6 us -> 16.6 us  [swapped(): return lax.ppermute(value, 'core', [(0, 1), (1, 0)])]
    ppermute x6, starting transfers between devices: 6.94 us -> 9.59 us  [crossed(): return lax.ppermute(value, AXES, pairs)]
    all_to_all x1, waiting for transfers between devices: 7.05 us -> 5.88 us  [exchanged(): return lax.all_to_all(value, AXES, 0, 0, axis_index_groups=groups)]
    ppermute x6, waiting for transfers between devices: 0.02 us -> 1.05 us  [crossed(): return lax.ppermute(value, AXES, pairs)]
where the time goes in v13:
time: 83.5 us; the launch traced here: 83.1 us
  starting transfers between devices  41.6 us (50%)
  Pallas kernels  22.1 us (26%)
  waiting for transfers between devices  8.46 us (10%)
  local copies, waits for them, and re-layouts  7.53 us (9%)
  other arithmetic  2.6 us (3%)
    pallas_call x8, Pallas kernels, kernel_call(): pl.pallas_call(body, grid=grid, in_specs=in_specs, out_specs=out_specs, o...  22.1 us
    ppermute x6, starting transfers between devices, swapped(): return lax.ppermute(value, 'core', [(0, 1), (1, 0)])  16.6 us
    ppermute x6, starting transfers between devices, crossed(): return lax.ppermute(value, AXES, pairs)  9.59 us
    all_to_all x1, starting transfers between devices, exchanged(): return lax.all_to_all(value, AXES, 0, 0, axis_index_groups=groups)  8.58 us
    ppermute x6, starting transfers between devices, around(): lax.ppermute(value, 'x', [(source, (source + steps) % X) for source in ra...  6.78 us
    transpose x1, local copies, waits for them, and re-layouts, per_device(): jnp.transpose(weight, (1, 2, 0)).reshape(9 * channels_out, channels_in)  6.63 us
    all_to_all x1, waiting for transfers between devices, exchanged(): return lax.all_to_all(value, AXES, 0, 0, axis_index_groups=groups)  5.88 us
    reduce_sum x1, other arithmetic, channel_sums(): jnp.sum(term, axis=(1, 2))  1.85 us
  transfers between devices with their start and end apart: 19, of which 5 were waited for; matrix products, arithmetic and copies ran while one was open for 8% of the time, Pallas kernels for 25%

profile of v13, /device:TPU:1, one launch (start us, length us, event | category | flops | bytes accessed | tf_op | source)
XLA Modules:
  0.0 83.1 jit_solution(1712844698839922513)
XLA Ops:
  0.6 1.9 %fusion.2 = (f32[2,256]{1,0:T(2,128)S(1)}, f32[2,256]{1,0:T(2,128)S(1)}, f32[2,256]{1,0:T(2,128)S(1)}, f32[2,256]{1,0:T(2,128)S(1)}) fusion(s32[2,6,72,256]{3,2,1,0:T(8,128)} %param.9, bf16[2,6,72,256]{3,2,1,0:T(8,128)(2,1)} %param.8, bf16[2,6,72,256]{3,2,1,0:T(8,128)(2,1)} %param.7), kind=kLoop, calls=%fused_computation.7 | loop fusion | flops 2209792 | bytes 1777664 | tf_op jit(solution)/shard_map/reduce_sum | solution.py:81
  2.5 3.3 %collective-permute-start = (f32[8,256]{1,0:T(8,128)S(1)}, f32[8,256]{1,0:T(8,128)S(1)}, u32[]{:S(2)}, u32[]{:S(2)}) collective-permute-start(f32[8,256]{1,0:T(8,128)S(1)} %reshape.45), channel_id=1, source_target_pairs={{0,1},{1,0},{2,3},{3,2},{4,5},{5,4},{6,7},{7,6},{8,9},{9,8},{10,11... | collective-permute-start | bytes 24584 | tf_op jit(solution)/shard_map/ppermute | solution.py:35
  5.8 2.4 %shard_map.77 = (bf16[2,864,128]{2,1,0:T(8,128)(2,1)}, bf16[2,864,128]{2,1,0:T(8,128)(2,1)}) custom-call(s32[1]{0:T(128)} %bitcast.place_ref, bf16[864,256]{1,0:T(8,128)(2,1)} %bitcast.25, bf16[864,256]{1,0:T(8,128)(2,1)} %bitcast.24, s32[864,256]{1,0:T(8,128)} %bitcast.23), custom_call_target="tpu_custom_call" | custom-call | bytes 2654212 | tf_op jit(solution)/shard_map/pallas_call | solution.py:65
  8.2 0.0 collective-permute-done
  8.2 0.1 collective-permute-start.1
  8.4 0.5 collective-permute-start.5
  8.8 1.0 %collective-permute-start.2 = (f32[8,256]{1,0:T(8,128)S(1)}, f32[8,256]{1,0:T(8,128)S(1)}, u32[]{:S(2)}, u32[]{:S(2)}) collective-permute-start(f32[8,256]{1,0:T(8,128)S(1)} %add.21.a_ref), channel_id=1, source_target_pairs={{0,4},{2,6},{4,0},{6,2},{1,5},{3,7},{5,1},{7,3},{8,12},{10,14},{12... | collective-permute-start | bytes 24584 | tf_op jit(solution)/shard_map/ppermute | solution.py:39
  9.8 0.3 collective-permute-start.3
  10.2 2.4 %collective-permute-start.4 = (f32[8,256]{1,0:T(8,128)S(1)}, f32[8,256]{1,0:T(8,128)S(1)}, u32[]{:S(2)}, u32[]{:S(2)}) collective-permute-start(f32[8,256]{1,0:T(8,128)S(1)} %add.21.a_ref), channel_id=1, source_target_pairs={{0,6},{2,0},{4,2},{6,4},{1,7},{3,1},{5,3},{7,5},{8,14},{10,8},{12,... | collective-permute-start | bytes 24584 | tf_op jit(solution)/shard_map/ppermute | solution.py:39
  12.5 0.1 collective-permute-done.1.other_ref
  12.6 1.7 %shard_map.78 = (bf16[1024,1792]{1,0:T(8,128)(2,1)S(1)}, f32[8,128]{1,0:T(8,128)S(1)}) custom-call(bf16[864,1024]{1,0:T(8,128)(2,1)S(1)} %bitcast.19, bf16[864,1024]{1,0:T(8,128)(2,1)S(1)} %collective-permute-done.1.other_ref), custom_call_target="tpu_custom_call" | custom-call | bytes 7213056 | tf_op jit(solution)/shard_map/pallas_call | solution.py:65
  14.3 0.0 collective-permute-done.2.b_ref
  14.4 0.0 collective-permute-done.3.c_ref
  14.4 0.0 collective-permute-done.4.d_ref
  14.4 0.0 collective-permute-done.5.theirs_ref
  14.4 0.4 shard_map.79
  14.8 0.1 collective-permute-start.6
  14.9 2.7 %collective-permute-start.7 = (bf16[864,128]{1,0:T(8,128)(2,1)S(1)}, bf16[864,128]{1,0:T(8,128)(2,1)S(1)}, u32[]{:S(2)}, u32[]{:S(2)}) collective-permute-start(bf16[864,128]{1,0:T(8,128)(2,1)S(1)} %get-tuple-element.55.odd_ref.refs_1_), channel_id=1, source_target_pairs={{0,6},{2,0},{4,2},{6,4},{1,7},{3,1},{5,3},{7,5},{8,14},{10,8},{12,... | collective-permute-start | bytes 663560 | tf_op jit(solution)/shard_map/ppermute | solution.py:39
  17.5 0.4 collective-permute-start.8
  17.9 2.7 %shard_map.80 = (bf16[256,384]{1,0:T(8,128)(2,1)S(1)}, bf16[256,384]{1,0:T(8,128)(2,1)S(1)}, bf16[256,384]{1,0:T(8,128)(2,1)S(1)}, bf16[256,384]{1,0:T(8,128)(2,1)S(1)}) custom-call(s32[1]{0:T(128)} %bitcast.place_ref, bf16[864,128]{1,0:T(8,128)(2,1)S(1)} %get-tuple-element.54.even_ref.refs_0_, bf16[864,128]{1,0:T(8,128)(2,1)S(1)} %get-tuple-element.55.odd_ref.refs_1_, ...), custom_call_target="tpu_custom_call" | custom-call | flops 1409286144 | bytes 4898820 | tf_op jit(solution)/shard_map/pallas_call | solution.py:65
  20.5 2.7 %collective-permute-start.9 = (bf16[256,384]{1,0:T(8,128)(2,1)S(1)}, bf16[256,384]{1,0:T(8,128)(2,1)S(1)}, u32[]{:S(2)}, u32[]{:S(2)}) collective-permute-start(bf16[256,384]{1,0:T(8,128)(2,1)S(1)} %get-tuple-element.66), channel_id=1, source_target_pairs={{0,16},{1,5},{2,18},{3,7},{4,20},{5,1},{6,22},{7,3},{8,24},{9,13},... | collective-permute-start | bytes 589832 | tf_op jit(solution)/shard_map/ppermute | solution.py:49
  23.2 0.0 collective-permute-start.10
  23.2 0.0 collective-permute-done.6.up_ref.refs_2_
  23.2 2.7 %collective-permute-start.11 = (bf16[256,384]{1,0:T(8,128)(2,1)S(1)}, bf16[256,384]{1,0:T(8,128)(2,1)S(1)}, u32[]{:S(2)}, u32[]{:S(2)}) collective-permute-start(bf16[256,384]{1,0:T(8,128)(2,1)S(1)} %get-tuple-element.68), channel_id=1, source_target_pairs={{0,24},{1,7},{2,26},{3,1},{4,28},{5,3},{6,30},{7,5},{8,0},{9,15},{... | collective-permute-start | bytes 589832 | tf_op jit(solution)/shard_map/ppermute | solution.py:49
  25.9 0.0 collective-permute-done.7.down_ref.refs_3_
  25.9 0.5 collective-permute-done.8.far_ref.refs_4_
  26.5 5.2 %shard_map.81 = (bf16[256,768]{1,0:T(8,128)(2,1)S(1)}, bf16[256,768]{1,0:T(8,128)(2,1)}, bf16[256,768]{1,0:T(8,128)(2,1)}, bf16[256,768]{1,0:T(8,128)(2,1)}, bf1...) custom-call(s32[1]{0:T(128)} %bitcast.place_ref, bf16[864,128]{1,0:T(8,128)(2,1)S(1)} %get-tuple-element.54.even_ref.refs_0_, ...), custom_call_target="tpu_custom_call" | custom-call | flops 2818572288 | bytes 7012356 | tf_op jit(solution)/shard_map/pallas_call | solution.py:65
  31.7 0.0 collective-permute-done.9.refs_1_
  31.7 1.0 %collective-permute-done.10.refs_2_ = bf16[256,384]{1,0:T(8,128)(2,1)S(1)} collective-permute-done((bf16[256,384]{1,0:T(8,128)(2,1)S(1)}, bf16[256,384]{1,0:T(8,128)(2,1)S(1)}, u32[]{:S(2)}, u32[]{:S(2)}) %collective-permute-start.10) | collective-permute-done | bytes 196640 | tf_op jit(solution)/shard_map/ppermute | solution.py:49
  32.7 1.5 %collective-permute-start.12 = (bf16[256,768]{1,0:T(8,128)(2,1)}, bf16[256,768]{1,0:T(8,128)(2,1)S(1)}, u32[]{:S(2)}, u32[]{:S(2)}) collective-permute-start(bf16[256,768]{1,0:T(8,128)(2,1)} %get-tuple-element.74), channel_id=1, source_target_pairs={{0,16},{1,5},{2,18},{3,7},{4,20},{5,1},{6,22},{7,3},{8,24},{9,13},... | collective-permute-start | bytes 1179656 | tf_op jit(solution)/shard_map/ppermute | solution.py:49
  34.3 1.1 %collective-permute-start.13 = (bf16[256,768]{1,0:T(8,128)(2,1)}, bf16[256,768]{1,0:T(8,128)(2,1)S(1)}, u32[]{:S(2)}, u32[]{:S(2)}) collective-permute-start(bf16[256,768]{1,0:T(8,128)(2,1)} %get-tuple-element.75), channel_id=1, source_target_pairs={{0,8},{1,3},{2,10},{3,5},{4,12},{5,7},{6,14},{7,1},{8,16},{9,11},{... | collective-permute-start | bytes 1179656 | tf_op jit(solution)/shard_map/ppermute | solution.py:49
  35.4 1.5 %collective-permute-start.14 = (bf16[256,768]{1,0:T(8,128)(2,1)}, bf16[256,768]{1,0:T(8,128)(2,1)S(1)}, u32[]{:S(2)}, u32[]{:S(2)}) collective-permute-start(bf16[256,768]{1,0:T(8,128)(2,1)} %get-tuple-element.76), channel_id=1, source_target_pairs={{0,24},{1,7},{2,26},{3,1},{4,28},{5,3},{6,30},{7,5},{8,0},{9,15},{... | collective-permute-start | bytes 1179656 | tf_op jit(solution)/shard_map/ppermute | solution.py:49
  36.9 6.1 %collective-permute-start.15 = (bf16[3,432,128]{2,1,0:T(8,128)(2,1)}, bf16[3,432,128]{2,1,0:T(8,128)(2,1)}, u32[]{:S(2)}, u32[]{:S(2)}) collective-permute-start(bf16[3,432,128]{2,1,0:T(8,128)(2,1)} %get-tuple-element.79), channel_id=1, source_target_pairs={{0,1},{1,0},{2,3},{3,2},{4,5},{5,4},{6,7},{7,6},{8,9},{9,8},{10,11... | collective-permute-start | bytes 995336 | tf_op jit(solution)/shard_map/ppermute | solution.py:35
  43.0 6.6 %copy.8 = bf16[9,256,1024]{2,1,0:T(8,128)(2,1)} copy(bf16[9,256,1024]{1,2,0:T(8,128)(2,1)} %bitcast.21) | data formatting | bytes 9437184 | tf_op jit(solution)/shard_map/transpose | solution.py:409
  49.7 0.2 shard_map.82.held_ref
  49.9 0.9 %copy-done.1 = bf16[3,864,128]{2,1,0:T(8,128)(2,1)} copy-done((bf16[3,864,128]{2,1,0:T(8,128)(2,1)}, bf16[3,864,128]{2,1,0:T(8,128)(2,1)S(1)}, u32[]{:S(2)}) %copy-start.1) | copy-done | bytes 663576
  50.8 0.0 collective-permute-done.15.rest_0_
  50.8 0.0 collective-permute-done.16.rest_1_
  50.8 0.0 collective-permute-done.12.refs_5_
  50.8 0.0 collective-permute-done.13.refs_6_
  50.8 1.1 %shard_map.83 = bf16[256,1152]{1,0:T(8,128)(2,1)} custom-call(bf16[256,384]{1,0:T(8,128)(2,1)S(1)} %get-tuple-element.58.refs_0_, bf16[256,384]{1,0:T(8,128)(2,1)S(1)} %collective-permute-done.9.refs_1_, bf16[256,384]{1,0:T(8,128)(2,1)S(1)} %collective-permute-done.10.refs_2_, bf16[256,384]{1,0:T(8,128)(2,1)S(1)} %collective-permute-done.11.refs_3_, ...), custom_call_target="tpu_custom_call" | custom-call | bytes 2949120 | tf_op jit(solution)/shard_map/pallas_call | solution.py:65
  51.9 8.6 %all-to-all-start = ((bf16[32,8,1152]{2,1,0:T(8,128)(2,1)}), bf16[32,8,1152]{2,1,0:T(8,128)(2,1)S(1)}, u32[]{:S(2)}, u32[]{:S(2)}) async-start(bf16[32,8,1152]{2,1,0:T(8,128)(2,1)} %bitcast.12), calls=%async_computation | async-start | bytes 1179648 | tf_op jit(solution)/shard_map/all_to_all | solution.py:55
  60.5 8.6 %shard_map.84 = bf16[864,1024]{1,0:T(8,128)(2,1)} custom-call(s32[1]{0:T(128)} %bitcast.place_ref, bf16[3,864,128]{2,1,0:T(8,128)(2,1)} %copy-done.1, bf16[3,432,128]{2,1,0:T(8,128)(2,1)} %collective-permute-done.15.rest_0_, bf16[3,432,128]{2,1,0:T(8,128)(2,1)} %collective-permute-done.16.rest_1_, bf16[2304,1024]{1,0:T(8,128)(2,1)} %bitcast.22), custom_call_target="tpu_custom_call" | custom-call | flops 4076863488 | bytes 7815172 | tf_op jit(solution)/shard_map/pallas_call | solution.py:65
  69.0 5.9 %all-to-all-done = bf16[32,8,1152]{2,1,0:T(8,128)(2,1)S(1)} async-done(((bf16[32,8,1152]{2,1,0:T(8,128)(2,1)}), bf16[32,8,1152]{2,1,0:T(8,128)(2,1)S(1)}, u32[]{:S(2)}, u32[]{:S(2)}) %all-to-all-start) | async-done | bytes 589856 | tf_op jit(solution)/shard_map/all_to_all | solution.py:55
  74.9 0.1 convert_reduce_fusion.1
  75.0 6.6 %collective-permute-start.17 = (f32[4,1152]{1,0:T(4,128)S(1)}, f32[4,1152]{1,0:T(4,128)S(1)}, u32[]{:S(2)}, u32[]{:S(2)}) collective-permute-start(f32[4,1152]{1,0:T(4,128)S(1)} %constant_dynamic-slice_fusion), channel_id=1, source_target_pairs={{0,1},{1,0},{2,3},{3,2},{4,5},{5,4},{6,7},{7,6},{8,9},{9,8},{10,11... | collective-permute-start | bytes 55304 | tf_op jit(solution)/shard_map/ppermute | solution.py:35
  81.6 0.8 %collective-permute-done.17 = f32[4,1152]{1,0:T(4,128)S(1)} collective-permute-done((f32[4,1152]{1,0:T(4,128)S(1)}, f32[4,1152]{1,0:T(4,128)S(1)}, u32[]{:S(2)}, u32[]{:S(2)}) %collective-permute-start.17) | collective-permute-done | bytes 18464 | tf_op jit(solution)/shard_map/ppermute | solution.py:35
  82.5 0.6 pad_maximum_fusion
  (16 shorter events, 0.1 us)
Async XLA Ops:
  0.6 7.6 %copy-start = (bf16[2,6,72,1024]{3,2,1,0:T(8,128)(2,1)S(1)}, bf16[2,6,72,1024]{3,2,1,0:T(8,128)(2,1)}, u32[]{:S(2)}) copy-start(bf16[2,6,72,1024]{3,2,1,0:T(8,128)(2,1)} %param.6) | copy-start | bytes 5308420
  2.5 5.7 %collective-permute-start = (f32[8,256]{1,0:T(8,128)S(1)}, f32[8,256]{1,0:T(8,128)S(1)}, u32[]{:S(2)}, u32[]{:S(2)}) collective-permute-start(f32[8,256]{1,0:T(8,128)S(1)} %reshape.45), channel_id=1, source_target_pairs={{0,1},{1,0},{2,3},{3,2},{4,5},{5,4},{6,7},{7,6},{8,9},{9,8},{10,11... | collective-permute-start | bytes 24584 | tf_op jit(solution)/shard_map/ppermute | solution.py:35
  8.2 4.4 %collective-permute-start.1 = (bf16[864,1024]{1,0:T(8,128)(2,1)S(1)}, bf16[864,1024]{1,0:T(8,128)(2,1)S(1)}, u32[]{:S(2)}, u32[]{:S(2)}) collective-permute-start(bf16[864,1024]{1,0:T(8,128)(2,1)S(1)} %bitcast.18), channel_id=1, source_target_pairs={{0,1},{1,0},{2,3},{3,2},{4,5},{5,4},{6,7},{7,6},{8,9},{9,8},{10,11... | collective-permute-start | bytes 5308424 | tf_op jit(solution)/shard_map/ppermute | solution.py:35
  8.4 6.0 %collective-permute-start.5 = (bf16[2,864,128]{2,1,0:T(8,128)(2,1)}, bf16[2,864,128]{2,1,0:T(8,128)(2,1)S(1)}, u32[]{:S(2)}, u32[]{:S(2)}) collective-permute-start(bf16[2,864,128]{2,1,0:T(8,128)(2,1)} %get-tuple-element.53), channel_id=1, source_target_pairs={{0,1},{1,0},{2,3},{3,2},{4,5},{5,4},{6,7},{7,6},{8,9},{9,8},{10,11... | collective-permute-start | bytes 1327112 | tf_op jit(solution)/shard_map/ppermute | solution.py:35
  8.8 5.6 %copy-start.2 = (bf16[2,864,128]{2,1,0:T(8,128)(2,1)S(1)}, bf16[2,864,128]{2,1,0:T(8,128)(2,1)}, u32[]{:S(2)}) copy-start(bf16[2,864,128]{2,1,0:T(8,128)(2,1)} %get-tuple-element.52.mine_ref) | copy-start | bytes 1327108
  8.8 5.6 %copy-start.3 = (f32[256]{0:T(256)S(1)}, f32[256]{0:T(256)}, u32[]{:S(2)}) copy-start(f32[256]{0:T(256)} %param.10) | copy-start | bytes 3076
  8.8 5.5 %collective-permute-start.2 = (f32[8,256]{1,0:T(8,128)S(1)}, f32[8,256]{1,0:T(8,128)S(1)}, u32[]{:S(2)}, u32[]{:S(2)}) collective-permute-start(f32[8,256]{1,0:T(8,128)S(1)} %add.21.a_ref), channel_id=1, source_target_pairs={{0,4},{2,6},{4,0},{6,2},{1,5},{3,7},{5,1},{7,3},{8,12},{10,14},{12... | collective-permute-start | bytes 24584 | tf_op jit(solution)/shard_map/ppermute | solution.py:39
  9.8 4.5 %collective-permute-start.3 = (f32[8,256]{1,0:T(8,128)S(1)}, f32[8,256]{1,0:T(8,128)S(1)}, u32[]{:S(2)}, u32[]{:S(2)}) collective-permute-start(f32[8,256]{1,0:T(8,128)S(1)} %add.21.a_ref), channel_id=1, source_target_pairs={{0,2},{2,4},{4,6},{6,0},{1,3},{3,5},{5,7},{7,1},{8,10},{10,12},{12... | collective-permute-start | bytes 24584 | tf_op jit(solution)/shard_map/ppermute | solution.py:39
  10.2 4.2 %collective-permute-start.4 = (f32[8,256]{1,0:T(8,128)S(1)}, f32[8,256]{1,0:T(8,128)S(1)}, u32[]{:S(2)}, u32[]{:S(2)}) collective-permute-start(f32[8,256]{1,0:T(8,128)S(1)} %add.21.a_ref), channel_id=1, source_target_pairs={{0,6},{2,0},{4,2},{6,4},{1,7},{3,1},{5,3},{7,5},{8,14},{10,8},{12,... | collective-permute-start | bytes 24584 | tf_op jit(solution)/shard_map/ppermute | solution.py:39
  14.8 8.5 %collective-permute-start.6 = (bf16[864,128]{1,0:T(8,128)(2,1)S(1)}, bf16[864,128]{1,0:T(8,128)(2,1)S(1)}, u32[]{:S(2)}, u32[]{:S(2)}) collective-permute-start(bf16[864,128]{1,0:T(8,128)(2,1)S(1)} %get-tuple-element.54.even_ref.refs_0_), channel_id=1, source_target_pairs={{0,2},{2,4},{4,6},{6,0},{1,3},{3,5},{5,7},{7,1},{8,10},{10,12},{12... | collective-permute-start | bytes 663560 | tf_op jit(solution)/shard_map/ppermute | solution.py:39
  14.9 11.1 %collective-permute-start.7 = (bf16[864,128]{1,0:T(8,128)(2,1)S(1)}, bf16[864,128]{1,0:T(8,128)(2,1)S(1)}, u32[]{:S(2)}, u32[]{:S(2)}) collective-permute-start(bf16[864,128]{1,0:T(8,128)(2,1)S(1)} %get-tuple-element.55.odd_ref.refs_1_), channel_id=1, source_target_pairs={{0,6},{2,0},{4,2},{6,4},{1,7},{3,1},{5,3},{7,5},{8,14},{10,8},{12,... | collective-permute-start | bytes 663560 | tf_op jit(solution)/shard_map/ppermute | solution.py:39
  17.5 8.9 %collective-permute-start.8 = (bf16[864,128]{1,0:T(8,128)(2,1)S(1)}, bf16[864,128]{1,0:T(8,128)(2,1)S(1)}, u32[]{:S(2)}, u32[]{:S(2)}) collective-permute-start(bf16[864,128]{1,0:T(8,128)(2,1)S(1)} %get-tuple-element.60), channel_id=1, source_target_pairs={{0,4},{2,6},{4,0},{6,2},{1,5},{3,7},{5,1},{7,3},{8,12},{10,14},{12... | collective-permute-start | bytes 663560 | tf_op jit(solution)/shard_map/ppermute | solution.py:39
  20.5 11.2 %collective-permute-start.9 = (bf16[256,384]{1,0:T(8,128)(2,1)S(1)}, bf16[256,384]{1,0:T(8,128)(2,1)S(1)}, u32[]{:S(2)}, u32[]{:S(2)}) collective-permute-start(bf16[256,384]{1,0:T(8,128)(2,1)S(1)} %get-tuple-element.66), channel_id=1, source_target_pairs={{0,16},{1,5},{2,18},{3,7},{4,20},{5,1},{6,22},{7,3},{8,24},{9,13},... | collective-permute-start | bytes 589832 | tf_op jit(solution)/shard_map/ppermute | solution.py:49
  23.2 9.5 %collective-permute-start.10 = (bf16[256,384]{1,0:T(8,128)(2,1)S(1)}, bf16[256,384]{1,0:T(8,128)(2,1)S(1)}, u32[]{:S(2)}, u32[]{:S(2)}) collective-permute-start(bf16[256,384]{1,0:T(8,128)(2,1)S(1)} %get-tuple-element.67), channel_id=1, source_target_pairs={{0,8},{1,3},{2,10},{3,5},{4,12},{5,7},{6,14},{7,1},{8,16},{9,11},{... | collective-permute-start | bytes 589832 | tf_op jit(solution)/shard_map/ppermute | solution.py:49
  23.2 9.5 %collective-permute-start.11 = (bf16[256,384]{1,0:T(8,128)(2,1)S(1)}, bf16[256,384]{1,0:T(8,128)(2,1)S(1)}, u32[]{:S(2)}, u32[]{:S(2)}) collective-permute-start(bf16[256,384]{1,0:T(8,128)(2,1)S(1)} %get-tuple-element.68), channel_id=1, source_target_pairs={{0,24},{1,7},{2,26},{3,1},{4,28},{5,3},{6,30},{7,5},{8,0},{9,15},{... | collective-permute-start | bytes 589832 | tf_op jit(solution)/shard_map/ppermute | solution.py:49
  32.7 18.0 %collective-permute-start.12 = (bf16[256,768]{1,0:T(8,128)(2,1)}, bf16[256,768]{1,0:T(8,128)(2,1)S(1)}, u32[]{:S(2)}, u32[]{:S(2)}) collective-permute-start(bf16[256,768]{1,0:T(8,128)(2,1)} %get-tuple-element.74), channel_id=1, source_target_pairs={{0,16},{1,5},{2,18},{3,7},{4,20},{5,1},{6,22},{7,3},{8,24},{9,13},... | collective-permute-start | bytes 1179656 | tf_op jit(solution)/shard_map/ppermute | solution.py:49
  34.3 16.5 %collective-permute-start.13 = (bf16[256,768]{1,0:T(8,128)(2,1)}, bf16[256,768]{1,0:T(8,128)(2,1)S(1)}, u32[]{:S(2)}, u32[]{:S(2)}) collective-permute-start(bf16[256,768]{1,0:T(8,128)(2,1)} %get-tuple-element.75), channel_id=1, source_target_pairs={{0,8},{1,3},{2,10},{3,5},{4,12},{5,7},{6,14},{7,1},{8,16},{9,11},{... | collective-permute-start | bytes 1179656 | tf_op jit(solution)/shard_map/ppermute | solution.py:49
  35.4 15.4 %collective-permute-start.14 = (bf16[256,768]{1,0:T(8,128)(2,1)}, bf16[256,768]{1,0:T(8,128)(2,1)S(1)}, u32[]{:S(2)}, u32[]{:S(2)}) collective-permute-start(bf16[256,768]{1,0:T(8,128)(2,1)} %get-tuple-element.76), channel_id=1, source_target_pairs={{0,24},{1,7},{2,26},{3,1},{4,28},{5,3},{6,30},{7,5},{8,0},{9,15},{... | collective-permute-start | bytes 1179656 | tf_op jit(solution)/shard_map/ppermute | solution.py:49
  36.9 13.8 %collective-permute-start.15 = (bf16[3,432,128]{2,1,0:T(8,128)(2,1)}, bf16[3,432,128]{2,1,0:T(8,128)(2,1)}, u32[]{:S(2)}, u32[]{:S(2)}) collective-permute-start(bf16[3,432,128]{2,1,0:T(8,128)(2,1)} %get-tuple-element.79), channel_id=1, source_target_pairs={{0,1},{1,0},{2,3},{3,2},{4,5},{5,4},{6,7},{7,6},{8,9},{9,8},{10,11... | collective-permute-start | bytes 995336 | tf_op jit(solution)/shard_map/ppermute | solution.py:35
  43.0 7.7 %collective-permute-start.16 = (bf16[3,432,128]{2,1,0:T(8,128)(2,1)}, bf16[3,432,128]{2,1,0:T(8,128)(2,1)}, u32[]{:S(2)}, u32[]{:S(2)}) collective-permute-start(bf16[3,432,128]{2,1,0:T(8,128)(2,1)} %get-tuple-element.80), channel_id=1, source_target_pairs={{0,1},{1,0},{2,3},{3,2},{4,5},{5,4},{6,7},{7,6},{8,9},{9,8},{10,11... | collective-permute-start | bytes 995336 | tf_op jit(solution)/shard_map/ppermute | solution.py:35
  49.9 0.9 %copy-start.1 = (bf16[3,864,128]{2,1,0:T(8,128)(2,1)}, bf16[3,864,128]{2,1,0:T(8,128)(2,1)S(1)}, u32[]{:S(2)}) copy-start(bf16[3,864,128]{2,1,0:T(8,128)(2,1)S(1)} %shard_map.82.held_ref) | copy-start | bytes 1990660
  51.9 23.0 %all-to-all-start = ((bf16[32,8,1152]{2,1,0:T(8,128)(2,1)}), bf16[32,8,1152]{2,1,0:T(8,128)(2,1)S(1)}, u32[]{:S(2)}, u32[]{:S(2)}) async-start(bf16[32,8,1152]{2,1,0:T(8,128)(2,1)} %bitcast.12), calls=%async_computation | async-start | bytes 1179648 | tf_op jit(solution)/shard_map/all_to_all | solution.py:55
  75.0 7.4 %collective-permute-start.17 = (f32[4,1152]{1,0:T(4,128)S(1)}, f32[4,1152]{1,0:T(4,128)S(1)}, u32[]{:S(2)}, u32[]{:S(2)}) collective-permute-start(f32[4,1152]{1,0:T(4,128)S(1)} %constant_dynamic-slice_fusion), channel_id=1, source_target_pairs={{0,1},{1,0},{2,3},{3,2},{4,5},{5,4},{6,7},{7,6},{8,9},{9,8},{10,11... | collective-permute-start | bytes 55304 | tf_op jit(solution)/shard_map/ppermute | solution.py:35

commit v14 on v12

--- a/solution.py
+++ b/solution.py
@@ -231,7 +231,7 @@
         (steps,),
         [pltpu.VMEM((deep, columns), BF16), pltpu.VMEM((tall // 128, Y, X, 8, columns), F32)],
         flops=2 * channels_in * deep * columns,
-        vmem=24,
+        vmem=10,
     )
 
 

time: 82.5 us -> 82.5 us (level)
  no operation moved by 1% of the time
where the time goes in v14:
time: 82.5 us; the launch traced here: 82.1 us
  starting transfers between devices  35.6 us (43%)
  Pallas kernels  22.2 us (27%)
  waiting for transfers between devices  13.4 us (16%)
  local copies, waits for them, and re-layouts  7.53 us (9%)
  other arithmetic  2.6 us (3%)
    pallas_call x8, Pallas kernels, kernel_call(): pl.pallas_call(body, grid=grid, in_specs=in_specs, out_specs=out_specs, o...  22.2 us
    ppermute x6, starting transfers between devices, swapped(): return lax.ppermute(value, 'core', [(0, 1), (1, 0)])  12.6 us
    all_to_all x1, starting transfers between devices, exchanged(): return lax.all_to_all(value, AXES, 0, 0, axis_index_groups=groups)  8.58 us
    ppermute x6, starting transfers between devices, around(): lax.ppermute(value, 'x', [(source, (source + steps) % X) for source in ra...  7.46 us
    all_to_all x1, waiting for transfers between devices, exchanged(): return lax.all_to_all(value, AXES, 0, 0, axis_index_groups=groups)  7.05 us
    ppermute x6, starting transfers between devices, crossed(): return lax.ppermute(value, AXES, pairs)  6.94 us
    transpose x1, local copies, waits for them, and re-layouts, per_device(): jnp.transpose(weight, (1, 2, 0)).reshape(9 * channels_out, channels_in)  6.63 us
    ppermute x6, waiting for transfers between devices, around(): lax.ppermute(value, 'x', [(source, (source + steps) % X) for source in ra...  5.39 us
  transfers between devices with their start and end apart: 19, of which 5 were waited for; matrix products, arithmetic and copies ran while one was open for 8% of the time, Pallas kernels for 25%

profile of v14, /device:TPU:1, one launch (start us, length us, event | category | flops | bytes accessed | tf_op | source)
XLA Modules:
  0.0 82.1 jit_solution(14506218438273528274)
XLA Ops:
  0.6 1.9 %fusion.2 = (f32[2,256]{1,0:T(2,128)S(1)}, f32[2,256]{1,0:T(2,128)S(1)}, f32[2,256]{1,0:T(2,128)S(1)}, f32[2,256]{1,0:T(2,128)S(1)}) fusion(s32[2,6,72,256]{3,2,1,0:T(8,128)} %param.9, bf16[2,6,72,256]{3,2,1,0:T(8,128)(2,1)} %param.8, bf16[2,6,72,256]{3,2,1,0:T(8,128)(2,1)} %param.7), kind=kLoop, calls=%fused_computation.7 | loop fusion | flops 2209792 | bytes 1777664 | tf_op jit(solution)/shard_map/reduce_sum | solution.py:81
  2.5 3.3 %collective-permute-start = (f32[8,256]{1,0:T(8,128)S(1)}, f32[8,256]{1,0:T(8,128)S(1)}, u32[]{:S(2)}, u32[]{:S(2)}) collective-permute-start(f32[8,256]{1,0:T(8,128)S(1)} %reshape.45), channel_id=1, source_target_pairs={{0,1},{1,0},{2,3},{3,2},{4,5},{5,4},{6,7},{7,6},{8,9},{9,8},{10,11... | collective-permute-start | bytes 24584 | tf_op jit(solution)/shard_map/ppermute | solution.py:35
  5.8 2.4 %shard_map.77 = (bf16[2,864,128]{2,1,0:T(8,128)(2,1)}, bf16[2,864,128]{2,1,0:T(8,128)(2,1)}) custom-call(s32[1]{0:T(128)} %bitcast.place_ref, bf16[864,256]{1,0:T(8,128)(2,1)} %bitcast.25, bf16[864,256]{1,0:T(8,128)(2,1)} %bitcast.24, s32[864,256]{1,0:T(8,128)} %bitcast.23), custom_call_target="tpu_custom_call" | custom-call | bytes 2654212 | tf_op jit(solution)/shard_map/pallas_call | solution.py:65
  8.2 0.0 collective-permute-done
  8.2 0.1 collective-permute-start.1
  8.4 0.5 collective-permute-start.5
  8.8 1.0 %collective-permute-start.2 = (f32[8,256]{1,0:T(8,128)S(1)}, f32[8,256]{1,0:T(8,128)S(1)}, u32[]{:S(2)}, u32[]{:S(2)}) collective-permute-start(f32[8,256]{1,0:T(8,128)S(1)} %add.21.a_ref), channel_id=1, source_target_pairs={{0,4},{2,6},{4,0},{6,2},{1,5},{3,7},{5,1},{7,3},{8,12},{10,14},{12... | collective-permute-start | bytes 24584 | tf_op jit(solution)/shard_map/ppermute | solution.py:39
  9.8 0.3 collective-permute-start.3
  10.2 2.4 %collective-permute-start.4 = (f32[8,256]{1,0:T(8,128)S(1)}, f32[8,256]{1,0:T(8,128)S(1)}, u32[]{:S(2)}, u32[]{:S(2)}) collective-permute-start(f32[8,256]{1,0:T(8,128)S(1)} %add.21.a_ref), channel_id=1, source_target_pairs={{0,6},{2,0},{4,2},{6,4},{1,7},{3,1},{5,3},{7,5},{8,14},{10,8},{12,... | collective-permute-start | bytes 24584 | tf_op jit(solution)/shard_map/ppermute | solution.py:39
  12.5 0.1 collective-permute-done.1.other_ref
  12.6 1.7 %shard_map.78 = (bf16[1024,1792]{1,0:T(8,128)(2,1)S(1)}, f32[8,128]{1,0:T(8,128)S(1)}) custom-call(bf16[864,1024]{1,0:T(8,128)(2,1)S(1)} %bitcast.19, bf16[864,1024]{1,0:T(8,128)(2,1)S(1)} %collective-permute-done.1.other_ref), custom_call_target="tpu_custom_call" | custom-call | bytes 7213056 | tf_op jit(solution)/shard_map/pallas_call | solution.py:65
  14.3 0.0 collective-permute-done.2.b_ref
  14.4 0.0 collective-permute-done.3.c_ref
  14.4 0.0 collective-permute-done.4.d_ref
  14.4 0.0 collective-permute-done.5.theirs_ref
  14.4 0.4 shard_map.79
  14.8 1.1 %collective-permute-start.6 = (bf16[864,128]{1,0:T(8,128)(2,1)S(1)}, bf16[864,128]{1,0:T(8,128)(2,1)S(1)}, u32[]{:S(2)}, u32[]{:S(2)}) collective-permute-start(bf16[864,128]{1,0:T(8,128)(2,1)S(1)} %get-tuple-element.60), channel_id=1, source_target_pairs={{0,4},{2,6},{4,0},{6,2},{1,5},{3,7},{5,1},{7,3},{8,12},{10,14},{12... | collective-permute-start | bytes 663560 | tf_op jit(solution)/shard_map/ppermute | solution.py:39
  15.9 1.4 %collective-permute-start.7 = (bf16[864,128]{1,0:T(8,128)(2,1)S(1)}, bf16[864,128]{1,0:T(8,128)(2,1)S(1)}, u32[]{:S(2)}, u32[]{:S(2)}) collective-permute-start(bf16[864,128]{1,0:T(8,128)(2,1)S(1)} %get-tuple-element.54.even_ref.refs_0_), channel_id=1, source_target_pairs={{0,2},{2,4},{4,6},{6,0},{1,3},{3,5},{5,7},{7,1},{8,10},{10,12},{12... | collective-permute-start | bytes 663560 | tf_op jit(solution)/shard_map/ppermute | solution.py:39
  17.3 1.3 %collective-permute-start.8 = (bf16[864,128]{1,0:T(8,128)(2,1)S(1)}, bf16[864,128]{1,0:T(8,128)(2,1)S(1)}, u32[]{:S(2)}, u32[]{:S(2)}) collective-permute-start(bf16[864,128]{1,0:T(8,128)(2,1)S(1)} %get-tuple-element.55.odd_ref.refs_1_), channel_id=1, source_target_pairs={{0,6},{2,0},{4,2},{6,4},{1,7},{3,1},{5,3},{7,5},{8,14},{10,8},{12,... | collective-permute-start | bytes 663560 | tf_op jit(solution)/shard_map/ppermute | solution.py:39
  18.5 2.7 %shard_map.80 = (bf16[256,384]{1,0:T(8,128)(2,1)S(1)}, bf16[256,384]{1,0:T(8,128)(2,1)S(1)}, bf16[256,384]{1,0:T(8,128)(2,1)S(1)}, bf16[256,384]{1,0:T(8,128)(2,1)S(1)}) custom-call(s32[1]{0:T(128)} %bitcast.place_ref, bf16[864,128]{1,0:T(8,128)(2,1)S(1)} %get-tuple-element.54.even_ref.refs_0_, bf16[864,128]{1,0:T(8,128)(2,1)S(1)} %get-tuple-element.55.odd_ref.refs_1_, ...), custom_call_target="tpu_custom_call" | custom-call | flops 1409286144 | bytes 4898820 | tf_op jit(solution)/shard_map/pallas_call | solution.py:65
  21.2 0.8 %collective-permute-start.9 = (bf16[256,384]{1,0:T(8,128)(2,1)S(1)}, bf16[256,384]{1,0:T(8,128)(2,1)S(1)}, u32[]{:S(2)}, u32[]{:S(2)}) collective-permute-start(bf16[256,384]{1,0:T(8,128)(2,1)S(1)} %get-tuple-element.66), channel_id=1, source_target_pairs={{0,16},{1,5},{2,18},{3,7},{4,20},{5,1},{6,22},{7,3},{8,24},{9,13},... | collective-permute-start | bytes 589832 | tf_op jit(solution)/shard_map/ppermute | solution.py:49
  22.0 0.0 collective-permute-start.10
  22.0 0.4 collective-permute-done.6.far_ref.refs_2_
  22.5 2.3 %collective-permute-start.11 = (bf16[256,384]{1,0:T(8,128)(2,1)S(1)}, bf16[256,384]{1,0:T(8,128)(2,1)S(1)}, u32[]{:S(2)}, u32[]{:S(2)}) collective-permute-start(bf16[256,384]{1,0:T(8,128)(2,1)S(1)} %get-tuple-element.68), channel_id=1, source_target_pairs={{0,24},{1,7},{2,26},{3,1},{4,28},{5,3},{6,30},{7,5},{8,0},{9,15},{... | collective-permute-start | bytes 589832 | tf_op jit(solution)/shard_map/ppermute | solution.py:49
  24.7 5.0 %collective-permute-done.7.up_ref.refs_3_ = bf16[864,128]{1,0:T(8,128)(2,1)S(1)} collective-permute-done((bf16[864,128]{1,0:T(8,128)(2,1)S(1)}, bf16[864,128]{1,0:T(8,128)(2,1)S(1)}, u32[]{:S(2)}, u32[]{:S(2)}) %collective-permute-start.7) | collective-permute-done | bytes 221216 | tf_op jit(solution)/shard_map/ppermute | solution.py:39
  29.7 0.0 collective-permute-done.8.down_ref.refs_4_
  29.7 5.2 %shard_map.81 = (bf16[256,768]{1,0:T(8,128)(2,1)S(1)}, bf16[256,768]{1,0:T(8,128)(2,1)}, bf16[256,768]{1,0:T(8,128)(2,1)}, bf16[256,768]{1,0:T(8,128)(2,1)}, bf1...) custom-call(s32[1]{0:T(128)} %bitcast.place_ref, bf16[864,128]{1,0:T(8,128)(2,1)S(1)} %get-tuple-element.54.even_ref.refs_0_, ...), custom_call_target="tpu_custom_call" | custom-call | flops 2818572288 | bytes 7012356 | tf_op jit(solution)/shard_map/pallas_call | solution.py:65
  34.9 0.0 collective-permute-done.9.refs_1_
  34.9 0.0 collective-permute-done.10.refs_2_
  34.9 1.2 %collective-permute-start.12 = (bf16[256,768]{1,0:T(8,128)(2,1)}, bf16[256,768]{1,0:T(8,128)(2,1)S(1)}, u32[]{:S(2)}, u32[]{:S(2)}) collective-permute-start(bf16[256,768]{1,0:T(8,128)(2,1)} %get-tuple-element.74), channel_id=1, source_target_pairs={{0,16},{1,5},{2,18},{3,7},{4,20},{5,1},{6,22},{7,3},{8,24},{9,13},... | collective-permute-start | bytes 1179656 | tf_op jit(solution)/shard_map/ppermute | solution.py:49
  36.1 1.3 %collective-permute-start.13 = (bf16[256,768]{1,0:T(8,128)(2,1)}, bf16[256,768]{1,0:T(8,128)(2,1)S(1)}, u32[]{:S(2)}, u32[]{:S(2)}) collective-permute-start(bf16[256,768]{1,0:T(8,128)(2,1)} %get-tuple-element.75), channel_id=1, source_target_pairs={{0,8},{1,3},{2,10},{3,5},{4,12},{5,7},{6,14},{7,1},{8,16},{9,11},{... | collective-permute-start | bytes 1179656 | tf_op jit(solution)/shard_map/ppermute | solution.py:49
  37.4 1.4 %collective-permute-start.14 = (bf16[256,768]{1,0:T(8,128)(2,1)}, bf16[256,768]{1,0:T(8,128)(2,1)S(1)}, u32[]{:S(2)}, u32[]{:S(2)}) collective-permute-start(bf16[256,768]{1,0:T(8,128)(2,1)} %get-tuple-element.76), channel_id=1, source_target_pairs={{0,24},{1,7},{2,26},{3,1},{4,28},{5,3},{6,30},{7,5},{8,0},{9,15},{... | collective-permute-start | bytes 1179656 | tf_op jit(solution)/shard_map/ppermute | solution.py:49
  38.8 3.8 %collective-permute-start.15 = (bf16[3,432,128]{2,1,0:T(8,128)(2,1)}, bf16[3,432,128]{2,1,0:T(8,128)(2,1)}, u32[]{:S(2)}, u32[]{:S(2)}) collective-permute-start(bf16[3,432,128]{2,1,0:T(8,128)(2,1)} %get-tuple-element.79), channel_id=1, source_target_pairs={{0,1},{1,0},{2,3},{3,2},{4,5},{5,4},{6,7},{7,6},{8,9},{9,8},{10,11... | collective-permute-start | bytes 995336 | tf_op jit(solution)/shard_map/ppermute | solution.py:35
  42.5 0.0 collective-permute-start.16
  42.5 6.6 %copy.8 = bf16[9,256,1024]{2,1,0:T(8,128)(2,1)} copy(bf16[9,256,1024]{1,2,0:T(8,128)(2,1)} %bitcast.21) | data formatting | bytes 9437184 | tf_op jit(solution)/shard_map/transpose | solution.py:409
  49.2 0.2 shard_map.82.held_ref
  49.4 0.9 %copy-done.1 = bf16[3,864,128]{2,1,0:T(8,128)(2,1)} copy-done((bf16[3,864,128]{2,1,0:T(8,128)(2,1)}, bf16[3,864,128]{2,1,0:T(8,128)(2,1)S(1)}, u32[]{:S(2)}) %copy-start.1) | copy-done | bytes 663576
  50.3 0.0 collective-permute-done.15.rest_0_
  50.3 0.0 collective-permute-done.16.rest_1_
  50.3 0.0 collective-permute-done.12.refs_5_
  50.3 1.1 %shard_map.83 = bf16[256,1152]{1,0:T(8,128)(2,1)} custom-call(bf16[256,384]{1,0:T(8,128)(2,1)S(1)} %get-tuple-element.58.refs_0_, bf16[256,384]{1,0:T(8,128)(2,1)S(1)} %collective-permute-done.9.refs_1_, bf16[256,384]{1,0:T(8,128)(2,1)S(1)} %collective-permute-done.10.refs_2_, bf16[256,384]{1,0:T(8,128)(2,1)S(1)} %collective-permute-done.11.refs_3_, ...), custom_call_target="tpu_custom_call" | custom-call | bytes 2949120 | tf_op jit(solution)/shard_map/pallas_call | solution.py:65
  51.4 8.6 %all-to-all-start = ((bf16[32,8,1152]{2,1,0:T(8,128)(2,1)}), bf16[32,8,1152]{2,1,0:T(8,128)(2,1)S(1)}, u32[]{:S(2)}, u32[]{:S(2)}) async-start(bf16[32,8,1152]{2,1,0:T(8,128)(2,1)} %bitcast.12), calls=%async_computation | async-start | bytes 1179648 | tf_op jit(solution)/shard_map/all_to_all | solution.py:55
  60.0 8.6 %shard_map.84 = bf16[864,1024]{1,0:T(8,128)(2,1)} custom-call(s32[1]{0:T(128)} %bitcast.place_ref, bf16[3,864,128]{2,1,0:T(8,128)(2,1)} %copy-done.1, bf16[3,432,128]{2,1,0:T(8,128)(2,1)} %collective-permute-done.15.rest_0_, bf16[3,432,128]{2,1,0:T(8,128)(2,1)} %collective-permute-done.16.rest_1_, bf16[2304,1024]{1,0:T(8,128)(2,1)} %bitcast.22), custom_call_target="tpu_custom_call" | custom-call | flops 4076863488 | bytes 7815172 | tf_op jit(solution)/shard_map/pallas_call | solution.py:65
  68.5 7.1 %all-to-all-done = bf16[32,8,1152]{2,1,0:T(8,128)(2,1)S(1)} async-done(((bf16[32,8,1152]{2,1,0:T(8,128)(2,1)}), bf16[32,8,1152]{2,1,0:T(8,128)(2,1)S(1)}, u32[]{:S(2)}, u32[]{:S(2)}) %all-to-all-start) | async-done | bytes 589856 | tf_op jit(solution)/shard_map/all_to_all | solution.py:55
  75.6 0.1 convert_reduce_fusion.1
  75.7 4.9 %collective-permute-start.17 = (f32[4,1152]{1,0:T(4,128)S(1)}, f32[4,1152]{1,0:T(4,128)S(1)}, u32[]{:S(2)}, u32[]{:S(2)}) collective-permute-start(f32[4,1152]{1,0:T(4,128)S(1)} %constant_dynamic-slice_fusion), channel_id=1, source_target_pairs={{0,1},{1,0},{2,3},{3,2},{4,5},{5,4},{6,7},{7,6},{8,9},{9,8},{10,11... | collective-permute-start | bytes 55304 | tf_op jit(solution)/shard_map/ppermute | solution.py:35
  80.6 0.8 %collective-permute-done.17 = f32[4,1152]{1,0:T(4,128)S(1)} collective-permute-done((f32[4,1152]{1,0:T(4,128)S(1)}, f32[4,1152]{1,0:T(4,128)S(1)}, u32[]{:S(2)}, u32[]{:S(2)}) %collective-permute-start.17) | collective-permute-done | bytes 18464 | tf_op jit(solution)/shard_map/ppermute | solution.py:35
  81.5 0.6 pad_maximum_fusion
  (16 shorter events, 0.1 us)
Async XLA Ops:
  0.6 7.6 %copy-start = (bf16[2,6,72,1024]{3,2,1,0:T(8,128)(2,1)S(1)}, bf16[2,6,72,1024]{3,2,1,0:T(8,128)(2,1)}, u32[]{:S(2)}) copy-start(bf16[2,6,72,1024]{3,2,1,0:T(8,128)(2,1)} %param.6) | copy-start | bytes 5308420
  2.5 5.7 %collective-permute-start = (f32[8,256]{1,0:T(8,128)S(1)}, f32[8,256]{1,0:T(8,128)S(1)}, u32[]{:S(2)}, u32[]{:S(2)}) collective-permute-start(f32[8,256]{1,0:T(8,128)S(1)} %reshape.45), channel_id=1, source_target_pairs={{0,1},{1,0},{2,3},{3,2},{4,5},{5,4},{6,7},{7,6},{8,9},{9,8},{10,11... | collective-permute-start | bytes 24584 | tf_op jit(solution)/shard_map/ppermute | solution.py:35
  8.2 4.4 %collective-permute-start.1 = (bf16[864,1024]{1,0:T(8,128)(2,1)S(1)}, bf16[864,1024]{1,0:T(8,128)(2,1)S(1)}, u32[]{:S(2)}, u32[]{:S(2)}) collective-permute-start(bf16[864,1024]{1,0:T(8,128)(2,1)S(1)} %bitcast.18), channel_id=1, source_target_pairs={{0,1},{1,0},{2,3},{3,2},{4,5},{5,4},{6,7},{7,6},{8,9},{9,8},{10,11... | collective-permute-start | bytes 5308424 | tf_op jit(solution)/shard_map/ppermute | solution.py:35
  8.4 6.0 %collective-permute-start.5 = (bf16[2,864,128]{2,1,0:T(8,128)(2,1)}, bf16[2,864,128]{2,1,0:T(8,128)(2,1)S(1)}, u32[]{:S(2)}, u32[]{:S(2)}) collective-permute-start(bf16[2,864,128]{2,1,0:T(8,128)(2,1)} %get-tuple-element.53), channel_id=1, source_target_pairs={{0,1},{1,0},{2,3},{3,2},{4,5},{5,4},{6,7},{7,6},{8,9},{9,8},{10,11... | collective-permute-start | bytes 1327112 | tf_op jit(solution)/shard_map/ppermute | solution.py:35
  8.8 5.6 %copy-start.2 = (bf16[2,864,128]{2,1,0:T(8,128)(2,1)S(1)}, bf16[2,864,128]{2,1,0:T(8,128)(2,1)}, u32[]{:S(2)}) copy-start(bf16[2,864,128]{2,1,0:T(8,128)(2,1)} %get-tuple-element.52.mine_ref) | copy-start | bytes 1327108
  8.8 5.6 %copy-start.3 = (f32[256]{0:T(256)S(1)}, f32[256]{0:T(256)}, u32[]{:S(2)}) copy-start(f32[256]{0:T(256)} %param.10) | copy-start | bytes 3076
  8.8 5.5 %collective-permute-start.2 = (f32[8,256]{1,0:T(8,128)S(1)}, f32[8,256]{1,0:T(8,128)S(1)}, u32[]{:S(2)}, u32[]{:S(2)}) collective-permute-start(f32[8,256]{1,0:T(8,128)S(1)} %add.21.a_ref), channel_id=1, source_target_pairs={{0,4},{2,6},{4,0},{6,2},{1,5},{3,7},{5,1},{7,3},{8,12},{10,14},{12... | collective-permute-start | bytes 24584 | tf_op jit(solution)/shard_map/ppermute | solution.py:39
  9.8 4.5 %collective-permute-start.3 = (f32[8,256]{1,0:T(8,128)S(1)}, f32[8,256]{1,0:T(8,128)S(1)}, u32[]{:S(2)}, u32[]{:S(2)}) collective-permute-start(f32[8,256]{1,0:T(8,128)S(1)} %add.21.a_ref), channel_id=1, source_target_pairs={{0,2},{2,4},{4,6},{6,0},{1,3},{3,5},{5,7},{7,1},{8,10},{10,12},{12... | collective-permute-start | bytes 24584 | tf_op jit(solution)/shard_map/ppermute | solution.py:39
  10.2 4.2 %collective-permute-start.4 = (f32[8,256]{1,0:T(8,128)S(1)}, f32[8,256]{1,0:T(8,128)S(1)}, u32[]{:S(2)}, u32[]{:S(2)}) collective-permute-start(f32[8,256]{1,0:T(8,128)S(1)} %add.21.a_ref), channel_id=1, source_target_pairs={{0,6},{2,0},{4,2},{6,4},{1,7},{3,1},{5,3},{7,5},{8,14},{10,8},{12,... | collective-permute-start | bytes 24584 | tf_op jit(solution)/shard_map/ppermute | solution.py:39
  14.8 7.7 %collective-permute-start.6 = (bf16[864,128]{1,0:T(8,128)(2,1)S(1)}, bf16[864,128]{1,0:T(8,128)(2,1)S(1)}, u32[]{:S(2)}, u32[]{:S(2)}) collective-permute-start(bf16[864,128]{1,0:T(8,128)(2,1)S(1)} %get-tuple-element.60), channel_id=1, source_target_pairs={{0,4},{2,6},{4,0},{6,2},{1,5},{3,7},{5,1},{7,3},{8,12},{10,14},{12... | collective-permute-start | bytes 663560 | tf_op jit(solution)/shard_map/ppermute | solution.py:39
  15.9 13.8 %collective-permute-start.7 = (bf16[864,128]{1,0:T(8,128)(2,1)S(1)}, bf16[864,128]{1,0:T(8,128)(2,1)S(1)}, u32[]{:S(2)}, u32[]{:S(2)}) collective-permute-start(bf16[864,128]{1,0:T(8,128)(2,1)S(1)} %get-tuple-element.54.even_ref.refs_0_), channel_id=1, source_target_pairs={{0,2},{2,4},{4,6},{6,0},{1,3},{3,5},{5,7},{7,1},{8,10},{10,12},{12... | collective-permute-start | bytes 663560 | tf_op jit(solution)/shard_map/ppermute | solution.py:39
  17.3 12.4 %collective-permute-start.8 = (bf16[864,128]{1,0:T(8,128)(2,1)S(1)}, bf16[864,128]{1,0:T(8,128)(2,1)S(1)}, u32[]{:S(2)}, u32[]{:S(2)}) collective-permute-start(bf16[864,128]{1,0:T(8,128)(2,1)S(1)} %get-tuple-element.55.odd_ref.refs_1_), channel_id=1, source_target_pairs={{0,6},{2,0},{4,2},{6,4},{1,7},{3,1},{5,3},{7,5},{8,14},{10,8},{12,... | collective-permute-start | bytes 663560 | tf_op jit(solution)/shard_map/ppermute | solution.py:39
  21.2 13.7 %collective-permute-start.9 = (bf16[256,384]{1,0:T(8,128)(2,1)S(1)}, bf16[256,384]{1,0:T(8,128)(2,1)S(1)}, u32[]{:S(2)}, u32[]{:S(2)}) collective-permute-start(bf16[256,384]{1,0:T(8,128)(2,1)S(1)} %get-tuple-element.66), channel_id=1, source_target_pairs={{0,16},{1,5},{2,18},{3,7},{4,20},{5,1},{6,22},{7,3},{8,24},{9,13},... | collective-permute-start | bytes 589832 | tf_op jit(solution)/shard_map/ppermute | solution.py:49
  22.0 12.9 %collective-permute-start.10 = (bf16[256,384]{1,0:T(8,128)(2,1)S(1)}, bf16[256,384]{1,0:T(8,128)(2,1)S(1)}, u32[]{:S(2)}, u32[]{:S(2)}) collective-permute-start(bf16[256,384]{1,0:T(8,128)(2,1)S(1)} %get-tuple-element.67), channel_id=1, source_target_pairs={{0,8},{1,3},{2,10},{3,5},{4,12},{5,7},{6,14},{7,1},{8,16},{9,11},{... | collective-permute-start | bytes 589832 | tf_op jit(solution)/shard_map/ppermute | solution.py:49
  22.5 12.5 %collective-permute-start.11 = (bf16[256,384]{1,0:T(8,128)(2,1)S(1)}, bf16[256,384]{1,0:T(8,128)(2,1)S(1)}, u32[]{:S(2)}, u32[]{:S(2)}) collective-permute-start(bf16[256,384]{1,0:T(8,128)(2,1)S(1)} %get-tuple-element.68), channel_id=1, source_target_pairs={{0,24},{1,7},{2,26},{3,1},{4,28},{5,3},{6,30},{7,5},{8,0},{9,15},{... | collective-permute-start | bytes 589832 | tf_op jit(solution)/shard_map/ppermute | solution.py:49
  34.9 15.4 %collective-permute-start.12 = (bf16[256,768]{1,0:T(8,128)(2,1)}, bf16[256,768]{1,0:T(8,128)(2,1)S(1)}, u32[]{:S(2)}, u32[]{:S(2)}) collective-permute-start(bf16[256,768]{1,0:T(8,128)(2,1)} %get-tuple-element.74), channel_id=1, source_target_pairs={{0,16},{1,5},{2,18},{3,7},{4,20},{5,1},{6,22},{7,3},{8,24},{9,13},... | collective-permute-start | bytes 1179656 | tf_op jit(solution)/shard_map/ppermute | solution.py:49
  36.1 14.2 %collective-permute-start.13 = (bf16[256,768]{1,0:T(8,128)(2,1)}, bf16[256,768]{1,0:T(8,128)(2,1)S(1)}, u32[]{:S(2)}, u32[]{:S(2)}) collective-permute-start(bf16[256,768]{1,0:T(8,128)(2,1)} %get-tuple-element.75), channel_id=1, source_target_pairs={{0,8},{1,3},{2,10},{3,5},{4,12},{5,7},{6,14},{7,1},{8,16},{9,11},{... | collective-permute-start | bytes 1179656 | tf_op jit(solution)/shard_map/ppermute | solution.py:49
  37.4 12.9 %collective-permute-start.14 = (bf16[256,768]{1,0:T(8,128)(2,1)}, bf16[256,768]{1,0:T(8,128)(2,1)S(1)}, u32[]{:S(2)}, u32[]{:S(2)}) collective-permute-start(bf16[256,768]{1,0:T(8,128)(2,1)} %get-tuple-element.76), channel_id=1, source_target_pairs={{0,24},{1,7},{2,26},{3,1},{4,28},{5,3},{6,30},{7,5},{8,0},{9,15},{... | collective-permute-start | bytes 1179656 | tf_op jit(solution)/shard_map/ppermute | solution.py:49
  38.8 11.5 %collective-permute-start.15 = (bf16[3,432,128]{2,1,0:T(8,128)(2,1)}, bf16[3,432,128]{2,1,0:T(8,128)(2,1)}, u32[]{:S(2)}, u32[]{:S(2)}) collective-permute-start(bf16[3,432,128]{2,1,0:T(8,128)(2,1)} %get-tuple-element.79), channel_id=1, source_target_pairs={{0,1},{1,0},{2,3},{3,2},{4,5},{5,4},{6,7},{7,6},{8,9},{9,8},{10,11... | collective-permute-start | bytes 995336 | tf_op jit(solution)/shard_map/ppermute | solution.py:35
  42.5 7.8 %collective-permute-start.16 = (bf16[3,432,128]{2,1,0:T(8,128)(2,1)}, bf16[3,432,128]{2,1,0:T(8,128)(2,1)}, u32[]{:S(2)}, u32[]{:S(2)}) collective-permute-start(bf16[3,432,128]{2,1,0:T(8,128)(2,1)} %get-tuple-element.80), channel_id=1, source_target_pairs={{0,1},{1,0},{2,3},{3,2},{4,5},{5,4},{6,7},{7,6},{8,9},{9,8},{10,11... | collective-permute-start | bytes 995336 | tf_op jit(solution)/shard_map/ppermute | solution.py:35
  49.4 0.9 %copy-start.1 = (bf16[3,864,128]{2,1,0:T(8,128)(2,1)}, bf16[3,864,128]{2,1,0:T(8,128)(2,1)S(1)}, u32[]{:S(2)}) copy-start(bf16[3,864,128]{2,1,0:T(8,128)(2,1)S(1)} %shard_map.82.held_ref) | copy-start | bytes 1990660
  51.4 24.2 %all-to-all-start = ((bf16[32,8,1152]{2,1,0:T(8,128)(2,1)}), bf16[32,8,1152]{2,1,0:T(8,128)(2,1)S(1)}, u32[]{:S(2)}, u32[]{:S(2)}) async-start(bf16[32,8,1152]{2,1,0:T(8,128)(2,1)} %bitcast.12), calls=%async_computation | async-start | bytes 1179648 | tf_op jit(solution)/shard_map/all_to_all | solution.py:55
  75.7 5.7 %collective-permute-start.17 = (f32[4,1152]{1,0:T(4,128)S(1)}, f32[4,1152]{1,0:T(4,128)S(1)}, u32[]{:S(2)}, u32[]{:S(2)}) collective-permute-start(f32[4,1152]{1,0:T(4,128)S(1)} %constant_dynamic-slice_fusion), channel_id=1, source_target_pairs={{0,1},{1,0},{2,3},{3,2},{4,5},{5,4},{6,7},{7,6},{8,9},{9,8},{10,11... | collective-permute-start | bytes 55304 | tf_op jit(solution)/shard_map/ppermute | solution.py:35

commit v15 on v8

--- a/solution.py
+++ b/solution.py
@@ -109,11 +109,11 @@
     )
 
 
-def pre_gradient(place, gain, sums, mine, theirs, images, cell_count):
+def pre_gradient(token, place, gain, sums, mine, theirs, images, cell_count):
     _, cells, half = mine.shape
     each = cells // images
 
-    def body(place_ref, gain_ref, a_ref, b_ref, c_ref, d_ref, mine_ref, theirs_ref, even_ref, odd_ref, far_ref):
+    def body(_, place_ref, gain_ref, a_ref, b_ref, c_ref, d_ref, mine_ref, theirs_ref, even_ref, odd_ref, far_ref):
         first = core_of(place_ref) == 0
         early = x_of(place_ref) < X // 2
         means = (a_ref[...] + b_ref[...] + c_ref[...] + d_ref[...]) / cell_count
@@ -141,8 +141,8 @@
     out = jax.ShapeDtypeStruct((cells, half), BF16)
     return kernel_call(
         body,
-        (place, gain, *sums, mine, theirs),
-        [SMEM, whole(gain.shape)] + [whole(sums[0].shape)] * 4 + [whole(mine.shape)] * 2,
+        (token, place, gain, *sums, mine, theirs),
+        [whole(token.shape), SMEM, whole(gain.shape)] + [whole(sums[0].shape)] * 4 + [whole(mine.shape)] * 2,
         [out] * 3,
         [whole(out.shape)] * 3,
     )
@@ -157,7 +157,8 @@
     deep = padded_count(cells)
     width = 256
 
-    def body(own_ref, other_ref, out_ref):
+    def body(own_ref, other_ref, out_ref, token_ref):
+        token_ref[...] = jnp.zeros_like(token_ref)
         for which, ref in enumerate((own_ref, other_ref)):
             block = jnp.concatenate([ref[...], jnp.zeros((deep - cells, width), BF16)], axis=0)
             out_ref[:, which * deep : (which + 1) * deep] = block.T
@@ -167,10 +168,10 @@
         body,
         (own, other),
         [spec, spec],
-        [jax.ShapeDtypeStruct((channels, 2 * deep), BF16)],
-        [pl.BlockSpec((width, 2 * deep), lambda i: (i, 0))],
+        [jax.ShapeDtypeStruct((channels, 2 * deep), BF16), jax.ShapeDtypeStruct((8, 128), F32)],
+        [pl.BlockSpec((width, 2 * deep), lambda i: (i, 0)), whole((8, 128))],
         (channels // width,),
-    )[0]
+    )
 
 
 def column_taps(block, col_count):
@@ -364,9 +365,9 @@
     input_other = swapped(input_flat)
     sums = sums + got_sums
     sums = [sums] + [around(sums, steps) for steps in (2, 1, 3)]
-    lhs = transposed(input_flat, input_other)
+    lhs, token = transposed(input_flat, input_other)
     gain = norm_gain.reshape(1, channels_out)
-    even, odd, far = pre_gradient(place, gain, sums, mine, theirs, image_count, cell_count)
+    even, odd, far = pre_gradient(token, place, gain, sums, mine, theirs, image_count, cell_count)
     far = around(far, 2)
     up = around(even, 1)
     down = around(odd, X - 1)

time: 81.1 us -> 80.8 us (level)
  local copies, waits for them, and re-layouts: 11.9 us -> 11 us
    unnamed x12, local copies, waits for them, and re-layouts: 5.28 us -> 4.28 us
  transfers between devices with their start and end apart: 18 -> 18, of which waited for: 7 -> 6; matrix products, arithmetic and copies ran while one was open for 8% -> 8% of each run, Pallas kernels for 24% -> 24%
where the time goes in v15:
time: 80.8 us; the launch traced here: 80.3 us
  starting transfers between devices  37.9 us (47%)
  Pallas kernels  20.3 us (25%)
  local copies, waits for them, and re-layouts  11 us (14%)
  waiting for transfers between devices  7.79 us (10%)
  other arithmetic  2.6 us (3%)
    pallas_call x7, Pallas kernels, kernel_call(): pl.pallas_call(body, grid=grid, in_specs=in_specs, out_specs=out_specs, o...  20.3 us
    ppermute x5, starting transfers between devices, swapped(): return lax.ppermute(value, 'core', [(0, 1), (1, 0)])  12.7 us
    all_to_all x1, starting transfers between devices, exchanged(): return lax.all_to_all(value, AXES, 0, 0, axis_index_groups=groups)  11 us
    ppermute x6, starting transfers between devices, crossed(): return lax.ppermute(value, AXES, pairs)  7.42 us
    ppermute x6, starting transfers between devices, around(): lax.ppermute(value, 'x', [(source, (source + steps) % X) for source in ra...  6.78 us
    transpose x1, local copies, waits for them, and re-layouts, per_device(): jnp.transpose(weight, (1, 2, 0)).reshape(9 * channels_out, channels_in)  6.66 us
    unnamed x12, local copies, waits for them, and re-layouts  4.28 us
    ppermute x6, waiting for transfers between devices, crossed(): return lax.ppermute(value, AXES, pairs)  3.31 us
  transfers between devices with their start and end apart: 18, of which 6 were waited for; matrix products, arithmetic and copies ran while one was open for 8% of the time, Pallas kernels for 24%

profile of v15, /device:TPU:1, one launch (start us, length us, event | category | flops | bytes accessed | tf_op | source)
XLA Modules:
  0.0 80.3 jit_solution(10752521476311629991)
XLA Ops:
  0.6 1.9 %fusion.2 = (f32[2,256]{1,0:T(2,128)S(1)}, f32[2,256]{1,0:T(2,128)S(1)}, f32[2,256]{1,0:T(2,128)S(1)}, f32[2,256]{1,0:T(2,128)S(1)}) fusion(s32[2,6,72,256]{3,2,1,0:T(8,128)} %param.9, bf16[2,6,72,256]{3,2,1,0:T(8,128)(2,1)} %param.8, bf16[2,6,72,256]{3,2,1,0:T(8,128)(2,1)} %param.7), kind=kLoop, calls=%fused_computation.7 | loop fusion | flops 2209792 | bytes 1777664 | tf_op jit(solution)/shard_map/reduce_sum | solution.py:81
  2.5 3.3 %collective-permute-start = (f32[8,256]{1,0:T(8,128)S(1)}, f32[8,256]{1,0:T(8,128)S(1)}, u32[]{:S(2)}, u32[]{:S(2)}) collective-permute-start(f32[8,256]{1,0:T(8,128)S(1)} %reshape.45), channel_id=1, source_target_pairs={{0,1},{1,0},{2,3},{3,2},{4,5},{5,4},{6,7},{7,6},{8,9},{9,8},{10,11... | collective-permute-start | bytes 24584 | tf_op jit(solution)/shard_map/ppermute | solution.py:35
  5.8 2.4 %shard_map.77 = (bf16[2,864,128]{2,1,0:T(8,128)(2,1)}, bf16[2,864,128]{2,1,0:T(8,128)(2,1)}) custom-call(s32[1]{0:T(128)} %bitcast.place_ref, bf16[864,256]{1,0:T(8,128)(2,1)} %bitcast.25, bf16[864,256]{1,0:T(8,128)(2,1)} %bitcast.24, s32[864,256]{1,0:T(8,128)} %bitcast.23), custom_call_target="tpu_custom_call" | custom-call | bytes 2654212 | tf_op jit(solution)/shard_map/pallas_call | solution.py:65
  8.2 0.0 collective-permute-done
  8.2 0.1 collective-permute-start.1
  8.4 0.5 collective-permute-start.5
  8.8 1.0 %collective-permute-start.2 = (f32[8,256]{1,0:T(8,128)S(1)}, f32[8,256]{1,0:T(8,128)S(1)}, u32[]{:S(2)}, u32[]{:S(2)}) collective-permute-start(f32[8,256]{1,0:T(8,128)S(1)} %add.21.a_ref), channel_id=1, source_target_pairs={{0,4},{2,6},{4,0},{6,2},{1,5},{3,7},{5,1},{7,3},{8,12},{10,14},{12... | collective-permute-start | bytes 24584 | tf_op jit(solution)/shard_map/ppermute | solution.py:39
  9.9 0.3 collective-permute-start.3
  10.2 2.4 %collective-permute-start.4 = (f32[8,256]{1,0:T(8,128)S(1)}, f32[8,256]{1,0:T(8,128)S(1)}, u32[]{:S(2)}, u32[]{:S(2)}) collective-permute-start(f32[8,256]{1,0:T(8,128)S(1)} %add.21.a_ref), channel_id=1, source_target_pairs={{0,6},{2,0},{4,2},{6,4},{1,7},{3,1},{5,3},{7,5},{8,14},{10,8},{12,... | collective-permute-start | bytes 24584 | tf_op jit(solution)/shard_map/ppermute | solution.py:39
  12.5 0.1 collective-permute-done.1.other_ref
  12.7 1.7 %shard_map.78 = (bf16[1024,1792]{1,0:T(8,128)(2,1)S(1)}, f32[8,128]{1,0:T(8,128)S(1)}) custom-call(bf16[864,1024]{1,0:T(8,128)(2,1)S(1)} %bitcast.20, bf16[864,1024]{1,0:T(8,128)(2,1)S(1)} %collective-permute-done.1.other_ref), custom_call_target="tpu_custom_call" | custom-call | bytes 7213056 | tf_op jit(solution)/shard_map/pallas_call | solution.py:65
  14.3 0.0 collective-permute-done.2.b_ref
  14.4 0.0 collective-permute-done.3.c_ref
  14.4 0.0 collective-permute-done.4.d_ref
  14.4 0.0 collective-permute-done.5.theirs_ref
  14.4 0.4 shard_map.79
  14.8 0.1 collective-permute-start.6
  14.9 2.7 %collective-permute-start.7 = (bf16[864,128]{1,0:T(8,128)(2,1)S(1)}, bf16[864,128]{1,0:T(8,128)(2,1)S(1)}, u32[]{:S(2)}, u32[]{:S(2)}) collective-permute-start(bf16[864,128]{1,0:T(8,128)(2,1)S(1)} %get-tuple-element.49.odd_ref), channel_id=1, source_target_pairs={{0,6},{2,0},{4,2},{6,4},{1,7},{3,1},{5,3},{7,5},{8,14},{10,8},{12,... | collective-permute-start | bytes 663560 | tf_op jit(solution)/shard_map/ppermute | solution.py:39
  17.5 0.4 collective-permute-start.8
  17.9 2.7 %shard_map.80 = (bf16[256,384]{1,0:T(8,128)(2,1)S(1)}, bf16[256,384]{1,0:T(8,128)(2,1)S(1)}, bf16[256,384]{1,0:T(8,128)(2,1)S(1)}, bf16[256,384]{1,0:T(8,128)(2,1)S(1)}) custom-call(s32[1]{0:T(128)} %bitcast.place_ref, bf16[864,128]{1,0:T(8,128)(2,1)S(1)} %get-tuple-element.48.even_ref, bf16[864,128]{1,0:T(8,128)(2,1)S(1)} %get-tuple-element.49.odd_ref, ...), custom_call_target="tpu_custom_call" | custom-call | flops 1409286144 | bytes 4898820 | tf_op jit(solution)/shard_map/pallas_call | solution.py:65
  20.5 0.9 %collective-permute-start.10 = (bf16[256,384]{1,0:T(8,128)(2,1)S(1)}, bf16[256,384]{1,0:T(8,128)(2,1)S(1)}, u32[]{:S(2)}, u32[]{:S(2)}) collective-permute-start(bf16[256,384]{1,0:T(8,128)(2,1)S(1)} %get-tuple-element.60), channel_id=1, source_target_pairs={{0,8},{1,3},{2,10},{3,5},{4,12},{5,7},{6,14},{7,1},{8,16},{9,11},{... | collective-permute-start | bytes 589832 | tf_op jit(solution)/shard_map/ppermute | solution.py:49
  21.5 1.8 %collective-permute-start.11 = (bf16[256,384]{1,0:T(8,128)(2,1)S(1)}, bf16[256,384]{1,0:T(8,128)(2,1)S(1)}, u32[]{:S(2)}, u32[]{:S(2)}) collective-permute-start(bf16[256,384]{1,0:T(8,128)(2,1)S(1)} %get-tuple-element.61), channel_id=1, source_target_pairs={{0,24},{1,7},{2,26},{3,1},{4,28},{5,3},{6,30},{7,5},{8,0},{9,15},{... | collective-permute-start | bytes 589832 | tf_op jit(solution)/shard_map/ppermute | solution.py:49
  23.3 0.0 collective-permute-done.6.up_ref
  23.3 1.4 %collective-permute-start.9 = (bf16[256,384]{1,0:T(8,128)(2,1)S(1)}, bf16[256,384]{1,0:T(8,128)(2,1)S(1)}, u32[]{:S(2)}, u32[]{:S(2)}) collective-permute-start(bf16[256,384]{1,0:T(8,128)(2,1)S(1)} %get-tuple-element.59), channel_id=1, source_target_pairs={{0,16},{1,5},{2,18},{3,7},{4,20},{5,1},{6,22},{7,3},{8,24},{9,13},... | collective-permute-start | bytes 589832 | tf_op jit(solution)/shard_map/ppermute | solution.py:49
  24.7 0.0 collective-permute-done.7.down_ref
  24.7 1.8 %collective-permute-done.8.far_ref = bf16[864,128]{1,0:T(8,128)(2,1)S(1)} collective-permute-done((bf16[864,128]{1,0:T(8,128)(2,1)S(1)}, bf16[864,128]{1,0:T(8,128)(2,1)S(1)}, u32[]{:S(2)}, u32[]{:S(2)}) %collective-permute-start.8) | collective-permute-done | bytes 221216 | tf_op jit(solution)/shard_map/ppermute | solution.py:39
  26.5 5.1 %shard_map.81 = (bf16[256,768]{1,0:T(8,128)(2,1)S(1)}, bf16[256,768]{1,0:T(8,128)(2,1)}, bf16[256,768]{1,0:T(8,128)(2,1)}, bf16[256,768]{1,0:T(8,128)(2,1)S(1)},...) custom-call(s32[1]{0:T(128)} %bitcast.place_ref, bf16[864,128]{1,0:T(8,128)(2,1)S(1)} %get-tuple-element.48.even_ref, ...), custom_call_target="tpu_custom_call" | custom-call | flops 2818572288 | bytes 7675908 | tf_op jit(solution)/shard_map/pallas_call | solution.py:65
  31.6 0.8 %copy-done.4 = bf16[3,864,128]{2,1,0:T(8,128)(2,1)} copy-done((bf16[3,864,128]{2,1,0:T(8,128)(2,1)}, bf16[3,864,128]{2,1,0:T(8,128)(2,1)S(1)}, u32[]{:S(2)}) %copy-start.4) | copy-done | bytes 663576
  32.4 0.0 collective-permute-done.10.refs_2_
  32.4 0.0 collective-permute-done.11.refs_3_
  32.4 0.4 collective-permute-done.9.refs_1_
  32.8 0.1 collective-permute-start.12
  32.9 2.5 %collective-permute-start.13 = (bf16[256,768]{1,0:T(8,128)(2,1)}, bf16[256,768]{1,0:T(8,128)(2,1)S(1)}, u32[]{:S(2)}, u32[]{:S(2)}) collective-permute-start(bf16[256,768]{1,0:T(8,128)(2,1)} %get-tuple-element.68), channel_id=1, source_target_pairs={{0,8},{1,3},{2,10},{3,5},{4,12},{5,7},{6,14},{7,1},{8,16},{9,11},{... | collective-permute-start | bytes 1179656 | tf_op jit(solution)/shard_map/ppermute | solution.py:49
  35.4 0.6 collective-permute-start.14
  36.1 6.7 %copy.8 = bf16[9,256,1024]{2,1,0:T(8,128)(2,1)} copy(bf16[9,256,1024]{1,2,0:T(8,128)(2,1)} %bitcast.22) | data formatting | bytes 9437184 | tf_op jit(solution)/shard_map/transpose | solution.py:382
  42.7 2.9 %collective-permute-done.13.refs_6_ = bf16[256,768]{1,0:T(8,128)(2,1)S(1)} collective-permute-done((bf16[256,768]{1,0:T(8,128)(2,1)}, bf16[256,768]{1,0:T(8,128)(2,1)S(1)}, u32[]{:S(2)}, u32[]{:S(2)}) %collective-permute-start.13) | collective-permute-done | bytes 393248 | tf_op jit(solution)/shard_map/ppermute | solution.py:49
  45.7 1.0 %shard_map.82 = bf16[256,1152]{1,0:T(8,128)(2,1)} custom-call(bf16[256,384]{1,0:T(8,128)(2,1)S(1)} %get-tuple-element.52.refs_0_, bf16[256,384]{1,0:T(8,128)(2,1)S(1)} %collective-permute-done.9.refs_1_, bf16[256,384]{1,0:T(8,128)(2,1)S(1)} %collective-permute-done.10.refs_2_, bf16[256,384]{1,0:T(8,128)(2,1)S(1)} %collective-permute-done.11.refs_3_, ...), custom_call_target="tpu_custom_call" | custom-call | bytes 2949120 | tf_op jit(solution)/shard_map/pallas_call | solution.py:65
  46.7 11.0 %all-to-all-start = ((bf16[32,8,1152]{2,1,0:T(8,128)(2,1)}), bf16[32,8,1152]{2,1,0:T(8,128)(2,1)S(1)}, u32[]{:S(2)}, u32[]{:S(2)}) async-start(bf16[32,8,1152]{2,1,0:T(8,128)(2,1)} %bitcast.12), calls=%async_computation | async-start | bytes 1179648 | tf_op jit(solution)/shard_map/all_to_all | solution.py:55
  57.7 6.6 %collective-permute-start.15 = (bf16[3,864,128]{2,1,0:T(8,128)(2,1)S(1)}, bf16[3,864,128]{2,1,0:T(8,128)(2,1)S(1)}, u32[]{:S(2)}, u32[]{:S(2)}) collective-permute-start(bf16[3,864,128]{2,1,0:T(8,128)(2,1)S(1)} %get-tuple-element.78), channel_id=1, source_target_pairs={{0,1},{1,0},{2,3},{3,2},{4,5},{5,4},{6,7},{7,6},{8,9},{9,8},{10,11... | collective-permute-start | bytes 1990664 | tf_op jit(solution)/shard_map/ppermute | solution.py:35
  64.3 1.7 %collective-permute-done.15.got_ref = bf16[3,864,128]{2,1,0:T(8,128)(2,1)S(1)} collective-permute-done((bf16[3,864,128]{2,1,0:T(8,128)(2,1)S(1)}, bf16[3,864,128]{2,1,0:T(8,128)(2,1)S(1)}, u32[]{:S(2)}, u32[]{:S(2)}) %collective-permute-start.15) | collective-permute-done | bytes 663584 | tf_op jit(solution)/shard_map/ppermute | solution.py:35
  66.1 2.3 %copy-done = bf16[9,256,1024]{2,1,0:T(8,128)(2,1)S(1)} copy-done((bf16[9,256,1024]{2,1,0:T(8,128)(2,1)S(1)}, bf16[9,256,1024]{2,1,0:T(8,128)(2,1)}, u32[]{:S(2)}) %copy-start) | copy-done | bytes 4718616
  68.4 1.1 %copy-done.5 = bf16[3,864,128]{2,1,0:T(8,128)(2,1)S(1)} copy-done((bf16[3,864,128]{2,1,0:T(8,128)(2,1)S(1)}, bf16[3,864,128]{2,1,0:T(8,128)(2,1)}, u32[]{:S(2)}) %copy-start.5) | copy-done | bytes 663576
  69.5 7.1 %shard_map.83 = bf16[864,1024]{1,0:T(8,128)(2,1)} custom-call(s32[1]{0:T(128)} %bitcast.place_ref, bf16[3,864,128]{2,1,0:T(8,128)(2,1)S(1)} %copy-done.5, bf16[3,864,128]{2,1,0:T(8,128)(2,1)S(1)} %collective-permute-done.15.got_ref, bf16[2304,1024]{1,0:T(8,128)(2,1)S(1)} %bitcast.18), custom_call_target="tpu_custom_call" | custom-call | flops 4076863488 | bytes 7815172 | tf_op jit(solution)/shard_map/pallas_call | solution.py:65
  76.6 0.0 all-to-all-done
  76.6 0.1 convert_reduce_fusion.1
  76.7 2.1 %collective-permute-start.16 = (f32[4,1152]{1,0:T(4,128)S(1)}, f32[4,1152]{1,0:T(4,128)S(1)}, u32[]{:S(2)}, u32[]{:S(2)}) collective-permute-start(f32[4,1152]{1,0:T(4,128)S(1)} %constant_dynamic-slice_fusion), channel_id=1, source_target_pairs={{0,1},{1,0},{2,3},{3,2},{4,5},{5,4},{6,7},{7,6},{8,9},{9,8},{10,11... | collective-permute-start | bytes 55304 | tf_op jit(solution)/shard_map/ppermute | solution.py:35
  78.9 0.8 %collective-permute-done.16 = f32[4,1152]{1,0:T(4,128)S(1)} collective-permute-done((f32[4,1152]{1,0:T(4,128)S(1)}, f32[4,1152]{1,0:T(4,128)S(1)}, u32[]{:S(2)}, u32[]{:S(2)}) %collective-permute-start.16) | collective-permute-done | bytes 18464 | tf_op jit(solution)/shard_map/ppermute | solution.py:35
  79.7 0.6 pad_maximum_fusion
  (17 shorter events, 0.1 us)
Async XLA Ops:
  0.6 7.6 %copy-start.1 = (bf16[2,6,72,1024]{3,2,1,0:T(8,128)(2,1)S(1)}, bf16[2,6,72,1024]{3,2,1,0:T(8,128)(2,1)}, u32[]{:S(2)}) copy-start(bf16[2,6,72,1024]{3,2,1,0:T(8,128)(2,1)} %param.6) | copy-start | bytes 5308420
  2.5 5.7 %collective-permute-start = (f32[8,256]{1,0:T(8,128)S(1)}, f32[8,256]{1,0:T(8,128)S(1)}, u32[]{:S(2)}, u32[]{:S(2)}) collective-permute-start(f32[8,256]{1,0:T(8,128)S(1)} %reshape.45), channel_id=1, source_target_pairs={{0,1},{1,0},{2,3},{3,2},{4,5},{5,4},{6,7},{7,6},{8,9},{9,8},{10,11... | collective-permute-start | bytes 24584 | tf_op jit(solution)/shard_map/ppermute | solution.py:35
  8.2 4.4 %collective-permute-start.1 = (bf16[864,1024]{1,0:T(8,128)(2,1)S(1)}, bf16[864,1024]{1,0:T(8,128)(2,1)S(1)}, u32[]{:S(2)}, u32[]{:S(2)}) collective-permute-start(bf16[864,1024]{1,0:T(8,128)(2,1)S(1)} %bitcast.19), channel_id=1, source_target_pairs={{0,1},{1,0},{2,3},{3,2},{4,5},{5,4},{6,7},{7,6},{8,9},{9,8},{10,11... | collective-permute-start | bytes 5308424 | tf_op jit(solution)/shard_map/ppermute | solution.py:35
  8.4 6.0 %collective-permute-start.5 = (bf16[2,864,128]{2,1,0:T(8,128)(2,1)}, bf16[2,864,128]{2,1,0:T(8,128)(2,1)S(1)}, u32[]{:S(2)}, u32[]{:S(2)}) collective-permute-start(bf16[2,864,128]{2,1,0:T(8,128)(2,1)} %get-tuple-element.47), channel_id=1, source_target_pairs={{0,1},{1,0},{2,3},{3,2},{4,5},{5,4},{6,7},{7,6},{8,9},{9,8},{10,11... | collective-permute-start | bytes 1327112 | tf_op jit(solution)/shard_map/ppermute | solution.py:35
  8.8 5.6 %copy-start.2 = (bf16[2,864,128]{2,1,0:T(8,128)(2,1)S(1)}, bf16[2,864,128]{2,1,0:T(8,128)(2,1)}, u32[]{:S(2)}) copy-start(bf16[2,864,128]{2,1,0:T(8,128)(2,1)} %get-tuple-element.46.mine_ref) | copy-start | bytes 1327108
  8.8 5.6 %copy-start.3 = (f32[256]{0:T(256)S(1)}, f32[256]{0:T(256)}, u32[]{:S(2)}) copy-start(f32[256]{0:T(256)} %param.10) | copy-start | bytes 3076
  8.8 5.5 %collective-permute-start.2 = (f32[8,256]{1,0:T(8,128)S(1)}, f32[8,256]{1,0:T(8,128)S(1)}, u32[]{:S(2)}, u32[]{:S(2)}) collective-permute-start(f32[8,256]{1,0:T(8,128)S(1)} %add.21.a_ref), channel_id=1, source_target_pairs={{0,4},{2,6},{4,0},{6,2},{1,5},{3,7},{5,1},{7,3},{8,12},{10,14},{12... | collective-permute-start | bytes 24584 | tf_op jit(solution)/shard_map/ppermute | solution.py:39
  9.9 4.5 %collective-permute-start.3 = (f32[8,256]{1,0:T(8,128)S(1)}, f32[8,256]{1,0:T(8,128)S(1)}, u32[]{:S(2)}, u32[]{:S(2)}) collective-permute-start(f32[8,256]{1,0:T(8,128)S(1)} %add.21.a_ref), channel_id=1, source_target_pairs={{0,2},{2,4},{4,6},{6,0},{1,3},{3,5},{5,7},{7,1},{8,10},{10,12},{12... | collective-permute-start | bytes 24584 | tf_op jit(solution)/shard_map/ppermute | solution.py:39
  10.2 4.2 %collective-permute-start.4 = (f32[8,256]{1,0:T(8,128)S(1)}, f32[8,256]{1,0:T(8,128)S(1)}, u32[]{:S(2)}, u32[]{:S(2)}) collective-permute-start(f32[8,256]{1,0:T(8,128)S(1)} %add.21.a_ref), channel_id=1, source_target_pairs={{0,6},{2,0},{4,2},{6,4},{1,7},{3,1},{5,3},{7,5},{8,14},{10,8},{12,... | collective-permute-start | bytes 24584 | tf_op jit(solution)/shard_map/ppermute | solution.py:39
  14.8 8.5 %collective-permute-start.6 = (bf16[864,128]{1,0:T(8,128)(2,1)S(1)}, bf16[864,128]{1,0:T(8,128)(2,1)S(1)}, u32[]{:S(2)}, u32[]{:S(2)}) collective-permute-start(bf16[864,128]{1,0:T(8,128)(2,1)S(1)} %get-tuple-element.48.even_ref), channel_id=1, source_target_pairs={{0,2},{2,4},{4,6},{6,0},{1,3},{3,5},{5,7},{7,1},{8,10},{10,12},{12... | collective-permute-start | bytes 663560 | tf_op jit(solution)/shard_map/ppermute | solution.py:39
  14.9 9.8 %collective-permute-start.7 = (bf16[864,128]{1,0:T(8,128)(2,1)S(1)}, bf16[864,128]{1,0:T(8,128)(2,1)S(1)}, u32[]{:S(2)}, u32[]{:S(2)}) collective-permute-start(bf16[864,128]{1,0:T(8,128)(2,1)S(1)} %get-tuple-element.49.odd_ref), channel_id=1, source_target_pairs={{0,6},{2,0},{4,2},{6,4},{1,7},{3,1},{5,3},{7,5},{8,14},{10,8},{12,... | collective-permute-start | bytes 663560 | tf_op jit(solution)/shard_map/ppermute | solution.py:39
  17.5 8.9 %collective-permute-start.8 = (bf16[864,128]{1,0:T(8,128)(2,1)S(1)}, bf16[864,128]{1,0:T(8,128)(2,1)S(1)}, u32[]{:S(2)}, u32[]{:S(2)}) collective-permute-start(bf16[864,128]{1,0:T(8,128)(2,1)S(1)} %get-tuple-element.54), channel_id=1, source_target_pairs={{0,4},{2,6},{4,0},{6,2},{1,5},{3,7},{5,1},{7,3},{8,12},{10,14},{12... | collective-permute-start | bytes 663560 | tf_op jit(solution)/shard_map/ppermute | solution.py:39
  20.5 11.9 %collective-permute-start.10 = (bf16[256,384]{1,0:T(8,128)(2,1)S(1)}, bf16[256,384]{1,0:T(8,128)(2,1)S(1)}, u32[]{:S(2)}, u32[]{:S(2)}) collective-permute-start(bf16[256,384]{1,0:T(8,128)(2,1)S(1)} %get-tuple-element.60), channel_id=1, source_target_pairs={{0,8},{1,3},{2,10},{3,5},{4,12},{5,7},{6,14},{7,1},{8,16},{9,11},{... | collective-permute-start | bytes 589832 | tf_op jit(solution)/shard_map/ppermute | solution.py:49
  21.5 11.0 %collective-permute-start.11 = (bf16[256,384]{1,0:T(8,128)(2,1)S(1)}, bf16[256,384]{1,0:T(8,128)(2,1)S(1)}, u32[]{:S(2)}, u32[]{:S(2)}) collective-permute-start(bf16[256,384]{1,0:T(8,128)(2,1)S(1)} %get-tuple-element.61), channel_id=1, source_target_pairs={{0,24},{1,7},{2,26},{3,1},{4,28},{5,3},{6,30},{7,5},{8,0},{9,15},{... | collective-permute-start | bytes 589832 | tf_op jit(solution)/shard_map/ppermute | solution.py:49
  23.3 9.5 %collective-permute-start.9 = (bf16[256,384]{1,0:T(8,128)(2,1)S(1)}, bf16[256,384]{1,0:T(8,128)(2,1)S(1)}, u32[]{:S(2)}, u32[]{:S(2)}) collective-permute-start(bf16[256,384]{1,0:T(8,128)(2,1)S(1)} %get-tuple-element.59), channel_id=1, source_target_pairs={{0,16},{1,5},{2,18},{3,7},{4,20},{5,1},{6,22},{7,3},{8,24},{9,13},... | collective-permute-start | bytes 589832 | tf_op jit(solution)/shard_map/ppermute | solution.py:49
  31.6 0.8 %copy-start.4 = (bf16[3,864,128]{2,1,0:T(8,128)(2,1)}, bf16[3,864,128]{2,1,0:T(8,128)(2,1)S(1)}, u32[]{:S(2)}) copy-start(bf16[3,864,128]{2,1,0:T(8,128)(2,1)S(1)} %get-tuple-element.77.held_ref) | copy-start | bytes 1990660
  32.8 9.9 %collective-permute-start.12 = (bf16[256,768]{1,0:T(8,128)(2,1)}, bf16[256,768]{1,0:T(8,128)(2,1)S(1)}, u32[]{:S(2)}, u32[]{:S(2)}) collective-permute-start(bf16[256,768]{1,0:T(8,128)(2,1)} %get-tuple-element.67), channel_id=1, source_target_pairs={{0,16},{1,5},{2,18},{3,7},{4,20},{5,1},{6,22},{7,3},{8,24},{9,13},... | collective-permute-start | bytes 1179656 | tf_op jit(solution)/shard_map/ppermute | solution.py:49
  32.9 12.8 %collective-permute-start.13 = (bf16[256,768]{1,0:T(8,128)(2,1)}, bf16[256,768]{1,0:T(8,128)(2,1)S(1)}, u32[]{:S(2)}, u32[]{:S(2)}) collective-permute-start(bf16[256,768]{1,0:T(8,128)(2,1)} %get-tuple-element.68), channel_id=1, source_target_pairs={{0,8},{1,3},{2,10},{3,5},{4,12},{5,7},{6,14},{7,1},{8,16},{9,11},{... | collective-permute-start | bytes 1179656 | tf_op jit(solution)/shard_map/ppermute | solution.py:49
  35.4 10.2 %collective-permute-start.14 = (bf16[256,768]{1,0:T(8,128)(2,1)S(1)}, bf16[256,768]{1,0:T(8,128)(2,1)S(1)}, u32[]{:S(2)}, u32[]{:S(2)}) collective-permute-start(bf16[256,768]{1,0:T(8,128)(2,1)S(1)} %get-tuple-element.69), channel_id=1, source_target_pairs={{0,24},{1,7},{2,26},{3,1},{4,28},{5,3},{6,30},{7,5},{8,0},{9,15},{... | collective-permute-start | bytes 1179656 | tf_op jit(solution)/shard_map/ppermute | solution.py:49
  46.7 29.9 %all-to-all-start = ((bf16[32,8,1152]{2,1,0:T(8,128)(2,1)}), bf16[32,8,1152]{2,1,0:T(8,128)(2,1)S(1)}, u32[]{:S(2)}, u32[]{:S(2)}) async-start(bf16[32,8,1152]{2,1,0:T(8,128)(2,1)} %bitcast.12), calls=%async_computation | async-start | bytes 1179648 | tf_op jit(solution)/shard_map/all_to_all | solution.py:55
  57.7 8.4 %collective-permute-start.15 = (bf16[3,864,128]{2,1,0:T(8,128)(2,1)S(1)}, bf16[3,864,128]{2,1,0:T(8,128)(2,1)S(1)}, u32[]{:S(2)}, u32[]{:S(2)}) collective-permute-start(bf16[3,864,128]{2,1,0:T(8,128)(2,1)S(1)} %get-tuple-element.78), channel_id=1, source_target_pairs={{0,1},{1,0},{2,3},{3,2},{4,5},{5,4},{6,7},{7,6},{8,9},{9,8},{10,11... | collective-permute-start | bytes 1990664 | tf_op jit(solution)/shard_map/ppermute | solution.py:35
  66.1 2.3 %copy-start = (bf16[9,256,1024]{2,1,0:T(8,128)(2,1)S(1)}, bf16[9,256,1024]{2,1,0:T(8,128)(2,1)}, u32[]{:S(2)}) copy-start(bf16[9,256,1024]{2,1,0:T(8,128)(2,1)} %copy.8) | copy-start | bytes 14155780
  68.4 1.1 %copy-start.5 = (bf16[3,864,128]{2,1,0:T(8,128)(2,1)S(1)}, bf16[3,864,128]{2,1,0:T(8,128)(2,1)}, u32[]{:S(2)}) copy-start(bf16[3,864,128]{2,1,0:T(8,128)(2,1)} %copy-done.4) | copy-start | bytes 1990660
  76.7 3.0 %collective-permute-start.16 = (f32[4,1152]{1,0:T(4,128)S(1)}, f32[4,1152]{1,0:T(4,128)S(1)}, u32[]{:S(2)}, u32[]{:S(2)}) collective-permute-start(f32[4,1152]{1,0:T(4,128)S(1)} %constant_dynamic-slice_fusion), channel_id=1, source_target_pairs={{0,1},{1,0},{2,3},{3,2},{4,5},{5,4},{6,7},{7,6},{8,9},{9,8},{10,11... | collective-permute-start | bytes 55304 | tf_op jit(solution)/shard_map/ppermute | solution.py:35
